TPU v7x, 256 devices: a whole 4x4x8 slice. The times are simulated.
256 devices in a mesh: batch: 4 (over y), lat: 4 (over x_hi, core), lon: 16 (over z, x_lo).
Axes of the slice: x: 4 (x_hi: 2, x_lo: 2; x = x_hi * 2 + x_lo), y: 4, z: 8, core: 2. Of those that a mesh axis runs over, the one named last changes fastest.
Arguments:
- bottom_codes: int32 [4, 128, 256], P('batch', 'lat', 'lon'), may hold values from 0 to 511
- mask_flags: int32 [4, 128, 256], P('batch', 'lat', 'lon'), may hold values 0 or 1
- top_codes: int32 [4, 64, 128], P('batch', 'lat', 'lon'), may hold values from 0 to 511
- bottom_table: bfloat16 [512, 1024], replicated, may hold values from -3 to 3
- top_table: bfloat16 [512, 1024], replicated, may hold values from -3 to 3
- mask_vector: bfloat16 [1024], replicated, may hold values from -3 to 3
- qkv_weight: bfloat16 [1024, 1536], replicated, may hold values from -0.3 to 0.3
- out_weight: bfloat16 [1024, 512], replicated, may hold values from -0.5 to 0.5
- cotangent: bfloat16 [4, 128, 256, 1024], P('batch', 'lat', 'lon'), may hold values from -6 to 6
Outputs:
- output: bfloat16 [4, 128, 256, 1024], P('batch', 'lat', 'lon')
- grad_input: bfloat16 [4, 128, 256, 1024], P('batch', 'lat', 'lon')
- grad_qkv: float32 [1024, 1536], P(('lat', 'lon'))
- grad_out: float32 [1024, 512], P(('lat', 'lon'))
All inputs are finite; a program needn't handle non-finite values. No bound on the sum of `mask_flags` on one device may be relied on, other than what follows from the above.
Results may differ from a plain program's by a relative error of at most 0.012.
Values may be sent and summed in bfloat16 or wider, within the bound.
No kernel may reach another device: no remote copies, remote signals or barrier semaphores. Data moves between devices by JAX's collectives and lax.ppermute only.
A program may use at most 192 MiB of HBM per device.

v0:
```python
import math

import jax
import jax.numpy as jnp
from jax import lax
from jax.sharding import PartitionSpec as P

HEADS = 8
HDIM = 64
WIN = 8
HW = 512
SHIFT = 4


epsilon = 1e-05


def from_behind(x, axis, by):
    peers = lax.axis_size(axis)
    return lax.ppermute(x, axis, [(i, (i + by) % peers) for i in range(peers)])


def contract(form, left_side, right_side):
    return jnp.einsum(form, left_side, right_side, preferred_element_type=jnp.float32)


def window_split(grid, height, breadth):
    features = grid.shape[-1]
    grid = grid.reshape(height // WIN, WIN, breadth // WIN, WIN, features)
    grid = grid.transpose(0, 2, 1, 3, 4)
    return grid.reshape(height // WIN * (breadth // WIN), WIN * WIN, features)


def window_join(windows, height, breadth):
    features = windows.shape[-1]
    grid = windows.reshape(height // WIN, breadth // WIN, WIN, WIN, features)
    grid = grid.transpose(0, 2, 1, 3, 4)
    return grid.reshape(height, breadth, features)


def embed_codes(bottom_grid, mask_grid, top_grid, bottom_table, top_table, mask_vector):
    bottom_rows = jnp.take(bottom_table, bottom_grid, axis=0).astype(jnp.float32)
    bottom_rows = jnp.where(
        (mask_grid == 1)[:, :, None], mask_vector.astype(jnp.float32)[None, None, :], bottom_rows
    )
    upper_rows = jnp.take(top_table, top_grid, axis=0).astype(jnp.float32)
    top_height, top_breadth, model_width = upper_rows.shape
    upper_rows = jnp.broadcast_to(
        upper_rows[:, None, :, None, :], (top_height, 2, top_breadth, 2, model_width)
    )
    upper_rows = upper_rows.reshape(2 * top_height, 2 * top_breadth, model_width)
    return (bottom_rows + upper_rows).astype(jnp.bfloat16)


def block_pass(embedded, cotangent, qkv_weight, out_weight, wrap_part):
    height, breadth, model_width = embedded.shape
    token_count = height * breadth
    score_scale = 1.0 / math.sqrt(HDIM)
    inputs = embedded.reshape(token_count, model_width).astype(jnp.float32)
    centred = inputs - jnp.mean(inputs, axis=1, keepdims=True)
    inverse = lax.rsqrt(jnp.mean(centred * centred, axis=1, keepdims=True) + epsilon)
    standard = centred * inverse
    normed = standard.astype(jnp.bfloat16)
    projected = jnp.dot(normed, qkv_weight, preferred_element_type=jnp.float32).astype(jnp.bfloat16)
    windows = window_split(projected.reshape(height, breadth, 3 * HW), height, breadth)
    window_count = windows.shape[0]
    per_head = windows.reshape(window_count, WIN * WIN, 3, HEADS, HDIM)
    query_heads = per_head[:, :, 0]
    key_heads = per_head[:, :, 1]
    value_heads = per_head[:, :, 2]
    parts = window_split(wrap_part.astype(jnp.int32)[:, :, None], height, breadth)[:, :, 0]
    allowed = parts[:, :, None] == parts[:, None, :]
    scores = contract("wqhd,wkhd->whqk", query_heads, key_heads) * score_scale
    scores = jnp.where(allowed[:, None, :, :], scores, -1e30)
    highest = jnp.max(scores, axis=-1, keepdims=True)
    powers = jnp.exp(scores - highest)
    shares = powers / jnp.sum(powers, axis=-1, keepdims=True)
    shares_bf = shares.astype(jnp.bfloat16)
    mixed = contract("whqk,wkhd->wqhd", shares_bf, value_heads).astype(jnp.bfloat16)
    attended = window_join(mixed.reshape(window_count, WIN * WIN, HW), height, breadth).reshape(
        token_count, HW
    )
    branch = lax.dot_general(
        attended, out_weight, (((1,), (1,)), ((), ())), preferred_element_type=jnp.float32
    )
    output = (inputs + branch).astype(jnp.bfloat16)
    upstream = cotangent.reshape(token_count, model_width)
    grad_attended = jnp.dot(upstream, out_weight, preferred_element_type=jnp.float32).astype(
        jnp.bfloat16
    )
    grad_heads = window_split(grad_attended.reshape(height, breadth, HW), height, breadth)
    grad_heads = grad_heads.reshape(window_count, WIN * WIN, HEADS, HDIM)
    grad_shares = contract("wqhd,wkhd->whqk", grad_heads, value_heads)
    row_delta = jnp.sum(shares * grad_shares, axis=-1, keepdims=True)
    grad_scores = (shares * (grad_shares - row_delta) * score_scale).astype(jnp.bfloat16)
    grad_query = contract("whqk,wkhd->wqhd", grad_scores, key_heads)
    grad_key = contract("whqk,wqhd->wkhd", grad_scores, query_heads)
    grad_value = contract("whqk,wqhd->wkhd", shares_bf, grad_heads)
    grad_windows = jnp.stack([grad_query, grad_key, grad_value], axis=2).astype(jnp.bfloat16)
    grad_windows = grad_windows.reshape(window_count, WIN * WIN, 3 * HW)
    grad_projected = window_join(grad_windows, height, breadth).reshape(token_count, 3 * HW)
    grad_standard = lax.dot_general(
        grad_projected, qkv_weight, (((1,), (1,)), ((), ())), preferred_element_type=jnp.float32
    )
    grad_inputs = inverse * (
        grad_standard
        - jnp.mean(grad_standard, axis=1, keepdims=True)
        - standard * jnp.mean(grad_standard * standard, axis=1, keepdims=True)
    )
    grad_embedded = (upstream.astype(jnp.float32) + grad_inputs).astype(jnp.bfloat16)
    return (
        output.reshape(height, breadth, model_width),
        grad_embedded.reshape(height, breadth, model_width),
        normed,
        grad_projected,
        attended,
        upstream,
    )


def roll_pair(first_grid, second_grid):
    arrived = from_behind((first_grid[-SHIFT:], second_grid[-SHIFT:]), "lat", 1)
    first_grid = jnp.concatenate([arrived[0], first_grid[:-SHIFT]], axis=0)
    second_grid = jnp.concatenate([arrived[1], second_grid[:-SHIFT]], axis=0)
    arrived = from_behind((first_grid[:, -SHIFT:], second_grid[:, -SHIFT:]), "lon", 1)
    first_grid = jnp.concatenate([arrived[0], first_grid[:, :-SHIFT]], axis=1)
    second_grid = jnp.concatenate([arrived[1], second_grid[:, :-SHIFT]], axis=1)
    return (first_grid, second_grid)


def roll_back(output_grid, grad_grid):
    arrived = from_behind((output_grid[:SHIFT], grad_grid[:SHIFT]), "lat", -1)
    output_grid = jnp.concatenate([output_grid[SHIFT:], arrived[0]], axis=0)
    grad_grid = jnp.concatenate([grad_grid[SHIFT:], arrived[1]], axis=0)
    arrived = from_behind((output_grid[:, :SHIFT], grad_grid[:, :SHIFT]), "lon", -1)
    output_grid = jnp.concatenate([output_grid[:, SHIFT:], arrived[0]], axis=1)
    grad_grid = jnp.concatenate([grad_grid[:, SHIFT:], arrived[1]], axis=1)
    return (output_grid, grad_grid)


def reduce_weight(left_side, right_side):
    own_rows = lax.psum_scatter(
        lax.dot_general(
            left_side, right_side, (((0,), (0,)), ((), ())), preferred_element_type=jnp.float32
        ),
        ("lat", "lon"),
        scatter_dimension=0,
        tiled=True,
    )
    return lax.psum(own_rows, "batch")


def shards(
    bottom_codes,
    mask_flags,
    top_codes,
    bottom_table,
    top_table,
    mask_vector,
    qkv_weight,
    out_weight,
    cotangent,
):
    bottom_grid = bottom_codes[0]
    mask_grid = mask_flags[0]
    top_grid = top_codes[0]
    grad_grid = cotangent[0]
    height, breadth = bottom_grid.shape
    embedded = embed_codes(bottom_grid, mask_grid, top_grid, bottom_table, top_table, mask_vector)
    embedded, grad_grid = roll_pair(embedded, grad_grid)
    first_band = lax.axis_index("lat") == 0
    wrap_part = jnp.broadcast_to(
        ((jnp.arange(height) < SHIFT) & first_band)[:, None], (height, breadth)
    )
    output_grid, grad_embedded, normed, grad_projected, attended, upstream = block_pass(
        embedded, grad_grid, qkv_weight, out_weight, wrap_part
    )
    out_rows = reduce_weight(upstream, attended)
    qkv_rows = reduce_weight(normed, grad_projected)
    output_grid, grad_embedded = roll_back(output_grid, grad_embedded)
    total_cells = (
        lax.axis_size("batch") * height * lax.axis_size("lat") * breadth * lax.axis_size("lon")
    )
    factor = 1.0 / math.sqrt(total_cells)
    return (output_grid[None], grad_embedded[None], qkv_rows * factor, out_rows * factor)


def solution(mesh):
    return jax.shard_map(
        shards,
        mesh=mesh,
        in_specs=(
            P("batch", "lat", "lon"),
            P("batch", "lat", "lon"),
            P("batch", "lat", "lon"),
            P(),
            P(),
            P(),
            P(),
            P(),
            P("batch", "lat", "lon", None),
        ),
        out_specs=(
            P("batch", "lat", "lon", None),
            P("batch", "lat", "lon", None),
            P(("lat", "lon"), None),
            P(("lat", "lon"), None),
        ),
        check_vma=False,
    )
```

profile of v0, /device:TPU:32, one launch (start us, length us, event | category | flops | bytes accessed | tf_op | source)
XLA Modules:
  0.0 671.0 jit_solution(1980307665537883377)
XLA Ops:
  14.9 2.4 gather_fusion.1
  18.1 2.3 broadcast_in_dim.80
  20.4 3.7 reshape.217
  24.1 4.8 gather_fusion
  28.9 2.3 add_convert_fusion
  31.3 3.2 collective-permute-start
  42.1 2.7 collective-permute-start.5
  44.8 4.7 collective-permute-done.1
  57.3 5.1 reshape_reshape.23
  62.3 3.7 fusion.64
  66.0 2.4 copy.56
  68.5 4.1 fusion.65
  72.5 3.3 fusion.32
  75.9 2.4 copy.36
  78.3 2.5 reshape_reshape.24
  90.3 2.4 reshape_reshape.27
  92.6 2.4 copy.45
  95.1 3.3 fusion.42
  98.4 5.8 fusion.37
  104.2 5.8 fusion.34
  110.0 2.7 fusion.33
  112.7 2.5 pad_maximum_fusion
  115.2 4.9 copy.47
  120.1 5.3 convert_element_type.101
  128.3 4.5 fusion.66
  132.9 2.6 fusion.15
  140.7 8.5 %collective-permute-done.6 = bf16[4,16,1024]{2,1,0:T(8,128)(2,1)S(1)} collective-permute-done((bf16[4,16,1024]{2,1,0:T(8,128)(2,1)S(1)}, bf16[4,16,1024]{2,1,0:T(8,128)(2,1)S(1)}, u32[]{:S(2)}, u32[]{:S(2)}) %collective-permute-start.6) | collective-permute-done | bytes 131104 | tf_op jit(solution)/shard_map/ppermute | solution.py:20
  151.5 6.6 collective-permute-done.7
  159.4 190.4 %reduce-scatter.5.cloned.1.call-done = f32[16,512]{1,0:T(8,128)} async-done(((f32[1024,512]{1,0:T(8,128)}), f32[16,512]{1,0:T(8,128)}) %reduce-scatter.5.cloned.1.call-update) | async-done | bytes 32784 | tf_op jit(solution)/shard_map/reduce_scatter | solution.py:142
  349.8 17.4 %psum.15 = f32[16,512]{1,0:T(8,128)S(1)} all-reduce(f32[16,512]{1,0:T(8,128)} %reduce-scatter.5.cloned.1.call-done), channel_id=1, replica_groups=mesh['batch'=4,'lat'=4,'lon'=16] {'batch'}, use_global_device_ids=true, to_apply=%region_10.11 | all-reduce | flops 8192 | bytes 65536 | tf_op jit(solution)/shard_map/psum | solution.py:150
  367.1 251.3 %reduce-scatter.3.cloned.1.call-done = f32[16,1536]{1,0:T(8,128)} async-done(((f32[1024,1536]{1,0:T(8,128)}), f32[16,1536]{1,0:T(8,128)}) %reduce-scatter.3.cloned.1.call-update) | async-done | bytes 98320 | tf_op jit(solution)/shard_map/reduce_scatter | solution.py:142
  619.0 43.9 %all-reduce.2.cloned.1.call-done = f32[16,1536]{1,0:T(8,128)} async-done(((f32[16,1536]{1,0:T(8,128)}), f32[16,1536]{1,0:T(8,128)}) %all-reduce.2.cloned.1.call-update) | async-done | bytes 98320 | tf_op jit(solution)/shard_map/psum | solution.py:150
  (100 shorter events, 47.1 us)
Async XLA Ops:
  7.2 47.0 %copy-start = (bf16[1024,1536]{1,0:T(8,128)(2,1)S(1)}, bf16[1024,1536]{1,0:T(8,128)(2,1)}, u32[]{:S(2)}) copy-start(bf16[1024,1536]{1,0:T(8,128)(2,1)} %param.15) | copy-start | bytes 9437188
  7.2 342.6 %reduce-scatter.5.cloned.1.call-start = ((), (), s32[]{:S(2)}) async-start(), calls=%async_computation.4 | async-start | bytes 2129920 | tf_op jit(solution)/shard_map/reduce_scatter | solution.py:142
  8.9 31.3 %collective-permute-start.4 = (bf16[4,16,1024]{2,1,0:T(8,128)(2,1)}, bf16[4,16,1024]{2,1,0:T(8,128)(2,1)S(1)}, u32[]{:S(2)}, u32[]{:S(2)}) collective-permute-start(bf16[4,16,1024]{2,1,0:T(8,128)(2,1)} %slice_bitcast_fusion.1), channel_id=1, source_target_pairs={{0,16},{16,32},{32,48},{48,0},{1,17},{17,33},{33,49},{49,1},{2,18}... | collective-permute-start | bytes 393224 | tf_op jit(solution)/shard_map/ppermute | solution.py:20
  24.1 4.8 copy-start.12
  28.9 5.6 copy-start.9
  31.3 6.7 %collective-permute-start = (bf16[4,16,1024]{2,1,0:T(8,128)(2,1)S(1)}, bf16[4,16,1024]{2,1,0:T(8,128)(2,1)S(1)}, u32[]{:S(2)}, u32[]{:S(2)}) collective-permute-start(bf16[4,16,1024]{2,1,0:T(8,128)(2,1)S(1)} %slice.104), channel_id=1, source_target_pairs={{0,16},{16,32},{32,48},{48,0},{1,17},{17,33},{33,49},{49,1},{2,18}... | collective-permute-start | bytes 393224 | tf_op jit(solution)/shard_map/ppermute | solution.py:20
  38.0 11.4 %copy-start.5 = (bf16[28,16,1024]{2,1,0:T(8,128)(2,1)S(1)}, bf16[28,16,1024]{2,1,0:T(8,128)(2,1)}, u32[]{:S(2)}) copy-start(bf16[28,16,1024]{2,1,0:T(8,128)(2,1)} %slice.105) | copy-start | bytes 2752516
  39.3 10.1 %collective-permute-start.1 = (bf16[32,4,1024]{2,1,0:T(4,128)(2,1)S(1)}, bf16[32,4,1024]{2,1,0:T(4,128)(2,1)S(1)}, u32[]{:S(2)}, u32[]{:S(2)}) collective-permute-start(bf16[32,4,1024]{2,1,0:T(4,128)(2,1)S(1)} %pad_maximum_fusion.6), channel_id=1, source_target_pairs={{0,1},{1,2},{2,3},{3,4},{4,5},{5,6},{6,7},{7,8},{8,9},{9,10},{10,1... | collective-permute-start | bytes 786440 | tf_op jit(solution)/shard_map/ppermute | solution.py:20
  42.1 39.8 %collective-permute-start.5 = (bf16[32,4,1024]{2,1,0:T(4,128)(2,1)}, bf16[32,4,1024]{2,1,0:T(4,128)(2,1)}, u32[]{:S(2)}, u32[]{:S(2)}) collective-permute-start(bf16[32,4,1024]{2,1,0:T(4,128)(2,1)} %pad_maximum_fusion.4), channel_id=1, source_target_pairs={{0,1},{1,2},{2,3},{3,4},{4,5},{5,6},{6,7},{7,8},{8,9},{9,10},{10,1... | collective-permute-start | bytes 786440 | tf_op jit(solution)/shard_map/ppermute | solution.py:20
  81.9 1.9 copy-start.6
  83.8 1.0 copy-start.3
  86.9 531.5 %reduce-scatter.3.cloned.1.call-start = ((), (), s32[]{:S(2)}) async-start(), calls=%async_computation.2 | async-start | bytes 6389760 | tf_op jit(solution)/shard_map/reduce_scatter | solution.py:142
  110.0 2.7 copy-start.10
  110.0 2.8 copy-start.11
  125.4 1.7 copy-start.1
  127.1 1.2 copy-start.7
  132.8 530.1 %all-reduce.2.cloned.1.call-start = ((), (), s32[]{:S(2)}) async-start(), calls=%async_computation.3 | async-start | bytes 196608 | tf_op jit(solution)/shard_map/psum | solution.py:150
  132.9 2.7 copy-start.2
  132.9 2.7 copy-start.8
  135.5 2.1 copy-start.4
  135.5 4.6 collective-permute-start.2
  138.5 10.7 %collective-permute-start.6 = (bf16[4,16,1024]{2,1,0:T(8,128)(2,1)S(1)}, bf16[4,16,1024]{2,1,0:T(8,128)(2,1)S(1)}, u32[]{:S(2)}, u32[]{:S(2)}) collective-permute-start(bf16[4,16,1024]{2,1,0:T(8,128)(2,1)S(1)} %bitcast.159), channel_id=1, source_target_pairs={{0,48},{16,0},{32,16},{48,32},{1,49},{17,1},{33,17},{49,33},{2,50}... | collective-permute-start | bytes 393224 | tf_op jit(solution)/shard_map/ppermute | solution.py:20
  140.2 10.1 %collective-permute-start.3 = (bf16[32,4,1024]{2,1,0:T(4,128)(2,1)S(1)}, bf16[32,4,1024]{2,1,0:T(4,128)(2,1)S(1)}, u32[]{:S(2)}, u32[]{:S(2)}) collective-permute-start(bf16[32,4,1024]{2,1,0:T(4,128)(2,1)S(1)} %pad_maximum_fusion.5), channel_id=1, source_target_pairs={{0,15},{1,0},{2,1},{3,2},{4,3},{5,4},{6,5},{7,6},{8,7},{9,8},{10,9... | collective-permute-start | bytes 786440 | tf_op jit(solution)/shard_map/ppermute | solution.py:20
  149.3 8.8 %collective-permute-start.7 = (bf16[32,4,1024]{2,1,0:T(4,128)(2,1)S(1)}, bf16[32,4,1024]{2,1,0:T(4,128)(2,1)S(1)}, u32[]{:S(2)}, u32[]{:S(2)}) collective-permute-start(bf16[32,4,1024]{2,1,0:T(4,128)(2,1)S(1)} %pad_maximum_fusion.3), channel_id=1, source_target_pairs={{0,15},{1,0},{2,1},{3,2},{4,3},{5,4},{6,5},{7,6},{8,7},{9,8},{10,9... | collective-permute-start | bytes 786440 | tf_op jit(solution)/shard_map/ppermute | solution.py:20
Sparse Core Ops, SparseCore 0:
  87.0 262.6 reduce-scatter.4
  352.4 265.8 reduce-scatter.2
  620.7 42.2 all-reduce.1
where the time goes:
time: 673 us; the launch traced here: 671 us
  waiting for transfers between devices  506 us (75%)
  local copies, waits for them, and re-layouts  57.9 us (9%)
  matrix products  40.3 us (6%)
  other arithmetic  26.5 us (4%)
  blocking collectives  17.4 us (3%)
  between operations  14.1 us (2%)
  starting transfers between devices  9.17 us (1%)
    reduce_scatter x2, waiting for transfers between devices, reduce_weight(): lax.psum_scatter(lax.dot_general(left_side, right_side, (((0,), (0,)), ((...  442 us
    psum x1, waiting for transfers between devices, reduce_weight(): return lax.psum(own_rows, 'batch')  43.9 us
    dot_general x5, matrix products, contract(): jnp.einsum(form, left_side, right_side, preferred_element_type=jnp.float32)  21 us
    ppermute x8, waiting for transfers between devices, from_behind(): return lax.ppermute(x, axis, [(i, (i + by) % peers) for i in range(peers)])  20.1 us
    psum x1, blocking collectives, reduce_weight(): return lax.psum(own_rows, 'batch')  17.4 us
  transfers between devices with their start and end apart: 11, of which 7 were waited for; matrix products, arithmetic and copies ran while one was open for 17% of the time, Pallas kernels for 0%

commit v1 on v0

v1 whole, which is shorter than its diff:
```python
import functools
import math

import jax
import jax.numpy as jnp
from jax import lax
from jax.experimental import pallas as pl
from jax.experimental.pallas import tpu as pltpu
from jax.sharding import PartitionSpec as P

HEADS = 8
HDIM = 64
WIN = 8
HW = 512
SHIFT = 4
EPS = 1e-05
MODEL = 1024
ROWS, COLS = 32, 16
TOKENS = ROWS * COLS
BAND = WIN * COLS
BANDS = TOKENS // BAND
CHUNKS = 2
CW = HW // CHUNKS
F32 = jnp.float32
BF16 = jnp.bfloat16
GRID = ("xh", "core", "z", "xl")
NB, NLAT, NLON = 4, 4, 16


def dot(a, b, ca, cb):
    return lax.dot_general(a, b, (((ca,), (cb,)), ((), ())), preferred_element_type=F32)


def vmem():
    return pl.BlockSpec(memory_space=pltpu.VMEM)


def smem():
    return pl.BlockSpec(memory_space=pltpu.SMEM)


def call(kernel, outs, operands, specs, flops, nbytes, trans=0, limit=28, name=None):
    return pl.pallas_call(
        kernel,
        out_shape=outs,
        in_specs=specs,
        out_specs=jax.tree.map(lambda _: vmem(), outs),
        compiler_params=pltpu.CompilerParams(vmem_limit_bytes=limit * 2**20),
        cost_estimate=pl.CostEstimate(flops=flops, bytes_accessed=nbytes, transcendentals=trans),
        name=name,
    )(*operands)


def sds(shape, dtype=BF16):
    return jax.ShapeDtypeStruct(shape, dtype)


def iota(shape, dim):
    return lax.broadcasted_iota(jnp.int32, shape, dim)


def moments(x):
    mean = jnp.mean(x, axis=1, keepdims=True)
    centred = x - mean
    inverse = lax.rsqrt(jnp.mean(centred * centred, axis=1, keepdims=True) + EPS)
    return centred, inverse


CODES = 128
WIDE = MODEL + CODES
MSG = SHIFT * (ROWS - SHIFT)
OWN = (ROWS - SHIFT) * COLS
LATE = COLS - SHIFT


def hot(mask):
    return mask.astype(F32).astype(BF16)


def pack_kernel(bottom, flags, top, cot, own, up, left, diag):
    def digits(codes, rows, row_of, lane_of):
        width = codes.shape[1]
        parts = jnp.concatenate([codes >> 4, codes & 15], axis=1).astype(F32).astype(BF16)
        pick = hot(row_of(iota((TOKENS, rows), 0)) == iota((TOKENS, rows), 1))
        spread = dot(pick, parts, 1, 0)
        t, lane = iota(spread.shape, 0), iota(spread.shape, 1)
        inside = jnp.where(lane < width, lane, lane - width) == lane_of(t)
        spread = jnp.where(inside, spread, 0.0)
        return (
            jnp.sum(jnp.where(lane < width, spread, 0.0), axis=1, keepdims=True),
            jnp.sum(jnp.where(lane < width, 0.0, spread), axis=1, keepdims=True),
        )

    code = jnp.where(flags[...] == 1, 512, bottom[...])
    bh, bl = digits(code, ROWS, lambda t: t >> 4, lambda t: t & 15)
    th, tl = digits(top[...], ROWS // 2, lambda t: t >> 5, lambda t: (t & 15) >> 1)
    lane = iota((TOKENS, CODES), 1)
    block = jnp.where(lane == 0, bh, jnp.where(lane == 1, bl, jnp.where(lane == 2, th, tl)))
    block = jnp.where(lane < 4, block, 0.0).astype(BF16)
    own[...] = block
    up[:, :MODEL] = cot[OWN:]
    up[:, MODEL:] = block[OWN:]
    m, t = iota((MSG, OWN), 0), iota((MSG, OWN), 1)
    pick = hot(t == (m >> 2) * COLS + LATE + (m & 3))
    left[:, :MODEL] = dot(pick, cot[:OWN], 1, 0).astype(BF16)
    left[:, MODEL:] = dot(pick, block[:OWN], 1, 0).astype(BF16)
    m, t = iota((16, 64), 0), iota((16, 64), 1)
    pick = hot(t == (m >> 2) * COLS + LATE + (m & 3))
    diag[:, :MODEL] = dot(pick, cot[OWN:], 1, 0).astype(BF16)
    diag[:, MODEL:] = dot(pick, block[OWN:], 1, 0).astype(BF16)


def embed(codes, bt, tt, mv, wq):
    digit = codes.astype(F32)
    cb = (digit[:, 0:1] * 16.0 + digit[:, 1:2]).astype(jnp.int32)
    ct = (digit[:, 2:3] * 16.0 + digit[:, 3:4]).astype(jnp.int32)
    lanes = iota((codes.shape[0], 512), 1)
    x = dot(hot(lanes == cb), bt[...], 1, 0)
    x = jnp.where(cb == 512, mv[...].astype(F32), x)
    x = (x + dot(hot(lanes == ct), tt[...], 1, 0)).astype(BF16)
    centred, inverse = moments(x.astype(F32))
    n = (centred * inverse).astype(BF16)
    return x, n, dot(n, wq[...], 1, 0).astype(BF16)


def own_kernel(codes, bt, tt, mv, wq, emb, normed, proj):
    step = 112
    for at in range(0, OWN, step):
        here = slice(at, at + step)
        emb[here], normed[here], proj[here] = embed(codes[here], bt, tt, mv, wq)


def halo_kernel(up, left, diag, cot, oemb, onormed, oproj, bt, tt, mv, wq, emb, normed, proj, grad):
    p = iota((64, 1), 0) & 15
    m, t = iota((64, 16), 1), iota((64, 16), 0)
    corner = dot(hot(t == (m >> 2) * COLS + LATE + (m & 3)), diag[...], 1, 0)
    upper = jnp.where(p >= LATE, corner, up[...].astype(F32)).astype(BF16)
    grad[0:64] = upper[:, :MODEL]
    emb[0:64], normed[0:64], proj[0:64] = embed(upper[:, MODEL:], bt, tt, mv, wq)
    new = embed(left[:, MODEL:], bt, tt, mv, wq)
    step = 64
    p = iota((step, 1), 0) & 15
    for at in range(0, OWN, step):
        m, t = iota((step, MSG), 1), at + iota((step, MSG), 0)
        spread = hot(t == (m >> 2) * COLS + LATE + (m & 3))
        old, out = slice(at, at + step), slice(64 + at, 64 + at + step)
        for source, values, ref in (
            (cot, left[:, :MODEL], grad),
            (oemb, new[0], emb),
            (onormed, new[1], normed),
            (oproj, new[2], proj),
        ):
            values = dot(spread, values, 1, 0)
            ref[out] = jnp.where(p >= LATE, values, source[old].astype(F32)).astype(BF16)


def attend_kernel(place, q, k, v, normed, cot, ow, att, gp, keep, send):
    grad = dot(cot[...], ow[...], 1, 0).astype(BF16)
    lane = iota((BAND, 128), 1) < 64
    tk, tq = iota((BAND, BAND), 0), iota((BAND, BAND), 1)

    def side(t):
        c = t & 15
        return ((c >= 4) & (c < 12)).astype(jnp.int32)

    same = side(tk) == side(tq)
    whole = (tk >> 6) == (tq >> 6)
    zero = jnp.zeros((BAND, BAND), F32)
    plain = jnp.where(same, zero, -1e30)
    first = jnp.where(whole | (place[0] != 0), plain, -1e30)

    def split(x):
        none = jnp.zeros_like(x)
        return jnp.concatenate([jnp.where(lane, x, none), jnp.where(lane, none, x)], axis=0)

    def pick(x):
        return jnp.where(lane, x[:BAND], x[BAND:])

    for b in range(BANDS):
        bias = first if b == 0 else plain
        here = slice(b * BAND, (b + 1) * BAND)
        for p in range(CW // 128):
            cols = slice(p * 128, (p + 1) * 128)
            qq = q[here, cols]
            kk, vv = split(k[here, cols]), split(v[here, cols])
            da = grad[here, cols]
            s = dot(kk, qq, 1, 1).reshape(2, BAND, BAND) * 0.125 + bias
            e = jnp.exp(s - jnp.max(s, axis=1, keepdims=True))
            share = e * (1.0 / jnp.sum(e, axis=1, keepdims=True))
            sb = share.astype(BF16).reshape(2 * BAND, BAND)
            att[here, cols] = dot(sb, vv, 0, 0).astype(BF16)
            gs = dot(vv, da, 1, 1).reshape(2, BAND, BAND)
            delta = jnp.sum(share * gs, axis=1, keepdims=True)
            ds = (share * (gs - delta) * 0.125).astype(BF16).reshape(2 * BAND, BAND)
            at = p * 128
            gp[here, at : at + 128] = dot(ds, kk, 0, 0).astype(BF16)
            gp[here, CW + at : CW + at + 128] = pick(dot(ds, qq, 1, 0)).astype(BF16)
            gp[here, 2 * CW + at : 2 * CW + at + 128] = pick(dot(sb, da, 1, 0)).astype(BF16)

    core = place[1]
    for half in range(2):
        for out, flip in ((send, 1), (keep, 0)):
            cut = pl.ds(pl.multiple_of(half * 512 + (core ^ flip) * 256, 256), 256)
            out[half, :, 0 : 3 * CW] = dot(normed[:, cut], gp[...], 0, 0).astype(out.dtype)
            out[half, :, 3 * CW :] = dot(cot[:, cut], att[...], 0, 0).astype(out.dtype)


def finish_kernel(emb, cot, wq, ow, att0, att1, gp0, gp1, both):
    for block in range(BANDS):
        here = slice(block * BAND, (block + 1) * BAND)
        x = emb[here].astype(F32)
        att = jnp.concatenate([att0[here], att1[here]], axis=1)
        both[0, here] = (x + dot(att, ow[...], 1, 1)).astype(BF16)
        g0, g1 = gp0[here], gp1[here]
        parts = []
        for i in range(3):
            parts += [g0[:, i * CW : (i + 1) * CW], g1[:, i * CW : (i + 1) * CW]]
        gst = dot(jnp.concatenate(parts, axis=1), wq[...], 1, 1)
        centred, inverse = moments(x)
        standard = centred * inverse
        m1 = jnp.mean(gst, axis=1, keepdims=True)
        m2 = jnp.mean(gst * standard, axis=1, keepdims=True)
        both[1, here] = (cot[here].astype(F32) + inverse * (gst - m1 - standard * m2)).astype(BF16)


W = 4 * CW
Q = W // 4


def cut_x1(place, total, keep, send):
    g = place[2] ^ place[3]
    for xh in range(2):
        keep[xh] = total(xh, xh ^ g)
        send[xh] = total(xh, xh ^ g ^ 1).astype(BF16)


def cut_y1(place, total, keep, send):
    g = place[4] ^ place[5]
    for yh in range(2):
        keep[..., yh * Q : (yh + 1) * Q] = total(2 * yh + (yh ^ g))
        send[..., yh * Q : (yh + 1) * Q] = total(2 * yh + (yh ^ g ^ 1)).astype(BF16)


def lanes(i):
    return pl.ds(pl.multiple_of(i * Q, Q), Q)


def x_core(place, a, b, keep, send):
    cut_x1(place, lambda u, v: a[u, :, v] + b[u, :, v].astype(F32), keep, send)


def x_pair(place, a, b, keep, send):
    xh = place[2]
    keep[...] = a[xh] + b[xh].astype(F32)
    send[...] = (a[xh ^ 1] + b[xh ^ 1].astype(F32)).astype(BF16)


def y_core(place, a, b, keep, send):
    cut_y1(place, lambda i: a[:, :, lanes(i)] + b[:, :, lanes(i)].astype(F32), keep, send)


def y_pair(place, a, b, keep, send):
    yh = place[4]
    keep[...] = a[:, :, lanes(yh)] + b[:, :, lanes(yh)].astype(F32)
    send[...] = (a[:, :, lanes(yh ^ 1)] + b[:, :, lanes(yh ^ 1)].astype(F32)).astype(BF16)


def z_first(place, a, b, c, d, keep, send):
    bit = place[6] & 1
    for k in range(4):
        for out, at in ((keep, 2 * k + bit), (send, 2 * k + (bit ^ 1))):
            out[k, :, 0:Q] = (a[at] + b[at].astype(F32)).astype(out.dtype)
            out[k, :, Q:] = (c[at] + d[at].astype(F32)).astype(out.dtype)


def z_second(place, a, b, keep, send):
    bit = (place[6] >> 1) & 1
    for k in range(2):
        for out, at in ((keep, 2 * k + bit), (send, 2 * k + (bit ^ 1))):
            out[k] = (a[at] + b[at].astype(F32)).astype(out.dtype)


def z_third(place, a, b, keep, send):
    bit = place[6] >> 2
    keep[...] = a[bit] + b[bit].astype(F32)
    send[...] = (a[bit ^ 1] + b[bit ^ 1].astype(F32)).astype(BF16)


def level_kernel(factor, a, b, out):
    out[...] = (a[...] + b[...].astype(F32)) * factor


def spread_kernel(place, *refs):
    qkv, outw = refs[4:]
    for d in range(4):
        who = (2 * place[4] + place[5]) ^ d
        for c in range(CHUNKS):

            @pl.when(who < 3)
            def _():
                qkv[:, pl.ds(pl.multiple_of(who * HW + c * CW, CW), CW)] = refs[d][:, c * Q : (c + 1) * Q]

            @pl.when(who == 3)
            def _():
                outw[:, c * CW : (c + 1) * CW] = refs[d][:, c * Q : (c + 1) * Q]


def permute(x, where):
    pairs = []
    for la in range(NLAT):
        for lo in range(NLON):
            tl, to = where(la, lo)
            pairs.append((la * NLON + lo, tl * NLON + to))
    return lax.ppermute(x, GRID, pairs)


def shift(x, down, right):
    return permute(x, lambda la, lo: ((la + down) % NLAT, (lo + right) % NLON))


def swap(x, axis, flip):
    return lax.ppermute(x, axis, [(i, i ^ flip) for i in range(lax.axis_size(axis))])


def swap_x(x, flip):
    return permute(x, lambda la, lo: (la ^ (flip & 2), lo ^ (flip & 1)))


def halve(kernel, shape, place, *terms):
    size = math.prod(shape)
    return call(
        kernel,
        [sds(shape, F32), sds(shape)],
        (place, *terms),
        [smem()] + [vmem()] * len(terms),
        2 * size,
        16 * size,
        limit=16,
        name=kernel.__name__,
    )


def sum_x_first(place, keep, send):
    fold = (2, 8, 2, 16, W)
    recv = swap(send, "core", 1)
    keep, send = halve(x_core, (2, 8, 16, W), place, keep.reshape(fold), recv.reshape(fold))
    keep, send = halve(x_pair, (8, 16, W), place, keep, swap_x(send, 1))
    keep, send = halve(y_core, (8, 16, 2 * Q), place, keep, swap_x(send, 3))
    keep, send = halve(y_pair, (8, 16, Q), place, keep, swap(send, "batch", 1))
    return keep, swap(send, "batch", 3)


def sum_y_first(place, keep, send):
    recv = swap(send, "core", 1)
    keep, send = halve(y_core, (2, 256, 2 * Q), place, keep, recv)
    keep, send = halve(y_pair, (2, 256, Q), place, keep, swap(send, "batch", 1))
    fold = (2, 8, 2, 16, Q)
    recv = swap(send, "batch", 3)
    keep, send = halve(x_core, (2, 8, 16, Q), place, keep.reshape(fold), recv.reshape(fold))
    keep, send = halve(x_pair, (8, 16, Q), place, keep, swap_x(send, 1))
    return keep, swap_x(send, 3)


def shards(
    bottom_codes, mask_flags, top_codes, bottom_table, top_table, mask_vector, qkv_weight, out_weight, cotangent
):
    core, xh, xl = lax.axis_index("core"), lax.axis_index("xh"), lax.axis_index("xl")
    y, z = lax.axis_index("batch"), lax.axis_index("z")
    place = jnp.stack([2 * xh + core, core, xh, xl, y >> 1, y & 1, z]).astype(jnp.int32)
    grads = cotangent.reshape(TOKENS, MODEL)
    codes, up, left, diag = call(
        pack_kernel,
        [sds((TOKENS, CODES)), sds((64, WIDE)), sds((MSG, WIDE)), sds((16, WIDE))],
        (bottom_codes[0], mask_flags[0], top_codes[0], grads),
        [vmem()] * 4,
        2**28,
        3 * 2**20,
        limit=16,
        name="pack",
    )
    up, left, diag = shift(up, 1, 0), shift(left, 0, 1), shift(diag, 1, 1)
    tables = (bottom_table, top_table, mask_vector.reshape(1, MODEL), qkv_weight)
    own = call(
        own_kernel,
        [sds((OWN, MODEL)), sds((OWN, MODEL)), sds((OWN, 3 * HW))],
        (codes, *tables),
        [vmem()] * 5,
        2 * OWN * 1024 * 2560,
        9 * 2**20,
        limit=24,
        name="own",
    )
    emb, normed, proj, cot = call(
        halo_kernel,
        [sds((TOKENS, MODEL)), sds((TOKENS, MODEL)), sds((TOKENS, 3 * HW)), sds((TOKENS, MODEL))],
        (up, left, diag, grads, *own, *tables),
        [vmem()] * 11,
        2 * 176 * 1024 * 2560,
        12 * 2**20,
        limit=32,
        name="halo",
    )
    atts, gps, summed = [], [], []
    for c in range(CHUNKS):
        block = lambda i: pl.BlockSpec((TOKENS, CW), lambda g, i=i: (0, i))
        full = lambda *shape: pl.BlockSpec(shape, lambda g: (0,) * len(shape))
        att, gp, keep, send = pl.pallas_call(
            attend_kernel,
            grid=(1,),
            out_shape=[
                sds((TOKENS, CW)),
                sds((TOKENS, 3 * CW)),
                sds((2, 256, W), F32),
                sds((2, 256, W)),
            ],
            in_specs=[
                smem(),
                block(c),
                block(CHUNKS + c),
                block(2 * CHUNKS + c),
                full(TOKENS, MODEL),
                full(TOKENS, MODEL),
                pl.BlockSpec((MODEL, CW), lambda g, c=c: (0, c)),
            ],
            out_specs=[
                full(TOKENS, CW),
                full(TOKENS, 3 * CW),
                full(2, 256, W),
                full(2, 256, W),
            ],
            compiler_params=pltpu.CompilerParams(vmem_limit_bytes=28 * 2**20),
            cost_estimate=pl.CostEstimate(flops=3 * 2**30, bytes_accessed=8 * 2**20, transcendentals=2**19),
            name="attend",
        )(place, proj, proj, proj, normed, cot, out_weight)
        atts.append(att)
        gps.append(gp)
        summed += (sum_y_first if c else sum_x_first)(place, keep, send)
    both = call(
        finish_kernel,
        sds((2, TOKENS, MODEL)),
        (emb, cot, qkv_weight, out_weight, *atts, *gps),
        [vmem()] * 8,
        2 * TOKENS * 1024 * 2048,
        10 * 2**20,
        name="finish",
    )
    both = both.reshape(2, ROWS, COLS, MODEL)
    r_up = shift(both[:, :SHIFT], -1, 0)
    r_left = shift(both[:, SHIFT:, LATE:], 0, -1)
    r_diag = shift(both[:, :SHIFT, LATE:], -1, -1)

    def back(i):
        upper = jnp.concatenate([both[i, SHIFT:, :LATE], r_left[i]], axis=1)
        lower = jnp.concatenate([r_up[i, :, :LATE], r_diag[i]], axis=1)
        return jnp.concatenate([upper, lower], axis=0)[None]

    factor = 1.0 / math.sqrt(TOKENS * NB * NLAT * NLON)
    keep, send = halve(z_first, (4, 16, 2 * Q), place, *summed)
    keep, send = halve(z_second, (2, 16, 2 * Q), place, keep, swap(send, "z", 1))
    keep, send = halve(z_third, (16, 2 * Q), place, keep, swap(send, "z", 2))
    level = call(
        functools.partial(level_kernel, factor),
        sds((16, 2 * Q), F32),
        (keep, swap(send, "z", 4)),
        [vmem()] * 2,
        2**14,
        2**16,
        limit=16,
        name="level",
    )
    g_qkv, g_out = call(
        spread_kernel,
        [sds((16, 3 * HW), F32), sds((16, HW), F32)],
        (place, level, *[swap(level, "batch", d) for d in (1, 2, 3)]),
        [smem()] + [vmem()] * 4,
        2**15,
        2**18,
        limit=16,
        name="spread",
    )
    return (back(0), back(1), g_qkv, g_out)


def solution(mesh):
    devices = mesh.devices.reshape(NB, 2, 2, 8, 2)
    fine = jax.sharding.Mesh(devices, ("batch",) + GRID)
    rows, cols = ("xh", "core"), ("z", "xl")
    grid, whole = P("batch", rows, cols), P()
    return jax.shard_map(
        shards,
        mesh=fine,
        in_specs=(grid, grid, grid, whole, whole, whole, whole, whole, P("batch", rows, cols, None)),
        out_specs=(
            P("batch", rows, cols, None),
            P("batch", rows, cols, None),
            P(GRID, None),
            P(GRID, None),
        ),
        check_vma=False,
    )
```

time: 673 us -> 129 us (0.19)
  the two profiles are of different devices: /device:TPU:32 before, /device:TPU:4 now
where the time goes in v1:
time: 129 us; the launch traced here: 128 us
  starting transfers between devices  38.3 us (30%)
  Pallas kernels  35.2 us (27%)
  waiting for transfers between devices  31.6 us (24%)
  local copies, waits for them, and re-layouts  20.4 us (16%)
  other arithmetic  1.97 us (2%)
    ppermute x12, waiting for transfers between devices, swap(): lax.ppermute(x, axis, [(i, i ^ flip) for i in range(lax.axis_size(axis))])  31.6 us
    pallas_call x17, Pallas kernels, call(): pl.pallas_call(kernel, out_shape=outs, in_specs=specs, out_specs=jax.tree...  24.9 us
    ppermute x10, starting transfers between devices, permute(): return lax.ppermute(x, GRID, pairs)  20.6 us
    unnamed x36, local copies, waits for them, and re-layouts  18.1 us
    ppermute x12, starting transfers between devices, swap(): lax.ppermute(x, axis, [(i, i ^ flip) for i in range(lax.axis_size(axis))])  17.7 us
    pallas_call x2, Pallas kernels, shards(): pl.pallas_call(attend_kernel, grid=(1,), out_shape=[sds((TOKENS, CW)), sd...  10.4 us
  transfers between devices with their start and end apart: 22, of which 7 were waited for; matrix products, arithmetic and copies ran while one was open for 3% of the time, Pallas kernels for 18%

profile of v1, /device:TPU:4, one launch (start us, length us, event | category | flops | bytes accessed | tf_op | source)
XLA Modules:
  0.0 128.4 jit_solution(15373222576470922427)
XLA Ops:
  2.9 1.2 copy-done.2
  4.2 1.4 %pack.1 = (bf16[512,128]{1,0:T(8,128)(2,1)S(1)}, bf16[64,1152]{1,0:T(8,128)(2,1)}, bf16[112,1152]{1,0:T(8,128)(2,1)}, bf16[16,1152]{1,0:T(8,128)(2,1)}) custom-call(s32[32,16]{1,0:T(8,128)S(1)} %bitcast.46, s32[32,16]{1,0:T(8,128)S(1)} %bitcast.47, s32[16,8]{1,0:T(8,128)S(1)} %copy.15.top, bf16[512,1024]{1,0:T(8,128)(2,1)S(1)} %bitcast.40), custom_call_target="tpu_custom_call" | custom-call | flops 268435456 | bytes 3145728 | tf_op jit(solution)/shard_map/pack/pallas_call | solution.py:43
  6.8 1.3 %collective-permute-start.2 = (bf16[16,1152]{1,0:T(8,128)(2,1)}, bf16[16,1152]{1,0:T(8,128)(2,1)}, u32[]{:S(2)}, u32[]{:S(2)}) collective-permute-start(bf16[16,1152]{1,0:T(8,128)(2,1)} %get-tuple-element.49), channel_id=1, source_target_pairs={{0,17},{1,18},{2,19},{3,20},{4,21},{5,22},{6,23},{7,24},{8,25},{9,... | collective-permute-start | bytes 110600 | tf_op jit(solution)/shard_map/ppermute | solution.py:314
  8.8 1.9 %copy-done = bf16[1024,1536]{1,0:T(8,128)(2,1)S(1)} copy-done((bf16[1024,1536]{1,0:T(8,128)(2,1)S(1)}, bf16[1024,1536]{1,0:T(8,128)(2,1)}, u32[]{:S(2)}) %copy-start) | copy-done | bytes 3145752
  10.7 1.2 copy-done.6
  11.9 1.2 copy-done.8
  13.2 4.6 %own.1 = (bf16[448,1024]{1,0:T(8,128)(2,1)S(1)}, bf16[448,1024]{1,0:T(8,128)(2,1)S(1)}, bf16[448,1536]{1,0:T(8,128)(2,1)S(1)}) custom-call(bf16[512,128]{1,0:T(8,128)(2,1)S(1)} %get-tuple-element.50.codes, bf16[512,1024]{1,0:T(8,128)(2,1)S(1)} %copy-done.6, bf16[512,1024]{1,0:T(8,128)(2,1)S(1)} %copy-done.8, bf16[1,1024]{1,0:T(2,128)(2,1)S(1)} %reshape.30.mv, ...), custom_call_target="tpu_custom_call" | custom-call | flops 2348810240 | bytes 9437184 | tf_op jit(solution)/shard_map/own/pallas_call | solution.py:43
  22.1 1.3 %copy-done.5 = bf16[448,1536]{1,0:T(8,128)(2,1)S(1)} copy-done((bf16[448,1536]{1,0:T(8,128)(2,1)S(1)}, bf16[448,1536]{1,0:T(8,128)(2,1)}, u32[]{:S(2)}) %copy-start.5) | copy-done | bytes 1376280
  23.4 1.2 copy-done.7
  24.6 1.2 copy-done.9
  28.9 4.7 %halo.1 = (bf16[512,1024]{1,0:T(8,128)(2,1)S(1)}, bf16[512,1024]{1,0:T(8,128)(2,1)S(1)}, bf16[512,1536]{1,0:T(8,128)(2,1)S(1)}, bf16[512,1024]{1,0:T(8,128)(2,1)S(1)}) custom-call(bf16[64,1152]{1,0:T(8,128)(2,1)S(1)} %collective-permute-done.up, bf16[112,1152]{1,0:T(8,128)(2,1)S(1)} %collective-permute-done.1.left, ...), custom_call_target="tpu_custom_call" | custom-call | flops 922746880 | bytes 12582912 | tf_op jit(solution)/shard_map/halo/pallas_call | solution.py:43
  33.6 5.2 %attend.3 = (bf16[512,256]{1,0:T(8,128)(2,1)S(1)}, bf16[512,768]{1,0:T(8,128)(2,1)S(1)}, f32[2,256,1024]{2,1,0:T(8,128)S(1)}, bf16[2,256,1024]{2,1,0:T(8,128)(2,1)S(1)}) custom-call(s32[7]{0:T(128)S(1)} %stack.31.place, bf16[512,1536]{1,0:T(8,128)(2,1)S(1)} %get-tuple-element.56.q.k.v, bf16[512,1536]{1,0:T(8,128)(2,1)S(1)} %get-tuple-element.56.q.k.v, ...), custom_call_target="tpu_custom_call" | custom-call | flops 3221225472 | bytes 8388608 | tf_op jit(solution)/shard_map/attend/pallas_call | solution.py:407
  39.7 5.2 %attend.2 = (bf16[512,256]{1,0:T(8,128)(2,1)S(1)}, bf16[512,768]{1,0:T(8,128)(2,1)S(1)}, f32[2,256,1024]{2,1,0:T(8,128)S(1)}, bf16[2,256,1024]{2,1,0:T(8,128)(2,1)S(1)}) custom-call(s32[7]{0:T(128)S(1)} %stack.31.place, bf16[512,1536]{1,0:T(8,128)(2,1)S(1)} %get-tuple-element.56.q.k.v, bf16[512,1536]{1,0:T(8,128)(2,1)S(1)} %get-tuple-element.56.q.k.v, ...), custom_call_target="tpu_custom_call" | custom-call | flops 3221225472 | bytes 8388608 | tf_op jit(solution)/shard_map/attend/pallas_call | solution.py:407
  45.9 1.7 %collective-permute-start.12 = (bf16[2,256,512]{2,1,0:T(8,128)(2,1)S(1)}, bf16[2,256,512]{2,1,0:T(8,128)(2,1)S(1)}, u32[]{:S(2)}, u32[]{:S(2)}) collective-permute-start(bf16[2,256,512]{2,1,0:T(8,128)(2,1)S(1)} %get-tuple-element.75), channel_id=1, source_target_pairs={{0,64},{64,0},{128,192},{192,128},{1,65},{65,1},{129,193},{193,129... | collective-permute-start | bytes 1572872 | tf_op jit(solution)/shard_map/ppermute | solution.py:322
  48.4 2.2 %collective-permute-start.7 = (bf16[2,8,16,1024]{3,2,1,0:T(8,128)(2,1)S(1)}, bf16[2,8,16,1024]{3,2,1,0:T(8,128)(2,1)S(1)}, u32[]{:S(2)}, u32[]{:S(2)}) collective-permute-start(bf16[2,8,16,1024]{3,2,1,0:T(8,128)(2,1)S(1)} %get-tuple-element.65), channel_id=1, source_target_pairs={{0,1},{1,0},{2,3},{3,2},{4,5},{5,4},{6,7},{7,6},{8,9},{9,8},{10,11... | collective-permute-start | bytes 1572872 | tf_op jit(solution)/shard_map/ppermute | solution.py:314
  50.6 9.7 %collective-permute-done.12.b = bf16[2,256,512]{2,1,0:T(8,128)(2,1)S(1)} collective-permute-done((bf16[2,256,512]{2,1,0:T(8,128)(2,1)S(1)}, bf16[2,256,512]{2,1,0:T(8,128)(2,1)S(1)}, u32[]{:S(2)}, u32[]{:S(2)}) %collective-permute-start.12) | collective-permute-done | bytes 524320 | tf_op jit(solution)/shard_map/ppermute | solution.py:322
  60.9 3.1 %collective-permute-start.13 = (bf16[2,256,256]{2,1,0:T(8,128)(2,1)S(1)}, bf16[2,256,256]{2,1,0:T(8,128)(2,1)S(1)}, u32[]{:S(2)}, u32[]{:S(2)}) collective-permute-start(bf16[2,256,256]{2,1,0:T(8,128)(2,1)S(1)} %get-tuple-element.77), channel_id=1, source_target_pairs={{0,192},{64,128},{128,64},{192,0},{1,193},{65,129},{129,65},{193,1... | collective-permute-start | bytes 786440 | tf_op jit(solution)/shard_map/ppermute | solution.py:322
  64.7 2.2 %collective-permute-start.8 = (bf16[8,16,1024]{2,1,0:T(8,128)(2,1)S(1)}, bf16[8,16,1024]{2,1,0:T(8,128)(2,1)S(1)}, u32[]{:S(2)}, u32[]{:S(2)}) collective-permute-start(bf16[8,16,1024]{2,1,0:T(8,128)(2,1)S(1)} %get-tuple-element.67), channel_id=1, source_target_pairs={{0,33},{1,32},{2,35},{3,34},{4,37},{5,36},{6,39},{7,38},{8,41},{9,... | collective-permute-start | bytes 786440 | tf_op jit(solution)/shard_map/ppermute | solution.py:314
  66.9 3.3 %collective-permute-done.13 = bf16[2,256,256]{2,1,0:T(8,128)(2,1)S(1)} collective-permute-done((bf16[2,256,256]{2,1,0:T(8,128)(2,1)S(1)}, bf16[2,256,256]{2,1,0:T(8,128)(2,1)S(1)}, u32[]{:S(2)}, u32[]{:S(2)}) %collective-permute-start.13) | collective-permute-done | bytes 262176 | tf_op jit(solution)/shard_map/ppermute | solution.py:322
  70.8 2.2 %collective-permute-start.14 = (bf16[2,8,16,256]{3,2,1,0:T(8,128)(2,1)S(1)}, bf16[2,8,16,256]{3,2,1,0:T(8,128)(2,1)S(1)}, u32[]{:S(2)}, u32[]{:S(2)}) collective-permute-start(bf16[2,8,16,256]{3,2,1,0:T(8,128)(2,1)S(1)} %get-tuple-element.79), channel_id=1, source_target_pairs={{0,1},{1,0},{2,3},{3,2},{4,5},{5,4},{6,7},{7,6},{8,9},{9,8},{10,11... | collective-permute-start | bytes 393224 | tf_op jit(solution)/shard_map/ppermute | solution.py:314
  74.0 6.0 %finish.1 = bf16[2,512,1024]{2,1,0:T(8,128)(2,1)S(1)} custom-call(bf16[512,1024]{1,0:T(8,128)(2,1)S(1)} %get-tuple-element.54.emb, bf16[512,1024]{1,0:T(8,128)(2,1)S(1)} %get-tuple-element.55.cot, bf16[1024,1536]{1,0:T(8,128)(2,1)S(1)} %copy-done.1, bf16[1024,512]{1,0:T(8,128)(2,1)S(1)} %copy-done.10, bf16[512,256]{1,0:T(8,128)(2,1)S(1)} %get-tuple-element.58.att0, ...), custom_call_target="tpu_custom_call" | custom-call | flops 2147483648 | bytes 10485760 | tf_op jit(solution)/shard_map/finish/pallas_call | solution.py:43
  80.1 3.7 %collective-permute-start.5 = (bf16[2,4,4,1024]{3,2,1,0:T(4,128)(2,1)S(1)}, bf16[2,4,4,1024]{3,2,1,0:T(4,128)(2,1)S(1)}, u32[]{:S(2)}, u32[]{:S(2)}) collective-permute-start(bf16[2,4,4,1024]{3,2,1,0:T(4,128)(2,1)S(1)} %slice.49), channel_id=1, source_target_pairs={{0,63},{1,48},{2,49},{3,50},{4,51},{5,52},{6,53},{7,54},{8,55},{9,... | collective-permute-start | bytes 196616 | tf_op jit(solution)/shard_map/ppermute | solution.py:314
  83.8 3.2 %collective-permute-start.4 = (bf16[2,4,16,1024]{3,2,1,0:T(8,128)(2,1)S(1)}, bf16[2,4,16,1024]{3,2,1,0:T(8,128)(2,1)S(1)}, u32[]{:S(2)}, u32[]{:S(2)}) collective-permute-start(bf16[2,4,16,1024]{3,2,1,0:T(8,128)(2,1)S(1)} %slice.47), channel_id=1, source_target_pairs={{0,48},{1,49},{2,50},{3,51},{4,52},{5,53},{6,54},{7,55},{8,56},{9,... | collective-permute-start | bytes 786440 | tf_op jit(solution)/shard_map/ppermute | solution.py:314
  88.3 2.8 %collective-permute-start.10 = (bf16[8,16,256]{2,1,0:T(8,128)(2,1)S(1)}, bf16[8,16,256]{2,1,0:T(8,128)(2,1)S(1)}, u32[]{:S(2)}, u32[]{:S(2)}) collective-permute-start(bf16[8,16,256]{2,1,0:T(8,128)(2,1)S(1)} %get-tuple-element.71), channel_id=1, source_target_pairs={{0,192},{64,128},{128,64},{192,0},{1,193},{65,129},{129,65},{193,1... | collective-permute-start | bytes 196616 | tf_op jit(solution)/shard_map/ppermute | solution.py:322
  91.6 4.5 %collective-permute-start.3 = (bf16[2,28,4,1024]{3,2,1,0:T(4,128)(2,1)S(1)}, bf16[2,28,4,1024]{3,2,1,0:T(4,128)(2,1)S(1)}, u32[]{:S(2)}, u32[]{:S(2)}) collective-permute-start(bf16[2,28,4,1024]{3,2,1,0:T(4,128)(2,1)S(1)} %slice.45), channel_id=1, source_target_pairs={{0,15},{1,0},{2,1},{3,2},{4,3},{5,4},{6,5},{7,6},{8,7},{9,8},{10,9... | collective-permute-start | bytes 1376264 | tf_op jit(solution)/shard_map/ppermute | solution.py:314
  96.8 9.1 %collective-permute-done.16.b = bf16[4,16,512]{2,1,0:T(8,128)(2,1)S(1)} collective-permute-done((bf16[4,16,512]{2,1,0:T(8,128)(2,1)S(1)}, bf16[4,16,512]{2,1,0:T(8,128)(2,1)S(1)}, u32[]{:S(2)}, u32[]{:S(2)}) %collective-permute-start.16) | collective-permute-done | bytes 65568 | tf_op jit(solution)/shard_map/ppermute | solution.py:322
  107.0 4.5 %collective-permute-done.17.b = bf16[2,16,512]{2,1,0:T(8,128)(2,1)S(1)} collective-permute-done((bf16[2,16,512]{2,1,0:T(8,128)(2,1)S(1)}, bf16[2,16,512]{2,1,0:T(8,128)(2,1)S(1)}, u32[]{:S(2)}, u32[]{:S(2)}) %collective-permute-start.17) | collective-permute-done | bytes 32800 | tf_op jit(solution)/shard_map/ppermute | solution.py:322
  112.1 4.0 %collective-permute-start.18 = (bf16[16,512]{1,0:T(8,128)(2,1)S(1)}, bf16[16,512]{1,0:T(8,128)(2,1)S(1)}, u32[]{:S(2)}, u32[]{:S(2)}) collective-permute-start(bf16[16,512]{1,0:T(8,128)(2,1)S(1)} %get-tuple-element.87), channel_id=1, source_target_pairs={{0,8},{2,10},{4,12},{6,14},{8,0},{10,2},{12,4},{14,6},{1,9},{3,11}... | collective-permute-start | bytes 49160 | tf_op jit(solution)/shard_map/ppermute | solution.py:322
  116.2 3.6 %collective-permute-done.18.b = bf16[16,512]{1,0:T(8,128)(2,1)S(1)} collective-permute-done((bf16[16,512]{1,0:T(8,128)(2,1)S(1)}, bf16[16,512]{1,0:T(8,128)(2,1)S(1)}, u32[]{:S(2)}, u32[]{:S(2)}) %collective-permute-start.18) | collective-permute-done | bytes 16416 | tf_op jit(solution)/shard_map/ppermute | solution.py:322
  120.3 2.9 %collective-permute-start.20 = (f32[16,512]{1,0:T(8,128)S(1)}, f32[16,512]{1,0:T(8,128)S(1)}, u32[]{:S(2)}, u32[]{:S(2)}) collective-permute-start(f32[16,512]{1,0:T(8,128)S(1)} %level.1.refs_0_), channel_id=1, source_target_pairs={{0,128},{64,192},{128,0},{192,64},{1,129},{65,193},{129,1},{193,65... | collective-permute-start | bytes 98312 | tf_op jit(solution)/shard_map/ppermute | solution.py:322
  124.0 2.0 %maximum_bitcast_fusion = (bf16[1,32,16,1024]{3,2,1,0:T(8,128)(2,1)}, bf16[1,32,16,1024]{3,2,1,0:T(8,128)(2,1)}) fusion(bf16[4,4,1024]{2,1,0:T(4,128)(2,1)S(1)} %get-tuple-element.97, bf16[4,12,1024]{2,1,0:T(8,128)(2,1)S(1)} %get-tuple-element.95, bf16[28,4,1024]{2,1,0:T(4,128)(2,1)S(1)} %get-tuple-element.93, bf16[28,12,1024]{2,1,0:T(8,128)(2,1)S(1)} %get-tuple-element.91, ...), kind=kLoop, calls=%fused_computation | loop fusion | flops 8388608 | bytes 4194304 | tf_op jit(solution)/shard_map/broadcast_in_dim | solution.py:455
  127.1 1.3 spread.1
  (78 shorter events, 23.9 us)
Async XLA Ops:
  2.9 1.2 copy-start.2
  5.6 15.2 %collective-permute-start.1 = (bf16[112,1152]{1,0:T(8,128)(2,1)}, bf16[112,1152]{1,0:T(8,128)(2,1)S(1)}, u32[]{:S(2)}, u32[]{:S(2)}) collective-permute-start(bf16[112,1152]{1,0:T(8,128)(2,1)} %get-tuple-element.48), channel_id=1, source_target_pairs={{0,1},{1,2},{2,3},{3,4},{4,5},{5,6},{6,7},{7,8},{8,9},{9,10},{10,1... | collective-permute-start | bytes 774152 | tf_op jit(solution)/shard_map/ppermute | solution.py:314
  6.8 14.0 %collective-permute-start.2 = (bf16[16,1152]{1,0:T(8,128)(2,1)}, bf16[16,1152]{1,0:T(8,128)(2,1)}, u32[]{:S(2)}, u32[]{:S(2)}) collective-permute-start(bf16[16,1152]{1,0:T(8,128)(2,1)} %get-tuple-element.49), channel_id=1, source_target_pairs={{0,17},{1,18},{2,19},{3,20},{4,21},{5,22},{6,23},{7,24},{8,25},{9,... | collective-permute-start | bytes 110600 | tf_op jit(solution)/shard_map/ppermute | solution.py:314
  8.1 12.7 %collective-permute-start = (bf16[64,1152]{1,0:T(8,128)(2,1)}, bf16[64,1152]{1,0:T(8,128)(2,1)S(1)}, u32[]{:S(2)}, u32[]{:S(2)}) collective-permute-start(bf16[64,1152]{1,0:T(8,128)(2,1)} %get-tuple-element.47), channel_id=1, source_target_pairs={{0,16},{1,17},{2,18},{3,19},{4,20},{5,21},{6,22},{7,23},{8,24},{9,... | collective-permute-start | bytes 442376 | tf_op jit(solution)/shard_map/ppermute | solution.py:314
  8.8 8.9 %copy-start.15 = (bf16[1,1024]{1,0:T(2,128)(2,1)}, bf16[1,1024]{1,0:T(2,128)(2,1)S(1)}, u32[]{:S(2)}) copy-start(bf16[1,1024]{1,0:T(2,128)(2,1)S(1)} %reshape.30.mv) | copy-start | bytes 6148
  8.8 1.9 %copy-start = (bf16[1024,1536]{1,0:T(8,128)(2,1)S(1)}, bf16[1024,1536]{1,0:T(8,128)(2,1)}, u32[]{:S(2)}) copy-start(bf16[1024,1536]{1,0:T(8,128)(2,1)} %wq.5) | copy-start | bytes 9437188
  10.7 1.2 copy-start.6
  11.9 1.2 copy-start.8
  13.2 7.7 %copy-start.1 = (bf16[1024,1536]{1,0:T(8,128)(2,1)S(1)}, bf16[1024,1536]{1,0:T(8,128)(2,1)}, u32[]{:S(2)}) copy-start(bf16[1024,1536]{1,0:T(8,128)(2,1)} %wq.5) | copy-start | bytes 9437188
  20.8 1.2 copy-start.3
  22.1 1.3 %copy-start.5 = (bf16[448,1536]{1,0:T(8,128)(2,1)S(1)}, bf16[448,1536]{1,0:T(8,128)(2,1)}, u32[]{:S(2)}) copy-start(bf16[448,1536]{1,0:T(8,128)(2,1)} %copy-done.4) | copy-start | bytes 4128772
  23.4 1.2 copy-start.7
  28.9 4.7 %copy-start.10 = (bf16[1024,512]{1,0:T(8,128)(2,1)S(1)}, bf16[1024,512]{1,0:T(8,128)(2,1)}, u32[]{:S(2)}) copy-start(bf16[1024,512]{1,0:T(8,128)(2,1)} %ow.5) | copy-start | bytes 3145732
  38.8 6.2 %collective-permute-start.11 = (bf16[2,256,1024]{2,1,0:T(8,128)(2,1)S(1)}, bf16[2,256,1024]{2,1,0:T(8,128)(2,1)S(1)}, u32[]{:S(2)}, u32[]{:S(2)}) collective-permute-start(bf16[2,256,1024]{2,1,0:T(8,128)(2,1)S(1)} %get-tuple-element.73), channel_id=1, source_target_pairs={{0,16},{16,0},{1,17},{17,1},{2,18},{18,2},{3,19},{19,3},{4,20},{20... | collective-permute-start | bytes 3145736 | tf_op jit(solution)/shard_map/ppermute | solution.py:322
  44.9 2.7 %collective-permute-start.6 = (bf16[2,256,1024]{2,1,0:T(8,128)(2,1)S(1)}, bf16[2,256,1024]{2,1,0:T(8,128)(2,1)S(1)}, u32[]{:S(2)}, u32[]{:S(2)}) collective-permute-start(bf16[2,256,1024]{2,1,0:T(8,128)(2,1)S(1)} %get-tuple-element.63), channel_id=1, source_target_pairs={{0,16},{16,0},{1,17},{17,1},{2,18},{18,2},{3,19},{19,3},{4,20},{20... | collective-permute-start | bytes 3145736 | tf_op jit(solution)/shard_map/ppermute | solution.py:322
  45.9 14.4 %collective-permute-start.12 = (bf16[2,256,512]{2,1,0:T(8,128)(2,1)S(1)}, bf16[2,256,512]{2,1,0:T(8,128)(2,1)S(1)}, u32[]{:S(2)}, u32[]{:S(2)}) collective-permute-start(bf16[2,256,512]{2,1,0:T(8,128)(2,1)S(1)} %get-tuple-element.75), channel_id=1, source_target_pairs={{0,64},{64,0},{128,192},{192,128},{1,65},{65,1},{129,193},{193,129... | collective-permute-start | bytes 1572872 | tf_op jit(solution)/shard_map/ppermute | solution.py:322
  48.4 15.7 %collective-permute-start.7 = (bf16[2,8,16,1024]{3,2,1,0:T(8,128)(2,1)S(1)}, bf16[2,8,16,1024]{3,2,1,0:T(8,128)(2,1)S(1)}, u32[]{:S(2)}, u32[]{:S(2)}) collective-permute-start(bf16[2,8,16,1024]{3,2,1,0:T(8,128)(2,1)S(1)} %get-tuple-element.65), channel_id=1, source_target_pairs={{0,1},{1,0},{2,3},{3,2},{4,5},{5,4},{6,7},{7,6},{8,9},{9,8},{10,11... | collective-permute-start | bytes 1572872 | tf_op jit(solution)/shard_map/ppermute | solution.py:314
  60.9 9.3 %collective-permute-start.13 = (bf16[2,256,256]{2,1,0:T(8,128)(2,1)S(1)}, bf16[2,256,256]{2,1,0:T(8,128)(2,1)S(1)}, u32[]{:S(2)}, u32[]{:S(2)}) collective-permute-start(bf16[2,256,256]{2,1,0:T(8,128)(2,1)S(1)} %get-tuple-element.77), channel_id=1, source_target_pairs={{0,192},{64,128},{128,64},{192,0},{1,193},{65,129},{129,65},{193,1... | collective-permute-start | bytes 786440 | tf_op jit(solution)/shard_map/ppermute | solution.py:322
  64.7 8.3 %collective-permute-start.8 = (bf16[8,16,1024]{2,1,0:T(8,128)(2,1)S(1)}, bf16[8,16,1024]{2,1,0:T(8,128)(2,1)S(1)}, u32[]{:S(2)}, u32[]{:S(2)}) collective-permute-start(bf16[8,16,1024]{2,1,0:T(8,128)(2,1)S(1)} %get-tuple-element.67), channel_id=1, source_target_pairs={{0,33},{1,32},{2,35},{3,34},{4,37},{5,36},{6,39},{7,38},{8,41},{9,... | collective-permute-start | bytes 786440 | tf_op jit(solution)/shard_map/ppermute | solution.py:314
  70.8 16.2 %collective-permute-start.14 = (bf16[2,8,16,256]{3,2,1,0:T(8,128)(2,1)S(1)}, bf16[2,8,16,256]{3,2,1,0:T(8,128)(2,1)S(1)}, u32[]{:S(2)}, u32[]{:S(2)}) collective-permute-start(bf16[2,8,16,256]{3,2,1,0:T(8,128)(2,1)S(1)} %get-tuple-element.79), channel_id=1, source_target_pairs={{0,1},{1,0},{2,3},{3,2},{4,5},{5,4},{6,7},{7,6},{8,9},{9,8},{10,11... | collective-permute-start | bytes 393224 | tf_op jit(solution)/shard_map/ppermute | solution.py:314
  73.6 14.0 %collective-permute-start.9 = (bf16[8,16,512]{2,1,0:T(8,128)(2,1)S(1)}, bf16[8,16,512]{2,1,0:T(8,128)(2,1)S(1)}, u32[]{:S(2)}, u32[]{:S(2)}) collective-permute-start(bf16[8,16,512]{2,1,0:T(8,128)(2,1)S(1)} %get-tuple-element.69), channel_id=1, source_target_pairs={{0,64},{64,0},{128,192},{192,128},{1,65},{65,1},{129,193},{193,129... | collective-permute-start | bytes 393224 | tf_op jit(solution)/shard_map/ppermute | solution.py:322
  80.1 16.6 %collective-permute-start.5 = (bf16[2,4,4,1024]{3,2,1,0:T(4,128)(2,1)S(1)}, bf16[2,4,4,1024]{3,2,1,0:T(4,128)(2,1)S(1)}, u32[]{:S(2)}, u32[]{:S(2)}) collective-permute-start(bf16[2,4,4,1024]{3,2,1,0:T(4,128)(2,1)S(1)} %slice.49), channel_id=1, source_target_pairs={{0,63},{1,48},{2,49},{3,50},{4,51},{5,52},{6,53},{7,54},{8,55},{9,... | collective-permute-start | bytes 196616 | tf_op jit(solution)/shard_map/ppermute | solution.py:314
  83.8 23.2 %collective-permute-start.4 = (bf16[2,4,16,1024]{3,2,1,0:T(8,128)(2,1)S(1)}, bf16[2,4,16,1024]{3,2,1,0:T(8,128)(2,1)S(1)}, u32[]{:S(2)}, u32[]{:S(2)}) collective-permute-start(bf16[2,4,16,1024]{3,2,1,0:T(8,128)(2,1)S(1)} %slice.47), channel_id=1, source_target_pairs={{0,48},{1,49},{2,50},{3,51},{4,52},{5,53},{6,54},{7,55},{8,56},{9,... | collective-permute-start | bytes 786440 | tf_op jit(solution)/shard_map/ppermute | solution.py:314
  87.6 8.5 %collective-permute-start.15 = (bf16[8,16,256]{2,1,0:T(8,128)(2,1)S(1)}, bf16[8,16,256]{2,1,0:T(8,128)(2,1)S(1)}, u32[]{:S(2)}, u32[]{:S(2)}) collective-permute-start(bf16[8,16,256]{2,1,0:T(8,128)(2,1)S(1)} %get-tuple-element.81), channel_id=1, source_target_pairs={{0,33},{1,32},{2,35},{3,34},{4,37},{5,36},{6,39},{7,38},{8,41},{9,... | collective-permute-start | bytes 196616 | tf_op jit(solution)/shard_map/ppermute | solution.py:314
  88.3 7.8 %collective-permute-start.10 = (bf16[8,16,256]{2,1,0:T(8,128)(2,1)S(1)}, bf16[8,16,256]{2,1,0:T(8,128)(2,1)S(1)}, u32[]{:S(2)}, u32[]{:S(2)}) collective-permute-start(bf16[8,16,256]{2,1,0:T(8,128)(2,1)S(1)} %get-tuple-element.71), channel_id=1, source_target_pairs={{0,192},{64,128},{128,64},{192,0},{1,193},{65,129},{129,65},{193,1... | collective-permute-start | bytes 196616 | tf_op jit(solution)/shard_map/ppermute | solution.py:322
  91.6 24.5 %collective-permute-start.3 = (bf16[2,28,4,1024]{3,2,1,0:T(4,128)(2,1)S(1)}, bf16[2,28,4,1024]{3,2,1,0:T(4,128)(2,1)S(1)}, u32[]{:S(2)}, u32[]{:S(2)}) collective-permute-start(bf16[2,28,4,1024]{3,2,1,0:T(4,128)(2,1)S(1)} %slice.45), channel_id=1, source_target_pairs={{0,15},{1,0},{2,1},{3,2},{4,3},{5,4},{6,5},{7,6},{8,7},{9,8},{10,9... | collective-permute-start | bytes 1376264 | tf_op jit(solution)/shard_map/ppermute | solution.py:314
  96.6 9.3 %collective-permute-start.16 = (bf16[4,16,512]{2,1,0:T(8,128)(2,1)S(1)}, bf16[4,16,512]{2,1,0:T(8,128)(2,1)S(1)}, u32[]{:S(2)}, u32[]{:S(2)}) collective-permute-start(bf16[4,16,512]{2,1,0:T(8,128)(2,1)S(1)} %get-tuple-element.83), channel_id=1, source_target_pairs={{0,2},{2,0},{4,6},{6,4},{8,10},{10,8},{12,14},{14,12},{1,3},{3,1},... | collective-permute-start | bytes 196616 | tf_op jit(solution)/shard_map/ppermute | solution.py:322
  106.5 5.1 %collective-permute-start.17 = (bf16[2,16,512]{2,1,0:T(8,128)(2,1)S(1)}, bf16[2,16,512]{2,1,0:T(8,128)(2,1)S(1)}, u32[]{:S(2)}, u32[]{:S(2)}) collective-permute-start(bf16[2,16,512]{2,1,0:T(8,128)(2,1)S(1)} %get-tuple-element.85), channel_id=1, source_target_pairs={{0,4},{2,6},{4,0},{6,2},{8,12},{10,14},{12,8},{14,10},{1,5},{3,7},... | collective-permute-start | bytes 98312 | tf_op jit(solution)/shard_map/ppermute | solution.py:322
  112.1 7.7 %collective-permute-start.18 = (bf16[16,512]{1,0:T(8,128)(2,1)S(1)}, bf16[16,512]{1,0:T(8,128)(2,1)S(1)}, u32[]{:S(2)}, u32[]{:S(2)}) collective-permute-start(bf16[16,512]{1,0:T(8,128)(2,1)S(1)} %get-tuple-element.87), channel_id=1, source_target_pairs={{0,8},{2,10},{4,12},{6,14},{8,0},{10,2},{12,4},{14,6},{1,9},{3,11}... | collective-permute-start | bytes 49160 | tf_op jit(solution)/shard_map/ppermute | solution.py:322
  119.8 6.1 %collective-permute-start.21 = (f32[16,512]{1,0:T(8,128)S(1)}, f32[16,512]{1,0:T(8,128)S(1)}, u32[]{:S(2)}, u32[]{:S(2)}) collective-permute-start(f32[16,512]{1,0:T(8,128)S(1)} %level.1.refs_0_), channel_id=1, source_target_pairs={{0,192},{64,128},{128,64},{192,0},{1,193},{65,129},{129,65},{193,1... | collective-permute-start | bytes 98312 | tf_op jit(solution)/shard_map/ppermute | solution.py:322
  120.3 5.7 %collective-permute-start.20 = (f32[16,512]{1,0:T(8,128)S(1)}, f32[16,512]{1,0:T(8,128)S(1)}, u32[]{:S(2)}, u32[]{:S(2)}) collective-permute-start(f32[16,512]{1,0:T(8,128)S(1)} %level.1.refs_0_), channel_id=1, source_target_pairs={{0,128},{64,192},{128,0},{192,64},{1,129},{65,193},{129,1},{193,65... | collective-permute-start | bytes 98312 | tf_op jit(solution)/shard_map/ppermute | solution.py:322
  123.2 3.9 %collective-permute-start.19 = (f32[16,512]{1,0:T(8,128)S(1)}, f32[16,512]{1,0:T(8,128)S(1)}, u32[]{:S(2)}, u32[]{:S(2)}) collective-permute-start(f32[16,512]{1,0:T(8,128)S(1)} %level.1.refs_0_), channel_id=1, source_target_pairs={{0,64},{64,0},{128,192},{192,128},{1,65},{65,1},{129,193},{193,129... | collective-permute-start | bytes 98312 | tf_op jit(solution)/shard_map/ppermute | solution.py:322
  (7 other events, 7.2 us)

commit v2 on v1

v2 whole, which is shorter than its diff:
```python
import functools
import math

import jax
import jax.numpy as jnp
from jax import lax
from jax.experimental import pallas as pl
from jax.experimental.pallas import tpu as pltpu
from jax.sharding import PartitionSpec as P

HEADS = 8
HDIM = 64
WIN = 8
HW = 512
SHIFT = 4
EPS = 1e-05
MODEL = 1024
ROWS, COLS = 32, 16
TOKENS = ROWS * COLS
BAND = WIN * COLS
BANDS = TOKENS // BAND
CHUNKS = 2
CW = HW // CHUNKS
F32 = jnp.float32
BF16 = jnp.bfloat16
GRID = ("xh", "core", "z", "xl")
NB, NLAT, NLON = 4, 4, 16


def dot(a, b, ca, cb):
    return lax.dot_general(a, b, (((ca,), (cb,)), ((), ())), preferred_element_type=F32)


def vmem():
    return pl.BlockSpec(memory_space=pltpu.VMEM)


def smem():
    return pl.BlockSpec(memory_space=pltpu.SMEM)


def call(kernel, outs, operands, specs, flops, nbytes, trans=0, limit=40, name=None, scratch=()):
    return pl.pallas_call(
        kernel,
        out_shape=outs,
        in_specs=specs,
        out_specs=jax.tree.map(lambda _: vmem(), outs),
        scratch_shapes=scratch,
        compiler_params=pltpu.CompilerParams(vmem_limit_bytes=limit * 2**20),
        cost_estimate=pl.CostEstimate(flops=flops, bytes_accessed=nbytes, transcendentals=trans),
        name=name,
    )(*operands)


def hbm():
    return pl.BlockSpec(memory_space=pltpu.HBM)


def sems(n):
    return pltpu.SemaphoreType.DMA((n,))


def sds(shape, dtype=BF16):
    return jax.ShapeDtypeStruct(shape, dtype)


def iota(shape, dim):
    return lax.broadcasted_iota(jnp.int32, shape, dim)


def moments(x):
    mean = jnp.mean(x, axis=1, keepdims=True)
    centred = x - mean
    inverse = lax.rsqrt(jnp.mean(centred * centred, axis=1, keepdims=True) + EPS)
    return centred, inverse


MSG = SHIFT * (ROWS - SHIFT)
OWN = (ROWS - SHIFT) * COLS
LATE = COLS - SHIFT


def hot(mask):
    return mask.astype(F32).astype(BF16)


def late_cells(cells, rows, by_row):
    dims = (0, 1) if by_row else (1, 0)
    shape = (rows, cells) if by_row else (cells, rows)
    m, t = iota(shape, dims[0]), iota(shape, dims[1])
    return hot(t == (m >> 2) * COLS + LATE + (m & 3))


def slice_kernel(cot, up, left, diag, held, sem):
    copy = pltpu.make_async_copy(cot, held, sem)
    copy.start()
    pick, corner = late_cells(OWN, MSG, True), late_cells(64, 16, True)
    copy.wait()
    up[...] = held[OWN:]
    left[...] = dot(pick, held[:OWN], 1, 0).astype(BF16)
    diag[...] = dot(corner, held[OWN:], 1, 0).astype(BF16)


def embed_kernel(own, up, left, diag, bt, tt, mv, wq, emb, normed, proj, tables, weight, sems):
    copies = [
        pltpu.make_async_copy(bt, tables.at[0], sems.at[0]),
        pltpu.make_async_copy(tt, tables.at[1], sems.at[1]),
        pltpu.make_async_copy(wq, weight, sems.at[2]),
    ]
    for copy in copies:
        copy.start()
    r, j = iota((80, 16), 0), iota((80, 16), 1)
    low = jnp.where(r >= 64, r - 50, r & 31) >= 28
    late = jnp.where(r >= 64, 2 * j, j) >= LATE
    grid = jnp.where(
        low,
        jnp.where(late, diag[...], up[...]),
        jnp.where(late, left[...], own[...]),
    )
    bottom = jnp.where(grid[32:64] == 1, 512, grid[0:32])
    upper = grid[64:80, 0:8]

    def column(codes, rows, row_of, lane_of):
        width = codes.shape[1]
        parts = jnp.concatenate([codes >> 4, codes & 15], axis=1).astype(F32).astype(BF16)
        pick = hot(row_of(iota((TOKENS, rows), 0)) == iota((TOKENS, rows), 1))
        spread = dot(pick, parts, 1, 0)
        t, lane = iota(spread.shape, 0), iota(spread.shape, 1)
        inside = jnp.where(lane < width, lane, lane - width) == lane_of(t)
        weight = jnp.where(lane < width, 16.0, 1.0)
        code = jnp.sum(jnp.where(inside, spread * weight, 0.0), axis=1, keepdims=True)
        return code.astype(jnp.int32)

    def source_row(t):
        return ((t >> 4) + (ROWS - SHIFT)) & (ROWS - 1)

    code_b = column(bottom, 32, source_row, lambda t: t & 15)
    code_t = column(upper, 16, lambda t: source_row(t) >> 1, lambda t: (t & 15) >> 1)
    copies[0].wait()
    copies[1].wait()
    for block in range(BANDS):
        here = slice(block * BAND, (block + 1) * BAND)
        cb, ct = code_b[here], code_t[here]
        lane = iota((BAND, 512), 1)
        x = dot(hot(lane == cb), tables[0], 1, 0)
        x = jnp.where(cb == 512, mv[...].astype(F32), x)
        x = (x + dot(hot(lane == ct), tables[1], 1, 0)).astype(BF16)
        emb[here] = x
        centred, inverse = moments(x.astype(F32))
        normed[here] = (centred * inverse).astype(BF16)
    copies[2].wait()
    for block in range(BANDS):
        here = slice(block * BAND, (block + 1) * BAND)
        proj[here] = dot(normed[here], weight[...], 1, 0).astype(BF16)


def merge(cot, grads, up, left, diag):
    p = iota((64, 1), 0) & 15
    corner = dot(late_cells(64, 16, False), diag[...], 1, 0)
    cot[0:64] = jnp.where(p >= LATE, corner, up[...].astype(F32)).astype(BF16)
    for at in range(0, OWN, 64):
        m, t = iota((64, MSG), 1), at + iota((64, MSG), 0)
        spread = hot(t == (m >> 2) * COLS + LATE + (m & 3))
        values = dot(spread, left[...], 1, 0)
        values = jnp.where(p >= LATE, values, grads[at : at + 64].astype(F32))
        cot[64 + at : 128 + at] = values.astype(BF16)


def attend_first(place, proj, normed, grads, up, left, diag, ow, att, gp, keep, send, cot, own, weight, sems):
    copies = [
        pltpu.make_async_copy(grads, own, sems.at[0]),
        pltpu.make_async_copy(ow.at[:, 0:CW], weight, sems.at[1]),
    ]
    for copy in copies:
        copy.start()
    copies[0].wait()
    merge(cot, own, up, left, diag)
    copies[1].wait()
    attend(0, place, proj, normed, cot, weight, att, gp, keep, send)


def attend_next(place, proj, normed, cot, ow, att, gp, keep, send, weight, sem):
    copy = pltpu.make_async_copy(ow.at[:, CW:], weight, sem)
    copy.start()
    copy.wait()
    attend(1, place, proj, normed, cot, weight, att, gp, keep, send)


def attend(chunk, place, proj, normed, cot, ow, att, gp, keep, send):
    grad = dot(cot[...], ow[...], 1, 0).astype(BF16)
    lane = iota((BAND, 128), 1) < 64
    tk, tq = iota((BAND, BAND), 0), iota((BAND, BAND), 1)

    def side(t):
        c = t & 15
        return ((c >= 4) & (c < 12)).astype(jnp.int32)

    same = side(tk) == side(tq)
    whole = (tk >> 6) == (tq >> 6)
    zero = jnp.zeros((BAND, BAND), F32)
    plain = jnp.where(same, zero, -1e30)
    first = jnp.where(whole | (place[0] != 0), plain, -1e30)

    def split(x):
        none = jnp.zeros_like(x)
        return jnp.concatenate([jnp.where(lane, x, none), jnp.where(lane, none, x)], axis=0)

    def pick(x):
        return jnp.where(lane, x[:BAND], x[BAND:])

    for b in range(BANDS):
        bias = first if b == 0 else plain
        here = slice(b * BAND, (b + 1) * BAND)
        for p in range(CW // 128):
            cols = slice(p * 128, (p + 1) * 128)
            first_col = chunk * CW + p * 128
            qq, kk, vv = (proj[here, i * HW + first_col : i * HW + first_col + 128] for i in range(3))
            kk, vv = split(kk), split(vv)
            da = grad[here, cols]
            s = dot(kk, qq, 1, 1).reshape(2, BAND, BAND) * 0.125 + bias
            e = jnp.exp(s - jnp.max(s, axis=1, keepdims=True))
            share = e * (1.0 / jnp.sum(e, axis=1, keepdims=True))
            sb = share.astype(BF16).reshape(2 * BAND, BAND)
            att[here, cols] = dot(sb, vv, 0, 0).astype(BF16)
            gs = dot(vv, da, 1, 1).reshape(2, BAND, BAND)
            delta = jnp.sum(share * gs, axis=1, keepdims=True)
            ds = (share * (gs - delta) * 0.125).astype(BF16).reshape(2 * BAND, BAND)
            at = p * 128
            gp[here, at : at + 128] = dot(ds, kk, 0, 0).astype(BF16)
            gp[here, CW + at : CW + at + 128] = pick(dot(ds, qq, 1, 0)).astype(BF16)
            gp[here, 2 * CW + at : 2 * CW + at + 128] = pick(dot(sb, da, 1, 0)).astype(BF16)

    core = place[1]
    for half in range(2):
        for out, flip in ((send, 1), (keep, 0)):
            cut = pl.ds(pl.multiple_of(half * 512 + (core ^ flip) * 256, 256), 256)
            out[half, :, 0 : 3 * CW] = dot(normed[:, cut], gp[...], 0, 0).astype(out.dtype)
            out[half, :, 3 * CW :] = dot(cot[:, cut], att[...], 0, 0).astype(out.dtype)


def finish_kernel(emb, cot, wq, ow, att0, att1, gp0, gp1, both, weight, last, sems):
    copies = [
        pltpu.make_async_copy(ow, last, sems.at[0]),
        pltpu.make_async_copy(wq, weight, sems.at[1]),
    ]
    for copy in copies:
        copy.start()
    for copy in copies:
        copy.wait()
    for block in range(BANDS):
        here = slice(block * BAND, (block + 1) * BAND)
        x = emb[here].astype(F32)
        att = jnp.concatenate([att0[here], att1[here]], axis=1)
        both[0, here] = (x + dot(att, last[...], 1, 1)).astype(BF16)
        g0, g1 = gp0[here], gp1[here]
        parts = []
        for i in range(3):
            parts += [g0[:, i * CW : (i + 1) * CW], g1[:, i * CW : (i + 1) * CW]]
        gst = dot(jnp.concatenate(parts, axis=1), weight[...], 1, 1)
        centred, inverse = moments(x)
        standard = centred * inverse
        m1 = jnp.mean(gst, axis=1, keepdims=True)
        m2 = jnp.mean(gst * standard, axis=1, keepdims=True)
        both[1, here] = (cot[here].astype(F32) + inverse * (gst - m1 - standard * m2)).astype(BF16)


W = 4 * CW
Q = W // 4


def parity_core(place, a, b, keep, send):
    g = place[2] ^ place[3]
    for u in range(2):
        for out, v in ((keep, u ^ g), (send, u ^ g ^ 1)):
            out[u] = (a[u, :, v] + b[u, :, v].astype(F32)).astype(out.dtype)


def parity_pair(place, a, b, keep, send):
    for out, u in ((keep, place[2]), (send, place[2] ^ 1)):
        out[...] = (a[u] + b[u].astype(F32)).astype(out.dtype)


def high_core(place, a, b, keep, send):
    for out, u in ((keep, place[2]), (send, place[2] ^ 1)):
        for v in range(2):
            out[v] = (a[u, :, v] + b[u, :, v].astype(F32)).astype(out.dtype)


def high_pair(place, a, b, keep, send):
    for out, v in ((keep, place[3]), (send, place[3] ^ 1)):
        out[...] = (a[v] + b[v].astype(F32)).astype(out.dtype)


def join_kernel(a, b, c, d, out):
    out[:, :, 0:W] = (a[...] + b[...].astype(F32)).astype(BF16)
    out[:, :, W:] = (c[...] + d[...].astype(F32)).astype(BF16)


def depth_kernel(ref, keep, send):
    total = sum(ref[i].astype(F32) for i in range(8))
    keep[...] = total
    send[...] = total.astype(BF16)


def level_kernel(factor, own, *refs):
    qkv, outw = refs[3:]
    total = (own[...] + sum(r[...].astype(F32) for r in refs[:3])) * factor
    for c in range(CHUNKS):
        for i in range(3):
            qkv[:, i * HW + c * CW : i * HW + (c + 1) * CW] = total[:, c * W + i * Q : c * W + (i + 1) * Q]
        outw[:, c * CW : (c + 1) * CW] = total[:, c * W + 3 * Q : (c + 1) * W]


def permute(x, where):
    pairs = []
    for la in range(NLAT):
        for lo in range(NLON):
            tl, to = where(la, lo)
            pairs.append((la * NLON + lo, tl * NLON + to))
    return lax.ppermute(x, GRID, pairs)


def shift(x, down, right):
    return permute(x, lambda la, lo: ((la + down) % NLAT, (lo + right) % NLON))


def swap(x, axis, flip):
    return lax.ppermute(x, axis, [(i, i ^ flip) for i in range(lax.axis_size(axis))])


def swap_x(x, flip):
    return permute(x, lambda la, lo: (la ^ (flip & 2), lo ^ (flip & 1)))


def halve(kernel, shape, place, *terms):
    size = math.prod(shape)
    return call(
        kernel,
        [sds(shape, F32), sds(shape)],
        (place, *terms),
        [smem()] + [vmem()] * len(terms),
        2 * size,
        16 * size,
        limit=16,
        name=kernel.__name__,
    )


def sum_x(place, keep, send, order):
    fold = (2, 8, 2, 16, W)
    core, pair = (parity_core, parity_pair) if order[0] == 1 else (high_core, high_pair)
    recv = swap(send, "core", 1)
    keep, send = halve(core, (2, 8, 16, W), place, keep.reshape(fold), recv.reshape(fold))
    keep, send = halve(pair, (8, 16, W), place, keep, swap_x(send, order[0]))
    return [keep, swap_x(send, order[1])]


def shards(
    bottom_codes, mask_flags, top_codes, bottom_table, top_table, mask_vector, qkv_weight, out_weight, cotangent
):
    core, xh, xl = lax.axis_index("core"), lax.axis_index("xh"), lax.axis_index("xl")
    place = jnp.stack([2 * xh + core, core, xh, xl]).astype(jnp.int32)
    own = jnp.concatenate(
        [bottom_codes[0], mask_flags[0], jnp.pad(top_codes[0], ((0, 0), (0, 8)))], axis=0
    )
    near = (own, shift(own, 1, 0), shift(own, 0, 1), shift(own, 1, 1))
    pin = lambda x: pltpu.with_memory_space_constraint(x, pltpu.HBM)
    grads = pin(cotangent.reshape(TOKENS, MODEL))
    bottom_table, top_table = pin(bottom_table), pin(top_table)
    qkv_weight, out_weight = pin(qkv_weight), pin(out_weight)
    up, left, diag = call(
        slice_kernel,
        [sds((64, MODEL)), sds((MSG, MODEL)), sds((16, MODEL))],
        (grads,),
        [hbm()],
        2**28,
        2**21,
        name="slices",
        scratch=[pltpu.VMEM((TOKENS, MODEL), BF16), pltpu.SemaphoreType.DMA],
    )
    up, left, diag = shift(up, 1, 0), shift(left, 0, 1), shift(diag, 1, 1)
    emb, normed, proj = call(
        embed_kernel,
        [sds((TOKENS, MODEL)), sds((TOKENS, MODEL)), sds((TOKENS, 3 * HW))],
        (*near, bottom_table, top_table, mask_vector.reshape(1, MODEL), qkv_weight),
        [vmem()] * 4 + [hbm(), hbm(), vmem(), hbm()],
        2 * TOKENS * 1024 * 2560,
        9 * 2**20,
        name="embed",
        scratch=[pltpu.VMEM((2, 512, MODEL), BF16), pltpu.VMEM((MODEL, 3 * HW), BF16), sems(3)],
    )
    outs = [sds((TOKENS, CW)), sds((TOKENS, 3 * CW)), sds((2, 256, W), F32), sds((2, 256, W))]
    column = pltpu.VMEM((MODEL, CW), BF16)
    att0, gp0, keep0, send0, cot = call(
        attend_first,
        outs + [sds((TOKENS, MODEL))],
        (place, proj, normed, grads, up, left, diag, out_weight),
        [smem(), vmem(), vmem(), hbm(), vmem(), vmem(), vmem(), hbm()],
        3 * 2**30,
        8 * 2**20,
        2**19,
        name="attend",
        scratch=[pltpu.VMEM((TOKENS, MODEL), BF16), column, sems(2)],
    )
    att1, gp1, keep1, send1 = call(
        attend_next,
        outs,
        (place, proj, normed, cot, out_weight),
        [smem(), vmem(), vmem(), vmem(), hbm()],
        3 * 2**30,
        8 * 2**20,
        2**19,
        name="attend",
        scratch=[column, pltpu.SemaphoreType.DMA],
    )
    summed = sum_x(place, keep0, send0, (1, 3)) + sum_x(place, keep1, send1, (3, 1))
    both = call(
        finish_kernel,
        sds((2, TOKENS, MODEL)),
        (emb, cot, qkv_weight, out_weight, att0, att1, gp0, gp1),
        [vmem(), vmem(), hbm(), hbm()] + [vmem()] * 4,
        2 * TOKENS * 1024 * 2048,
        10 * 2**20,
        name="finish",
        scratch=[pltpu.VMEM((MODEL, 3 * HW), BF16), pltpu.VMEM((MODEL, HW), BF16), sems(2)],
    )
    both = both.reshape(2, ROWS, COLS, MODEL)
    r_up = shift(both[:, :SHIFT], -1, 0)
    r_left = shift(both[:, SHIFT:, LATE:], 0, -1)
    r_diag = shift(both[:, :SHIFT, LATE:], -1, -1)

    def back(i):
        upper = jnp.concatenate([both[i, SHIFT:, :LATE], r_left[i]], axis=1)
        lower = jnp.concatenate([r_up[i, :, :LATE], r_diag[i]], axis=1)
        return jnp.concatenate([upper, lower], axis=0)[None]

    factor = 1.0 / math.sqrt(TOKENS * NB * NLAT * NLON)
    joined = call(
        join_kernel, sds((8, 16, 2 * W)), summed, [vmem()] * 4, 2**19, 2**21, limit=16, name="join"
    )
    depth = lax.all_to_all(joined, "z", 0, 0, tiled=True)
    keep, send = call(
        depth_kernel,
        [sds((16, 2 * W), F32), sds((16, 2 * W))],
        (depth,),
        [vmem()],
        2**18,
        2**20,
        limit=16,
        name="depth",
    )
    g_qkv, g_out = call(
        functools.partial(level_kernel, factor),
        [sds((16, 3 * HW), F32), sds((16, HW), F32)],
        (keep, *[swap(send, "batch", d) for d in (1, 2, 3)]),
        [vmem()] * 4,
        2**17,
        2**19,
        limit=16,
        name="level",
    )
    return (back(0), back(1), g_qkv, g_out)


def solution(mesh):
    devices = mesh.devices.reshape(NB, 2, 2, 8, 2)
    fine = jax.sharding.Mesh(devices, ("batch",) + GRID)
    rows, cols = ("xh", "core"), ("z", "xl")
    grid, whole = P("batch", rows, cols), P()
    return jax.shard_map(
        shards,
        mesh=fine,
        in_specs=(grid, grid, grid, whole, whole, whole, whole, whole, P("batch", rows, cols, None)),
        out_specs=(
            P("batch", rows, cols, None),
            P("batch", rows, cols, None),
            P(GRID, None),
            P(GRID, None),
        ),
        check_vma=False,
    )
```

time: 129 us -> 109 us (0.84)
  the two profiles are of different devices: /device:TPU:4 before, /device:TPU:2 now
where the time goes in v2:
time: 109 us; the launch traced here: 108 us
  waiting for transfers between devices  39.4 us (36%)
  Pallas kernels  32.4 us (30%)
  starting transfers between devices  26.1 us (24%)
  local copies, waits for them, and re-layouts  6.11 us (6%)
  other arithmetic  3.59 us (3%)
    ppermute x13, waiting for transfers between devices, permute(): return lax.ppermute(x, GRID, pairs)  36 us
    pallas_call x12, Pallas kernels, call(): pl.pallas_call(kernel, out_shape=outs, in_specs=specs, out_specs=jax.tree...  32.4 us
    ppermute x13, starting transfers between devices, permute(): return lax.ppermute(x, GRID, pairs)  13.9 us
    all_to_all x1, starting transfers between devices, shards(): depth = lax.all_to_all(joined, 'z', 0, 0, tiled=True)  7.17 us
    ppermute x5, starting transfers between devices, swap(): lax.ppermute(x, axis, [(i, i ^ flip) for i in range(lax.axis_size(axis))])  5.07 us
    ppermute x5, waiting for transfers between devices, swap(): lax.ppermute(x, axis, [(i, i ^ flip) for i in range(lax.axis_size(axis))])  3.45 us
    broadcast_in_dim x1, other arithmetic, back(): return jnp.concatenate([upper, lower], axis=0)[None]  2.71 us
    squeeze x2, local copies, waits for them, and re-layouts, back(): lower = jnp.concatenate([r_up[i, :, :LATE], r_diag[i]], axis=1)  2.41 us
  transfers between devices with their start and end apart: 19, of which 6 were waited for; matrix products, arithmetic and copies ran while one was open for 8% of the time, Pallas kernels for 23%

profile of v2, /device:TPU:2, one launch (start us, length us, event | category | flops | bytes accessed | tf_op | source)
XLA Modules:
  0.0 108.5 jit_solution(2455482672214256704)
XLA Ops:
  0.6 0.8 pad_add_fusion
  1.5 1.4 %collective-permute-start.2 = (s32[80,16]{1,0:T(8,128)S(1)}, s32[80,16]{1,0:T(8,128)S(1)}, u32[]{:S(2)}, u32[]{:S(2)}) collective-permute-start(s32[80,16]{1,0:T(8,128)S(1)} %copy.19.own), channel_id=1, source_target_pairs={{0,17},{1,18},{2,19},{3,20},{4,21},{5,22},{6,23},{7,24},{8,25},{9,... | collective-permute-start | bytes 15368 | tf_op jit(solution)/shard_map/ppermute | solution.py:320
  2.9 1.5 %collective-permute-start.1 = (s32[80,16]{1,0:T(8,128)S(1)}, s32[80,16]{1,0:T(8,128)S(1)}, u32[]{:S(2)}, u32[]{:S(2)}) collective-permute-start(s32[80,16]{1,0:T(8,128)S(1)} %copy.19.own), channel_id=1, source_target_pairs={{0,1},{1,2},{2,3},{3,4},{4,5},{5,6},{6,7},{7,8},{8,9},{9,10},{10,1... | collective-permute-start | bytes 15368 | tf_op jit(solution)/shard_map/ppermute | solution.py:320
  4.4 1.7 %collective-permute-start = (s32[80,16]{1,0:T(8,128)S(1)}, s32[80,16]{1,0:T(8,128)S(1)}, u32[]{:S(2)}, u32[]{:S(2)}) collective-permute-start(s32[80,16]{1,0:T(8,128)S(1)} %copy.19.own), channel_id=1, source_target_pairs={{0,16},{1,17},{2,18},{3,19},{4,20},{5,21},{6,22},{7,23},{8,24},{9,... | collective-permute-start | bytes 15368 | tf_op jit(solution)/shard_map/ppermute | solution.py:320
  6.1 1.6 %slices.1 = (bf16[64,1024]{1,0:T(8,128)(2,1)S(1)}, bf16[112,1024]{1,0:T(8,128)(2,1)S(1)}, bf16[16,1024]{1,0:T(8,128)(2,1)S(1)}) custom-call(bf16[512,1024]{1,0:T(8,128)(2,1)} %bitcast.41), custom_call_target="tpu_custom_call" | custom-call | flops 268435456 | bytes 2097152 | tf_op jit(solution)/shard_map/slices/pallas_call | solution.py:43
  7.7 3.0 %collective-permute-start.5 = (bf16[16,1024]{1,0:T(8,128)(2,1)S(1)}, bf16[16,1024]{1,0:T(8,128)(2,1)S(1)}, u32[]{:S(2)}, u32[]{:S(2)}) collective-permute-start(bf16[16,1024]{1,0:T(8,128)(2,1)S(1)} %get-tuple-element.36), channel_id=1, source_target_pairs={{0,17},{1,18},{2,19},{3,20},{4,21},{5,22},{6,23},{7,24},{8,25},{9,... | collective-permute-start | bytes 98312 | tf_op jit(solution)/shard_map/ppermute | solution.py:320
  10.8 0.7 reshape.29.mv
  12.1 5.2 %embed.1 = (bf16[512,1024]{1,0:T(8,128)(2,1)S(1)}, bf16[512,1024]{1,0:T(8,128)(2,1)S(1)}, bf16[512,1536]{1,0:T(8,128)(2,1)S(1)}) custom-call(s32[80,16]{1,0:T(8,128)S(1)} %copy.19.own, s32[80,16]{1,0:T(8,128)S(1)} %collective-permute-done.up, s32[80,16]{1,0:T(8,128)S(1)} %collective-permute-done.1.left, s32[80,16]{1,0:T(8,128)S(1)} %collective-permute-done.2.diag, ...), custom_call_target="tpu_custom_call" | custom-call | flops 2684354560 | bytes 9437184 | tf_op jit(solution)/shard_map/embed/pallas_call | solution.py:43
  17.3 4.2 %collective-permute-done.3.up = bf16[64,1024]{1,0:T(8,128)(2,1)S(1)} collective-permute-done((bf16[64,1024]{1,0:T(8,128)(2,1)S(1)}, bf16[64,1024]{1,0:T(8,128)(2,1)S(1)}, u32[]{:S(2)}, u32[]{:S(2)}) %collective-permute-start.3) | collective-permute-done | bytes 131104 | tf_op jit(solution)/shard_map/ppermute | solution.py:320
  21.5 6.9 %attend.2 = (bf16[512,256]{1,0:T(8,128)(2,1)S(1)}, bf16[512,768]{1,0:T(8,128)(2,1)S(1)}, f32[2,256,1024]{2,1,0:T(8,128)S(1)}, bf16[2,256,1024]{2,1,0:T(8,128)(2,1)S(1)}, bf16[512,1024]{1,0:T(8,128)(2,1)S(1)}) custom-call(s32[4]{0:T(128)S(1)} %pad_add_fusion.1.place, bf16[512,1536]{1,0:T(8,128)(2,1)S(1)} %get-tuple-element.32.proj, ...), custom_call_target="tpu_custom_call" | custom-call | flops 3221225472 | bytes 8388608 | tf_op jit(solution)/shard_map/attend/pallas_call | solution.py:43
  28.5 6.3 %attend.3 = (bf16[512,256]{1,0:T(8,128)(2,1)S(1)}, bf16[512,768]{1,0:T(8,128)(2,1)S(1)}, f32[2,256,1024]{2,1,0:T(8,128)S(1)}, bf16[2,256,1024]{2,1,0:T(8,128)(2,1)S(1)}) custom-call(s32[4]{0:T(128)S(1)} %pad_add_fusion.1.place, bf16[512,1536]{1,0:T(8,128)(2,1)S(1)} %get-tuple-element.32.proj, bf16[512,1024]{1,0:T(8,128)(2,1)S(1)} %get-tuple-element.33.normed, ...), custom_call_target="tpu_custom_call" | custom-call | flops 3221225472 | bytes 8388608 | tf_op jit(solution)/shard_map/attend/pallas_call | solution.py:43
  34.8 0.8 collective-permute-start.12
  35.6 0.7 parity_core.1
  36.4 1.5 %collective-permute-done.12 = bf16[2,256,1024]{2,1,0:T(8,128)(2,1)S(1)} collective-permute-done((bf16[2,256,1024]{2,1,0:T(8,128)(2,1)S(1)}, bf16[2,256,1024]{2,1,0:T(8,128)(2,1)S(1)}, u32[]{:S(2)}, u32[]{:S(2)}) %collective-permute-start.12) | collective-permute-done | bytes 1048608 | tf_op jit(solution)/shard_map/ppermute | solution.py:328
  37.9 0.8 high_core.1
  38.7 11.5 %collective-permute-done.10.b = bf16[2,8,16,1024]{3,2,1,0:T(8,128)(2,1)S(1)} collective-permute-done((bf16[2,8,16,1024]{3,2,1,0:T(8,128)(2,1)S(1)}, bf16[2,8,16,1024]{3,2,1,0:T(8,128)(2,1)S(1)}, u32[]{:S(2)}, u32[]{:S(2)}) %collective-permute-start.10) | collective-permute-done | bytes 524320 | tf_op jit(solution)/shard_map/ppermute | solution.py:320
  51.0 2.0 %collective-permute-done.13.b = bf16[2,8,16,1024]{3,2,1,0:T(8,128)(2,1)S(1)} collective-permute-done((bf16[2,8,16,1024]{3,2,1,0:T(8,128)(2,1)S(1)}, bf16[2,8,16,1024]{3,2,1,0:T(8,128)(2,1)S(1)}, u32[]{:S(2)}, u32[]{:S(2)}) %collective-permute-start.13) | collective-permute-done | bytes 524320 | tf_op jit(solution)/shard_map/ppermute | solution.py:320
  53.7 1.1 %collective-permute-start.14 = (bf16[8,16,1024]{2,1,0:T(8,128)(2,1)S(1)}, bf16[8,16,1024]{2,1,0:T(8,128)(2,1)S(1)}, u32[]{:S(2)}, u32[]{:S(2)}) collective-permute-start(bf16[8,16,1024]{2,1,0:T(8,128)(2,1)S(1)} %get-tuple-element.53), channel_id=1, source_target_pairs={{0,1},{1,0},{2,3},{3,2},{4,5},{5,4},{6,7},{7,6},{8,9},{9,8},{10,11... | collective-permute-start | bytes 786440 | tf_op jit(solution)/shard_map/ppermute | solution.py:320
  54.8 8.1 %finish.1 = bf16[2,512,1024]{2,1,0:T(8,128)(2,1)S(1)} custom-call(bf16[512,1024]{1,0:T(8,128)(2,1)S(1)} %get-tuple-element.31.emb, bf16[512,1024]{1,0:T(8,128)(2,1)S(1)} %get-tuple-element.37.cot, bf16[1024,1536]{1,0:T(8,128)(2,1)} %wq.3, bf16[1024,512]{1,0:T(8,128)(2,1)} %ow.5, bf16[512,256]{1,0:T(8,128)(2,1)S(1)} %get-tuple-element.38.att0, ...), custom_call_target="tpu_custom_call" | custom-call | flops 2147483648 | bytes 10485760 | tf_op jit(solution)/shard_map/finish/pallas_call | solution.py:43
  63.6 0.7 slice.47
  64.3 1.1 %collective-permute-start.7 = (bf16[2,4,16,1024]{3,2,1,0:T(8,128)(2,1)}, bf16[2,4,16,1024]{3,2,1,0:T(8,128)(2,1)}, u32[]{:S(2)}, u32[]{:S(2)}) collective-permute-start(bf16[2,4,16,1024]{3,2,1,0:T(8,128)(2,1)} %slice.47), channel_id=1, source_target_pairs={{0,48},{1,49},{2,50},{3,51},{4,52},{5,53},{6,54},{7,55},{8,56},{9,... | collective-permute-start | bytes 786440 | tf_op jit(solution)/shard_map/ppermute | solution.py:320
  65.4 0.9 join.1
  66.3 7.2 %all-to-all-start = ((bf16[8,16,2048]{2,1,0:T(8,128)(2,1)}), bf16[8,16,2048]{2,1,0:T(8,128)(2,1)S(1)}, u32[]{:S(2)}, u32[]{:S(2)}) async-start(bf16[8,16,2048]{2,1,0:T(8,128)(2,1)} %join.1), calls=%async_computation | async-start | bytes 1048576 | tf_op jit(solution)/shard_map/all_to_all | solution.py:441
  73.5 1.1 %slice_bitcast_fusion = (bf16[28,12,1024]{2,1,0:T(8,128)(2,1)S(1)}, bf16[28,12,1024]{2,1,0:T(8,128)(2,1)}) fusion(bf16[2,32,16,1024]{3,2,1,0:T(8,128)(2,1)S(1)} %bitcast.35), kind=kLoop, calls=%fused_computation.2 | loop fusion | bytes 2752512 | tf_op jit(solution)/shard_map/squeeze | solution.py:433
  74.9 3.2 %collective-permute-start.6 = (bf16[2,28,4,1024]{3,2,1,0:T(4,128)(2,1)S(1)}, bf16[2,28,4,1024]{3,2,1,0:T(4,128)(2,1)S(1)}, u32[]{:S(2)}, u32[]{:S(2)}) collective-permute-start(bf16[2,28,4,1024]{3,2,1,0:T(4,128)(2,1)S(1)} %slice.45), channel_id=1, source_target_pairs={{0,15},{1,0},{2,1},{3,2},{4,3},{5,4},{6,5},{7,6},{8,7},{9,8},{10,9... | collective-permute-start | bytes 1376264 | tf_op jit(solution)/shard_map/ppermute | solution.py:320
  78.0 1.4 %slice_bitcast_fusion.6 = (bf16[4,4,1024]{2,1,0:T(4,128)(2,1)}, bf16[4,4,1024]{2,1,0:T(4,128)(2,1)}) fusion(bf16[2,4,4,1024]{3,2,1,0:T(4,128)(2,1)} %collective-permute-done.8), kind=kLoop, calls=%fused_computation.8 | loop fusion | bytes 131072 | tf_op jit(solution)/shard_map/squeeze | solution.py:434
  79.5 1.0 slice_bitcast_fusion.4
  80.5 18.2 %collective-permute-done.6 = bf16[2,28,4,1024]{3,2,1,0:T(4,128)(2,1)S(1)} collective-permute-done((bf16[2,28,4,1024]{3,2,1,0:T(4,128)(2,1)S(1)}, bf16[2,28,4,1024]{3,2,1,0:T(4,128)(2,1)S(1)}, u32[]{:S(2)}, u32[]{:S(2)}) %collective-permute-start.6) | collective-permute-done | bytes 458784 | tf_op jit(solution)/shard_map/ppermute | solution.py:320
  98.9 3.1 %collective-permute-start.17 = (bf16[16,2048]{1,0:T(8,128)(2,1)S(1)}, bf16[16,2048]{1,0:T(8,128)(2,1)S(1)}, u32[]{:S(2)}, u32[]{:S(2)}) collective-permute-start(bf16[16,2048]{1,0:T(8,128)(2,1)S(1)} %get-tuple-element.55), channel_id=1, source_target_pairs={{0,192},{64,128},{128,64},{192,0},{1,193},{65,129},{129,65},{193,1... | collective-permute-start | bytes 196616 | tf_op jit(solution)/shard_map/ppermute | solution.py:328
  103.1 2.7 %maximum_bitcast_fusion = (bf16[1,32,16,1024]{3,2,1,0:T(8,128)(2,1)}, bf16[1,32,16,1024]{3,2,1,0:T(8,128)(2,1)}) fusion(bf16[4,4,1024]{2,1,0:T(4,128)(2,1)} %get-tuple-element.65, bf16[4,12,1024]{2,1,0:T(8,128)(2,1)S(1)} %get-tuple-element.63, bf16[28,4,1024]{2,1,0:T(4,128)(2,1)S(1)} %get-tuple-element.61, bf16[28,12,1024]{2,1,0:T(8,128)(2,1)S(1)} %copy-done, ...), kind=kLoop, calls=%fused_computation | loop fusion | flops 8388608 | bytes 4194304 | tf_op jit(solution)/shard_map/broadcast_in_dim | solution.py:435
  105.8 2.0 %collective-permute-done.16.refs_1_ = bf16[16,2048]{1,0:T(8,128)(2,1)S(1)} collective-permute-done((bf16[16,2048]{1,0:T(8,128)(2,1)S(1)}, bf16[16,2048]{1,0:T(8,128)(2,1)S(1)}, u32[]{:S(2)}, u32[]{:S(2)}) %collective-permute-start.16) | collective-permute-done | bytes 65568 | tf_op jit(solution)/shard_map/ppermute | solution.py:328
  107.8 0.7 level.1
  (32 shorter events, 4.7 us)
Async XLA Ops:
  1.5 9.9 %collective-permute-start.2 = (s32[80,16]{1,0:T(8,128)S(1)}, s32[80,16]{1,0:T(8,128)S(1)}, u32[]{:S(2)}, u32[]{:S(2)}) collective-permute-start(s32[80,16]{1,0:T(8,128)S(1)} %copy.19.own), channel_id=1, source_target_pairs={{0,17},{1,18},{2,19},{3,20},{4,21},{5,22},{6,23},{7,24},{8,25},{9,... | collective-permute-start | bytes 15368 | tf_op jit(solution)/shard_map/ppermute | solution.py:320
  2.9 9.1 %collective-permute-start.1 = (s32[80,16]{1,0:T(8,128)S(1)}, s32[80,16]{1,0:T(8,128)S(1)}, u32[]{:S(2)}, u32[]{:S(2)}) collective-permute-start(s32[80,16]{1,0:T(8,128)S(1)} %copy.19.own), channel_id=1, source_target_pairs={{0,1},{1,2},{2,3},{3,4},{4,5},{5,6},{6,7},{7,8},{8,9},{9,10},{10,1... | collective-permute-start | bytes 15368 | tf_op jit(solution)/shard_map/ppermute | solution.py:320
  4.4 7.6 %collective-permute-start = (s32[80,16]{1,0:T(8,128)S(1)}, s32[80,16]{1,0:T(8,128)S(1)}, u32[]{:S(2)}, u32[]{:S(2)}) collective-permute-start(s32[80,16]{1,0:T(8,128)S(1)} %copy.19.own), channel_id=1, source_target_pairs={{0,16},{1,17},{2,18},{3,19},{4,20},{5,21},{6,22},{7,23},{8,24},{9,... | collective-permute-start | bytes 15368 | tf_op jit(solution)/shard_map/ppermute | solution.py:320
  7.7 9.6 %collective-permute-start.5 = (bf16[16,1024]{1,0:T(8,128)(2,1)S(1)}, bf16[16,1024]{1,0:T(8,128)(2,1)S(1)}, u32[]{:S(2)}, u32[]{:S(2)}) collective-permute-start(bf16[16,1024]{1,0:T(8,128)(2,1)S(1)} %get-tuple-element.36), channel_id=1, source_target_pairs={{0,17},{1,18},{2,19},{3,20},{4,21},{5,22},{6,23},{7,24},{8,25},{9,... | collective-permute-start | bytes 98312 | tf_op jit(solution)/shard_map/ppermute | solution.py:320
  10.7 10.8 %collective-permute-start.3 = (bf16[64,1024]{1,0:T(8,128)(2,1)S(1)}, bf16[64,1024]{1,0:T(8,128)(2,1)S(1)}, u32[]{:S(2)}, u32[]{:S(2)}) collective-permute-start(bf16[64,1024]{1,0:T(8,128)(2,1)S(1)} %get-tuple-element.34), channel_id=1, source_target_pairs={{0,16},{1,17},{2,18},{3,19},{4,20},{5,21},{6,22},{7,23},{8,24},{9,... | collective-permute-start | bytes 393224 | tf_op jit(solution)/shard_map/ppermute | solution.py:320
  11.5 10.0 %collective-permute-start.4 = (bf16[112,1024]{1,0:T(8,128)(2,1)S(1)}, bf16[112,1024]{1,0:T(8,128)(2,1)S(1)}, u32[]{:S(2)}, u32[]{:S(2)}) collective-permute-start(bf16[112,1024]{1,0:T(8,128)(2,1)S(1)} %get-tuple-element.35), channel_id=1, source_target_pairs={{0,1},{1,2},{2,3},{3,4},{4,5},{5,6},{6,7},{7,8},{8,9},{9,10},{10,1... | collective-permute-start | bytes 688136 | tf_op jit(solution)/shard_map/ppermute | solution.py:320
  28.4 7.2 %collective-permute-start.9 = (bf16[2,256,1024]{2,1,0:T(8,128)(2,1)S(1)}, bf16[2,256,1024]{2,1,0:T(8,128)(2,1)S(1)}, u32[]{:S(2)}, u32[]{:S(2)}) collective-permute-start(bf16[2,256,1024]{2,1,0:T(8,128)(2,1)S(1)} %get-tuple-element.43), channel_id=1, source_target_pairs={{0,16},{16,0},{1,17},{17,1},{2,18},{18,2},{3,19},{19,3},{4,20},{20... | collective-permute-start | bytes 3145736 | tf_op jit(solution)/shard_map/ppermute | solution.py:328
  34.8 3.1 %collective-permute-start.12 = (bf16[2,256,1024]{2,1,0:T(8,128)(2,1)S(1)}, bf16[2,256,1024]{2,1,0:T(8,128)(2,1)S(1)}, u32[]{:S(2)}, u32[]{:S(2)}) collective-permute-start(bf16[2,256,1024]{2,1,0:T(8,128)(2,1)S(1)} %get-tuple-element.49), channel_id=1, source_target_pairs={{0,16},{16,0},{1,17},{17,1},{2,18},{18,2},{3,19},{19,3},{4,20},{20... | collective-permute-start | bytes 3145736 | tf_op jit(solution)/shard_map/ppermute | solution.py:328
  36.3 13.9 %collective-permute-start.10 = (bf16[2,8,16,1024]{3,2,1,0:T(8,128)(2,1)S(1)}, bf16[2,8,16,1024]{3,2,1,0:T(8,128)(2,1)S(1)}, u32[]{:S(2)}, u32[]{:S(2)}) collective-permute-start(bf16[2,8,16,1024]{3,2,1,0:T(8,128)(2,1)S(1)} %get-tuple-element.45), channel_id=1, source_target_pairs={{0,1},{1,0},{2,3},{3,2},{4,5},{5,4},{6,7},{7,6},{8,9},{9,8},{10,11... | collective-permute-start | bytes 1572872 | tf_op jit(solution)/shard_map/ppermute | solution.py:320
  38.6 14.4 %collective-permute-start.13 = (bf16[2,8,16,1024]{3,2,1,0:T(8,128)(2,1)S(1)}, bf16[2,8,16,1024]{3,2,1,0:T(8,128)(2,1)S(1)}, u32[]{:S(2)}, u32[]{:S(2)}) collective-permute-start(bf16[2,8,16,1024]{3,2,1,0:T(8,128)(2,1)S(1)} %get-tuple-element.51), channel_id=1, source_target_pairs={{0,33},{1,32},{2,35},{3,34},{4,37},{5,36},{6,39},{7,38},{8,41},{9,... | collective-permute-start | bytes 1572872 | tf_op jit(solution)/shard_map/ppermute | solution.py:320
  50.9 14.5 %collective-permute-start.11 = (bf16[8,16,1024]{2,1,0:T(8,128)(2,1)S(1)}, bf16[8,16,1024]{2,1,0:T(8,128)(2,1)S(1)}, u32[]{:S(2)}, u32[]{:S(2)}) collective-permute-start(bf16[8,16,1024]{2,1,0:T(8,128)(2,1)S(1)} %get-tuple-element.47), channel_id=1, source_target_pairs={{0,33},{1,32},{2,35},{3,34},{4,37},{5,36},{6,39},{7,38},{8,41},{9,... | collective-permute-start | bytes 786440 | tf_op jit(solution)/shard_map/ppermute | solution.py:320
  53.7 11.7 %collective-permute-start.14 = (bf16[8,16,1024]{2,1,0:T(8,128)(2,1)S(1)}, bf16[8,16,1024]{2,1,0:T(8,128)(2,1)S(1)}, u32[]{:S(2)}, u32[]{:S(2)}) collective-permute-start(bf16[8,16,1024]{2,1,0:T(8,128)(2,1)S(1)} %get-tuple-element.53), channel_id=1, source_target_pairs={{0,1},{1,0},{2,3},{3,2},{4,5},{5,4},{6,7},{7,6},{8,9},{9,8},{10,11... | collective-permute-start | bytes 786440 | tf_op jit(solution)/shard_map/ppermute | solution.py:320
  64.3 13.8 %collective-permute-start.8 = (bf16[2,4,4,1024]{3,2,1,0:T(4,128)(2,1)}, bf16[2,4,4,1024]{3,2,1,0:T(4,128)(2,1)}, u32[]{:S(2)}, u32[]{:S(2)}) collective-permute-start(bf16[2,4,4,1024]{3,2,1,0:T(4,128)(2,1)} %slice.49), channel_id=1, source_target_pairs={{0,63},{1,48},{2,49},{3,50},{4,51},{5,52},{6,53},{7,54},{8,55},{9,... | collective-permute-start | bytes 196616 | tf_op jit(solution)/shard_map/ppermute | solution.py:320
  64.3 15.2 %collective-permute-start.7 = (bf16[2,4,16,1024]{3,2,1,0:T(8,128)(2,1)}, bf16[2,4,16,1024]{3,2,1,0:T(8,128)(2,1)}, u32[]{:S(2)}, u32[]{:S(2)}) collective-permute-start(bf16[2,4,16,1024]{3,2,1,0:T(8,128)(2,1)} %slice.47), channel_id=1, source_target_pairs={{0,48},{1,49},{2,50},{3,51},{4,52},{5,53},{6,54},{7,55},{8,56},{9,... | collective-permute-start | bytes 786440 | tf_op jit(solution)/shard_map/ppermute | solution.py:320
  66.3 32.5 %all-to-all-start = ((bf16[8,16,2048]{2,1,0:T(8,128)(2,1)}), bf16[8,16,2048]{2,1,0:T(8,128)(2,1)S(1)}, u32[]{:S(2)}, u32[]{:S(2)}) async-start(bf16[8,16,2048]{2,1,0:T(8,128)(2,1)} %join.1), calls=%async_computation | async-start | bytes 1048576 | tf_op jit(solution)/shard_map/all_to_all | solution.py:441
  74.8 28.2 %copy-start = (bf16[28,12,1024]{2,1,0:T(8,128)(2,1)S(1)}, bf16[28,12,1024]{2,1,0:T(8,128)(2,1)}, u32[]{:S(2)}) copy-start(bf16[28,12,1024]{2,1,0:T(8,128)(2,1)} %get-tuple-element.59) | copy-start | bytes 2064388
  74.9 23.8 %collective-permute-start.6 = (bf16[2,28,4,1024]{3,2,1,0:T(4,128)(2,1)S(1)}, bf16[2,28,4,1024]{3,2,1,0:T(4,128)(2,1)S(1)}, u32[]{:S(2)}, u32[]{:S(2)}) collective-permute-start(bf16[2,28,4,1024]{3,2,1,0:T(4,128)(2,1)S(1)} %slice.45), channel_id=1, source_target_pairs={{0,15},{1,0},{2,1},{3,2},{4,3},{5,4},{6,5},{7,6},{8,7},{9,8},{10,9... | collective-permute-start | bytes 1376264 | tf_op jit(solution)/shard_map/ppermute | solution.py:320
  98.9 6.9 %collective-permute-start.17 = (bf16[16,2048]{1,0:T(8,128)(2,1)S(1)}, bf16[16,2048]{1,0:T(8,128)(2,1)S(1)}, u32[]{:S(2)}, u32[]{:S(2)}) collective-permute-start(bf16[16,2048]{1,0:T(8,128)(2,1)S(1)} %get-tuple-element.55), channel_id=1, source_target_pairs={{0,192},{64,128},{128,64},{192,0},{1,193},{65,129},{129,65},{193,1... | collective-permute-start | bytes 196616 | tf_op jit(solution)/shard_map/ppermute | solution.py:328
  102.0 5.8 %collective-permute-start.16 = (bf16[16,2048]{1,0:T(8,128)(2,1)S(1)}, bf16[16,2048]{1,0:T(8,128)(2,1)S(1)}, u32[]{:S(2)}, u32[]{:S(2)}) collective-permute-start(bf16[16,2048]{1,0:T(8,128)(2,1)S(1)} %get-tuple-element.55), channel_id=1, source_target_pairs={{0,128},{64,192},{128,0},{192,64},{1,129},{65,193},{129,1},{193,65... | collective-permute-start | bytes 196616 | tf_op jit(solution)/shard_map/ppermute | solution.py:328
  102.6 5.2 %collective-permute-start.15 = (bf16[16,2048]{1,0:T(8,128)(2,1)S(1)}, bf16[16,2048]{1,0:T(8,128)(2,1)S(1)}, u32[]{:S(2)}, u32[]{:S(2)}) collective-permute-start(bf16[16,2048]{1,0:T(8,128)(2,1)S(1)} %get-tuple-element.55), channel_id=1, source_target_pairs={{0,64},{64,0},{128,192},{192,128},{1,65},{65,1},{129,193},{193,129... | collective-permute-start | bytes 196616 | tf_op jit(solution)/shard_map/ppermute | solution.py:328

commit v3 on v2

--- a/solution.py
+++ b/solution.py
@@ -143,7 +143,7 @@
         cb, ct = code_b[here], code_t[here]
         lane = iota((BAND, 512), 1)
         x = dot(hot(lane == cb), tables[0], 1, 0)
-        x = jnp.where(cb == 512, mv[...].astype(F32), x)
+        x = jnp.where(cb == 512, mv[...].astype(F32).reshape(1, MODEL), x)
         x = (x + dot(hot(lane == ct), tables[1], 1, 0)).astype(BF16)
         emb[here] = x
         centred, inverse = moments(x.astype(F32))
@@ -238,30 +238,58 @@
             out[half, :, 3 * CW :] = dot(cot[:, cut], att[...], 0, 0).astype(out.dtype)
 
 
-def finish_kernel(emb, cot, wq, ow, att0, att1, gp0, gp1, both, weight, last, sems):
+def finish_kernel(emb, cot, wq, ow, att0, att1, gp0, gp1, mid, up, left, diag, tick, weight, last, sems):
     copies = [
         pltpu.make_async_copy(ow, last, sems.at[0]),
         pltpu.make_async_copy(wq, weight, sems.at[1]),
     ]
     for copy in copies:
         copy.start()
-    for copy in copies:
-        copy.wait()
+    copies[0].wait()
+
+    def put(i, block, values):
+        if block == 0:
+            up[i] = values[:64]
+            mid[i, 0:64] = values[64:]
+        else:
+            at = block * BAND - 64
+            mid[i, at : at + BAND] = values
+
     for block in range(BANDS):
         here = slice(block * BAND, (block + 1) * BAND)
-        x = emb[here].astype(F32)
         att = jnp.concatenate([att0[here], att1[here]], axis=1)
-        both[0, here] = (x + dot(att, last[...], 1, 1)).astype(BF16)
+        put(0, block, (emb[here].astype(F32) + dot(att, last[...], 1, 1)).astype(BF16))
+    copies[1].wait()
+    for block in range(BANDS):
+        here = slice(block * BAND, (block + 1) * BAND)
         g0, g1 = gp0[here], gp1[here]
         parts = []
         for i in range(3):
             parts += [g0[:, i * CW : (i + 1) * CW], g1[:, i * CW : (i + 1) * CW]]
         gst = dot(jnp.concatenate(parts, axis=1), weight[...], 1, 1)
-        centred, inverse = moments(x)
+        centred, inverse = moments(emb[here].astype(F32))
         standard = centred * inverse
         m1 = jnp.mean(gst, axis=1, keepdims=True)
         m2 = jnp.mean(gst * standard, axis=1, keepdims=True)
-        both[1, here] = (cot[here].astype(F32) + inverse * (gst - m1 - standard * m2)).astype(BF16)
+        values = cot[here].astype(F32) + inverse * (gst - m1 - standard * m2)
+        put(1, block, values.astype(BF16))
+    pick, corner = late_cells(OWN, MSG, True), late_cells(64, 16, True)
+    for i in range(2):
+        left[i] = dot(pick, mid[i], 1, 0).astype(BF16)
+        diag[i] = dot(corner, up[i], 1, 0).astype(BF16)
+    tick[...] = jnp.zeros(tick.shape, F32)
+
+
+def place_kernel(mid, up, left, diag, out, gin):
+    late = (iota((64, 1), 0) & 15) >= LATE
+    corner = late_cells(64, 16, False)
+    for i, ref in enumerate((out, gin)):
+        ref[OWN:] = jnp.where(late, dot(corner, diag[i], 1, 0), up[i].astype(F32)).astype(BF16)
+        for at in range(0, OWN, 64):
+            m, t = iota((64, MSG), 1), at + iota((64, MSG), 0)
+            spread = hot(t == (m >> 2) * COLS + LATE + (m & 3))
+            values = dot(spread, left[i], 1, 0)
+            ref[at : at + 64] = jnp.where(late, values, mid[i, at : at + 64].astype(F32)).astype(BF16)
 
 
 W = 4 * CW
@@ -275,7 +303,7 @@
             out[u] = (a[u, :, v] + b[u, :, v].astype(F32)).astype(out.dtype)
 
 
-def parity_pair(place, a, b, keep, send):
+def parity_pair(place, a, b, tick, keep, send):
     for out, u in ((keep, place[2]), (send, place[2] ^ 1)):
         out[...] = (a[u] + b[u].astype(F32)).astype(out.dtype)
 
@@ -286,7 +314,7 @@
             out[v] = (a[u, :, v] + b[u, :, v].astype(F32)).astype(out.dtype)
 
 
-def high_pair(place, a, b, keep, send):
+def high_pair(place, a, b, tick, keep, send):
     for out, v in ((keep, place[3]), (send, place[3] ^ 1)):
         out[...] = (a[v] + b[v].astype(F32)).astype(out.dtype)
 
@@ -346,12 +374,12 @@
     )
 
 
-def sum_x(place, keep, send, order):
+def sum_x(place, keep, send, tick, order):
     fold = (2, 8, 2, 16, W)
     core, pair = (parity_core, parity_pair) if order[0] == 1 else (high_core, high_pair)
     recv = swap(send, "core", 1)
     keep, send = halve(core, (2, 8, 16, W), place, keep.reshape(fold), recv.reshape(fold))
-    keep, send = halve(pair, (8, 16, W), place, keep, swap_x(send, order[0]))
+    keep, send = halve(pair, (8, 16, W), place, keep, swap_x(send, order[0]), tick)
     return [keep, swap_x(send, order[1])]
 
 
@@ -382,7 +410,7 @@
     emb, normed, proj = call(
         embed_kernel,
         [sds((TOKENS, MODEL)), sds((TOKENS, MODEL)), sds((TOKENS, 3 * HW))],
-        (*near, bottom_table, top_table, mask_vector.reshape(1, MODEL), qkv_weight),
+        (*near, bottom_table, top_table, mask_vector, qkv_weight),
         [vmem()] * 4 + [hbm(), hbm(), vmem(), hbm()],
         2 * TOKENS * 1024 * 2560,
         9 * 2**20,
@@ -413,10 +441,9 @@
         name="attend",
         scratch=[column, pltpu.SemaphoreType.DMA],
     )
-    summed = sum_x(place, keep0, send0, (1, 3)) + sum_x(place, keep1, send1, (3, 1))
-    both = call(
+    *sent, tick = call(
         finish_kernel,
-        sds((2, TOKENS, MODEL)),
+        [sds((2, OWN, MODEL)), sds((2, 64, MODEL)), sds((2, MSG, MODEL)), sds((2, 16, MODEL)), sds((8, 128), F32)],
         (emb, cot, qkv_weight, out_weight, att0, att1, gp0, gp1),
         [vmem(), vmem(), hbm(), hbm()] + [vmem()] * 4,
         2 * TOKENS * 1024 * 2048,
@@ -424,16 +451,19 @@
         name="finish",
         scratch=[pltpu.VMEM((MODEL, 3 * HW), BF16), pltpu.VMEM((MODEL, HW), BF16), sems(2)],
     )
-    both = both.reshape(2, ROWS, COLS, MODEL)
-    r_up = shift(both[:, :SHIFT], -1, 0)
-    r_left = shift(both[:, SHIFT:, LATE:], 0, -1)
-    r_diag = shift(both[:, :SHIFT, LATE:], -1, -1)
-
-    def back(i):
-        upper = jnp.concatenate([both[i, SHIFT:, :LATE], r_left[i]], axis=1)
-        lower = jnp.concatenate([r_up[i, :, :LATE], r_diag[i]], axis=1)
-        return jnp.concatenate([upper, lower], axis=0)[None]
-
+    summed = sum_x(place, keep0, send0, tick, (1, 3)) + sum_x(place, keep1, send1, tick, (3, 1))
+    mid, up, left, diag = sent
+    up, left, diag = shift(up, -1, 0), shift(left, 0, -1), shift(diag, -1, -1)
+    out, gin = call(
+        place_kernel,
+        [sds((TOKENS, MODEL))] * 2,
+        (mid, up, left, diag),
+        [vmem()] * 4,
+        2**28,
+        5 * 2**20,
+        limit=24,
+        name="place",
+    )
     factor = 1.0 / math.sqrt(TOKENS * NB * NLAT * NLON)
     joined = call(
         join_kernel, sds((8, 16, 2 * W)), summed, [vmem()] * 4, 2**19, 2**21, limit=16, name="join"
@@ -459,7 +489,8 @@
         limit=16,
         name="level",
     )
-    return (back(0), back(1), g_qkv, g_out)
+    shape = (1, ROWS, COLS, MODEL)
+    return (out.reshape(shape), gin.reshape(shape), g_qkv, g_out)
 
 
 def solution(mesh):

time: 109 us -> 97.3 us (0.89)
  the two profiles are of different devices: /device:TPU:2 before, /device:TPU:3 now
where the time goes in v3:
time: 97.3 us; the launch traced here: 97 us
  Pallas kernels  34.7 us (36%)
  starting transfers between devices  32.5 us (33%)
  waiting for transfers between devices  27.3 us (28%)
    pallas_call x13, Pallas kernels, call(): pl.pallas_call(kernel, out_shape=outs, in_specs=specs, out_specs=jax.tree...  34.7 us
    ppermute x13, starting transfers between devices, permute(): return lax.ppermute(x, GRID, pairs)  18.4 us
    ppermute x13, waiting for transfers between devices, permute(): return lax.ppermute(x, GRID, pairs)  16.6 us
    all_to_all x1, waiting for transfers between devices, shards(): depth = lax.all_to_all(joined, 'z', 0, 0, tiled=True)  8.98 us
    ppermute x5, starting transfers between devices, swap(): lax.ppermute(x, axis, [(i, i ^ flip) for i in range(lax.axis_size(axis))])  7.75 us
    all_to_all x1, starting transfers between devices, shards(): depth = lax.all_to_all(joined, 'z', 0, 0, tiled=True)  6.38 us
  transfers between devices with their start and end apart: 19, of which 7 were waited for; matrix products, arithmetic and copies ran while one was open for 0% of the time, Pallas kernels for 27%

profile of v3, /device:TPU:3, one launch (start us, length us, event | category | flops | bytes accessed | tf_op | source)
XLA Modules:
  0.0 97.0 jit_solution(17304611051492749230)
XLA Ops:
  0.6 0.8 pad_add_fusion
  1.5 3.2 %collective-permute-start.2 = (s32[80,16]{1,0:T(8,128)S(1)}, s32[80,16]{1,0:T(8,128)S(1)}, u32[]{:S(2)}, u32[]{:S(2)}) collective-permute-start(s32[80,16]{1,0:T(8,128)S(1)} %copy.19.own), channel_id=1, source_target_pairs={{0,17},{1,18},{2,19},{3,20},{4,21},{5,22},{6,23},{7,24},{8,25},{9,... | collective-permute-start | bytes 15368 | tf_op jit(solution)/shard_map/ppermute | solution.py:348
  4.7 1.5 %collective-permute-start.1 = (s32[80,16]{1,0:T(8,128)S(1)}, s32[80,16]{1,0:T(8,128)S(1)}, u32[]{:S(2)}, u32[]{:S(2)}) collective-permute-start(s32[80,16]{1,0:T(8,128)S(1)} %copy.19.own), channel_id=1, source_target_pairs={{0,1},{1,2},{2,3},{3,4},{4,5},{5,6},{6,7},{7,8},{8,9},{9,10},{10,1... | collective-permute-start | bytes 15368 | tf_op jit(solution)/shard_map/ppermute | solution.py:348
  6.8 1.6 %slices.1 = (bf16[64,1024]{1,0:T(8,128)(2,1)S(1)}, bf16[112,1024]{1,0:T(8,128)(2,1)S(1)}, bf16[16,1024]{1,0:T(8,128)(2,1)S(1)}) custom-call(bf16[512,1024]{1,0:T(8,128)(2,1)} %bitcast.18), custom_call_target="tpu_custom_call" | custom-call | flops 268435456 | bytes 2097152 | tf_op jit(solution)/shard_map/slices/pallas_call | solution.py:43
  8.4 0.8 collective-permute-start.5
  9.2 1.6 %collective-permute-start.3 = (bf16[64,1024]{1,0:T(8,128)(2,1)S(1)}, bf16[64,1024]{1,0:T(8,128)(2,1)S(1)}, u32[]{:S(2)}, u32[]{:S(2)}) collective-permute-start(bf16[64,1024]{1,0:T(8,128)(2,1)S(1)} %get-tuple-element.41), channel_id=1, source_target_pairs={{0,16},{1,17},{2,18},{3,19},{4,20},{5,21},{6,22},{7,23},{8,24},{9,... | collective-permute-start | bytes 393224 | tf_op jit(solution)/shard_map/ppermute | solution.py:348
  11.0 2.6 %collective-permute-start.4 = (bf16[112,1024]{1,0:T(8,128)(2,1)S(1)}, bf16[112,1024]{1,0:T(8,128)(2,1)S(1)}, u32[]{:S(2)}, u32[]{:S(2)}) collective-permute-start(bf16[112,1024]{1,0:T(8,128)(2,1)S(1)} %get-tuple-element.42), channel_id=1, source_target_pairs={{0,1},{1,2},{2,3},{3,4},{4,5},{5,6},{6,7},{7,8},{8,9},{9,10},{10,1... | collective-permute-start | bytes 688136 | tf_op jit(solution)/shard_map/ppermute | solution.py:348
  13.6 0.7 copy-done
  14.3 5.2 %embed.1 = (bf16[512,1024]{1,0:T(8,128)(2,1)S(1)}, bf16[512,1024]{1,0:T(8,128)(2,1)S(1)}, bf16[512,1536]{1,0:T(8,128)(2,1)S(1)}) custom-call(s32[80,16]{1,0:T(8,128)S(1)} %copy.19.own, s32[80,16]{1,0:T(8,128)S(1)} %collective-permute-done.up, s32[80,16]{1,0:T(8,128)S(1)} %collective-permute-done.1.left, s32[80,16]{1,0:T(8,128)S(1)} %collective-permute-done.2.diag, ...), custom_call_target="tpu_custom_call" | custom-call | flops 2684354560 | bytes 9437184 | tf_op jit(solution)/shard_map/embed/pallas_call | solution.py:43
  19.5 6.9 %attend.2 = (bf16[512,256]{1,0:T(8,128)(2,1)S(1)}, bf16[512,768]{1,0:T(8,128)(2,1)S(1)}, f32[2,256,1024]{2,1,0:T(8,128)S(1)}, bf16[2,256,1024]{2,1,0:T(8,128)(2,1)S(1)}, bf16[512,1024]{1,0:T(8,128)(2,1)S(1)}) custom-call(s32[4]{0:T(128)S(1)} %pad_add_fusion.1.place, bf16[512,1536]{1,0:T(8,128)(2,1)S(1)} %get-tuple-element.39.proj, ...), custom_call_target="tpu_custom_call" | custom-call | flops 3221225472 | bytes 8388608 | tf_op jit(solution)/shard_map/attend/pallas_call | solution.py:43
  26.4 2.8 %collective-permute-start.9 = (bf16[2,256,1024]{2,1,0:T(8,128)(2,1)S(1)}, bf16[2,256,1024]{2,1,0:T(8,128)(2,1)S(1)}, u32[]{:S(2)}, u32[]{:S(2)}) collective-permute-start(bf16[2,256,1024]{2,1,0:T(8,128)(2,1)S(1)} %get-tuple-element.56), channel_id=1, source_target_pairs={{0,16},{16,0},{1,17},{17,1},{2,18},{18,2},{3,19},{19,3},{4,20},{20... | collective-permute-start | bytes 3145736 | tf_op jit(solution)/shard_map/ppermute | solution.py:356
  29.2 6.2 %attend.3 = (bf16[512,256]{1,0:T(8,128)(2,1)S(1)}, bf16[512,768]{1,0:T(8,128)(2,1)S(1)}, f32[2,256,1024]{2,1,0:T(8,128)S(1)}, bf16[2,256,1024]{2,1,0:T(8,128)(2,1)S(1)}) custom-call(s32[4]{0:T(128)S(1)} %pad_add_fusion.1.place, bf16[512,1536]{1,0:T(8,128)(2,1)S(1)} %get-tuple-element.39.proj, bf16[512,1024]{1,0:T(8,128)(2,1)S(1)} %get-tuple-element.40.normed, ...), custom_call_target="tpu_custom_call" | custom-call | flops 3221225472 | bytes 8388608 | tf_op jit(solution)/shard_map/attend/pallas_call | solution.py:43
  35.8 0.7 parity_core.1
  36.7 1.7 %collective-permute-done.12 = bf16[2,256,1024]{2,1,0:T(8,128)(2,1)S(1)} collective-permute-done((bf16[2,256,1024]{2,1,0:T(8,128)(2,1)S(1)}, bf16[2,256,1024]{2,1,0:T(8,128)(2,1)S(1)}, u32[]{:S(2)}, u32[]{:S(2)}) %collective-permute-start.12) | collective-permute-done | bytes 1048608 | tf_op jit(solution)/shard_map/ppermute | solution.py:356
  38.4 0.7 high_core.1
  39.2 8.5 %finish.1 = (bf16[2,448,1024]{2,1,0:T(8,128)(2,1)S(1)}, bf16[2,64,1024]{2,1,0:T(8,128)(2,1)S(1)}, bf16[2,112,1024]{2,1,0:T(8,128)(2,1)}, bf16[2,16,1024]{2,1,0:T(8,128)(2,1)S(1)}, f32[8,128]{1,0:T(8,128)S(1)}) custom-call(bf16[512,1024]{1,0:T(8,128)(2,1)S(1)} %get-tuple-element.38.emb, bf16[512,1024]{1,0:T(8,128)(2,1)S(1)} %get-tuple-element.44.cot, ...), custom_call_target="tpu_custom_call" | custom-call | flops 2147483648 | bytes 10485760 | tf_op jit(solution)/shard_map/finish/pallas_call | solution.py:43
  47.7 1.9 %collective-permute-done.10.b = bf16[2,8,16,1024]{3,2,1,0:T(8,128)(2,1)S(1)} collective-permute-done((bf16[2,8,16,1024]{3,2,1,0:T(8,128)(2,1)S(1)}, bf16[2,8,16,1024]{3,2,1,0:T(8,128)(2,1)S(1)}, u32[]{:S(2)}, u32[]{:S(2)}) %collective-permute-start.10) | collective-permute-done | bytes 524320 | tf_op jit(solution)/shard_map/ppermute | solution.py:348
  49.6 0.7 parity_pair.1
  50.3 2.3 %collective-permute-done.13.b = bf16[2,8,16,1024]{3,2,1,0:T(8,128)(2,1)S(1)} collective-permute-done((bf16[2,8,16,1024]{3,2,1,0:T(8,128)(2,1)S(1)}, bf16[2,8,16,1024]{3,2,1,0:T(8,128)(2,1)S(1)}, u32[]{:S(2)}, u32[]{:S(2)}) %collective-permute-start.13) | collective-permute-done | bytes 524320 | tf_op jit(solution)/shard_map/ppermute | solution.py:348
  53.3 1.1 %collective-permute-start.14 = (bf16[8,16,1024]{2,1,0:T(8,128)(2,1)S(1)}, bf16[8,16,1024]{2,1,0:T(8,128)(2,1)S(1)}, u32[]{:S(2)}, u32[]{:S(2)}) collective-permute-start(bf16[8,16,1024]{2,1,0:T(8,128)(2,1)S(1)} %get-tuple-element.67), channel_id=1, source_target_pairs={{0,1},{1,0},{2,3},{3,2},{4,5},{5,4},{6,7},{7,6},{8,9},{9,8},{10,11... | collective-permute-start | bytes 786440 | tf_op jit(solution)/shard_map/ppermute | solution.py:348
  54.3 2.7 %collective-permute-done.11.b = bf16[8,16,1024]{2,1,0:T(8,128)(2,1)S(1)} collective-permute-done((bf16[8,16,1024]{2,1,0:T(8,128)(2,1)S(1)}, bf16[8,16,1024]{2,1,0:T(8,128)(2,1)S(1)}, u32[]{:S(2)}, u32[]{:S(2)}) %collective-permute-start.11) | collective-permute-done | bytes 262176 | tf_op jit(solution)/shard_map/ppermute | solution.py:348
  57.0 3.1 %collective-permute-done.14.d = bf16[8,16,1024]{2,1,0:T(8,128)(2,1)S(1)} collective-permute-done((bf16[8,16,1024]{2,1,0:T(8,128)(2,1)S(1)}, bf16[8,16,1024]{2,1,0:T(8,128)(2,1)S(1)}, u32[]{:S(2)}, u32[]{:S(2)}) %collective-permute-start.14) | collective-permute-done | bytes 262176 | tf_op jit(solution)/shard_map/ppermute | solution.py:348
  60.2 0.9 join.1
  61.1 6.4 %all-to-all-start = ((bf16[8,16,2048]{2,1,0:T(8,128)(2,1)}), bf16[8,16,2048]{2,1,0:T(8,128)(2,1)S(1)}, u32[]{:S(2)}, u32[]{:S(2)}) async-start(bf16[8,16,2048]{2,1,0:T(8,128)(2,1)} %join.1), calls=%async_computation | async-start | bytes 1048576 | tf_op jit(solution)/shard_map/all_to_all | solution.py:471
  67.4 2.6 %collective-permute-start.6 = (bf16[2,64,1024]{2,1,0:T(8,128)(2,1)S(1)}, bf16[2,64,1024]{2,1,0:T(8,128)(2,1)S(1)}, u32[]{:S(2)}, u32[]{:S(2)}) collective-permute-start(bf16[2,64,1024]{2,1,0:T(8,128)(2,1)S(1)} %get-tuple-element.50), channel_id=1, source_target_pairs={{0,48},{1,49},{2,50},{3,51},{4,52},{5,53},{6,54},{7,55},{8,56},{9,... | collective-permute-start | bytes 786440 | tf_op jit(solution)/shard_map/ppermute | solution.py:348
  70.1 3.9 %collective-permute-start.8 = (bf16[2,16,1024]{2,1,0:T(8,128)(2,1)S(1)}, bf16[2,16,1024]{2,1,0:T(8,128)(2,1)S(1)}, u32[]{:S(2)}, u32[]{:S(2)}) collective-permute-start(bf16[2,16,1024]{2,1,0:T(8,128)(2,1)S(1)} %get-tuple-element.52), channel_id=1, source_target_pairs={{0,63},{1,48},{2,49},{3,50},{4,51},{5,52},{6,53},{7,54},{8,55},{9,... | collective-permute-start | bytes 196616 | tf_op jit(solution)/shard_map/ppermute | solution.py:348
  73.9 9.0 %all-to-all-done.ref = bf16[8,16,2048]{2,1,0:T(8,128)(2,1)S(1)} async-done(((bf16[8,16,2048]{2,1,0:T(8,128)(2,1)}), bf16[8,16,2048]{2,1,0:T(8,128)(2,1)S(1)}, u32[]{:S(2)}, u32[]{:S(2)}) %all-to-all-start) | async-done | bytes 524320 | tf_op jit(solution)/shard_map/all_to_all | solution.py:471
  83.0 2.8 %collective-permute-start.17 = (bf16[16,2048]{1,0:T(8,128)(2,1)S(1)}, bf16[16,2048]{1,0:T(8,128)(2,1)S(1)}, u32[]{:S(2)}, u32[]{:S(2)}) collective-permute-start(bf16[16,2048]{1,0:T(8,128)(2,1)S(1)} %get-tuple-element.69), channel_id=1, source_target_pairs={{0,192},{64,128},{128,64},{192,0},{1,193},{65,129},{129,65},{193,1... | collective-permute-start | bytes 196616 | tf_op jit(solution)/shard_map/ppermute | solution.py:356
  86.2 6.7 %collective-permute-done.8.diag = bf16[2,16,1024]{2,1,0:T(8,128)(2,1)S(1)} collective-permute-done((bf16[2,16,1024]{2,1,0:T(8,128)(2,1)S(1)}, bf16[2,16,1024]{2,1,0:T(8,128)(2,1)S(1)}, u32[]{:S(2)}, u32[]{:S(2)}) %collective-permute-start.8) | collective-permute-done | bytes 65568 | tf_op jit(solution)/shard_map/ppermute | solution.py:348
  92.8 1.5 %collective-permute-start.15 = (bf16[16,2048]{1,0:T(8,128)(2,1)S(1)}, bf16[16,2048]{1,0:T(8,128)(2,1)S(1)}, u32[]{:S(2)}, u32[]{:S(2)}) collective-permute-start(bf16[16,2048]{1,0:T(8,128)(2,1)S(1)} %get-tuple-element.69), channel_id=1, source_target_pairs={{0,64},{64,0},{128,192},{192,128},{1,65},{65,1},{129,193},{193,129... | collective-permute-start | bytes 196616 | tf_op jit(solution)/shard_map/ppermute | solution.py:356
  94.3 2.0 %place.1 = (bf16[512,1024]{1,0:T(8,128)(2,1)}, bf16[512,1024]{1,0:T(8,128)(2,1)}) custom-call(bf16[2,448,1024]{2,1,0:T(8,128)(2,1)S(1)} %get-tuple-element.49.mid, bf16[2,64,1024]{2,1,0:T(8,128)(2,1)S(1)} %collective-permute-done.6.up, bf16[2,112,1024]{2,1,0:T(8,128)(2,1)S(1)} %collective-permute-done.7.left, ...), custom_call_target="tpu_custom_call" | custom-call | flops 268435456 | bytes 5242880 | tf_op jit(solution)/shard_map/place/pallas_call | solution.py:43
  96.3 0.7 level.1
  (24 shorter events, 2.6 us)
Async XLA Ops:
  1.5 9.4 %collective-permute-start.2 = (s32[80,16]{1,0:T(8,128)S(1)}, s32[80,16]{1,0:T(8,128)S(1)}, u32[]{:S(2)}, u32[]{:S(2)}) collective-permute-start(s32[80,16]{1,0:T(8,128)S(1)} %copy.19.own), channel_id=1, source_target_pairs={{0,17},{1,18},{2,19},{3,20},{4,21},{5,22},{6,23},{7,24},{8,25},{9,... | collective-permute-start | bytes 15368 | tf_op jit(solution)/shard_map/ppermute | solution.py:348
  4.7 8.9 %collective-permute-start.1 = (s32[80,16]{1,0:T(8,128)S(1)}, s32[80,16]{1,0:T(8,128)S(1)}, u32[]{:S(2)}, u32[]{:S(2)}) collective-permute-start(s32[80,16]{1,0:T(8,128)S(1)} %copy.19.own), channel_id=1, source_target_pairs={{0,1},{1,2},{2,3},{3,4},{4,5},{5,6},{6,7},{7,8},{8,9},{9,10},{10,1... | collective-permute-start | bytes 15368 | tf_op jit(solution)/shard_map/ppermute | solution.py:348
  6.2 7.3 %collective-permute-start = (s32[80,16]{1,0:T(8,128)S(1)}, s32[80,16]{1,0:T(8,128)S(1)}, u32[]{:S(2)}, u32[]{:S(2)}) collective-permute-start(s32[80,16]{1,0:T(8,128)S(1)} %copy.19.own), channel_id=1, source_target_pairs={{0,16},{1,17},{2,18},{3,19},{4,20},{5,21},{6,22},{7,23},{8,24},{9,... | collective-permute-start | bytes 15368 | tf_op jit(solution)/shard_map/ppermute | solution.py:348
  8.4 11.1 %collective-permute-start.5 = (bf16[16,1024]{1,0:T(8,128)(2,1)S(1)}, bf16[16,1024]{1,0:T(8,128)(2,1)S(1)}, u32[]{:S(2)}, u32[]{:S(2)}) collective-permute-start(bf16[16,1024]{1,0:T(8,128)(2,1)S(1)} %get-tuple-element.43), channel_id=1, source_target_pairs={{0,17},{1,18},{2,19},{3,20},{4,21},{5,22},{6,23},{7,24},{8,25},{9,... | collective-permute-start | bytes 98312 | tf_op jit(solution)/shard_map/ppermute | solution.py:348
  9.2 10.3 %collective-permute-start.3 = (bf16[64,1024]{1,0:T(8,128)(2,1)S(1)}, bf16[64,1024]{1,0:T(8,128)(2,1)S(1)}, u32[]{:S(2)}, u32[]{:S(2)}) collective-permute-start(bf16[64,1024]{1,0:T(8,128)(2,1)S(1)} %get-tuple-element.41), channel_id=1, source_target_pairs={{0,16},{1,17},{2,18},{3,19},{4,20},{5,21},{6,22},{7,23},{8,24},{9,... | collective-permute-start | bytes 393224 | tf_op jit(solution)/shard_map/ppermute | solution.py:348
  11.0 8.5 %collective-permute-start.4 = (bf16[112,1024]{1,0:T(8,128)(2,1)S(1)}, bf16[112,1024]{1,0:T(8,128)(2,1)S(1)}, u32[]{:S(2)}, u32[]{:S(2)}) collective-permute-start(bf16[112,1024]{1,0:T(8,128)(2,1)S(1)} %get-tuple-element.42), channel_id=1, source_target_pairs={{0,1},{1,2},{2,3},{3,4},{4,5},{5,6},{6,7},{7,8},{8,9},{9,10},{10,1... | collective-permute-start | bytes 688136 | tf_op jit(solution)/shard_map/ppermute | solution.py:348
  13.6 0.7 copy-start
  26.4 9.4 %collective-permute-start.9 = (bf16[2,256,1024]{2,1,0:T(8,128)(2,1)S(1)}, bf16[2,256,1024]{2,1,0:T(8,128)(2,1)S(1)}, u32[]{:S(2)}, u32[]{:S(2)}) collective-permute-start(bf16[2,256,1024]{2,1,0:T(8,128)(2,1)S(1)} %get-tuple-element.56), channel_id=1, source_target_pairs={{0,16},{16,0},{1,17},{17,1},{2,18},{18,2},{3,19},{19,3},{4,20},{20... | collective-permute-start | bytes 3145736 | tf_op jit(solution)/shard_map/ppermute | solution.py:356
  35.4 3.0 %collective-permute-start.12 = (bf16[2,256,1024]{2,1,0:T(8,128)(2,1)S(1)}, bf16[2,256,1024]{2,1,0:T(8,128)(2,1)S(1)}, u32[]{:S(2)}, u32[]{:S(2)}) collective-permute-start(bf16[2,256,1024]{2,1,0:T(8,128)(2,1)S(1)} %get-tuple-element.63), channel_id=1, source_target_pairs={{0,16},{16,0},{1,17},{17,1},{2,18},{18,2},{3,19},{19,3},{4,20},{20... | collective-permute-start | bytes 3145736 | tf_op jit(solution)/shard_map/ppermute | solution.py:356
  36.5 13.1 %collective-permute-start.10 = (bf16[2,8,16,1024]{3,2,1,0:T(8,128)(2,1)S(1)}, bf16[2,8,16,1024]{3,2,1,0:T(8,128)(2,1)S(1)}, u32[]{:S(2)}, u32[]{:S(2)}) collective-permute-start(bf16[2,8,16,1024]{3,2,1,0:T(8,128)(2,1)S(1)} %get-tuple-element.58), channel_id=1, source_target_pairs={{0,1},{1,0},{2,3},{3,2},{4,5},{5,4},{6,7},{7,6},{8,9},{9,8},{10,11... | collective-permute-start | bytes 1572872 | tf_op jit(solution)/shard_map/ppermute | solution.py:348
  39.1 13.5 %collective-permute-start.13 = (bf16[2,8,16,1024]{3,2,1,0:T(8,128)(2,1)S(1)}, bf16[2,8,16,1024]{3,2,1,0:T(8,128)(2,1)S(1)}, u32[]{:S(2)}, u32[]{:S(2)}) collective-permute-start(bf16[2,8,16,1024]{3,2,1,0:T(8,128)(2,1)S(1)} %get-tuple-element.65), channel_id=1, source_target_pairs={{0,33},{1,32},{2,35},{3,34},{4,37},{5,36},{6,39},{7,38},{8,41},{9,... | collective-permute-start | bytes 1572872 | tf_op jit(solution)/shard_map/ppermute | solution.py:348
  50.2 6.8 %collective-permute-start.11 = (bf16[8,16,1024]{2,1,0:T(8,128)(2,1)S(1)}, bf16[8,16,1024]{2,1,0:T(8,128)(2,1)S(1)}, u32[]{:S(2)}, u32[]{:S(2)}) collective-permute-start(bf16[8,16,1024]{2,1,0:T(8,128)(2,1)S(1)} %get-tuple-element.61), channel_id=1, source_target_pairs={{0,33},{1,32},{2,35},{3,34},{4,37},{5,36},{6,39},{7,38},{8,41},{9,... | collective-permute-start | bytes 786440 | tf_op jit(solution)/shard_map/ppermute | solution.py:348
  53.3 6.9 %collective-permute-start.14 = (bf16[8,16,1024]{2,1,0:T(8,128)(2,1)S(1)}, bf16[8,16,1024]{2,1,0:T(8,128)(2,1)S(1)}, u32[]{:S(2)}, u32[]{:S(2)}) collective-permute-start(bf16[8,16,1024]{2,1,0:T(8,128)(2,1)S(1)} %get-tuple-element.67), channel_id=1, source_target_pairs={{0,1},{1,0},{2,3},{3,2},{4,5},{5,4},{6,7},{7,6},{8,9},{9,8},{10,11... | collective-permute-start | bytes 786440 | tf_op jit(solution)/shard_map/ppermute | solution.py:348
  61.1 21.9 %all-to-all-start = ((bf16[8,16,2048]{2,1,0:T(8,128)(2,1)}), bf16[8,16,2048]{2,1,0:T(8,128)(2,1)S(1)}, u32[]{:S(2)}, u32[]{:S(2)}) async-start(bf16[8,16,2048]{2,1,0:T(8,128)(2,1)} %join.1), calls=%async_computation | async-start | bytes 1048576 | tf_op jit(solution)/shard_map/all_to_all | solution.py:471
  67.4 26.9 %collective-permute-start.7 = (bf16[2,112,1024]{2,1,0:T(8,128)(2,1)}, bf16[2,112,1024]{2,1,0:T(8,128)(2,1)S(1)}, u32[]{:S(2)}, u32[]{:S(2)}) collective-permute-start(bf16[2,112,1024]{2,1,0:T(8,128)(2,1)} %get-tuple-element.51), channel_id=1, source_target_pairs={{0,15},{1,0},{2,1},{3,2},{4,3},{5,4},{6,5},{7,6},{8,7},{9,8},{10,9... | collective-permute-start | bytes 1376264 | tf_op jit(solution)/shard_map/ppermute | solution.py:348
  67.4 26.8 %collective-permute-start.6 = (bf16[2,64,1024]{2,1,0:T(8,128)(2,1)S(1)}, bf16[2,64,1024]{2,1,0:T(8,128)(2,1)S(1)}, u32[]{:S(2)}, u32[]{:S(2)}) collective-permute-start(bf16[2,64,1024]{2,1,0:T(8,128)(2,1)S(1)} %get-tuple-element.50), channel_id=1, source_target_pairs={{0,48},{1,49},{2,50},{3,51},{4,52},{5,53},{6,54},{7,55},{8,56},{9,... | collective-permute-start | bytes 786440 | tf_op jit(solution)/shard_map/ppermute | solution.py:348
  70.1 22.7 %collective-permute-start.8 = (bf16[2,16,1024]{2,1,0:T(8,128)(2,1)S(1)}, bf16[2,16,1024]{2,1,0:T(8,128)(2,1)S(1)}, u32[]{:S(2)}, u32[]{:S(2)}) collective-permute-start(bf16[2,16,1024]{2,1,0:T(8,128)(2,1)S(1)} %get-tuple-element.52), channel_id=1, source_target_pairs={{0,63},{1,48},{2,49},{3,50},{4,51},{5,52},{6,53},{7,54},{8,55},{9,... | collective-permute-start | bytes 196616 | tf_op jit(solution)/shard_map/ppermute | solution.py:348
  83.0 13.3 %collective-permute-start.17 = (bf16[16,2048]{1,0:T(8,128)(2,1)S(1)}, bf16[16,2048]{1,0:T(8,128)(2,1)S(1)}, u32[]{:S(2)}, u32[]{:S(2)}) collective-permute-start(bf16[16,2048]{1,0:T(8,128)(2,1)S(1)} %get-tuple-element.69), channel_id=1, source_target_pairs={{0,192},{64,128},{128,64},{192,0},{1,193},{65,129},{129,65},{193,1... | collective-permute-start | bytes 196616 | tf_op jit(solution)/shard_map/ppermute | solution.py:356
  85.8 10.5 %collective-permute-start.16 = (bf16[16,2048]{1,0:T(8,128)(2,1)S(1)}, bf16[16,2048]{1,0:T(8,128)(2,1)S(1)}, u32[]{:S(2)}, u32[]{:S(2)}) collective-permute-start(bf16[16,2048]{1,0:T(8,128)(2,1)S(1)} %get-tuple-element.69), channel_id=1, source_target_pairs={{0,128},{64,192},{128,0},{192,64},{1,129},{65,193},{129,1},{193,65... | collective-permute-start | bytes 196616 | tf_op jit(solution)/shard_map/ppermute | solution.py:356
  92.8 3.5 %collective-permute-start.15 = (bf16[16,2048]{1,0:T(8,128)(2,1)S(1)}, bf16[16,2048]{1,0:T(8,128)(2,1)S(1)}, u32[]{:S(2)}, u32[]{:S(2)}) collective-permute-start(bf16[16,2048]{1,0:T(8,128)(2,1)S(1)} %get-tuple-element.69), channel_id=1, source_target_pairs={{0,64},{64,0},{128,192},{192,128},{1,65},{65,1},{129,193},{193,129... | collective-permute-start | bytes 196616 | tf_op jit(solution)/shard_map/ppermute | solution.py:356

commit v4 on v3

--- a/solution.py
+++ b/solution.py
@@ -138,10 +138,11 @@
     code_t = column(upper, 16, lambda t: source_row(t) >> 1, lambda t: (t & 15) >> 1)
     copies[0].wait()
     copies[1].wait()
-    for block in range(BANDS):
-        here = slice(block * BAND, (block + 1) * BAND)
+    step = 256
+    for at in range(0, TOKENS, step):
+        here = slice(at, at + step)
         cb, ct = code_b[here], code_t[here]
-        lane = iota((BAND, 512), 1)
+        lane = iota((step, 512), 1)
         x = dot(hot(lane == cb), tables[0], 1, 0)
         x = jnp.where(cb == 512, mv[...].astype(F32).reshape(1, MODEL), x)
         x = (x + dot(hot(lane == ct), tables[1], 1, 0)).astype(BF16)
@@ -149,9 +150,7 @@
         centred, inverse = moments(x.astype(F32))
         normed[here] = (centred * inverse).astype(BF16)
     copies[2].wait()
-    for block in range(BANDS):
-        here = slice(block * BAND, (block + 1) * BAND)
-        proj[here] = dot(normed[here], weight[...], 1, 0).astype(BF16)
+    proj[...] = dot(normed[...], weight[...], 1, 0).astype(BF16)
 
 
 def merge(cot, grads, up, left, diag):
@@ -238,7 +237,7 @@
             out[half, :, 3 * CW :] = dot(cot[:, cut], att[...], 0, 0).astype(out.dtype)
 
 
-def finish_kernel(emb, cot, wq, ow, att0, att1, gp0, gp1, mid, up, left, diag, tick, weight, last, sems):
+def finish_kernel(emb, cot, wq, ow, att0, att1, gp0, gp1, mid, up, left, diag, tick, weight, last, big, sems):
     copies = [
         pltpu.make_async_copy(ow, last, sems.at[0]),
         pltpu.make_async_copy(wq, weight, sems.at[1]),
@@ -255,24 +254,27 @@
             at = block * BAND - 64
             mid[i, at : at + BAND] = values
 
-    for block in range(BANDS):
-        here = slice(block * BAND, (block + 1) * BAND)
-        att = jnp.concatenate([att0[here], att1[here]], axis=1)
-        put(0, block, (emb[here].astype(F32) + dot(att, last[...], 1, 1)).astype(BF16))
-    copies[1].wait()
-    for block in range(BANDS):
-        here = slice(block * BAND, (block + 1) * BAND)
-        g0, g1 = gp0[here], gp1[here]
-        parts = []
-        for i in range(3):
-            parts += [g0[:, i * CW : (i + 1) * CW], g1[:, i * CW : (i + 1) * CW]]
-        gst = dot(jnp.concatenate(parts, axis=1), weight[...], 1, 1)
-        centred, inverse = moments(emb[here].astype(F32))
+    def each(i, update):
+        for block in range(BANDS):
+            here = slice(block * BAND, (block + 1) * BAND)
+            put(i, block, update(here, emb[here].astype(F32), big[here]).astype(BF16))
+
+    def gradient(here, x, gst):
+        centred, inverse = moments(x)
         standard = centred * inverse
         m1 = jnp.mean(gst, axis=1, keepdims=True)
         m2 = jnp.mean(gst * standard, axis=1, keepdims=True)
-        values = cot[here].astype(F32) + inverse * (gst - m1 - standard * m2)
-        put(1, block, values.astype(BF16))
+        return cot[here].astype(F32) + inverse * (gst - m1 - standard * m2)
+
+    att = jnp.concatenate([att0[...], att1[...]], axis=1)
+    big[...] = dot(att, last[...], 1, 1)
+    each(0, lambda here, x, branch: x + branch)
+    copies[1].wait()
+    parts = []
+    for i in range(3):
+        parts += [g[:, i * CW : (i + 1) * CW] for g in (gp0, gp1)]
+    big[...] = dot(jnp.concatenate(parts, axis=1), weight[...], 1, 1)
+    each(1, gradient)
     pick, corner = late_cells(OWN, MSG, True), late_cells(64, 16, True)
     for i in range(2):
         left[i] = dot(pick, mid[i], 1, 0).astype(BF16)
@@ -280,7 +282,8 @@
     tick[...] = jnp.zeros(tick.shape, F32)
 
 
-def place_kernel(mid, up, left, diag, out, gin):
+def place_kernel(mid, up, left, diag, out, gin, tick):
+    tick[...] = jnp.zeros(tick.shape, F32)
     late = (iota((64, 1), 0) & 15) >= LATE
     corner = late_cells(64, 16, False)
     for i, ref in enumerate((out, gin)):
@@ -296,47 +299,53 @@
 Q = W // 4
 
 
+def lanes(i):
+    return pl.ds(pl.multiple_of(i * Q, Q), Q)
+
+
 def parity_core(place, a, b, keep, send):
     g = place[2] ^ place[3]
     for u in range(2):
         for out, v in ((keep, u ^ g), (send, u ^ g ^ 1)):
-            out[u] = (a[u, :, v] + b[u, :, v].astype(F32)).astype(out.dtype)
-
-
-def parity_pair(place, a, b, tick, keep, send):
-    for out, u in ((keep, place[2]), (send, place[2] ^ 1)):
-        out[...] = (a[u] + b[u].astype(F32)).astype(out.dtype)
+            cut = lanes(2 * u + v)
+            out[:, :, u * Q : (u + 1) * Q] = (a[:, :, cut] + b[:, :, cut].astype(F32)).astype(out.dtype)
 
 
 def high_core(place, a, b, keep, send):
     for out, u in ((keep, place[2]), (send, place[2] ^ 1)):
         for v in range(2):
-            out[v] = (a[u, :, v] + b[u, :, v].astype(F32)).astype(out.dtype)
-
-
-def high_pair(place, a, b, tick, keep, send):
-    for out, v in ((keep, place[3]), (send, place[3] ^ 1)):
-        out[...] = (a[v] + b[v].astype(F32)).astype(out.dtype)
-
-
-def join_kernel(a, b, c, d, out):
-    out[:, :, 0:W] = (a[...] + b[...].astype(F32)).astype(BF16)
-    out[:, :, W:] = (c[...] + d[...].astype(F32)).astype(BF16)
-
-
-def depth_kernel(ref, keep, send):
-    total = sum(ref[i].astype(F32) for i in range(8))
-    keep[...] = total
-    send[...] = total.astype(BF16)
-
-
-def level_kernel(factor, own, *refs):
-    qkv, outw = refs[3:]
-    total = (own[...] + sum(r[...].astype(F32) for r in refs[:3])) * factor
-    for c in range(CHUNKS):
-        for i in range(3):
-            qkv[:, i * HW + c * CW : i * HW + (c + 1) * CW] = total[:, c * W + i * Q : c * W + (i + 1) * Q]
-        outw[:, c * CW : (c + 1) * CW] = total[:, c * W + 3 * Q : (c + 1) * W]
+            cut = lanes(2 * u + v)
+            out[:, :, v * Q : (v + 1) * Q] = (a[:, :, cut] + b[:, :, cut].astype(F32)).astype(out.dtype)
+
+
+def pair(bit, place, a, b, tick, keep, send):
+    for out, u in ((keep, place[bit]), (send, place[bit] ^ 1)):
+        out[...] = (a[:, :, lanes(u)] + b[:, :, lanes(u)].astype(F32)).astype(out.dtype)
+
+
+def join_kernel(a, b, c, d, placed, out):
+    out[:, :, 0:Q] = (a[...] + b[...].astype(F32)).astype(BF16)
+    out[:, :, Q:] = (c[...] + d[...].astype(F32)).astype(BF16)
+
+
+def total_kernel(factor, ref, out):
+    out[...] = sum(ref[i].astype(F32) for i in range(32)) * factor
+
+
+def level_kernel(place, *refs):
+    qkv, outw = refs[4:]
+    for d in range(4):
+        who = (2 * place[2] + place[3]) ^ d
+        for c in range(CHUNKS):
+            cut = slice(c * Q, (c + 1) * Q)
+
+            @pl.when(who < 3)
+            def _():
+                qkv[:, pl.ds(pl.multiple_of(who * HW + c * CW, CW), CW)] = refs[d][:, cut]
+
+            @pl.when(who == 3)
+            def _():
+                outw[:, c * CW : (c + 1) * CW] = refs[d][:, cut]
 
 
 def permute(x, where):
@@ -356,11 +365,7 @@
     return lax.ppermute(x, axis, [(i, i ^ flip) for i in range(lax.axis_size(axis))])
 
 
-def swap_x(x, flip):
-    return permute(x, lambda la, lo: (la ^ (flip & 2), lo ^ (flip & 1)))
-
-
-def halve(kernel, shape, place, *terms):
+def halve(name, kernel, shape, place, *terms):
     size = math.prod(shape)
     return call(
         kernel,
@@ -370,24 +375,24 @@
         2 * size,
         16 * size,
         limit=16,
-        name=kernel.__name__,
-    )
-
-
-def sum_x(place, keep, send, tick, order):
-    fold = (2, 8, 2, 16, W)
-    core, pair = (parity_core, parity_pair) if order[0] == 1 else (high_core, high_pair)
+        name=name,
+    )
+
+
+def sum_y(place, keep, send, tick, order):
+    core, bit = (parity_core, 2) if order[0] == 1 else (high_core, 3)
     recv = swap(send, "core", 1)
-    keep, send = halve(core, (2, 8, 16, W), place, keep.reshape(fold), recv.reshape(fold))
-    keep, send = halve(pair, (8, 16, W), place, keep, swap_x(send, order[0]), tick)
-    return [keep, swap_x(send, order[1])]
+    keep, send = halve("sum_core", core, (2, 256, 2 * Q), place, keep, recv)
+    recv = swap(send, "batch", order[0])
+    keep, send = halve("sum_pair", functools.partial(pair, bit), (2, 256, Q), place, keep, recv, tick)
+    return [x.reshape(32, 16, Q) for x in (keep, swap(send, "batch", order[1]))]
 
 
 def shards(
     bottom_codes, mask_flags, top_codes, bottom_table, top_table, mask_vector, qkv_weight, out_weight, cotangent
 ):
-    core, xh, xl = lax.axis_index("core"), lax.axis_index("xh"), lax.axis_index("xl")
-    place = jnp.stack([2 * xh + core, core, xh, xl]).astype(jnp.int32)
+    core, y = lax.axis_index("core"), lax.axis_index("batch")
+    place = jnp.stack([2 * lax.axis_index("xh") + core, core, y >> 1, y & 1]).astype(jnp.int32)
     own = jnp.concatenate(
         [bottom_codes[0], mask_flags[0], jnp.pad(top_codes[0], ((0, 0), (0, 8)))], axis=0
     )
@@ -449,14 +454,19 @@
         2 * TOKENS * 1024 * 2048,
         10 * 2**20,
         name="finish",
-        scratch=[pltpu.VMEM((MODEL, 3 * HW), BF16), pltpu.VMEM((MODEL, HW), BF16), sems(2)],
-    )
-    summed = sum_x(place, keep0, send0, tick, (1, 3)) + sum_x(place, keep1, send1, tick, (3, 1))
+        scratch=[
+            pltpu.VMEM((MODEL, 3 * HW), BF16),
+            pltpu.VMEM((MODEL, HW), BF16),
+            pltpu.VMEM((TOKENS, MODEL), F32),
+            sems(2),
+        ],
+    )
+    summed = sum_y(place, keep0, send0, tick, (1, 3)) + sum_y(place, keep1, send1, tick, (3, 1))
     mid, up, left, diag = sent
     up, left, diag = shift(up, -1, 0), shift(left, 0, -1), shift(diag, -1, -1)
-    out, gin = call(
+    out, gin, placed = call(
         place_kernel,
-        [sds((TOKENS, MODEL))] * 2,
+        [sds((TOKENS, MODEL))] * 2 + [sds((8, 128), F32)],
         (mid, up, left, diag),
         [vmem()] * 4,
         2**28,
@@ -466,26 +476,26 @@
     )
     factor = 1.0 / math.sqrt(TOKENS * NB * NLAT * NLON)
     joined = call(
-        join_kernel, sds((8, 16, 2 * W)), summed, [vmem()] * 4, 2**19, 2**21, limit=16, name="join"
-    )
-    depth = lax.all_to_all(joined, "z", 0, 0, tiled=True)
-    keep, send = call(
-        depth_kernel,
-        [sds((16, 2 * W), F32), sds((16, 2 * W))],
-        (depth,),
+        join_kernel, sds((32, 16, 2 * Q)), (*summed, placed), [vmem()] * 5, 2**19, 2**21, limit=16, name="join"
+    )
+    spread = lax.all_to_all(joined, ("xh", "z", "xl"), 0, 0, tiled=True)
+    total = call(
+        functools.partial(total_kernel, factor),
+        sds((16, 2 * Q), F32),
+        (spread,),
         [vmem()],
         2**18,
         2**20,
         limit=16,
-        name="depth",
+        name="total",
     )
     g_qkv, g_out = call(
-        functools.partial(level_kernel, factor),
+        level_kernel,
         [sds((16, 3 * HW), F32), sds((16, HW), F32)],
-        (keep, *[swap(send, "batch", d) for d in (1, 2, 3)]),
-        [vmem()] * 4,
-        2**17,
-        2**19,
+        (place, total, *[swap(total, "batch", d) for d in (1, 2, 3)]),
+        [smem()] + [vmem()] * 4,
+        2**15,
+        2**18,
         limit=16,
         name="level",
     )

time: 97.3 us -> 101 us (1.038)
  the two profiles are of different devices: /device:TPU:3 before, /device:TPU:32 now
where the time goes in v4:
time: 101 us; the launch traced here: 99.4 us
  Pallas kernels  31.5 us (31%)
  starting transfers between devices  28.2 us (28%)
  blocking collectives  25.1 us (25%)
  waiting for transfers between devices  12.1 us (12%)
    pallas_call x13, Pallas kernels, call(): pl.pallas_call(kernel, out_shape=outs, in_specs=specs, out_specs=jax.tree...  31.5 us
    all_to_all x1, blocking collectives, shards(): spread = lax.all_to_all(joined, ('xh', 'z', 'xl'), 0, 0, tiled=True)  25.1 us
    ppermute x9, starting transfers between devices, permute(): return lax.ppermute(x, GRID, pairs)  14.7 us
    ppermute x9, starting transfers between devices, swap(): lax.ppermute(x, axis, [(i, i ^ flip) for i in range(lax.axis_size(axis))])  13.6 us
    ppermute x9, waiting for transfers between devices, permute(): return lax.ppermute(x, GRID, pairs)  8.09 us
    ppermute x9, waiting for transfers between devices, swap(): lax.ppermute(x, axis, [(i, i ^ flip) for i in range(lax.axis_size(axis))])  4.05 us
  transfers between devices with their start and end apart: 18, of which 6 were waited for; matrix products, arithmetic and copies ran while one was open for 0% of the time, Pallas kernels for 23%

profile of v4, /device:TPU:32, one launch (start us, length us, event | category | flops | bytes accessed | tf_op | source)
XLA Modules:
  0.0 99.4 jit_solution(7463760792257895288)
XLA Ops:
  0.6 0.8 pad_add_fusion
  1.5 1.0 %collective-permute-start.2 = (s32[80,16]{1,0:T(8,128)S(1)}, s32[80,16]{1,0:T(8,128)S(1)}, u32[]{:S(2)}, u32[]{:S(2)}) collective-permute-start(s32[80,16]{1,0:T(8,128)S(1)} %copy.19.own), channel_id=1, source_target_pairs={{0,17},{1,18},{2,19},{3,20},{4,21},{5,22},{6,23},{7,24},{8,25},{9,... | collective-permute-start | bytes 15368 | tf_op jit(solution)/shard_map/ppermute | solution.py:357
  2.5 1.9 %collective-permute-start.1 = (s32[80,16]{1,0:T(8,128)S(1)}, s32[80,16]{1,0:T(8,128)S(1)}, u32[]{:S(2)}, u32[]{:S(2)}) collective-permute-start(s32[80,16]{1,0:T(8,128)S(1)} %copy.19.own), channel_id=1, source_target_pairs={{0,1},{1,2},{2,3},{3,4},{4,5},{5,6},{6,7},{7,8},{8,9},{9,10},{10,1... | collective-permute-start | bytes 15368 | tf_op jit(solution)/shard_map/ppermute | solution.py:357
  4.4 1.4 %collective-permute-start = (s32[80,16]{1,0:T(8,128)S(1)}, s32[80,16]{1,0:T(8,128)S(1)}, u32[]{:S(2)}, u32[]{:S(2)}) collective-permute-start(s32[80,16]{1,0:T(8,128)S(1)} %copy.19.own), channel_id=1, source_target_pairs={{0,16},{1,17},{2,18},{3,19},{4,20},{5,21},{6,22},{7,23},{8,24},{9,... | collective-permute-start | bytes 15368 | tf_op jit(solution)/shard_map/ppermute | solution.py:357
  5.8 1.6 %slices.1 = (bf16[64,1024]{1,0:T(8,128)(2,1)S(1)}, bf16[112,1024]{1,0:T(8,128)(2,1)S(1)}, bf16[16,1024]{1,0:T(8,128)(2,1)S(1)}) custom-call(bf16[512,1024]{1,0:T(8,128)(2,1)} %bitcast.18), custom_call_target="tpu_custom_call" | custom-call | flops 268435456 | bytes 2097152 | tf_op jit(solution)/shard_map/slices/pallas_call | solution.py:43
  7.3 2.1 %collective-permute-start.5 = (bf16[16,1024]{1,0:T(8,128)(2,1)S(1)}, bf16[16,1024]{1,0:T(8,128)(2,1)S(1)}, u32[]{:S(2)}, u32[]{:S(2)}) collective-permute-start(bf16[16,1024]{1,0:T(8,128)(2,1)S(1)} %get-tuple-element.42), channel_id=1, source_target_pairs={{0,17},{1,18},{2,19},{3,20},{4,21},{5,22},{6,23},{7,24},{8,25},{9,... | collective-permute-start | bytes 98312 | tf_op jit(solution)/shard_map/ppermute | solution.py:357
  9.5 3.0 %collective-permute-start.4 = (bf16[112,1024]{1,0:T(8,128)(2,1)S(1)}, bf16[112,1024]{1,0:T(8,128)(2,1)S(1)}, u32[]{:S(2)}, u32[]{:S(2)}) collective-permute-start(bf16[112,1024]{1,0:T(8,128)(2,1)S(1)} %get-tuple-element.41), channel_id=1, source_target_pairs={{0,1},{1,2},{2,3},{3,4},{4,5},{5,6},{6,7},{7,8},{8,9},{9,10},{10,1... | collective-permute-start | bytes 688136 | tf_op jit(solution)/shard_map/ppermute | solution.py:357
  12.5 0.7 copy-done
  13.2 5.1 %embed.1 = (bf16[512,1024]{1,0:T(8,128)(2,1)S(1)}, bf16[512,1024]{1,0:T(8,128)(2,1)S(1)}, bf16[512,1536]{1,0:T(8,128)(2,1)S(1)}) custom-call(s32[80,16]{1,0:T(8,128)S(1)} %copy.19.own, s32[80,16]{1,0:T(8,128)S(1)} %collective-permute-done.up, s32[80,16]{1,0:T(8,128)S(1)} %collective-permute-done.1.left, s32[80,16]{1,0:T(8,128)S(1)} %collective-permute-done.2.diag, ...), custom_call_target="tpu_custom_call" | custom-call | flops 2684354560 | bytes 9437184 | tf_op jit(solution)/shard_map/embed/pallas_call | solution.py:43
  18.3 6.9 %attend.2 = (bf16[512,256]{1,0:T(8,128)(2,1)S(1)}, bf16[512,768]{1,0:T(8,128)(2,1)S(1)}, f32[2,256,1024]{2,1,0:T(8,128)S(1)}, bf16[2,256,1024]{2,1,0:T(8,128)(2,1)S(1)}, bf16[512,1024]{1,0:T(8,128)(2,1)S(1)}) custom-call(s32[4]{0:T(128)S(1)} %pad_add_fusion.1.place, bf16[512,1536]{1,0:T(8,128)(2,1)S(1)} %get-tuple-element.38.proj, ...), custom_call_target="tpu_custom_call" | custom-call | flops 3221225472 | bytes 8388608 | tf_op jit(solution)/shard_map/attend/pallas_call | solution.py:43
  25.2 0.6 collective-permute-start.9
  25.9 6.3 %attend.3 = (bf16[512,256]{1,0:T(8,128)(2,1)S(1)}, bf16[512,768]{1,0:T(8,128)(2,1)S(1)}, f32[2,256,1024]{2,1,0:T(8,128)S(1)}, bf16[2,256,1024]{2,1,0:T(8,128)(2,1)S(1)}) custom-call(s32[4]{0:T(128)S(1)} %pad_add_fusion.1.place, bf16[512,1536]{1,0:T(8,128)(2,1)S(1)} %get-tuple-element.38.proj, bf16[512,1024]{1,0:T(8,128)(2,1)S(1)} %get-tuple-element.39.normed, ...), custom_call_target="tpu_custom_call" | custom-call | flops 3221225472 | bytes 8388608 | tf_op jit(solution)/shard_map/attend/pallas_call | solution.py:43
  32.1 0.3 collective-permute-start.12
  32.4 0.8 sum_core.2
  33.3 1.6 %collective-permute-start.10 = (bf16[2,256,512]{2,1,0:T(8,128)(2,1)S(1)}, bf16[2,256,512]{2,1,0:T(8,128)(2,1)S(1)}, u32[]{:S(2)}, u32[]{:S(2)}) collective-permute-start(bf16[2,256,512]{2,1,0:T(8,128)(2,1)S(1)} %get-tuple-element.57), channel_id=1, source_target_pairs={{0,64},{64,0},{128,192},{192,128},{1,65},{65,1},{129,193},{193,129... | collective-permute-start | bytes 1572872 | tf_op jit(solution)/shard_map/ppermute | solution.py:365
  35.1 0.8 sum_core.3
  35.9 3.1 %collective-permute-start.13 = (bf16[2,256,512]{2,1,0:T(8,128)(2,1)S(1)}, bf16[2,256,512]{2,1,0:T(8,128)(2,1)S(1)}, u32[]{:S(2)}, u32[]{:S(2)}) collective-permute-start(bf16[2,256,512]{2,1,0:T(8,128)(2,1)S(1)} %get-tuple-element.64), channel_id=1, source_target_pairs={{0,192},{64,128},{128,64},{192,0},{1,193},{65,129},{129,65},{193,1... | collective-permute-start | bytes 1572872 | tf_op jit(solution)/shard_map/ppermute | solution.py:365
  39.0 5.2 %finish.1 = (bf16[2,448,1024]{2,1,0:T(8,128)(2,1)S(1)}, bf16[2,64,1024]{2,1,0:T(8,128)(2,1)S(1)}, bf16[2,112,1024]{2,1,0:T(8,128)(2,1)S(1)}, bf16[2,16,1024]{2,1,0:T(8,128)(2,1)S(1)}, f32[8,128]{1,0:T(8,128)S(1)}) custom-call(bf16[512,1024]{1,0:T(8,128)(2,1)S(1)} %get-tuple-element.37.emb, bf16[512,1024]{1,0:T(8,128)(2,1)S(1)} %get-tuple-element.43.cot, ...), custom_call_target="tpu_custom_call" | custom-call | flops 2147483648 | bytes 10485760 | tf_op jit(solution)/shard_map/finish/pallas_call | solution.py:43
  44.3 3.9 %collective-permute-start.7 = (bf16[2,112,1024]{2,1,0:T(8,128)(2,1)S(1)}, bf16[2,112,1024]{2,1,0:T(8,128)(2,1)S(1)}, u32[]{:S(2)}, u32[]{:S(2)}) collective-permute-start(bf16[2,112,1024]{2,1,0:T(8,128)(2,1)S(1)} %get-tuple-element.50), channel_id=1, source_target_pairs={{0,15},{1,0},{2,1},{3,2},{4,3},{5,4},{6,5},{7,6},{8,7},{9,8},{10,9... | collective-permute-start | bytes 1376264 | tf_op jit(solution)/shard_map/ppermute | solution.py:357
  48.2 0.7 sum_pair.2
  48.8 2.6 %collective-permute-start.11 = (bf16[2,256,256]{2,1,0:T(8,128)(2,1)S(1)}, bf16[2,256,256]{2,1,0:T(8,128)(2,1)S(1)}, u32[]{:S(2)}, u32[]{:S(2)}) collective-permute-start(bf16[2,256,256]{2,1,0:T(8,128)(2,1)S(1)} %get-tuple-element.60), channel_id=1, source_target_pairs={{0,192},{64,128},{128,64},{192,0},{1,193},{65,129},{129,65},{193,1... | collective-permute-start | bytes 786440 | tf_op jit(solution)/shard_map/ppermute | solution.py:365
  51.5 0.7 sum_pair.3
  52.4 1.5 %collective-permute-start.8 = (bf16[2,16,1024]{2,1,0:T(8,128)(2,1)S(1)}, bf16[2,16,1024]{2,1,0:T(8,128)(2,1)S(1)}, u32[]{:S(2)}, u32[]{:S(2)}) collective-permute-start(bf16[2,16,1024]{2,1,0:T(8,128)(2,1)S(1)} %get-tuple-element.51), channel_id=1, source_target_pairs={{0,63},{1,48},{2,49},{3,50},{4,51},{5,52},{6,53},{7,54},{8,55},{9,... | collective-permute-start | bytes 196616 | tf_op jit(solution)/shard_map/ppermute | solution.py:357
  53.8 5.8 %collective-permute-done.8.diag = bf16[2,16,1024]{2,1,0:T(8,128)(2,1)S(1)} collective-permute-done((bf16[2,16,1024]{2,1,0:T(8,128)(2,1)S(1)}, bf16[2,16,1024]{2,1,0:T(8,128)(2,1)S(1)}, u32[]{:S(2)}, u32[]{:S(2)}) %collective-permute-start.8) | collective-permute-done | bytes 65568 | tf_op jit(solution)/shard_map/ppermute | solution.py:357
  59.6 2.3 %collective-permute-done.6.up = bf16[2,64,1024]{2,1,0:T(8,128)(2,1)S(1)} collective-permute-done((bf16[2,64,1024]{2,1,0:T(8,128)(2,1)S(1)}, bf16[2,64,1024]{2,1,0:T(8,128)(2,1)S(1)}, u32[]{:S(2)}, u32[]{:S(2)}) %collective-permute-start.6) | collective-permute-done | bytes 262176 | tf_op jit(solution)/shard_map/ppermute | solution.py:357
  61.9 2.0 %place.1 = (bf16[512,1024]{1,0:T(8,128)(2,1)}, bf16[512,1024]{1,0:T(8,128)(2,1)}, f32[8,128]{1,0:T(8,128)S(1)}) custom-call(bf16[2,448,1024]{2,1,0:T(8,128)(2,1)S(1)} %get-tuple-element.48.mid, bf16[2,64,1024]{2,1,0:T(8,128)(2,1)S(1)} %collective-permute-done.6.up, bf16[2,112,1024]{2,1,0:T(8,128)(2,1)S(1)} %collective-permute-done.7.left, ...), custom_call_target="tpu_custom_call" | custom-call | flops 268435456 | bytes 5242880 | tf_op jit(solution)/shard_map/place/pallas_call | solution.py:43
  64.0 25.1 %all_to_all.5.ref = bf16[32,16,512]{2,1,0:T(8,128)(2,1)S(1)} all-to-all(bf16[32,16,512]{2,1,0:T(8,128)(2,1)S(1)} %join.1), channel_id=1, replica_groups=mesh['batch'=4,'xh'=2,'core'=2,'z'=8,'xl'=2] {'xh','z','xl'}, dimensions={0} | all-to-all | bytes 1048576 | tf_op jit(solution)/shard_map/all_to_all | solution.py:481
  89.2 2.9 %collective-permute-start.17 = (f32[16,512]{1,0:T(8,128)S(1)}, f32[16,512]{1,0:T(8,128)S(1)}, u32[]{:S(2)}, u32[]{:S(2)}) collective-permute-start(f32[16,512]{1,0:T(8,128)S(1)} %total.1.refs_0_), channel_id=1, source_target_pairs={{0,192},{64,128},{128,64},{192,0},{1,193},{65,129},{129,65},{193,1... | collective-permute-start | bytes 98312 | tf_op jit(solution)/shard_map/ppermute | solution.py:365
  92.1 2.1 %collective-permute-start.16 = (f32[16,512]{1,0:T(8,128)S(1)}, f32[16,512]{1,0:T(8,128)S(1)}, u32[]{:S(2)}, u32[]{:S(2)}) collective-permute-start(f32[16,512]{1,0:T(8,128)S(1)} %total.1.refs_0_), channel_id=1, source_target_pairs={{0,128},{64,192},{128,0},{192,64},{1,129},{65,193},{129,1},{193,65... | collective-permute-start | bytes 98312 | tf_op jit(solution)/shard_map/ppermute | solution.py:365
  94.4 3.4 %collective-permute-done.16.refs_2_ = f32[16,512]{1,0:T(8,128)S(1)} collective-permute-done((f32[16,512]{1,0:T(8,128)S(1)}, f32[16,512]{1,0:T(8,128)S(1)}, u32[]{:S(2)}, u32[]{:S(2)}) %collective-permute-start.16) | collective-permute-done | bytes 32800 | tf_op jit(solution)/shard_map/ppermute | solution.py:365
  97.8 0.4 collective-permute-done.15.refs_1_
  98.1 1.3 %level.1 = (f32[16,1536]{1,0:T(8,128)}, f32[16,512]{1,0:T(8,128)}) custom-call(s32[4]{0:T(128)S(1)} %pad_add_fusion.1.place, f32[16,512]{1,0:T(8,128)S(1)} %total.1.refs_0_, f32[16,512]{1,0:T(8,128)S(1)} %collective-permute-done.15.refs_1_, f32[16,512]{1,0:T(8,128)S(1)} %collective-permute-done.16.refs_2_, f32[16,512]{1,0:T(8,128)S(1)} %collective-permute-done.17.refs_3_), custom_call_target="tpu_custom_call" | custom-call | flops 32768 | bytes 262144 | tf_op jit(solution)/shard_map/level/pallas_call | solution.py:43
  (23 shorter events, 0.9 us)
Async XLA Ops:
  1.5 8.0 %collective-permute-start.2 = (s32[80,16]{1,0:T(8,128)S(1)}, s32[80,16]{1,0:T(8,128)S(1)}, u32[]{:S(2)}, u32[]{:S(2)}) collective-permute-start(s32[80,16]{1,0:T(8,128)S(1)} %copy.19.own), channel_id=1, source_target_pairs={{0,17},{1,18},{2,19},{3,20},{4,21},{5,22},{6,23},{7,24},{8,25},{9,... | collective-permute-start | bytes 15368 | tf_op jit(solution)/shard_map/ppermute | solution.py:357
  2.5 9.9 %collective-permute-start.1 = (s32[80,16]{1,0:T(8,128)S(1)}, s32[80,16]{1,0:T(8,128)S(1)}, u32[]{:S(2)}, u32[]{:S(2)}) collective-permute-start(s32[80,16]{1,0:T(8,128)S(1)} %copy.19.own), channel_id=1, source_target_pairs={{0,1},{1,2},{2,3},{3,4},{4,5},{5,6},{6,7},{7,8},{8,9},{9,10},{10,1... | collective-permute-start | bytes 15368 | tf_op jit(solution)/shard_map/ppermute | solution.py:357
  4.4 8.1 %collective-permute-start = (s32[80,16]{1,0:T(8,128)S(1)}, s32[80,16]{1,0:T(8,128)S(1)}, u32[]{:S(2)}, u32[]{:S(2)}) collective-permute-start(s32[80,16]{1,0:T(8,128)S(1)} %copy.19.own), channel_id=1, source_target_pairs={{0,16},{1,17},{2,18},{3,19},{4,20},{5,21},{6,22},{7,23},{8,24},{9,... | collective-permute-start | bytes 15368 | tf_op jit(solution)/shard_map/ppermute | solution.py:357
  7.3 11.0 %collective-permute-start.5 = (bf16[16,1024]{1,0:T(8,128)(2,1)S(1)}, bf16[16,1024]{1,0:T(8,128)(2,1)S(1)}, u32[]{:S(2)}, u32[]{:S(2)}) collective-permute-start(bf16[16,1024]{1,0:T(8,128)(2,1)S(1)} %get-tuple-element.42), channel_id=1, source_target_pairs={{0,17},{1,18},{2,19},{3,20},{4,21},{5,22},{6,23},{7,24},{8,25},{9,... | collective-permute-start | bytes 98312 | tf_op jit(solution)/shard_map/ppermute | solution.py:357
  9.4 8.9 %collective-permute-start.3 = (bf16[64,1024]{1,0:T(8,128)(2,1)S(1)}, bf16[64,1024]{1,0:T(8,128)(2,1)S(1)}, u32[]{:S(2)}, u32[]{:S(2)}) collective-permute-start(bf16[64,1024]{1,0:T(8,128)(2,1)S(1)} %get-tuple-element.40), channel_id=1, source_target_pairs={{0,16},{1,17},{2,18},{3,19},{4,20},{5,21},{6,22},{7,23},{8,24},{9,... | collective-permute-start | bytes 393224 | tf_op jit(solution)/shard_map/ppermute | solution.py:357
  9.5 8.8 %collective-permute-start.4 = (bf16[112,1024]{1,0:T(8,128)(2,1)S(1)}, bf16[112,1024]{1,0:T(8,128)(2,1)S(1)}, u32[]{:S(2)}, u32[]{:S(2)}) collective-permute-start(bf16[112,1024]{1,0:T(8,128)(2,1)S(1)} %get-tuple-element.41), channel_id=1, source_target_pairs={{0,1},{1,2},{2,3},{3,4},{4,5},{5,6},{6,7},{7,8},{8,9},{9,10},{10,1... | collective-permute-start | bytes 688136 | tf_op jit(solution)/shard_map/ppermute | solution.py:357
  12.5 0.7 copy-start
  25.2 7.2 %collective-permute-start.9 = (bf16[2,256,1024]{2,1,0:T(8,128)(2,1)S(1)}, bf16[2,256,1024]{2,1,0:T(8,128)(2,1)S(1)}, u32[]{:S(2)}, u32[]{:S(2)}) collective-permute-start(bf16[2,256,1024]{2,1,0:T(8,128)(2,1)S(1)} %get-tuple-element.55), channel_id=1, source_target_pairs={{0,16},{16,0},{1,17},{17,1},{2,18},{18,2},{3,19},{19,3},{4,20},{20... | collective-permute-start | bytes 3145736 | tf_op jit(solution)/shard_map/ppermute | solution.py:365
  32.1 3.0 %collective-permute-start.12 = (bf16[2,256,1024]{2,1,0:T(8,128)(2,1)S(1)}, bf16[2,256,1024]{2,1,0:T(8,128)(2,1)S(1)}, u32[]{:S(2)}, u32[]{:S(2)}) collective-permute-start(bf16[2,256,1024]{2,1,0:T(8,128)(2,1)S(1)} %get-tuple-element.62), channel_id=1, source_target_pairs={{0,16},{16,0},{1,17},{17,1},{2,18},{18,2},{3,19},{19,3},{4,20},{20... | collective-permute-start | bytes 3145736 | tf_op jit(solution)/shard_map/ppermute | solution.py:365
  33.3 14.9 %collective-permute-start.10 = (bf16[2,256,512]{2,1,0:T(8,128)(2,1)S(1)}, bf16[2,256,512]{2,1,0:T(8,128)(2,1)S(1)}, u32[]{:S(2)}, u32[]{:S(2)}) collective-permute-start(bf16[2,256,512]{2,1,0:T(8,128)(2,1)S(1)} %get-tuple-element.57), channel_id=1, source_target_pairs={{0,64},{64,0},{128,192},{192,128},{1,65},{65,1},{129,193},{193,129... | collective-permute-start | bytes 1572872 | tf_op jit(solution)/shard_map/ppermute | solution.py:365
  35.9 15.6 %collective-permute-start.13 = (bf16[2,256,512]{2,1,0:T(8,128)(2,1)S(1)}, bf16[2,256,512]{2,1,0:T(8,128)(2,1)S(1)}, u32[]{:S(2)}, u32[]{:S(2)}) collective-permute-start(bf16[2,256,512]{2,1,0:T(8,128)(2,1)S(1)} %get-tuple-element.64), channel_id=1, source_target_pairs={{0,192},{64,128},{128,64},{192,0},{1,193},{65,129},{129,65},{193,1... | collective-permute-start | bytes 1572872 | tf_op jit(solution)/shard_map/ppermute | solution.py:365
  44.3 17.6 %collective-permute-start.7 = (bf16[2,112,1024]{2,1,0:T(8,128)(2,1)S(1)}, bf16[2,112,1024]{2,1,0:T(8,128)(2,1)S(1)}, u32[]{:S(2)}, u32[]{:S(2)}) collective-permute-start(bf16[2,112,1024]{2,1,0:T(8,128)(2,1)S(1)} %get-tuple-element.50), channel_id=1, source_target_pairs={{0,15},{1,0},{2,1},{3,2},{4,3},{5,4},{6,5},{7,6},{8,7},{9,8},{10,9... | collective-permute-start | bytes 1376264 | tf_op jit(solution)/shard_map/ppermute | solution.py:357
  48.2 13.7 %collective-permute-start.6 = (bf16[2,64,1024]{2,1,0:T(8,128)(2,1)S(1)}, bf16[2,64,1024]{2,1,0:T(8,128)(2,1)S(1)}, u32[]{:S(2)}, u32[]{:S(2)}) collective-permute-start(bf16[2,64,1024]{2,1,0:T(8,128)(2,1)S(1)} %get-tuple-element.49), channel_id=1, source_target_pairs={{0,48},{1,49},{2,50},{3,51},{4,52},{5,53},{6,54},{7,55},{8,56},{9,... | collective-permute-start | bytes 786440 | tf_op jit(solution)/shard_map/ppermute | solution.py:357
  48.8 15.0 %collective-permute-start.11 = (bf16[2,256,256]{2,1,0:T(8,128)(2,1)S(1)}, bf16[2,256,256]{2,1,0:T(8,128)(2,1)S(1)}, u32[]{:S(2)}, u32[]{:S(2)}) collective-permute-start(bf16[2,256,256]{2,1,0:T(8,128)(2,1)S(1)} %get-tuple-element.60), channel_id=1, source_target_pairs={{0,192},{64,128},{128,64},{192,0},{1,193},{65,129},{129,65},{193,1... | collective-permute-start | bytes 786440 | tf_op jit(solution)/shard_map/ppermute | solution.py:365
  52.2 11.7 %collective-permute-start.14 = (bf16[2,256,256]{2,1,0:T(8,128)(2,1)S(1)}, bf16[2,256,256]{2,1,0:T(8,128)(2,1)S(1)}, u32[]{:S(2)}, u32[]{:S(2)}) collective-permute-start(bf16[2,256,256]{2,1,0:T(8,128)(2,1)S(1)} %get-tuple-element.66), channel_id=1, source_target_pairs={{0,64},{64,0},{128,192},{192,128},{1,65},{65,1},{129,193},{193,129... | collective-permute-start | bytes 786440 | tf_op jit(solution)/shard_map/ppermute | solution.py:365
  52.4 7.3 %collective-permute-start.8 = (bf16[2,16,1024]{2,1,0:T(8,128)(2,1)S(1)}, bf16[2,16,1024]{2,1,0:T(8,128)(2,1)S(1)}, u32[]{:S(2)}, u32[]{:S(2)}) collective-permute-start(bf16[2,16,1024]{2,1,0:T(8,128)(2,1)S(1)} %get-tuple-element.51), channel_id=1, source_target_pairs={{0,63},{1,48},{2,49},{3,50},{4,51},{5,52},{6,53},{7,54},{8,55},{9,... | collective-permute-start | bytes 196616 | tf_op jit(solution)/shard_map/ppermute | solution.py:357
  89.2 5.2 %collective-permute-start.17 = (f32[16,512]{1,0:T(8,128)S(1)}, f32[16,512]{1,0:T(8,128)S(1)}, u32[]{:S(2)}, u32[]{:S(2)}) collective-permute-start(f32[16,512]{1,0:T(8,128)S(1)} %total.1.refs_0_), channel_id=1, source_target_pairs={{0,192},{64,128},{128,64},{192,0},{1,193},{65,129},{129,65},{193,1... | collective-permute-start | bytes 98312 | tf_op jit(solution)/shard_map/ppermute | solution.py:365
  92.1 5.7 %collective-permute-start.16 = (f32[16,512]{1,0:T(8,128)S(1)}, f32[16,512]{1,0:T(8,128)S(1)}, u32[]{:S(2)}, u32[]{:S(2)}) collective-permute-start(f32[16,512]{1,0:T(8,128)S(1)} %total.1.refs_0_), channel_id=1, source_target_pairs={{0,128},{64,192},{128,0},{192,64},{1,129},{65,193},{129,1},{193,65... | collective-permute-start | bytes 98312 | tf_op jit(solution)/shard_map/ppermute | solution.py:365
  94.2 3.9 %collective-permute-start.15 = (f32[16,512]{1,0:T(8,128)S(1)}, f32[16,512]{1,0:T(8,128)S(1)}, u32[]{:S(2)}, u32[]{:S(2)}) collective-permute-start(f32[16,512]{1,0:T(8,128)S(1)} %total.1.refs_0_), channel_id=1, source_target_pairs={{0,64},{64,0},{128,192},{192,128},{1,65},{65,1},{129,193},{193,129... | collective-permute-start | bytes 98312 | tf_op jit(solution)/shard_map/ppermute | solution.py:365

commit v5 on v3

--- a/solution.py
+++ b/solution.py
@@ -107,8 +107,8 @@
         pltpu.make_async_copy(tt, tables.at[1], sems.at[1]),
         pltpu.make_async_copy(wq, weight, sems.at[2]),
     ]
-    for copy in copies:
-        copy.start()
+    copies[0].start()
+    copies[1].start()
     r, j = iota((80, 16), 0), iota((80, 16), 1)
     low = jnp.where(r >= 64, r - 50, r & 31) >= 28
     late = jnp.where(r >= 64, 2 * j, j) >= LATE
@@ -138,10 +138,12 @@
     code_t = column(upper, 16, lambda t: source_row(t) >> 1, lambda t: (t & 15) >> 1)
     copies[0].wait()
     copies[1].wait()
-    for block in range(BANDS):
-        here = slice(block * BAND, (block + 1) * BAND)
+    copies[2].start()
+    step = 256
+    for at in range(0, TOKENS, step):
+        here = slice(at, at + step)
         cb, ct = code_b[here], code_t[here]
-        lane = iota((BAND, 512), 1)
+        lane = iota((step, 512), 1)
         x = dot(hot(lane == cb), tables[0], 1, 0)
         x = jnp.where(cb == 512, mv[...].astype(F32).reshape(1, MODEL), x)
         x = (x + dot(hot(lane == ct), tables[1], 1, 0)).astype(BF16)
@@ -149,9 +151,7 @@
         centred, inverse = moments(x.astype(F32))
         normed[here] = (centred * inverse).astype(BF16)
     copies[2].wait()
-    for block in range(BANDS):
-        here = slice(block * BAND, (block + 1) * BAND)
-        proj[here] = dot(normed[here], weight[...], 1, 0).astype(BF16)
+    proj[...] = dot(normed[...], weight[...], 1, 0).astype(BF16)
 
 
 def merge(cot, grads, up, left, diag):
@@ -166,29 +166,39 @@
         cot[64 + at : 128 + at] = values.astype(BF16)
 
 
-def attend_first(place, proj, normed, grads, up, left, diag, ow, att, gp, keep, send, cot, own, weight, sems):
+def attend_first(place, proj, normed, grads, up, left, diag, ow, att, gp, keep, send, cot, own, weight, sems, *held):
     copies = [
         pltpu.make_async_copy(grads, own, sems.at[0]),
         pltpu.make_async_copy(ow.at[:, 0:CW], weight, sems.at[1]),
     ]
     for copy in copies:
         copy.start()
+    units = forward(0, place, proj, att, *held)
     copies[0].wait()
     merge(cot, own, up, left, diag)
     copies[1].wait()
-    attend(0, place, proj, normed, cot, weight, att, gp, keep, send)
-
-
-def attend_next(place, proj, normed, cot, ow, att, gp, keep, send, weight, sem):
+    backward(units, place, normed, cot, weight, att, gp, keep, send, *held)
+
+
+def attend_next(place, proj, normed, cot, ow, att, gp, keep, send, weight, sem, *held):
     copy = pltpu.make_async_copy(ow.at[:, CW:], weight, sem)
     copy.start()
+    units = forward(1, place, proj, att, *held)
     copy.wait()
-    attend(1, place, proj, normed, cot, weight, att, gp, keep, send)
-
-
-def attend(chunk, place, proj, normed, cot, ow, att, gp, keep, send):
-    grad = dot(cot[...], ow[...], 1, 0).astype(BF16)
-    lane = iota((BAND, 128), 1) < 64
+    backward(units, place, normed, cot, weight, att, gp, keep, send, *held)
+
+
+def first_lanes():
+    return iota((BAND, 128), 1) < 64
+
+
+def split(x):
+    none = jnp.zeros_like(x)
+    first = first_lanes()
+    return jnp.concatenate([jnp.where(first, x, none), jnp.where(first, none, x)], axis=0)
+
+
+def forward(chunk, place, proj, att, share, share_bf, ds):
     tk, tq = iota((BAND, BAND), 0), iota((BAND, BAND), 1)
 
     def side(t):
@@ -200,36 +210,44 @@
     zero = jnp.zeros((BAND, BAND), F32)
     plain = jnp.where(same, zero, -1e30)
     first = jnp.where(whole | (place[0] != 0), plain, -1e30)
-
-    def split(x):
-        none = jnp.zeros_like(x)
-        return jnp.concatenate([jnp.where(lane, x, none), jnp.where(lane, none, x)], axis=0)
+    units = []
+    for p in range(CW // 128):
+        for b in range(BANDS):
+            here, at = slice(b * BAND, (b + 1) * BAND), chunk * CW + p * 128
+            loads = [functools.partial(lambda c, h: proj[h, c : c + 128], i * HW + at, here) for i in range(3)]
+            units.append((b, here, p * 128, *loads))
+    for u, (b, here, at, q, k, v) in enumerate(units):
+        share[u] = dot(split(k()), q(), 1, 1).reshape(2, BAND, BAND) * 0.125 + (first if b == 0 else plain)
+    for u in range(len(units)):
+        s = share[u]
+        e = jnp.exp(s - jnp.max(s, axis=1, keepdims=True))
+        e = e * (1.0 / jnp.sum(e, axis=1, keepdims=True))
+        share[u] = e
+        share_bf[u] = e.astype(BF16).reshape(2 * BAND, BAND)
+    for u, (b, here, at, q, k, v) in enumerate(units):
+        att[here, at : at + 128] = dot(share_bf[u], split(v()), 0, 0).astype(BF16)
+    return units
+
+
+def backward(units, place, normed, cot, ow, att, gp, keep, send, share, share_bf, ds):
+    grad = dot(cot[...], ow[...], 1, 0).astype(BF16)
+    lane = first_lanes()
 
     def pick(x):
         return jnp.where(lane, x[:BAND], x[BAND:])
 
-    for b in range(BANDS):
-        bias = first if b == 0 else plain
-        here = slice(b * BAND, (b + 1) * BAND)
-        for p in range(CW // 128):
-            cols = slice(p * 128, (p + 1) * 128)
-            first_col = chunk * CW + p * 128
-            qq, kk, vv = (proj[here, i * HW + first_col : i * HW + first_col + 128] for i in range(3))
-            kk, vv = split(kk), split(vv)
-            da = grad[here, cols]
-            s = dot(kk, qq, 1, 1).reshape(2, BAND, BAND) * 0.125 + bias
-            e = jnp.exp(s - jnp.max(s, axis=1, keepdims=True))
-            share = e * (1.0 / jnp.sum(e, axis=1, keepdims=True))
-            sb = share.astype(BF16).reshape(2 * BAND, BAND)
-            att[here, cols] = dot(sb, vv, 0, 0).astype(BF16)
-            gs = dot(vv, da, 1, 1).reshape(2, BAND, BAND)
-            delta = jnp.sum(share * gs, axis=1, keepdims=True)
-            ds = (share * (gs - delta) * 0.125).astype(BF16).reshape(2 * BAND, BAND)
-            at = p * 128
-            gp[here, at : at + 128] = dot(ds, kk, 0, 0).astype(BF16)
-            gp[here, CW + at : CW + at + 128] = pick(dot(ds, qq, 1, 0)).astype(BF16)
-            gp[here, 2 * CW + at : 2 * CW + at + 128] = pick(dot(sb, da, 1, 0)).astype(BF16)
-
+    for u, (b, here, at, q, k, v) in enumerate(units):
+        gs = dot(split(v()), grad[here, at : at + 128], 1, 1).reshape(2, BAND, BAND)
+        e = share[u]
+        delta = jnp.sum(e * gs, axis=1, keepdims=True)
+        ds[u] = (e * (gs - delta) * 0.125).astype(BF16).reshape(2 * BAND, BAND)
+    for u, (b, here, at, q, k, v) in enumerate(units):
+        d = ds[u]
+        gp[here, at : at + 128] = dot(d, split(k()), 0, 0).astype(BF16)
+        gp[here, CW + at : CW + at + 128] = pick(dot(d, q(), 1, 0)).astype(BF16)
+        gp[here, 2 * CW + at : 2 * CW + at + 128] = pick(
+            dot(share_bf[u], grad[here, at : at + 128], 1, 0)
+        ).astype(BF16)
     core = place[1]
     for half in range(2):
         for out, flip in ((send, 1), (keep, 0)):
@@ -238,7 +256,7 @@
             out[half, :, 3 * CW :] = dot(cot[:, cut], att[...], 0, 0).astype(out.dtype)
 
 
-def finish_kernel(emb, cot, wq, ow, att0, att1, gp0, gp1, mid, up, left, diag, tick, weight, last, sems):
+def finish_kernel(emb, cot, wq, ow, att0, att1, gp0, gp1, mid, up, left, diag, tick, weight, last, big, sems):
     copies = [
         pltpu.make_async_copy(ow, last, sems.at[0]),
         pltpu.make_async_copy(wq, weight, sems.at[1]),
@@ -255,24 +273,27 @@
             at = block * BAND - 64
             mid[i, at : at + BAND] = values
 
-    for block in range(BANDS):
-        here = slice(block * BAND, (block + 1) * BAND)
-        att = jnp.concatenate([att0[here], att1[here]], axis=1)
-        put(0, block, (emb[here].astype(F32) + dot(att, last[...], 1, 1)).astype(BF16))
-    copies[1].wait()
-    for block in range(BANDS):
-        here = slice(block * BAND, (block + 1) * BAND)
-        g0, g1 = gp0[here], gp1[here]
-        parts = []
-        for i in range(3):
-            parts += [g0[:, i * CW : (i + 1) * CW], g1[:, i * CW : (i + 1) * CW]]
-        gst = dot(jnp.concatenate(parts, axis=1), weight[...], 1, 1)
-        centred, inverse = moments(emb[here].astype(F32))
+    def each(i, update):
+        for block in range(BANDS):
+            here = slice(block * BAND, (block + 1) * BAND)
+            put(i, block, update(here, emb[here].astype(F32), big[here]).astype(BF16))
+
+    def gradient(here, x, gst):
+        centred, inverse = moments(x)
         standard = centred * inverse
         m1 = jnp.mean(gst, axis=1, keepdims=True)
         m2 = jnp.mean(gst * standard, axis=1, keepdims=True)
-        values = cot[here].astype(F32) + inverse * (gst - m1 - standard * m2)
-        put(1, block, values.astype(BF16))
+        return cot[here].astype(F32) + inverse * (gst - m1 - standard * m2)
+
+    att = jnp.concatenate([att0[...], att1[...]], axis=1)
+    big[...] = dot(att, last[...], 1, 1)
+    each(0, lambda here, x, branch: x + branch)
+    copies[1].wait()
+    parts = []
+    for i in range(3):
+        parts += [g[:, i * CW : (i + 1) * CW] for g in (gp0, gp1)]
+    big[...] = dot(jnp.concatenate(parts, axis=1), weight[...], 1, 1)
+    each(1, gradient)
     pick, corner = late_cells(OWN, MSG, True), late_cells(64, 16, True)
     for i in range(2):
         left[i] = dot(pick, mid[i], 1, 0).astype(BF16)
@@ -319,7 +340,7 @@
         out[...] = (a[v] + b[v].astype(F32)).astype(out.dtype)
 
 
-def join_kernel(a, b, c, d, out):
+def join_kernel(a, b, c, d, arrived, out):
     out[:, :, 0:W] = (a[...] + b[...].astype(F32)).astype(BF16)
     out[:, :, W:] = (c[...] + d[...].astype(F32)).astype(BF16)
 
@@ -360,7 +381,7 @@
     return permute(x, lambda la, lo: (la ^ (flip & 2), lo ^ (flip & 1)))
 
 
-def halve(kernel, shape, place, *terms):
+def halve(name, kernel, shape, place, *terms):
     size = math.prod(shape)
     return call(
         kernel,
@@ -370,7 +391,7 @@
         2 * size,
         16 * size,
         limit=16,
-        name=kernel.__name__,
+        name=name,
     )
 
 
@@ -378,8 +399,8 @@
     fold = (2, 8, 2, 16, W)
     core, pair = (parity_core, parity_pair) if order[0] == 1 else (high_core, high_pair)
     recv = swap(send, "core", 1)
-    keep, send = halve(core, (2, 8, 16, W), place, keep.reshape(fold), recv.reshape(fold))
-    keep, send = halve(pair, (8, 16, W), place, keep, swap_x(send, order[0]), tick)
+    keep, send = halve("sum_core", core, (2, 8, 16, W), place, keep.reshape(fold), recv.reshape(fold))
+    keep, send = halve("sum_pair", pair, (8, 16, W), place, keep, swap_x(send, order[0]), tick)
     return [keep, swap_x(send, order[1])]
 
 
@@ -419,6 +440,8 @@
     )
     outs = [sds((TOKENS, CW)), sds((TOKENS, 3 * CW)), sds((2, 256, W), F32), sds((2, 256, W))]
     column = pltpu.VMEM((MODEL, CW), BF16)
+    units = BANDS * CW // 128
+    held = [pltpu.VMEM((units, 2, BAND, BAND), F32)] + [pltpu.VMEM((units, 2 * BAND, BAND), BF16)] * 2
     att0, gp0, keep0, send0, cot = call(
         attend_first,
         outs + [sds((TOKENS, MODEL))],
@@ -428,7 +451,7 @@
         8 * 2**20,
         2**19,
         name="attend",
-        scratch=[pltpu.VMEM((TOKENS, MODEL), BF16), column, sems(2)],
+        scratch=[pltpu.VMEM((TOKENS, MODEL), BF16), column, sems(2), *held],
     )
     att1, gp1, keep1, send1 = call(
         attend_next,
@@ -439,7 +462,7 @@
         8 * 2**20,
         2**19,
         name="attend",
-        scratch=[column, pltpu.SemaphoreType.DMA],
+        scratch=[column, pltpu.SemaphoreType.DMA, *held],
     )
     *sent, tick = call(
         finish_kernel,
@@ -449,7 +472,12 @@
         2 * TOKENS * 1024 * 2048,
         10 * 2**20,
         name="finish",
-        scratch=[pltpu.VMEM((MODEL, 3 * HW), BF16), pltpu.VMEM((MODEL, HW), BF16), sems(2)],
+        scratch=[
+            pltpu.VMEM((MODEL, 3 * HW), BF16),
+            pltpu.VMEM((MODEL, HW), BF16),
+            pltpu.VMEM((TOKENS, MODEL), F32),
+            sems(2),
+        ],
     )
     summed = sum_x(place, keep0, send0, tick, (1, 3)) + sum_x(place, keep1, send1, tick, (3, 1))
     mid, up, left, diag = sent
@@ -466,7 +494,14 @@
     )
     factor = 1.0 / math.sqrt(TOKENS * NB * NLAT * NLON)
     joined = call(
-        join_kernel, sds((8, 16, 2 * W)), summed, [vmem()] * 4, 2**19, 2**21, limit=16, name="join"
+        join_kernel,
+        sds((8, 16, 2 * W)),
+        (*summed, left),
+        [vmem()] * 4 + [hbm()],
+        2**19,
+        2**21,
+        limit=16,
+        name="join",
     )
     depth = lax.all_to_all(joined, "z", 0, 0, tiled=True)
     keep, send = call(

time: 97.3 us -> 98.7 us (1.014)
  the two profiles are of different devices: /device:TPU:3 before, /device:TPU:32 now
where the time goes in v5:
time: 98.7 us; the launch traced here: 97.2 us
  waiting for transfers between devices  35.6 us (36%)
  starting transfers between devices  31.4 us (32%)
  Pallas kernels  27.8 us (28%)
    pallas_call x13, Pallas kernels, call(): pl.pallas_call(kernel, out_shape=outs, in_specs=specs, out_specs=jax.tree...  27.8 us
    ppermute x13, starting transfers between devices, permute(): return lax.ppermute(x, GRID, pairs)  20.3 us
    ppermute x13, waiting for transfers between devices, permute(): return lax.ppermute(x, GRID, pairs)  19.9 us
    all_to_all x1, waiting for transfers between devices, shards(): depth = lax.all_to_all(joined, 'z', 0, 0, tiled=True)  13.1 us
    all_to_all x1, starting transfers between devices, shards(): depth = lax.all_to_all(joined, 'z', 0, 0, tiled=True)  5.95 us
    ppermute x5, starting transfers between devices, swap(): lax.ppermute(x, axis, [(i, i ^ flip) for i in range(lax.axis_size(axis))])  5.06 us
    ppermute x5, waiting for transfers between devices, swap(): lax.ppermute(x, axis, [(i, i ^ flip) for i in range(lax.axis_size(axis))])  2.73 us
  transfers between devices with their start and end apart: 19, of which 5 were waited for; matrix products, arithmetic and copies ran while one was open for 0% of the time, Pallas kernels for 22%

profile of v5, /device:TPU:32, one launch (start us, length us, event | category | flops | bytes accessed | tf_op | source)
XLA Modules:
  0.0 97.2 jit_solution(3017952545106861129)
XLA Ops:
  0.6 0.8 pad_add_fusion
  1.5 1.0 %collective-permute-start.2 = (s32[80,16]{1,0:T(8,128)S(1)}, s32[80,16]{1,0:T(8,128)S(1)}, u32[]{:S(2)}, u32[]{:S(2)}) collective-permute-start(s32[80,16]{1,0:T(8,128)S(1)} %copy.19.own), channel_id=1, source_target_pairs={{0,17},{1,18},{2,19},{3,20},{4,21},{5,22},{6,23},{7,24},{8,25},{9,... | collective-permute-start | bytes 15368 | tf_op jit(solution)/shard_map/ppermute | solution.py:369
  2.5 1.9 %collective-permute-start.1 = (s32[80,16]{1,0:T(8,128)S(1)}, s32[80,16]{1,0:T(8,128)S(1)}, u32[]{:S(2)}, u32[]{:S(2)}) collective-permute-start(s32[80,16]{1,0:T(8,128)S(1)} %copy.19.own), channel_id=1, source_target_pairs={{0,1},{1,2},{2,3},{3,4},{4,5},{5,6},{6,7},{7,8},{8,9},{9,10},{10,1... | collective-permute-start | bytes 15368 | tf_op jit(solution)/shard_map/ppermute | solution.py:369
  4.4 1.4 %collective-permute-start = (s32[80,16]{1,0:T(8,128)S(1)}, s32[80,16]{1,0:T(8,128)S(1)}, u32[]{:S(2)}, u32[]{:S(2)}) collective-permute-start(s32[80,16]{1,0:T(8,128)S(1)} %copy.19.own), channel_id=1, source_target_pairs={{0,16},{1,17},{2,18},{3,19},{4,20},{5,21},{6,22},{7,23},{8,24},{9,... | collective-permute-start | bytes 15368 | tf_op jit(solution)/shard_map/ppermute | solution.py:369
  5.8 1.6 %slices.1 = (bf16[64,1024]{1,0:T(8,128)(2,1)S(1)}, bf16[112,1024]{1,0:T(8,128)(2,1)S(1)}, bf16[16,1024]{1,0:T(8,128)(2,1)S(1)}) custom-call(bf16[512,1024]{1,0:T(8,128)(2,1)} %bitcast.18), custom_call_target="tpu_custom_call" | custom-call | flops 268435456 | bytes 2097152 | tf_op jit(solution)/shard_map/slices/pallas_call | solution.py:43
  7.3 2.1 %collective-permute-start.5 = (bf16[16,1024]{1,0:T(8,128)(2,1)S(1)}, bf16[16,1024]{1,0:T(8,128)(2,1)S(1)}, u32[]{:S(2)}, u32[]{:S(2)}) collective-permute-start(bf16[16,1024]{1,0:T(8,128)(2,1)S(1)} %get-tuple-element.43), channel_id=1, source_target_pairs={{0,17},{1,18},{2,19},{3,20},{4,21},{5,22},{6,23},{7,24},{8,25},{9,... | collective-permute-start | bytes 98312 | tf_op jit(solution)/shard_map/ppermute | solution.py:369
  9.5 2.8 %collective-permute-start.4 = (bf16[112,1024]{1,0:T(8,128)(2,1)S(1)}, bf16[112,1024]{1,0:T(8,128)(2,1)S(1)}, u32[]{:S(2)}, u32[]{:S(2)}) collective-permute-start(bf16[112,1024]{1,0:T(8,128)(2,1)S(1)} %get-tuple-element.42), channel_id=1, source_target_pairs={{0,1},{1,2},{2,3},{3,4},{4,5},{5,6},{6,7},{7,8},{8,9},{9,10},{10,1... | collective-permute-start | bytes 688136 | tf_op jit(solution)/shard_map/ppermute | solution.py:369
  12.3 0.7 copy-done
  13.0 5.3 %embed.1 = (bf16[512,1024]{1,0:T(8,128)(2,1)S(1)}, bf16[512,1024]{1,0:T(8,128)(2,1)S(1)}, bf16[512,1536]{1,0:T(8,128)(2,1)S(1)}) custom-call(s32[80,16]{1,0:T(8,128)S(1)} %copy.19.own, s32[80,16]{1,0:T(8,128)S(1)} %collective-permute-done.up, s32[80,16]{1,0:T(8,128)S(1)} %collective-permute-done.1.left, s32[80,16]{1,0:T(8,128)S(1)} %collective-permute-done.2.diag, ...), custom_call_target="tpu_custom_call" | custom-call | flops 2684354560 | bytes 9437184 | tf_op jit(solution)/shard_map/embed/pallas_call | solution.py:43
  18.3 5.0 %attend.2 = (bf16[512,256]{1,0:T(8,128)(2,1)S(1)}, bf16[512,768]{1,0:T(8,128)(2,1)S(1)}, f32[2,256,1024]{2,1,0:T(8,128)S(1)}, bf16[2,256,1024]{2,1,0:T(8,128)(2,1)S(1)}, bf16[512,1024]{1,0:T(8,128)(2,1)S(1)}) custom-call(s32[4]{0:T(128)S(1)} %pad_add_fusion.1.place, bf16[512,1536]{1,0:T(8,128)(2,1)S(1)} %get-tuple-element.39.proj, ...), custom_call_target="tpu_custom_call" | custom-call | flops 3221225472 | bytes 8388608 | tf_op jit(solution)/shard_map/attend/pallas_call | solution.py:43
  23.3 0.7 collective-permute-start.9
  24.0 4.4 %attend.3 = (bf16[512,256]{1,0:T(8,128)(2,1)S(1)}, bf16[512,768]{1,0:T(8,128)(2,1)S(1)}, f32[2,256,1024]{2,1,0:T(8,128)S(1)}, bf16[2,256,1024]{2,1,0:T(8,128)(2,1)S(1)}) custom-call(s32[4]{0:T(128)S(1)} %pad_add_fusion.1.place, bf16[512,1536]{1,0:T(8,128)(2,1)S(1)} %get-tuple-element.39.proj, bf16[512,1024]{1,0:T(8,128)(2,1)S(1)} %get-tuple-element.40.normed, ...), custom_call_target="tpu_custom_call" | custom-call | flops 3221225472 | bytes 8388608 | tf_op jit(solution)/shard_map/attend/pallas_call | solution.py:43
  28.6 0.7 sum_core.2
  29.3 3.5 %collective-permute-start.10 = (bf16[2,8,16,1024]{3,2,1,0:T(8,128)(2,1)S(1)}, bf16[2,8,16,1024]{3,2,1,0:T(8,128)(2,1)S(1)}, u32[]{:S(2)}, u32[]{:S(2)}) collective-permute-start(bf16[2,8,16,1024]{3,2,1,0:T(8,128)(2,1)S(1)} %get-tuple-element.58), channel_id=1, source_target_pairs={{0,1},{1,0},{2,3},{3,2},{4,5},{5,4},{6,7},{7,6},{8,9},{9,8},{10,11... | collective-permute-start | bytes 1572872 | tf_op jit(solution)/shard_map/ppermute | solution.py:369
  32.8 0.7 sum_core.3
  33.5 2.3 %collective-permute-start.13 = (bf16[2,8,16,1024]{3,2,1,0:T(8,128)(2,1)S(1)}, bf16[2,8,16,1024]{3,2,1,0:T(8,128)(2,1)S(1)}, u32[]{:S(2)}, u32[]{:S(2)}) collective-permute-start(bf16[2,8,16,1024]{3,2,1,0:T(8,128)(2,1)S(1)} %get-tuple-element.65), channel_id=1, source_target_pairs={{0,33},{1,32},{2,35},{3,34},{4,37},{5,36},{6,39},{7,38},{8,41},{9,... | collective-permute-start | bytes 1572872 | tf_op jit(solution)/shard_map/ppermute | solution.py:369
  35.8 5.2 %finish.1 = (bf16[2,448,1024]{2,1,0:T(8,128)(2,1)S(1)}, bf16[2,64,1024]{2,1,0:T(8,128)(2,1)S(1)}, bf16[2,112,1024]{2,1,0:T(8,128)(2,1)S(1)}, bf16[2,16,1024]{2,1,0:T(8,128)(2,1)S(1)}, f32[8,128]{1,0:T(8,128)S(1)}) custom-call(bf16[512,1024]{1,0:T(8,128)(2,1)S(1)} %get-tuple-element.38.emb, bf16[512,1024]{1,0:T(8,128)(2,1)S(1)} %get-tuple-element.44.cot, ...), custom_call_target="tpu_custom_call" | custom-call | flops 2147483648 | bytes 10485760 | tf_op jit(solution)/shard_map/finish/pallas_call | solution.py:43
  41.3 12.7 %collective-permute-done.10.b = bf16[2,8,16,1024]{3,2,1,0:T(8,128)(2,1)S(1)} collective-permute-done((bf16[2,8,16,1024]{3,2,1,0:T(8,128)(2,1)S(1)}, bf16[2,8,16,1024]{3,2,1,0:T(8,128)(2,1)S(1)}, u32[]{:S(2)}, u32[]{:S(2)}) %collective-permute-start.10) | collective-permute-done | bytes 524320 | tf_op jit(solution)/shard_map/ppermute | solution.py:369
  54.0 0.7 sum_pair.2
  54.7 3.2 %collective-permute-start.11 = (bf16[8,16,1024]{2,1,0:T(8,128)(2,1)S(1)}, bf16[8,16,1024]{2,1,0:T(8,128)(2,1)S(1)}, u32[]{:S(2)}, u32[]{:S(2)}) collective-permute-start(bf16[8,16,1024]{2,1,0:T(8,128)(2,1)S(1)} %get-tuple-element.61), channel_id=1, source_target_pairs={{0,33},{1,32},{2,35},{3,34},{4,37},{5,36},{6,39},{7,38},{8,41},{9,... | collective-permute-start | bytes 786440 | tf_op jit(solution)/shard_map/ppermute | solution.py:369
  58.0 0.7 sum_pair.3
  58.7 4.9 %collective-permute-done.11.b = bf16[8,16,1024]{2,1,0:T(8,128)(2,1)S(1)} collective-permute-done((bf16[8,16,1024]{2,1,0:T(8,128)(2,1)S(1)}, bf16[8,16,1024]{2,1,0:T(8,128)(2,1)S(1)}, u32[]{:S(2)}, u32[]{:S(2)}) %collective-permute-start.11) | collective-permute-done | bytes 262176 | tf_op jit(solution)/shard_map/ppermute | solution.py:369
  63.6 2.2 %collective-permute-done.14.d = bf16[8,16,1024]{2,1,0:T(8,128)(2,1)S(1)} collective-permute-done((bf16[8,16,1024]{2,1,0:T(8,128)(2,1)S(1)}, bf16[8,16,1024]{2,1,0:T(8,128)(2,1)S(1)}, u32[]{:S(2)}, u32[]{:S(2)}) %collective-permute-start.14) | collective-permute-done | bytes 262176 | tf_op jit(solution)/shard_map/ppermute | solution.py:369
  65.8 0.9 join.1
  66.7 5.9 %all-to-all-start = ((bf16[8,16,2048]{2,1,0:T(8,128)(2,1)}), bf16[8,16,2048]{2,1,0:T(8,128)(2,1)S(1)}, u32[]{:S(2)}, u32[]{:S(2)}) async-start(bf16[8,16,2048]{2,1,0:T(8,128)(2,1)} %join.1), calls=%async_computation | async-start | bytes 1048576 | tf_op jit(solution)/shard_map/all_to_all | solution.py:506
  73.2 1.4 %collective-permute-start.8 = (bf16[2,16,1024]{2,1,0:T(8,128)(2,1)S(1)}, bf16[2,16,1024]{2,1,0:T(8,128)(2,1)S(1)}, u32[]{:S(2)}, u32[]{:S(2)}) collective-permute-start(bf16[2,16,1024]{2,1,0:T(8,128)(2,1)S(1)} %get-tuple-element.52), channel_id=1, source_target_pairs={{0,63},{1,48},{2,49},{3,50},{4,51},{5,52},{6,53},{7,54},{8,55},{9,... | collective-permute-start | bytes 196616 | tf_op jit(solution)/shard_map/ppermute | solution.py:369
  74.5 13.1 %all-to-all-done.ref = bf16[8,16,2048]{2,1,0:T(8,128)(2,1)S(1)} async-done(((bf16[8,16,2048]{2,1,0:T(8,128)(2,1)}), bf16[8,16,2048]{2,1,0:T(8,128)(2,1)S(1)}, u32[]{:S(2)}, u32[]{:S(2)}) %all-to-all-start) | async-done | bytes 524320 | tf_op jit(solution)/shard_map/all_to_all | solution.py:506
  87.7 3.1 %collective-permute-start.17 = (bf16[16,2048]{1,0:T(8,128)(2,1)S(1)}, bf16[16,2048]{1,0:T(8,128)(2,1)S(1)}, u32[]{:S(2)}, u32[]{:S(2)}) collective-permute-start(bf16[16,2048]{1,0:T(8,128)(2,1)S(1)} %get-tuple-element.69), channel_id=1, source_target_pairs={{0,192},{64,128},{128,64},{192,0},{1,193},{65,129},{129,65},{193,1... | collective-permute-start | bytes 196616 | tf_op jit(solution)/shard_map/ppermute | solution.py:377
  90.8 0.6 collective-permute-start.16
  91.8 2.0 %place.1 = (bf16[512,1024]{1,0:T(8,128)(2,1)}, bf16[512,1024]{1,0:T(8,128)(2,1)}) custom-call(bf16[2,448,1024]{2,1,0:T(8,128)(2,1)S(1)} %get-tuple-element.49.mid, bf16[2,64,1024]{2,1,0:T(8,128)(2,1)S(1)} %collective-permute-done.6.up, bf16[2,112,1024]{2,1,0:T(8,128)(2,1)S(1)} %collective-permute-done.7.left.arrived, ...), custom_call_target="tpu_custom_call" | custom-call | flops 268435456 | bytes 5242880 | tf_op jit(solution)/shard_map/place/pallas_call | solution.py:43
  93.8 2.7 %collective-permute-done.16.refs_1_ = bf16[16,2048]{1,0:T(8,128)(2,1)S(1)} collective-permute-done((bf16[16,2048]{1,0:T(8,128)(2,1)S(1)}, bf16[16,2048]{1,0:T(8,128)(2,1)S(1)}, u32[]{:S(2)}, u32[]{:S(2)}) %collective-permute-start.16) | collective-permute-done | bytes 65568 | tf_op jit(solution)/shard_map/ppermute | solution.py:377
  96.5 0.7 level.1
  (24 shorter events, 1.8 us)
Async XLA Ops:
  1.5 8.0 %collective-permute-start.2 = (s32[80,16]{1,0:T(8,128)S(1)}, s32[80,16]{1,0:T(8,128)S(1)}, u32[]{:S(2)}, u32[]{:S(2)}) collective-permute-start(s32[80,16]{1,0:T(8,128)S(1)} %copy.19.own), channel_id=1, source_target_pairs={{0,17},{1,18},{2,19},{3,20},{4,21},{5,22},{6,23},{7,24},{8,25},{9,... | collective-permute-start | bytes 15368 | tf_op jit(solution)/shard_map/ppermute | solution.py:369
  2.5 9.8 %collective-permute-start.1 = (s32[80,16]{1,0:T(8,128)S(1)}, s32[80,16]{1,0:T(8,128)S(1)}, u32[]{:S(2)}, u32[]{:S(2)}) collective-permute-start(s32[80,16]{1,0:T(8,128)S(1)} %copy.19.own), channel_id=1, source_target_pairs={{0,1},{1,2},{2,3},{3,4},{4,5},{5,6},{6,7},{7,8},{8,9},{9,10},{10,1... | collective-permute-start | bytes 15368 | tf_op jit(solution)/shard_map/ppermute | solution.py:369
  4.4 7.9 %collective-permute-start = (s32[80,16]{1,0:T(8,128)S(1)}, s32[80,16]{1,0:T(8,128)S(1)}, u32[]{:S(2)}, u32[]{:S(2)}) collective-permute-start(s32[80,16]{1,0:T(8,128)S(1)} %copy.19.own), channel_id=1, source_target_pairs={{0,16},{1,17},{2,18},{3,19},{4,20},{5,21},{6,22},{7,23},{8,24},{9,... | collective-permute-start | bytes 15368 | tf_op jit(solution)/shard_map/ppermute | solution.py:369
  7.3 10.9 %collective-permute-start.5 = (bf16[16,1024]{1,0:T(8,128)(2,1)S(1)}, bf16[16,1024]{1,0:T(8,128)(2,1)S(1)}, u32[]{:S(2)}, u32[]{:S(2)}) collective-permute-start(bf16[16,1024]{1,0:T(8,128)(2,1)S(1)} %get-tuple-element.43), channel_id=1, source_target_pairs={{0,17},{1,18},{2,19},{3,20},{4,21},{5,22},{6,23},{7,24},{8,25},{9,... | collective-permute-start | bytes 98312 | tf_op jit(solution)/shard_map/ppermute | solution.py:369
  9.4 8.9 %collective-permute-start.3 = (bf16[64,1024]{1,0:T(8,128)(2,1)S(1)}, bf16[64,1024]{1,0:T(8,128)(2,1)S(1)}, u32[]{:S(2)}, u32[]{:S(2)}) collective-permute-start(bf16[64,1024]{1,0:T(8,128)(2,1)S(1)} %get-tuple-element.41), channel_id=1, source_target_pairs={{0,16},{1,17},{2,18},{3,19},{4,20},{5,21},{6,22},{7,23},{8,24},{9,... | collective-permute-start | bytes 393224 | tf_op jit(solution)/shard_map/ppermute | solution.py:369
  9.5 8.8 %collective-permute-start.4 = (bf16[112,1024]{1,0:T(8,128)(2,1)S(1)}, bf16[112,1024]{1,0:T(8,128)(2,1)S(1)}, u32[]{:S(2)}, u32[]{:S(2)}) collective-permute-start(bf16[112,1024]{1,0:T(8,128)(2,1)S(1)} %get-tuple-element.42), channel_id=1, source_target_pairs={{0,1},{1,2},{2,3},{3,4},{4,5},{5,6},{6,7},{7,8},{8,9},{9,10},{10,1... | collective-permute-start | bytes 688136 | tf_op jit(solution)/shard_map/ppermute | solution.py:369
  12.3 0.7 copy-start
  23.3 5.3 %collective-permute-start.9 = (bf16[2,256,1024]{2,1,0:T(8,128)(2,1)S(1)}, bf16[2,256,1024]{2,1,0:T(8,128)(2,1)S(1)}, u32[]{:S(2)}, u32[]{:S(2)}) collective-permute-start(bf16[2,256,1024]{2,1,0:T(8,128)(2,1)S(1)} %get-tuple-element.56), channel_id=1, source_target_pairs={{0,16},{16,0},{1,17},{17,1},{2,18},{18,2},{3,19},{19,3},{4,20},{20... | collective-permute-start | bytes 3145736 | tf_op jit(solution)/shard_map/ppermute | solution.py:377
  28.4 4.4 %collective-permute-start.12 = (bf16[2,256,1024]{2,1,0:T(8,128)(2,1)S(1)}, bf16[2,256,1024]{2,1,0:T(8,128)(2,1)S(1)}, u32[]{:S(2)}, u32[]{:S(2)}) collective-permute-start(bf16[2,256,1024]{2,1,0:T(8,128)(2,1)S(1)} %get-tuple-element.63), channel_id=1, source_target_pairs={{0,16},{16,0},{1,17},{17,1},{2,18},{18,2},{3,19},{19,3},{4,20},{20... | collective-permute-start | bytes 3145736 | tf_op jit(solution)/shard_map/ppermute | solution.py:377
  29.3 24.7 %collective-permute-start.10 = (bf16[2,8,16,1024]{3,2,1,0:T(8,128)(2,1)S(1)}, bf16[2,8,16,1024]{3,2,1,0:T(8,128)(2,1)S(1)}, u32[]{:S(2)}, u32[]{:S(2)}) collective-permute-start(bf16[2,8,16,1024]{3,2,1,0:T(8,128)(2,1)S(1)} %get-tuple-element.58), channel_id=1, source_target_pairs={{0,1},{1,0},{2,3},{3,2},{4,5},{5,4},{6,7},{7,6},{8,9},{9,8},{10,11... | collective-permute-start | bytes 1572872 | tf_op jit(solution)/shard_map/ppermute | solution.py:369
  33.5 24.4 %collective-permute-start.13 = (bf16[2,8,16,1024]{3,2,1,0:T(8,128)(2,1)S(1)}, bf16[2,8,16,1024]{3,2,1,0:T(8,128)(2,1)S(1)}, u32[]{:S(2)}, u32[]{:S(2)}) collective-permute-start(bf16[2,8,16,1024]{3,2,1,0:T(8,128)(2,1)S(1)} %get-tuple-element.65), channel_id=1, source_target_pairs={{0,33},{1,32},{2,35},{3,34},{4,37},{5,36},{6,39},{7,38},{8,41},{9,... | collective-permute-start | bytes 1572872 | tf_op jit(solution)/shard_map/ppermute | solution.py:369
  41.1 17.7 %collective-permute-start.7 = (bf16[2,112,1024]{2,1,0:T(8,128)(2,1)S(1)}, bf16[2,112,1024]{2,1,0:T(8,128)(2,1)S(1)}, u32[]{:S(2)}, u32[]{:S(2)}) collective-permute-start(bf16[2,112,1024]{2,1,0:T(8,128)(2,1)S(1)} %get-tuple-element.51), channel_id=1, source_target_pairs={{0,15},{1,0},{2,1},{3,2},{4,3},{5,4},{6,5},{7,6},{8,7},{9,8},{10,9... | collective-permute-start | bytes 1376264 | tf_op jit(solution)/shard_map/ppermute | solution.py:369
  54.7 8.9 %collective-permute-start.11 = (bf16[8,16,1024]{2,1,0:T(8,128)(2,1)S(1)}, bf16[8,16,1024]{2,1,0:T(8,128)(2,1)S(1)}, u32[]{:S(2)}, u32[]{:S(2)}) collective-permute-start(bf16[8,16,1024]{2,1,0:T(8,128)(2,1)S(1)} %get-tuple-element.61), channel_id=1, source_target_pairs={{0,33},{1,32},{2,35},{3,34},{4,37},{5,36},{6,39},{7,38},{8,41},{9,... | collective-permute-start | bytes 786440 | tf_op jit(solution)/shard_map/ppermute | solution.py:369
  58.6 7.2 %collective-permute-start.14 = (bf16[8,16,1024]{2,1,0:T(8,128)(2,1)S(1)}, bf16[8,16,1024]{2,1,0:T(8,128)(2,1)S(1)}, u32[]{:S(2)}, u32[]{:S(2)}) collective-permute-start(bf16[8,16,1024]{2,1,0:T(8,128)(2,1)S(1)} %get-tuple-element.67), channel_id=1, source_target_pairs={{0,1},{1,0},{2,3},{3,2},{4,5},{5,4},{6,7},{7,6},{8,9},{9,8},{10,11... | collective-permute-start | bytes 786440 | tf_op jit(solution)/shard_map/ppermute | solution.py:369
  66.7 20.9 %all-to-all-start = ((bf16[8,16,2048]{2,1,0:T(8,128)(2,1)}), bf16[8,16,2048]{2,1,0:T(8,128)(2,1)S(1)}, u32[]{:S(2)}, u32[]{:S(2)}) async-start(bf16[8,16,2048]{2,1,0:T(8,128)(2,1)} %join.1), calls=%async_computation | async-start | bytes 1048576 | tf_op jit(solution)/shard_map/all_to_all | solution.py:506
  72.6 19.2 %collective-permute-start.6 = (bf16[2,64,1024]{2,1,0:T(8,128)(2,1)S(1)}, bf16[2,64,1024]{2,1,0:T(8,128)(2,1)S(1)}, u32[]{:S(2)}, u32[]{:S(2)}) collective-permute-start(bf16[2,64,1024]{2,1,0:T(8,128)(2,1)S(1)} %get-tuple-element.50), channel_id=1, source_target_pairs={{0,48},{1,49},{2,50},{3,51},{4,52},{5,53},{6,54},{7,55},{8,56},{9,... | collective-permute-start | bytes 786440 | tf_op jit(solution)/shard_map/ppermute | solution.py:369
  73.2 18.7 %collective-permute-start.8 = (bf16[2,16,1024]{2,1,0:T(8,128)(2,1)S(1)}, bf16[2,16,1024]{2,1,0:T(8,128)(2,1)S(1)}, u32[]{:S(2)}, u32[]{:S(2)}) collective-permute-start(bf16[2,16,1024]{2,1,0:T(8,128)(2,1)S(1)} %get-tuple-element.52), channel_id=1, source_target_pairs={{0,63},{1,48},{2,49},{3,50},{4,51},{5,52},{6,53},{7,54},{8,55},{9,... | collective-permute-start | bytes 196616 | tf_op jit(solution)/shard_map/ppermute | solution.py:369
  87.7 6.2 %collective-permute-start.17 = (bf16[16,2048]{1,0:T(8,128)(2,1)S(1)}, bf16[16,2048]{1,0:T(8,128)(2,1)S(1)}, u32[]{:S(2)}, u32[]{:S(2)}) collective-permute-start(bf16[16,2048]{1,0:T(8,128)(2,1)S(1)} %get-tuple-element.69), channel_id=1, source_target_pairs={{0,192},{64,128},{128,64},{192,0},{1,193},{65,129},{129,65},{193,1... | collective-permute-start | bytes 196616 | tf_op jit(solution)/shard_map/ppermute | solution.py:377
  90.8 5.8 %collective-permute-start.16 = (bf16[16,2048]{1,0:T(8,128)(2,1)S(1)}, bf16[16,2048]{1,0:T(8,128)(2,1)S(1)}, u32[]{:S(2)}, u32[]{:S(2)}) collective-permute-start(bf16[16,2048]{1,0:T(8,128)(2,1)S(1)} %get-tuple-element.69), channel_id=1, source_target_pairs={{0,128},{64,192},{128,0},{192,64},{1,129},{65,193},{129,1},{193,65... | collective-permute-start | bytes 196616 | tf_op jit(solution)/shard_map/ppermute | solution.py:377
  91.4 5.2 %collective-permute-start.15 = (bf16[16,2048]{1,0:T(8,128)(2,1)S(1)}, bf16[16,2048]{1,0:T(8,128)(2,1)S(1)}, u32[]{:S(2)}, u32[]{:S(2)}) collective-permute-start(bf16[16,2048]{1,0:T(8,128)(2,1)S(1)} %get-tuple-element.69), channel_id=1, source_target_pairs={{0,64},{64,0},{128,192},{192,128},{1,65},{65,1},{129,193},{193,129... | collective-permute-start | bytes 196616 | tf_op jit(solution)/shard_map/ppermute | solution.py:377

commit v6 on v5

--- a/solution.py
+++ b/solution.py
@@ -54,6 +54,10 @@
 
 def hbm():
     return pl.BlockSpec(memory_space=pltpu.HBM)
+
+
+def anywhere():
+    return pl.BlockSpec(memory_space=pl.ANY)
 
 
 def sems(n):
@@ -180,10 +184,11 @@
     backward(units, place, normed, cot, weight, att, gp, keep, send, *held)
 
 
-def attend_next(place, proj, normed, cot, ow, att, gp, keep, send, weight, sem, *held):
-    copy = pltpu.make_async_copy(ow.at[:, CW:], weight, sem)
+def attend_next(chunk, place, proj, normed, cot, ow, *refs):
+    att, gp, keep, send, weight, sem, *held = refs[1:] if chunk > 1 else refs
+    copy = pltpu.make_async_copy(ow.at[:, chunk * CW : (chunk + 1) * CW], weight, sem)
     copy.start()
-    units = forward(1, place, proj, att, *held)
+    units = forward(chunk, place, proj, att, *held)
     copy.wait()
     backward(units, place, normed, cot, weight, att, gp, keep, send, *held)
 
@@ -256,7 +261,9 @@
             out[half, :, 3 * CW :] = dot(cot[:, cut], att[...], 0, 0).astype(out.dtype)
 
 
-def finish_kernel(emb, cot, wq, ow, att0, att1, gp0, gp1, mid, up, left, diag, tick, weight, last, big, sems):
+def finish_kernel(emb, cot, wq, ow, *refs):
+    atts, gps = refs[:CHUNKS], refs[CHUNKS : 2 * CHUNKS]
+    mid, up, left, diag, tick, weight, last, big, sems = refs[2 * CHUNKS :]
     copies = [
         pltpu.make_async_copy(ow, last, sems.at[0]),
         pltpu.make_async_copy(wq, weight, sems.at[1]),
@@ -285,13 +292,13 @@
         m2 = jnp.mean(gst * standard, axis=1, keepdims=True)
         return cot[here].astype(F32) + inverse * (gst - m1 - standard * m2)
 
-    att = jnp.concatenate([att0[...], att1[...]], axis=1)
+    att = jnp.concatenate([a[...] for a in atts], axis=1)
     big[...] = dot(att, last[...], 1, 1)
     each(0, lambda here, x, branch: x + branch)
     copies[1].wait()
     parts = []
     for i in range(3):
-        parts += [g[:, i * CW : (i + 1) * CW] for g in (gp0, gp1)]
+        parts += [g[:, i * CW : (i + 1) * CW] for g in gps]
     big[...] = dot(jnp.concatenate(parts, axis=1), weight[...], 1, 1)
     each(1, gradient)
     pick, corner = late_cells(OWN, MSG, True), late_cells(64, 16, True)
@@ -340,20 +347,22 @@
         out[...] = (a[v] + b[v].astype(F32)).astype(out.dtype)
 
 
-def join_kernel(a, b, c, d, arrived, out):
-    out[:, :, 0:W] = (a[...] + b[...].astype(F32)).astype(BF16)
-    out[:, :, W:] = (c[...] + d[...].astype(F32)).astype(BF16)
-
-
-def depth_kernel(ref, keep, send):
-    total = sum(ref[i].astype(F32) for i in range(8))
-    keep[...] = total
-    send[...] = total.astype(BF16)
-
-
-def level_kernel(factor, own, *refs):
-    qkv, outw = refs[3:]
-    total = (own[...] + sum(r[...].astype(F32) for r in refs[:3])) * factor
+def join_kernel(*refs):
+    out = refs[-1]
+    for c in range(CHUNKS):
+        out[:, :, c * W : (c + 1) * W] = (refs[2 * c][...] + refs[2 * c + 1][...].astype(F32)).astype(BF16)
+
+
+def depth_kernel(ref, out):
+    out[...] = sum(ref[i].astype(F32) for i in range(8)).astype(BF16)
+
+
+def couple_kernel(a, b, out):
+    out[...] = (a[...].astype(F32) + b[...].astype(F32)).astype(BF16)
+
+
+def level_kernel(factor, a, b, qkv, outw):
+    total = (a[...].astype(F32) + b[...].astype(F32)) * factor
     for c in range(CHUNKS):
         for i in range(3):
             qkv[:, i * HW + c * CW : i * HW + (c + 1) * CW] = total[:, c * W + i * Q : c * W + (i + 1) * Q]
@@ -381,27 +390,37 @@
     return permute(x, lambda la, lo: (la ^ (flip & 2), lo ^ (flip & 1)))
 
 
-def halve(name, kernel, shape, place, *terms):
-    size = math.prod(shape)
+def halve(name, kernel, shape, operands, specs):
     return call(
         kernel,
         [sds(shape, F32), sds(shape)],
-        (place, *terms),
-        [smem()] + [vmem()] * len(terms),
-        2 * size,
-        16 * size,
+        operands,
+        specs,
+        2**10,
+        2**10,
         limit=16,
         name=name,
     )
 
 
-def sum_x(place, keep, send, tick, order):
+def order(c):
+    return (3, 1) if c % 2 else (1, 3)
+
+
+def sum_core(place, keep, send, c):
     fold = (2, 8, 2, 16, W)
-    core, pair = (parity_core, parity_pair) if order[0] == 1 else (high_core, high_pair)
+    kernel = high_core if c % 2 else parity_core
     recv = swap(send, "core", 1)
-    keep, send = halve("sum_core", core, (2, 8, 16, W), place, keep.reshape(fold), recv.reshape(fold))
-    keep, send = halve("sum_pair", pair, (8, 16, W), place, keep, swap_x(send, order[0]), tick)
-    return [keep, swap_x(send, order[1])]
+    operands = (place, keep.reshape(fold), recv.reshape(fold))
+    return halve("sum_core", kernel, (2, 8, 16, W), operands, [smem(), vmem(), vmem()])
+
+
+def sum_pair(place, keep, send, tick, c):
+    kernel = high_pair if c % 2 else parity_pair
+    recv = swap_x(send, order(c)[0])
+    specs = [smem(), vmem(), vmem(), anywhere()]
+    keep, send = halve("sum_pair", kernel, (8, 16, W), (place, keep, recv, tick), specs)
+    return [keep, swap_x(send, order(c)[1])]
 
 
 def shards(
@@ -442,35 +461,38 @@
     column = pltpu.VMEM((MODEL, CW), BF16)
     units = BANDS * CW // 128
     held = [pltpu.VMEM((units, 2, BAND, BAND), F32)] + [pltpu.VMEM((units, 2 * BAND, BAND), BF16)] * 2
-    att0, gp0, keep0, send0, cot = call(
+    att, gp, keep, send, cot = call(
         attend_first,
         outs + [sds((TOKENS, MODEL))],
         (place, proj, normed, grads, up, left, diag, out_weight),
         [smem(), vmem(), vmem(), hbm(), vmem(), vmem(), vmem(), hbm()],
-        3 * 2**30,
-        8 * 2**20,
-        2**19,
+        2**20,
+        2**12,
         name="attend",
         scratch=[pltpu.VMEM((TOKENS, MODEL), BF16), column, sems(2), *held],
     )
-    att1, gp1, keep1, send1 = call(
-        attend_next,
-        outs,
-        (place, proj, normed, cot, out_weight),
-        [smem(), vmem(), vmem(), vmem(), hbm()],
-        3 * 2**30,
-        8 * 2**20,
-        2**19,
-        name="attend",
-        scratch=[column, pltpu.SemaphoreType.DMA, *held],
-    )
+    parts, cores = [(att, gp)], [sum_core(place, keep, send, 0)]
+    for c in range(1, CHUNKS):
+        after = [cores[c - 2][0]] if c > 1 else []
+        att, gp, keep, send = call(
+            functools.partial(attend_next, c),
+            outs,
+            (place, proj, normed, cot, out_weight, *after),
+            [smem(), vmem(), vmem(), vmem(), hbm()] + [anywhere()] * len(after),
+            2**20,
+            2**12,
+            name="attend",
+            scratch=[column, pltpu.SemaphoreType.DMA, *held],
+        )
+        parts.append((att, gp))
+        cores.append(sum_core(place, keep, send, c))
     *sent, tick = call(
         finish_kernel,
         [sds((2, OWN, MODEL)), sds((2, 64, MODEL)), sds((2, MSG, MODEL)), sds((2, 16, MODEL)), sds((8, 128), F32)],
-        (emb, cot, qkv_weight, out_weight, att0, att1, gp0, gp1),
-        [vmem(), vmem(), hbm(), hbm()] + [vmem()] * 4,
-        2 * TOKENS * 1024 * 2048,
-        10 * 2**20,
+        (emb, cot, qkv_weight, out_weight, *[p[0] for p in parts], *[p[1] for p in parts]),
+        [vmem(), vmem(), hbm(), hbm()] + [vmem()] * 2 * CHUNKS,
+        2**20,
+        2**12,
         name="finish",
         scratch=[
             pltpu.VMEM((MODEL, 3 * HW), BF16),
@@ -479,9 +501,11 @@
             sems(2),
         ],
     )
-    summed = sum_x(place, keep0, send0, tick, (1, 3)) + sum_x(place, keep1, send1, tick, (3, 1))
     mid, up, left, diag = sent
     up, left, diag = shift(up, -1, 0), shift(left, 0, -1), shift(diag, -1, -1)
+    summed = []
+    for c, (keep, send) in enumerate(cores):
+        summed += sum_pair(place, keep, send, diag if c else tick, c)
     out, gin = call(
         place_kernel,
         [sds((TOKENS, MODEL))] * 2,
@@ -495,34 +519,26 @@
     factor = 1.0 / math.sqrt(TOKENS * NB * NLAT * NLON)
     joined = call(
         join_kernel,
-        sds((8, 16, 2 * W)),
-        (*summed, left),
-        [vmem()] * 4 + [hbm()],
+        sds((8, 16, CHUNKS * W)),
+        summed,
+        [vmem()] * 2 * CHUNKS,
         2**19,
         2**21,
         limit=16,
         name="join",
     )
     depth = lax.all_to_all(joined, "z", 0, 0, tiled=True)
-    keep, send = call(
-        depth_kernel,
-        [sds((16, 2 * W), F32), sds((16, 2 * W))],
-        (depth,),
-        [vmem()],
-        2**18,
-        2**20,
-        limit=16,
-        name="depth",
-    )
+    small = dict(flops=2**17, nbytes=2**19, limit=16)
+    wide = (16, CHUNKS * W)
+    total = call(depth_kernel, sds(wide), (depth,), [vmem()], name="depth", **small)
+    total = call(couple_kernel, sds(wide), (total, swap(total, "batch", 1)), [vmem()] * 2, name="couple", **small)
     g_qkv, g_out = call(
         functools.partial(level_kernel, factor),
         [sds((16, 3 * HW), F32), sds((16, HW), F32)],
-        (keep, *[swap(send, "batch", d) for d in (1, 2, 3)]),
-        [vmem()] * 4,
-        2**17,
-        2**19,
-        limit=16,
+        (total, swap(total, "batch", 3)),
+        [vmem()] * 2,
         name="level",
+        **small,
     )
     shape = (1, ROWS, COLS, MODEL)
     return (out.reshape(shape), gin.reshape(shape), g_qkv, g_out)

time: 98.7 us -> 95.5 us (0.968); the launches traced: 97.2 us -> 95.1 us
  waiting for transfers between devices: 35.6 us -> 30.4 us
  starting transfers between devices: 31.4 us -> 34.5 us
    ppermute x13, waiting for transfers between devices: 19.9 us -> 9.82 us  [permute(): return lax.ppermute(x, GRID, pairs)]
    all_to_all x1, waiting for transfers between devices: 13.1 us -> 17.4 us  [shards(): depth = lax.all_to_all(joined, 'z', 0, 0, tiled=True)]
    all_to_all x1, starting transfers between devices: 5.95 us -> 8.08 us  [shards(): depth = lax.all_to_all(joined, 'z', 0, 0, tiled=True)]
    ppermute x5 -> x4, starting transfers between devices: 5.06 us -> 5.64 us  [swap(): lax.ppermute(x, axis, [(i, i ^ flip) for i in range(lax.axis_size(axis))])]
    ppermute x5 -> x4, waiting for transfers between devices: 2.73 us -> 3.18 us  [swap(): lax.ppermute(x, axis, [(i, i ^ flip) for i in range(lax.axis_size(axis))])]
    pallas_call x13 -> x14, Pallas kernels: 27.8 us -> 27.8 us  [call(): pl.pallas_call(kernel, out_shape=outs, in_specs=specs, out_specs=jax.tree...]
  transfers between devices with their start and end apart: 19 -> 18, of which waited for: 5 -> 6; matrix products, arithmetic and copies ran while one was open for 0% -> 0% of each run, Pallas kernels for 22% -> 22%
where the time goes in v6:
time: 95.5 us; the launch traced here: 95.1 us
  starting transfers between devices  34.5 us (36%)
  waiting for transfers between devices  30.4 us (32%)
  Pallas kernels  27.8 us (29%)
    pallas_call x14, Pallas kernels, call(): pl.pallas_call(kernel, out_shape=outs, in_specs=specs, out_specs=jax.tree...  27.8 us
    ppermute x13, starting transfers between devices, permute(): return lax.ppermute(x, GRID, pairs)  20.8 us
    all_to_all x1, waiting for transfers between devices, shards(): depth = lax.all_to_all(joined, 'z', 0, 0, tiled=True)  17.4 us
    ppermute x13, waiting for transfers between devices, permute(): return lax.ppermute(x, GRID, pairs)  9.82 us
    all_to_all x1, starting transfers between devices, shards(): depth = lax.all_to_all(joined, 'z', 0, 0, tiled=True)  8.08 us
    ppermute x4, starting transfers between devices, swap(): lax.ppermute(x, axis, [(i, i ^ flip) for i in range(lax.axis_size(axis))])  5.64 us
    ppermute x4, waiting for transfers between devices, swap(): lax.ppermute(x, axis, [(i, i ^ flip) for i in range(lax.axis_size(axis))])  3.18 us
  transfers between devices with their start and end apart: 18, of which 6 were waited for; matrix products, arithmetic and copies ran while one was open for 0% of the time, Pallas kernels for 22%

profile of v6, /device:TPU:32, one launch (start us, length us, event | category | flops | bytes accessed | tf_op | source)
XLA Modules:
  0.0 95.1 jit_solution(16999613753006014472)
XLA Ops:
  0.6 0.8 pad_add_fusion
  1.5 1.0 %collective-permute-start.2 = (s32[80,16]{1,0:T(8,128)S(1)}, s32[80,16]{1,0:T(8,128)S(1)}, u32[]{:S(2)}, u32[]{:S(2)}) collective-permute-start(s32[80,16]{1,0:T(8,128)S(1)} %copy.19.own), channel_id=1, source_target_pairs={{0,17},{1,18},{2,19},{3,20},{4,21},{5,22},{6,23},{7,24},{8,25},{9,... | collective-permute-start | bytes 15368 | tf_op jit(solution)/shard_map/ppermute | solution.py:378
  2.5 1.9 %collective-permute-start.1 = (s32[80,16]{1,0:T(8,128)S(1)}, s32[80,16]{1,0:T(8,128)S(1)}, u32[]{:S(2)}, u32[]{:S(2)}) collective-permute-start(s32[80,16]{1,0:T(8,128)S(1)} %copy.19.own), channel_id=1, source_target_pairs={{0,1},{1,2},{2,3},{3,4},{4,5},{5,6},{6,7},{7,8},{8,9},{9,10},{10,1... | collective-permute-start | bytes 15368 | tf_op jit(solution)/shard_map/ppermute | solution.py:378
  4.4 1.4 %collective-permute-start = (s32[80,16]{1,0:T(8,128)S(1)}, s32[80,16]{1,0:T(8,128)S(1)}, u32[]{:S(2)}, u32[]{:S(2)}) collective-permute-start(s32[80,16]{1,0:T(8,128)S(1)} %copy.19.own), channel_id=1, source_target_pairs={{0,16},{1,17},{2,18},{3,19},{4,20},{5,21},{6,22},{7,23},{8,24},{9,... | collective-permute-start | bytes 15368 | tf_op jit(solution)/shard_map/ppermute | solution.py:378
  5.8 1.6 %slices.1 = (bf16[64,1024]{1,0:T(8,128)(2,1)S(1)}, bf16[112,1024]{1,0:T(8,128)(2,1)S(1)}, bf16[16,1024]{1,0:T(8,128)(2,1)S(1)}) custom-call(bf16[512,1024]{1,0:T(8,128)(2,1)} %bitcast.18), custom_call_target="tpu_custom_call" | custom-call | flops 268435456 | bytes 2097152 | tf_op jit(solution)/shard_map/slices/pallas_call | solution.py:43
  7.3 2.1 %collective-permute-start.5 = (bf16[16,1024]{1,0:T(8,128)(2,1)S(1)}, bf16[16,1024]{1,0:T(8,128)(2,1)S(1)}, u32[]{:S(2)}, u32[]{:S(2)}) collective-permute-start(bf16[16,1024]{1,0:T(8,128)(2,1)S(1)} %get-tuple-element.41), channel_id=1, source_target_pairs={{0,17},{1,18},{2,19},{3,20},{4,21},{5,22},{6,23},{7,24},{8,25},{9,... | collective-permute-start | bytes 98312 | tf_op jit(solution)/shard_map/ppermute | solution.py:378
  9.5 2.8 %collective-permute-start.4 = (bf16[112,1024]{1,0:T(8,128)(2,1)S(1)}, bf16[112,1024]{1,0:T(8,128)(2,1)S(1)}, u32[]{:S(2)}, u32[]{:S(2)}) collective-permute-start(bf16[112,1024]{1,0:T(8,128)(2,1)S(1)} %get-tuple-element.40), channel_id=1, source_target_pairs={{0,1},{1,2},{2,3},{3,4},{4,5},{5,6},{6,7},{7,8},{8,9},{9,10},{10,1... | collective-permute-start | bytes 688136 | tf_op jit(solution)/shard_map/ppermute | solution.py:378
  12.3 0.7 copy-done.1
  13.0 5.3 %embed.1 = (bf16[512,1024]{1,0:T(8,128)(2,1)S(1)}, bf16[512,1024]{1,0:T(8,128)(2,1)S(1)}, bf16[512,1536]{1,0:T(8,128)(2,1)S(1)}) custom-call(s32[80,16]{1,0:T(8,128)S(1)} %copy.19.own, s32[80,16]{1,0:T(8,128)S(1)} %collective-permute-done.up, s32[80,16]{1,0:T(8,128)S(1)} %collective-permute-done.1.left, s32[80,16]{1,0:T(8,128)S(1)} %collective-permute-done.2.diag, ...), custom_call_target="tpu_custom_call" | custom-call | flops 2684354560 | bytes 9437184 | tf_op jit(solution)/shard_map/embed/pallas_call | solution.py:43
  18.3 5.0 %attend.2 = (bf16[512,256]{1,0:T(8,128)(2,1)S(1)}, bf16[512,768]{1,0:T(8,128)(2,1)S(1)}, f32[2,256,1024]{2,1,0:T(8,128)S(1)}, bf16[2,256,1024]{2,1,0:T(8,128)(2,1)S(1)}, bf16[512,1024]{1,0:T(8,128)(2,1)S(1)}) custom-call(s32[4]{0:T(128)S(1)} %pad_add_fusion.1.place, bf16[512,1536]{1,0:T(8,128)(2,1)S(1)} %get-tuple-element.37.proj, ...), custom_call_target="tpu_custom_call" | custom-call | flops 1048576 | bytes 4096 | tf_op jit(solution)/shard_map/attend/pallas_call | solution.py:43
  23.3 0.7 collective-permute-start.9
  24.0 4.4 %attend.3 = (bf16[512,256]{1,0:T(8,128)(2,1)S(1)}, bf16[512,768]{1,0:T(8,128)(2,1)S(1)}, f32[2,256,1024]{2,1,0:T(8,128)S(1)}, bf16[2,256,1024]{2,1,0:T(8,128)(2,1)S(1)}) custom-call(s32[4]{0:T(128)S(1)} %pad_add_fusion.1.place, bf16[512,1536]{1,0:T(8,128)(2,1)S(1)} %get-tuple-element.37.proj, bf16[512,1024]{1,0:T(8,128)(2,1)S(1)} %get-tuple-element.38.normed, ...), custom_call_target="tpu_custom_call" | custom-call | flops 1048576 | bytes 4096 | tf_op jit(solution)/shard_map/attend/pallas_call | solution.py:43
  28.6 0.7 sum_core.2
  29.3 3.5 %collective-permute-start.10 = (bf16[2,8,16,1024]{3,2,1,0:T(8,128)(2,1)S(1)}, bf16[2,8,16,1024]{3,2,1,0:T(8,128)(2,1)S(1)}, u32[]{:S(2)}, u32[]{:S(2)}) collective-permute-start(bf16[2,8,16,1024]{3,2,1,0:T(8,128)(2,1)S(1)} %get-tuple-element.56), channel_id=1, source_target_pairs={{0,1},{1,0},{2,3},{3,2},{4,5},{5,4},{6,7},{7,6},{8,9},{9,8},{10,11... | collective-permute-start | bytes 1572872 | tf_op jit(solution)/shard_map/ppermute | solution.py:378
  32.8 0.8 sum_core.3
  33.6 2.3 %collective-permute-start.13 = (bf16[2,8,16,1024]{3,2,1,0:T(8,128)(2,1)S(1)}, bf16[2,8,16,1024]{3,2,1,0:T(8,128)(2,1)S(1)}, u32[]{:S(2)}, u32[]{:S(2)}) collective-permute-start(bf16[2,8,16,1024]{3,2,1,0:T(8,128)(2,1)S(1)} %get-tuple-element.63), channel_id=1, source_target_pairs={{0,33},{1,32},{2,35},{3,34},{4,37},{5,36},{6,39},{7,38},{8,41},{9,... | collective-permute-start | bytes 1572872 | tf_op jit(solution)/shard_map/ppermute | solution.py:378
  35.9 5.2 %finish.1 = (bf16[2,448,1024]{2,1,0:T(8,128)(2,1)S(1)}, bf16[2,64,1024]{2,1,0:T(8,128)(2,1)S(1)}, bf16[2,112,1024]{2,1,0:T(8,128)(2,1)S(1)}, bf16[2,16,1024]{2,1,0:T(8,128)(2,1)S(1)}, f32[8,128]{1,0:T(8,128)S(1)}) custom-call(bf16[512,1024]{1,0:T(8,128)(2,1)S(1)} %get-tuple-element.36.emb, bf16[512,1024]{1,0:T(8,128)(2,1)S(1)} %get-tuple-element.42.cot, ...), custom_call_target="tpu_custom_call" | custom-call | flops 1048576 | bytes 4096 | tf_op jit(solution)/shard_map/finish/pallas_call | solution.py:43
  41.1 1.4 %collective-permute-start.8 = (bf16[2,16,1024]{2,1,0:T(8,128)(2,1)S(1)}, bf16[2,16,1024]{2,1,0:T(8,128)(2,1)S(1)}, u32[]{:S(2)}, u32[]{:S(2)}) collective-permute-start(bf16[2,16,1024]{2,1,0:T(8,128)(2,1)S(1)} %get-tuple-element.50), channel_id=1, source_target_pairs={{0,63},{1,48},{2,49},{3,50},{4,51},{5,52},{6,53},{7,54},{8,55},{9,... | collective-permute-start | bytes 196616 | tf_op jit(solution)/shard_map/ppermute | solution.py:378
  42.5 3.0 %collective-permute-done.10.b = bf16[2,8,16,1024]{3,2,1,0:T(8,128)(2,1)S(1)} collective-permute-done((bf16[2,8,16,1024]{3,2,1,0:T(8,128)(2,1)S(1)}, bf16[2,8,16,1024]{3,2,1,0:T(8,128)(2,1)S(1)}, u32[]{:S(2)}, u32[]{:S(2)}) %collective-permute-start.10) | collective-permute-done | bytes 524320 | tf_op jit(solution)/shard_map/ppermute | solution.py:378
  45.5 0.6 sum_pair.2
  46.2 2.6 %collective-permute-start.11 = (bf16[8,16,1024]{2,1,0:T(8,128)(2,1)S(1)}, bf16[8,16,1024]{2,1,0:T(8,128)(2,1)S(1)}, u32[]{:S(2)}, u32[]{:S(2)}) collective-permute-start(bf16[8,16,1024]{2,1,0:T(8,128)(2,1)S(1)} %get-tuple-element.59), channel_id=1, source_target_pairs={{0,33},{1,32},{2,35},{3,34},{4,37},{5,36},{6,39},{7,38},{8,41},{9,... | collective-permute-start | bytes 786440 | tf_op jit(solution)/shard_map/ppermute | solution.py:378
  49.5 1.9 %collective-permute-start.14 = (bf16[8,16,1024]{2,1,0:T(8,128)(2,1)S(1)}, bf16[8,16,1024]{2,1,0:T(8,128)(2,1)S(1)}, u32[]{:S(2)}, u32[]{:S(2)}) collective-permute-start(bf16[8,16,1024]{2,1,0:T(8,128)(2,1)S(1)} %get-tuple-element.65), channel_id=1, source_target_pairs={{0,1},{1,0},{2,3},{3,2},{4,5},{5,4},{6,7},{7,6},{8,9},{9,8},{10,11... | collective-permute-start | bytes 786440 | tf_op jit(solution)/shard_map/ppermute | solution.py:378
  51.3 3.4 %collective-permute-done.11.refs_1_ = bf16[8,16,1024]{2,1,0:T(8,128)(2,1)S(1)} collective-permute-done((bf16[8,16,1024]{2,1,0:T(8,128)(2,1)S(1)}, bf16[8,16,1024]{2,1,0:T(8,128)(2,1)S(1)}, u32[]{:S(2)}, u32[]{:S(2)}) %collective-permute-start.11) | collective-permute-done | bytes 262176 | tf_op jit(solution)/shard_map/ppermute | solution.py:378
  54.8 3.3 %collective-permute-done.14.refs_3_ = bf16[8,16,1024]{2,1,0:T(8,128)(2,1)S(1)} collective-permute-done((bf16[8,16,1024]{2,1,0:T(8,128)(2,1)S(1)}, bf16[8,16,1024]{2,1,0:T(8,128)(2,1)S(1)}, u32[]{:S(2)}, u32[]{:S(2)}) %collective-permute-start.14) | collective-permute-done | bytes 262176 | tf_op jit(solution)/shard_map/ppermute | solution.py:378
  58.1 0.9 join.1
  59.0 8.1 %all-to-all-start = ((bf16[8,16,2048]{2,1,0:T(8,128)(2,1)}), bf16[8,16,2048]{2,1,0:T(8,128)(2,1)S(1)}, u32[]{:S(2)}, u32[]{:S(2)}) async-start(bf16[8,16,2048]{2,1,0:T(8,128)(2,1)} %join.1), calls=%async_computation | async-start | bytes 1048576 | tf_op jit(solution)/shard_map/all_to_all | solution.py:530
  67.0 17.4 %all-to-all-done.ref = bf16[8,16,2048]{2,1,0:T(8,128)(2,1)S(1)} async-done(((bf16[8,16,2048]{2,1,0:T(8,128)(2,1)}), bf16[8,16,2048]{2,1,0:T(8,128)(2,1)S(1)}, u32[]{:S(2)}, u32[]{:S(2)}) %all-to-all-start) | async-done | bytes 524320 | tf_op jit(solution)/shard_map/all_to_all | solution.py:530
  84.5 1.7 %collective-permute-start.15 = (bf16[16,2048]{1,0:T(8,128)(2,1)S(1)}, bf16[16,2048]{1,0:T(8,128)(2,1)S(1)}, u32[]{:S(2)}, u32[]{:S(2)}) collective-permute-start(bf16[16,2048]{1,0:T(8,128)(2,1)S(1)} %depth.1.a), channel_id=1, source_target_pairs={{0,64},{64,0},{128,192},{192,128},{1,65},{65,1},{129,193},{193,129... | collective-permute-start | bytes 196616 | tf_op jit(solution)/shard_map/ppermute | solution.py:386
  86.2 2.7 %collective-permute-done.15.b = bf16[16,2048]{1,0:T(8,128)(2,1)S(1)} collective-permute-done((bf16[16,2048]{1,0:T(8,128)(2,1)S(1)}, bf16[16,2048]{1,0:T(8,128)(2,1)S(1)}, u32[]{:S(2)}, u32[]{:S(2)}) %collective-permute-start.15) | collective-permute-done | bytes 65568 | tf_op jit(solution)/shard_map/ppermute | solution.py:386
  88.9 3.1 %collective-permute-start.16 = (bf16[16,2048]{1,0:T(8,128)(2,1)S(1)}, bf16[16,2048]{1,0:T(8,128)(2,1)S(1)}, u32[]{:S(2)}, u32[]{:S(2)}) collective-permute-start(bf16[16,2048]{1,0:T(8,128)(2,1)S(1)} %couple.1.a), channel_id=1, source_target_pairs={{0,192},{64,128},{128,64},{192,0},{1,193},{65,129},{129,65},{193,1... | collective-permute-start | bytes 196616 | tf_op jit(solution)/shard_map/ppermute | solution.py:386
  92.0 2.0 %place.1 = (bf16[512,1024]{1,0:T(8,128)(2,1)}, bf16[512,1024]{1,0:T(8,128)(2,1)}) custom-call(bf16[2,448,1024]{2,1,0:T(8,128)(2,1)S(1)} %get-tuple-element.47.mid, bf16[2,64,1024]{2,1,0:T(8,128)(2,1)S(1)} %collective-permute-done.6.up, bf16[2,112,1024]{2,1,0:T(8,128)(2,1)S(1)} %collective-permute-done.7.left, ...), custom_call_target="tpu_custom_call" | custom-call | flops 268435456 | bytes 5242880 | tf_op jit(solution)/shard_map/place/pallas_call | solution.py:43
  94.5 0.7 level.1
  (25 shorter events, 1.6 us)
Async XLA Ops:
  1.5 8.0 %collective-permute-start.2 = (s32[80,16]{1,0:T(8,128)S(1)}, s32[80,16]{1,0:T(8,128)S(1)}, u32[]{:S(2)}, u32[]{:S(2)}) collective-permute-start(s32[80,16]{1,0:T(8,128)S(1)} %copy.19.own), channel_id=1, source_target_pairs={{0,17},{1,18},{2,19},{3,20},{4,21},{5,22},{6,23},{7,24},{8,25},{9,... | collective-permute-start | bytes 15368 | tf_op jit(solution)/shard_map/ppermute | solution.py:378
  2.5 9.8 %collective-permute-start.1 = (s32[80,16]{1,0:T(8,128)S(1)}, s32[80,16]{1,0:T(8,128)S(1)}, u32[]{:S(2)}, u32[]{:S(2)}) collective-permute-start(s32[80,16]{1,0:T(8,128)S(1)} %copy.19.own), channel_id=1, source_target_pairs={{0,1},{1,2},{2,3},{3,4},{4,5},{5,6},{6,7},{7,8},{8,9},{9,10},{10,1... | collective-permute-start | bytes 15368 | tf_op jit(solution)/shard_map/ppermute | solution.py:378
  4.4 7.9 %collective-permute-start = (s32[80,16]{1,0:T(8,128)S(1)}, s32[80,16]{1,0:T(8,128)S(1)}, u32[]{:S(2)}, u32[]{:S(2)}) collective-permute-start(s32[80,16]{1,0:T(8,128)S(1)} %copy.19.own), channel_id=1, source_target_pairs={{0,16},{1,17},{2,18},{3,19},{4,20},{5,21},{6,22},{7,23},{8,24},{9,... | collective-permute-start | bytes 15368 | tf_op jit(solution)/shard_map/ppermute | solution.py:378
  7.3 10.9 %collective-permute-start.5 = (bf16[16,1024]{1,0:T(8,128)(2,1)S(1)}, bf16[16,1024]{1,0:T(8,128)(2,1)S(1)}, u32[]{:S(2)}, u32[]{:S(2)}) collective-permute-start(bf16[16,1024]{1,0:T(8,128)(2,1)S(1)} %get-tuple-element.41), channel_id=1, source_target_pairs={{0,17},{1,18},{2,19},{3,20},{4,21},{5,22},{6,23},{7,24},{8,25},{9,... | collective-permute-start | bytes 98312 | tf_op jit(solution)/shard_map/ppermute | solution.py:378
  9.4 8.9 %collective-permute-start.3 = (bf16[64,1024]{1,0:T(8,128)(2,1)S(1)}, bf16[64,1024]{1,0:T(8,128)(2,1)S(1)}, u32[]{:S(2)}, u32[]{:S(2)}) collective-permute-start(bf16[64,1024]{1,0:T(8,128)(2,1)S(1)} %get-tuple-element.39), channel_id=1, source_target_pairs={{0,16},{1,17},{2,18},{3,19},{4,20},{5,21},{6,22},{7,23},{8,24},{9,... | collective-permute-start | bytes 393224 | tf_op jit(solution)/shard_map/ppermute | solution.py:378
  9.5 8.8 %collective-permute-start.4 = (bf16[112,1024]{1,0:T(8,128)(2,1)S(1)}, bf16[112,1024]{1,0:T(8,128)(2,1)S(1)}, u32[]{:S(2)}, u32[]{:S(2)}) collective-permute-start(bf16[112,1024]{1,0:T(8,128)(2,1)S(1)} %get-tuple-element.40), channel_id=1, source_target_pairs={{0,1},{1,2},{2,3},{3,4},{4,5},{5,6},{6,7},{7,8},{8,9},{9,10},{10,1... | collective-permute-start | bytes 688136 | tf_op jit(solution)/shard_map/ppermute | solution.py:378
  12.3 0.7 copy-start.1
  23.3 5.3 %collective-permute-start.9 = (bf16[2,256,1024]{2,1,0:T(8,128)(2,1)S(1)}, bf16[2,256,1024]{2,1,0:T(8,128)(2,1)S(1)}, u32[]{:S(2)}, u32[]{:S(2)}) collective-permute-start(bf16[2,256,1024]{2,1,0:T(8,128)(2,1)S(1)} %get-tuple-element.54), channel_id=1, source_target_pairs={{0,16},{16,0},{1,17},{17,1},{2,18},{18,2},{3,19},{19,3},{4,20},{20... | collective-permute-start | bytes 3145736 | tf_op jit(solution)/shard_map/ppermute | solution.py:386
  28.4 4.4 %collective-permute-start.12 = (bf16[2,256,1024]{2,1,0:T(8,128)(2,1)S(1)}, bf16[2,256,1024]{2,1,0:T(8,128)(2,1)S(1)}, u32[]{:S(2)}, u32[]{:S(2)}) collective-permute-start(bf16[2,256,1024]{2,1,0:T(8,128)(2,1)S(1)} %get-tuple-element.61), channel_id=1, source_target_pairs={{0,16},{16,0},{1,17},{17,1},{2,18},{18,2},{3,19},{19,3},{4,20},{20... | collective-permute-start | bytes 3145736 | tf_op jit(solution)/shard_map/ppermute | solution.py:386
  29.3 16.2 %collective-permute-start.10 = (bf16[2,8,16,1024]{3,2,1,0:T(8,128)(2,1)S(1)}, bf16[2,8,16,1024]{3,2,1,0:T(8,128)(2,1)S(1)}, u32[]{:S(2)}, u32[]{:S(2)}) collective-permute-start(bf16[2,8,16,1024]{3,2,1,0:T(8,128)(2,1)S(1)} %get-tuple-element.56), channel_id=1, source_target_pairs={{0,1},{1,0},{2,3},{3,2},{4,5},{5,4},{6,7},{7,6},{8,9},{9,8},{10,11... | collective-permute-start | bytes 1572872 | tf_op jit(solution)/shard_map/ppermute | solution.py:378
  33.6 15.2 %collective-permute-start.13 = (bf16[2,8,16,1024]{3,2,1,0:T(8,128)(2,1)S(1)}, bf16[2,8,16,1024]{3,2,1,0:T(8,128)(2,1)S(1)}, u32[]{:S(2)}, u32[]{:S(2)}) collective-permute-start(bf16[2,8,16,1024]{3,2,1,0:T(8,128)(2,1)S(1)} %get-tuple-element.63), channel_id=1, source_target_pairs={{0,33},{1,32},{2,35},{3,34},{4,37},{5,36},{6,39},{7,38},{8,41},{9,... | collective-permute-start | bytes 1572872 | tf_op jit(solution)/shard_map/ppermute | solution.py:378
  41.1 17.0 %copy-start = (bf16[2,112,1024]{2,1,0:T(8,128)(2,1)}, bf16[2,112,1024]{2,1,0:T(8,128)(2,1)S(1)}, u32[]{:S(2)}) copy-start(bf16[2,112,1024]{2,1,0:T(8,128)(2,1)S(1)} %get-tuple-element.49) | copy-start | bytes 1376260
  41.1 7.7 %collective-permute-start.8 = (bf16[2,16,1024]{2,1,0:T(8,128)(2,1)S(1)}, bf16[2,16,1024]{2,1,0:T(8,128)(2,1)S(1)}, u32[]{:S(2)}, u32[]{:S(2)}) collective-permute-start(bf16[2,16,1024]{2,1,0:T(8,128)(2,1)S(1)} %get-tuple-element.50), channel_id=1, source_target_pairs={{0,63},{1,48},{2,49},{3,50},{4,51},{5,52},{6,53},{7,54},{8,55},{9,... | collective-permute-start | bytes 196616 | tf_op jit(solution)/shard_map/ppermute | solution.py:378
  46.2 8.6 %collective-permute-start.11 = (bf16[8,16,1024]{2,1,0:T(8,128)(2,1)S(1)}, bf16[8,16,1024]{2,1,0:T(8,128)(2,1)S(1)}, u32[]{:S(2)}, u32[]{:S(2)}) collective-permute-start(bf16[8,16,1024]{2,1,0:T(8,128)(2,1)S(1)} %get-tuple-element.59), channel_id=1, source_target_pairs={{0,33},{1,32},{2,35},{3,34},{4,37},{5,36},{6,39},{7,38},{8,41},{9,... | collective-permute-start | bytes 786440 | tf_op jit(solution)/shard_map/ppermute | solution.py:378
  49.5 8.6 %collective-permute-start.14 = (bf16[8,16,1024]{2,1,0:T(8,128)(2,1)S(1)}, bf16[8,16,1024]{2,1,0:T(8,128)(2,1)S(1)}, u32[]{:S(2)}, u32[]{:S(2)}) collective-permute-start(bf16[8,16,1024]{2,1,0:T(8,128)(2,1)S(1)} %get-tuple-element.65), channel_id=1, source_target_pairs={{0,1},{1,0},{2,3},{3,2},{4,5},{5,4},{6,7},{7,6},{8,9},{9,8},{10,11... | collective-permute-start | bytes 786440 | tf_op jit(solution)/shard_map/ppermute | solution.py:378
  59.0 25.5 %all-to-all-start = ((bf16[8,16,2048]{2,1,0:T(8,128)(2,1)}), bf16[8,16,2048]{2,1,0:T(8,128)(2,1)S(1)}, u32[]{:S(2)}, u32[]{:S(2)}) async-start(bf16[8,16,2048]{2,1,0:T(8,128)(2,1)} %join.1), calls=%async_computation | async-start | bytes 1048576 | tf_op jit(solution)/shard_map/all_to_all | solution.py:530
  67.0 25.0 %collective-permute-start.7 = (bf16[2,112,1024]{2,1,0:T(8,128)(2,1)}, bf16[2,112,1024]{2,1,0:T(8,128)(2,1)S(1)}, u32[]{:S(2)}, u32[]{:S(2)}) collective-permute-start(bf16[2,112,1024]{2,1,0:T(8,128)(2,1)} %copy-done), channel_id=1, source_target_pairs={{0,15},{1,0},{2,1},{3,2},{4,3},{5,4},{6,5},{7,6},{8,7},{9,8},{10,9... | collective-permute-start | bytes 1376264 | tf_op jit(solution)/shard_map/ppermute | solution.py:378
  67.0 25.0 %collective-permute-start.6 = (bf16[2,64,1024]{2,1,0:T(8,128)(2,1)S(1)}, bf16[2,64,1024]{2,1,0:T(8,128)(2,1)S(1)}, u32[]{:S(2)}, u32[]{:S(2)}) collective-permute-start(bf16[2,64,1024]{2,1,0:T(8,128)(2,1)S(1)} %get-tuple-element.48), channel_id=1, source_target_pairs={{0,48},{1,49},{2,50},{3,51},{4,52},{5,53},{6,54},{7,55},{8,56},{9,... | collective-permute-start | bytes 786440 | tf_op jit(solution)/shard_map/ppermute | solution.py:378
  84.5 4.4 %collective-permute-start.15 = (bf16[16,2048]{1,0:T(8,128)(2,1)S(1)}, bf16[16,2048]{1,0:T(8,128)(2,1)S(1)}, u32[]{:S(2)}, u32[]{:S(2)}) collective-permute-start(bf16[16,2048]{1,0:T(8,128)(2,1)S(1)} %depth.1.a), channel_id=1, source_target_pairs={{0,64},{64,0},{128,192},{192,128},{1,65},{65,1},{129,193},{193,129... | collective-permute-start | bytes 196616 | tf_op jit(solution)/shard_map/ppermute | solution.py:386
  88.9 5.6 %collective-permute-start.16 = (bf16[16,2048]{1,0:T(8,128)(2,1)S(1)}, bf16[16,2048]{1,0:T(8,128)(2,1)S(1)}, u32[]{:S(2)}, u32[]{:S(2)}) collective-permute-start(bf16[16,2048]{1,0:T(8,128)(2,1)S(1)} %couple.1.a), channel_id=1, source_target_pairs={{0,192},{64,128},{128,64},{192,0},{1,193},{65,129},{129,65},{193,1... | collective-permute-start | bytes 196616 | tf_op jit(solution)/shard_map/ppermute | solution.py:386

commit v7 on v6

--- a/solution.py
+++ b/solution.py
@@ -347,26 +347,59 @@
         out[...] = (a[v] + b[v].astype(F32)).astype(out.dtype)
 
 
-def join_kernel(*refs):
-    out = refs[-1]
-    for c in range(CHUNKS):
-        out[:, :, c * W : (c + 1) * W] = (refs[2 * c][...] + refs[2 * c + 1][...].astype(F32)).astype(BF16)
+def parity_cut(place, a, b, keep, send):
+    g = place[4] ^ place[5]
+    for u in range(2):
+        for out, v in ((keep, u ^ g), (send, u ^ g ^ 1)):
+            cut = pl.ds(pl.multiple_of((2 * u + v) * Q, Q), Q)
+            out[:, :, u * Q : (u + 1) * Q] = (a[:, :, cut] + b[:, :, cut].astype(F32)).astype(out.dtype)
+
+
+def high_cut(place, a, b, keep, send):
+    for out, u in ((keep, place[4]), (send, place[4] ^ 1)):
+        cut = pl.ds(pl.multiple_of(u * 2 * Q, Q), 2 * Q)
+        out[...] = (a[:, :, cut] + b[:, :, cut].astype(F32)).astype(out.dtype)
+
+
+def join_kernel(a, b, c, d, out):
+    out[:, :, 0 : 2 * Q] = (a[...] + b[...].astype(F32)).astype(BF16)
+    out[:, :, 2 * Q :] = (c[...] + d[...].astype(F32)).astype(BF16)
 
 
 def depth_kernel(ref, out):
     out[...] = sum(ref[i].astype(F32) for i in range(8)).astype(BF16)
 
 
-def couple_kernel(a, b, out):
-    out[...] = (a[...].astype(F32) + b[...].astype(F32)).astype(BF16)
-
-
-def level_kernel(factor, a, b, qkv, outw):
-    total = (a[...].astype(F32) + b[...].astype(F32)) * factor
-    for c in range(CHUNKS):
-        for i in range(3):
-            qkv[:, i * HW + c * CW : i * HW + (c + 1) * CW] = total[:, c * W + i * Q : c * W + (i + 1) * Q]
-        outw[:, c * CW : (c + 1) * CW] = total[:, c * W + 3 * Q : (c + 1) * W]
+def level_kernel(factor, place, r0, r1, r2, r3, qkv, outw):
+    yh, yl = place[4], place[5]
+
+    def add(a, b, at):
+        return (a[:, at : at + Q].astype(F32) + b[:, at : at + Q].astype(F32)) * factor
+
+    for a, b, g in ((r0, r3, yh ^ yl), (r1, r2, yh ^ yl ^ 1)):
+        qkv[:, pl.ds(pl.multiple_of(g * HW, HW), CW)] = add(a, b, 0)
+        second = add(a, b, Q)
+
+        @pl.when(g == 1)
+        def _():
+            qkv[:, 2 * HW : 2 * HW + CW] = second
+
+        @pl.when(g == 0)
+        def _():
+            outw[:, 0:CW] = second
+
+    for a, b, high in ((r0, r1, yh), (r2, r3, yh ^ 1)):
+        first, second = add(a, b, 2 * Q), add(a, b, 3 * Q)
+
+        @pl.when(high == 0)
+        def _():
+            qkv[:, CW : 2 * CW] = first
+            qkv[:, HW + CW : HW + 2 * CW] = second
+
+        @pl.when(high == 1)
+        def _():
+            qkv[:, 2 * HW + CW : 2 * HW + 2 * CW] = first
+            outw[:, CW : 2 * CW] = second
 
 
 def permute(x, where):
@@ -419,15 +452,22 @@
     kernel = high_pair if c % 2 else parity_pair
     recv = swap_x(send, order(c)[0])
     specs = [smem(), vmem(), vmem(), anywhere()]
-    keep, send = halve("sum_pair", kernel, (8, 16, W), (place, keep, recv, tick), specs)
-    return [keep, swap_x(send, order(c)[1])]
+    return halve("sum_pair", kernel, (8, 16, W), (place, keep, recv, tick), specs)
+
+
+def sum_cut(place, keep, send, c):
+    recv = swap_x(send, order(c)[1])
+    kernel, flip = (high_cut, 3) if c % 2 else (parity_cut, 1)
+    keep, send = halve("sum_cut", kernel, (8, 16, 2 * Q), (place, keep, recv), [smem(), vmem(), vmem()])
+    return [keep, swap(send, "batch", flip)]
 
 
 def shards(
     bottom_codes, mask_flags, top_codes, bottom_table, top_table, mask_vector, qkv_weight, out_weight, cotangent
 ):
     core, xh, xl = lax.axis_index("core"), lax.axis_index("xh"), lax.axis_index("xl")
-    place = jnp.stack([2 * xh + core, core, xh, xl]).astype(jnp.int32)
+    y = lax.axis_index("batch")
+    place = jnp.stack([2 * xh + core, core, xh, xl, y >> 1, y & 1]).astype(jnp.int32)
     own = jnp.concatenate(
         [bottom_codes[0], mask_flags[0], jnp.pad(top_codes[0], ((0, 0), (0, 8)))], axis=0
     )
@@ -505,7 +545,8 @@
     up, left, diag = shift(up, -1, 0), shift(left, 0, -1), shift(diag, -1, -1)
     summed = []
     for c, (keep, send) in enumerate(cores):
-        summed += sum_pair(place, keep, send, diag if c else tick, c)
+        keep, send = sum_pair(place, keep, send, diag if c else tick, c)
+        summed += sum_cut(place, keep, send, c)
     out, gin = call(
         place_kernel,
         [sds((TOKENS, MODEL))] * 2,
@@ -519,9 +560,9 @@
     factor = 1.0 / math.sqrt(TOKENS * NB * NLAT * NLON)
     joined = call(
         join_kernel,
-        sds((8, 16, CHUNKS * W)),
+        sds((8, 16, 4 * Q)),
         summed,
-        [vmem()] * 2 * CHUNKS,
+        [vmem()] * 4,
         2**19,
         2**21,
         limit=16,
@@ -529,14 +570,12 @@
     )
     depth = lax.all_to_all(joined, "z", 0, 0, tiled=True)
     small = dict(flops=2**17, nbytes=2**19, limit=16)
-    wide = (16, CHUNKS * W)
-    total = call(depth_kernel, sds(wide), (depth,), [vmem()], name="depth", **small)
-    total = call(couple_kernel, sds(wide), (total, swap(total, "batch", 1)), [vmem()] * 2, name="couple", **small)
+    total = call(depth_kernel, sds((16, 4 * Q)), (depth,), [vmem()], name="depth", **small)
     g_qkv, g_out = call(
         functools.partial(level_kernel, factor),
         [sds((16, 3 * HW), F32), sds((16, HW), F32)],
-        (total, swap(total, "batch", 3)),
-        [vmem()] * 2,
+        (place, total, *[swap(total, "batch", d) for d in (1, 2, 3)]),
+        [smem()] + [vmem()] * 4,
         name="level",
         **small,
     )

time: 95.5 us -> 96.2 us (level); the launches traced: 95.1 us -> 94.5 us
  waiting for transfers between devices: 30.4 us -> 22.8 us
  starting transfers between devices: 34.5 us -> 39.3 us
  Pallas kernels: 27.8 us -> 29.2 us
    all_to_all x1, waiting for transfers between devices: 17.4 us -> 10.8 us  [shards(): depth = lax.all_to_all(joined, 'z', 0, 0, tiled=True)]
    ppermute x4 -> x7, starting transfers between devices: 5.64 us -> 9.81 us  [swap(): lax.ppermute(x, axis, [(i, i ^ flip) for i in range(lax.axis_size(axis))])]
    ppermute x13, waiting for transfers between devices: 9.82 us -> 6.52 us  [permute(): return lax.ppermute(x, GRID, pairs)]
    ppermute x4 -> x7, waiting for transfers between devices: 3.18 us -> 5.48 us  [swap(): lax.ppermute(x, axis, [(i, i ^ flip) for i in range(lax.axis_size(axis))])]
    pallas_call x14 -> x15, Pallas kernels: 27.8 us -> 29.2 us  [call(): pl.pallas_call(kernel, out_shape=outs, in_specs=specs, out_specs=jax.tree...]
  transfers between devices with their start and end apart: 18 -> 21, of which waited for: 6 -> 6; matrix products, arithmetic and copies ran while one was open for 0% -> 0% of each run, Pallas kernels for 22% -> 24%
where the time goes in v7:
time: 96.2 us; the launch traced here: 94.5 us
  starting transfers between devices  39.3 us (41%)
  Pallas kernels  29.2 us (30%)
  waiting for transfers between devices  22.8 us (24%)
  local copies, waits for them, and re-layouts  1.55 us (2%)
    pallas_call x15, Pallas kernels, call(): pl.pallas_call(kernel, out_shape=outs, in_specs=specs, out_specs=jax.tree...  29.2 us
    ppermute x13, starting transfers between devices, permute(): return lax.ppermute(x, GRID, pairs)  21.1 us
    all_to_all x1, waiting for transfers between devices, shards(): depth = lax.all_to_all(joined, 'z', 0, 0, tiled=True)  10.8 us
    ppermute x7, starting transfers between devices, swap(): lax.ppermute(x, axis, [(i, i ^ flip) for i in range(lax.axis_size(axis))])  9.81 us
    all_to_all x1, starting transfers between devices, shards(): depth = lax.all_to_all(joined, 'z', 0, 0, tiled=True)  8.4 us
    ppermute x13, waiting for transfers between devices, permute(): return lax.ppermute(x, GRID, pairs)  6.52 us
    ppermute x7, waiting for transfers between devices, swap(): lax.ppermute(x, axis, [(i, i ^ flip) for i in range(lax.axis_size(axis))])  5.48 us
  transfers between devices with their start and end apart: 21, of which 6 were waited for; matrix products, arithmetic and copies ran while one was open for 0% of the time, Pallas kernels for 24%

profile of v7, /device:TPU:32, one launch (start us, length us, event | category | flops | bytes accessed | tf_op | source)
XLA Modules:
  0.0 94.5 jit_solution(15962137294585565283)
XLA Ops:
  0.6 0.8 pad_add_fusion
  1.5 1.0 %collective-permute-start.2 = (s32[80,16]{1,0:T(8,128)S(1)}, s32[80,16]{1,0:T(8,128)S(1)}, u32[]{:S(2)}, u32[]{:S(2)}) collective-permute-start(s32[80,16]{1,0:T(8,128)S(1)} %copy.19.own), channel_id=1, source_target_pairs={{0,17},{1,18},{2,19},{3,20},{4,21},{5,22},{6,23},{7,24},{8,25},{9,... | collective-permute-start | bytes 15368 | tf_op jit(solution)/shard_map/ppermute | solution.py:411
  2.5 1.9 %collective-permute-start.1 = (s32[80,16]{1,0:T(8,128)S(1)}, s32[80,16]{1,0:T(8,128)S(1)}, u32[]{:S(2)}, u32[]{:S(2)}) collective-permute-start(s32[80,16]{1,0:T(8,128)S(1)} %copy.19.own), channel_id=1, source_target_pairs={{0,1},{1,2},{2,3},{3,4},{4,5},{5,6},{6,7},{7,8},{8,9},{9,10},{10,1... | collective-permute-start | bytes 15368 | tf_op jit(solution)/shard_map/ppermute | solution.py:411
  4.4 1.4 %collective-permute-start = (s32[80,16]{1,0:T(8,128)S(1)}, s32[80,16]{1,0:T(8,128)S(1)}, u32[]{:S(2)}, u32[]{:S(2)}) collective-permute-start(s32[80,16]{1,0:T(8,128)S(1)} %copy.19.own), channel_id=1, source_target_pairs={{0,16},{1,17},{2,18},{3,19},{4,20},{5,21},{6,22},{7,23},{8,24},{9,... | collective-permute-start | bytes 15368 | tf_op jit(solution)/shard_map/ppermute | solution.py:411
  5.8 1.6 %slices.1 = (bf16[64,1024]{1,0:T(8,128)(2,1)S(1)}, bf16[112,1024]{1,0:T(8,128)(2,1)S(1)}, bf16[16,1024]{1,0:T(8,128)(2,1)S(1)}) custom-call(bf16[512,1024]{1,0:T(8,128)(2,1)} %bitcast.20), custom_call_target="tpu_custom_call" | custom-call | flops 268435456 | bytes 2097152 | tf_op jit(solution)/shard_map/slices/pallas_call | solution.py:43
  7.3 2.1 %collective-permute-start.5 = (bf16[16,1024]{1,0:T(8,128)(2,1)S(1)}, bf16[16,1024]{1,0:T(8,128)(2,1)S(1)}, u32[]{:S(2)}, u32[]{:S(2)}) collective-permute-start(bf16[16,1024]{1,0:T(8,128)(2,1)S(1)} %get-tuple-element.45), channel_id=1, source_target_pairs={{0,17},{1,18},{2,19},{3,20},{4,21},{5,22},{6,23},{7,24},{8,25},{9,... | collective-permute-start | bytes 98312 | tf_op jit(solution)/shard_map/ppermute | solution.py:411
  9.5 2.8 %collective-permute-start.4 = (bf16[112,1024]{1,0:T(8,128)(2,1)S(1)}, bf16[112,1024]{1,0:T(8,128)(2,1)S(1)}, u32[]{:S(2)}, u32[]{:S(2)}) collective-permute-start(bf16[112,1024]{1,0:T(8,128)(2,1)S(1)} %get-tuple-element.44), channel_id=1, source_target_pairs={{0,1},{1,2},{2,3},{3,4},{4,5},{5,6},{6,7},{7,8},{8,9},{9,10},{10,1... | collective-permute-start | bytes 688136 | tf_op jit(solution)/shard_map/ppermute | solution.py:411
  13.0 5.3 %embed.1 = (bf16[512,1024]{1,0:T(8,128)(2,1)S(1)}, bf16[512,1024]{1,0:T(8,128)(2,1)S(1)}, bf16[512,1536]{1,0:T(8,128)(2,1)S(1)}) custom-call(s32[80,16]{1,0:T(8,128)S(1)} %copy.19.own, s32[80,16]{1,0:T(8,128)S(1)} %collective-permute-done.up, s32[80,16]{1,0:T(8,128)S(1)} %collective-permute-done.1.left, s32[80,16]{1,0:T(8,128)S(1)} %collective-permute-done.2.diag, ...), custom_call_target="tpu_custom_call" | custom-call | flops 2684354560 | bytes 9437184 | tf_op jit(solution)/shard_map/embed/pallas_call | solution.py:43
  18.3 5.0 %attend.2 = (bf16[512,256]{1,0:T(8,128)(2,1)S(1)}, bf16[512,768]{1,0:T(8,128)(2,1)S(1)}, f32[2,256,1024]{2,1,0:T(8,128)S(1)}, bf16[2,256,1024]{2,1,0:T(8,128)(2,1)S(1)}, bf16[512,1024]{1,0:T(8,128)(2,1)S(1)}) custom-call(s32[6]{0:T(128)S(1)} %stack.27.place, bf16[512,1536]{1,0:T(8,128)(2,1)S(1)} %get-tuple-element.41.proj, ...), custom_call_target="tpu_custom_call" | custom-call | flops 1048576 | bytes 4096 | tf_op jit(solution)/shard_map/attend/pallas_call | solution.py:43
  24.0 4.4 %attend.3 = (bf16[512,256]{1,0:T(8,128)(2,1)S(1)}, bf16[512,768]{1,0:T(8,128)(2,1)S(1)}, f32[2,256,1024]{2,1,0:T(8,128)S(1)}, bf16[2,256,1024]{2,1,0:T(8,128)(2,1)S(1)}) custom-call(s32[6]{0:T(128)S(1)} %stack.27.place, bf16[512,1536]{1,0:T(8,128)(2,1)S(1)} %get-tuple-element.41.proj, bf16[512,1024]{1,0:T(8,128)(2,1)S(1)} %get-tuple-element.42.normed, ...), custom_call_target="tpu_custom_call" | custom-call | flops 1048576 | bytes 4096 | tf_op jit(solution)/shard_map/attend/pallas_call | solution.py:43
  28.5 0.7 sum_core.2
  29.3 3.5 %collective-permute-start.10 = (bf16[2,8,16,1024]{3,2,1,0:T(8,128)(2,1)S(1)}, bf16[2,8,16,1024]{3,2,1,0:T(8,128)(2,1)S(1)}, u32[]{:S(2)}, u32[]{:S(2)}) collective-permute-start(bf16[2,8,16,1024]{3,2,1,0:T(8,128)(2,1)S(1)} %get-tuple-element.60), channel_id=1, source_target_pairs={{0,1},{1,0},{2,3},{3,2},{4,5},{5,4},{6,7},{7,6},{8,9},{9,8},{10,11... | collective-permute-start | bytes 1572872 | tf_op jit(solution)/shard_map/ppermute | solution.py:411
  32.8 0.7 sum_core.3
  33.5 2.2 %collective-permute-start.14 = (bf16[2,8,16,1024]{3,2,1,0:T(8,128)(2,1)S(1)}, bf16[2,8,16,1024]{3,2,1,0:T(8,128)(2,1)S(1)}, u32[]{:S(2)}, u32[]{:S(2)}) collective-permute-start(bf16[2,8,16,1024]{3,2,1,0:T(8,128)(2,1)S(1)} %get-tuple-element.69), channel_id=1, source_target_pairs={{0,33},{1,32},{2,35},{3,34},{4,37},{5,36},{6,39},{7,38},{8,41},{9,... | collective-permute-start | bytes 1572872 | tf_op jit(solution)/shard_map/ppermute | solution.py:411
  35.8 5.2 %finish.1 = (bf16[2,448,1024]{2,1,0:T(8,128)(2,1)S(1)}, bf16[2,64,1024]{2,1,0:T(8,128)(2,1)S(1)}, bf16[2,112,1024]{2,1,0:T(8,128)(2,1)S(1)}, bf16[2,16,1024]{2,1,0:T(8,128)(2,1)S(1)}, f32[8,128]{1,0:T(8,128)S(1)}) custom-call(bf16[512,1024]{1,0:T(8,128)(2,1)S(1)} %get-tuple-element.40.emb, bf16[512,1024]{1,0:T(8,128)(2,1)S(1)} %get-tuple-element.46.cot, ...), custom_call_target="tpu_custom_call" | custom-call | flops 1048576 | bytes 4096 | tf_op jit(solution)/shard_map/finish/pallas_call | solution.py:43
  41.7 1.3 %collective-permute-start.8 = (bf16[2,16,1024]{2,1,0:T(8,128)(2,1)S(1)}, bf16[2,16,1024]{2,1,0:T(8,128)(2,1)S(1)}, u32[]{:S(2)}, u32[]{:S(2)}) collective-permute-start(bf16[2,16,1024]{2,1,0:T(8,128)(2,1)S(1)} %get-tuple-element.54), channel_id=1, source_target_pairs={{0,63},{1,48},{2,49},{3,50},{4,51},{5,52},{6,53},{7,54},{8,55},{9,... | collective-permute-start | bytes 196616 | tf_op jit(solution)/shard_map/ppermute | solution.py:411
  43.0 2.1 %collective-permute-done.10.b = bf16[2,8,16,1024]{3,2,1,0:T(8,128)(2,1)S(1)} collective-permute-done((bf16[2,8,16,1024]{3,2,1,0:T(8,128)(2,1)S(1)}, bf16[2,8,16,1024]{3,2,1,0:T(8,128)(2,1)S(1)}, u32[]{:S(2)}, u32[]{:S(2)}) %collective-permute-start.10) | collective-permute-done | bytes 524320 | tf_op jit(solution)/shard_map/ppermute | solution.py:411
  45.7 3.0 %collective-permute-start.11 = (bf16[8,16,1024]{2,1,0:T(8,128)(2,1)S(1)}, bf16[8,16,1024]{2,1,0:T(8,128)(2,1)S(1)}, u32[]{:S(2)}, u32[]{:S(2)}) collective-permute-start(bf16[8,16,1024]{2,1,0:T(8,128)(2,1)S(1)} %get-tuple-element.63), channel_id=1, source_target_pairs={{0,33},{1,32},{2,35},{3,34},{4,37},{5,36},{6,39},{7,38},{8,41},{9,... | collective-permute-start | bytes 786440 | tf_op jit(solution)/shard_map/ppermute | solution.py:411
  49.4 1.9 %collective-permute-start.15 = (bf16[8,16,1024]{2,1,0:T(8,128)(2,1)S(1)}, bf16[8,16,1024]{2,1,0:T(8,128)(2,1)S(1)}, u32[]{:S(2)}, u32[]{:S(2)}) collective-permute-start(bf16[8,16,1024]{2,1,0:T(8,128)(2,1)S(1)} %get-tuple-element.71), channel_id=1, source_target_pairs={{0,1},{1,0},{2,3},{3,2},{4,5},{5,4},{6,7},{7,6},{8,9},{9,8},{10,11... | collective-permute-start | bytes 786440 | tf_op jit(solution)/shard_map/ppermute | solution.py:411
  51.3 3.4 %collective-permute-done.11.b = bf16[8,16,1024]{2,1,0:T(8,128)(2,1)S(1)} collective-permute-done((bf16[8,16,1024]{2,1,0:T(8,128)(2,1)S(1)}, bf16[8,16,1024]{2,1,0:T(8,128)(2,1)S(1)}, u32[]{:S(2)}, u32[]{:S(2)}) %collective-permute-start.11) | collective-permute-done | bytes 262176 | tf_op jit(solution)/shard_map/ppermute | solution.py:411
  55.3 1.7 %collective-permute-start.12 = (bf16[8,16,512]{2,1,0:T(8,128)(2,1)S(1)}, bf16[8,16,512]{2,1,0:T(8,128)(2,1)S(1)}, u32[]{:S(2)}, u32[]{:S(2)}) collective-permute-start(bf16[8,16,512]{2,1,0:T(8,128)(2,1)S(1)} %get-tuple-element.65), channel_id=1, source_target_pairs={{0,64},{64,0},{128,192},{192,128},{1,65},{65,1},{129,193},{193,129... | collective-permute-start | bytes 393224 | tf_op jit(solution)/shard_map/ppermute | solution.py:419
  57.0 1.0 %collective-permute-done.15.b = bf16[8,16,1024]{2,1,0:T(8,128)(2,1)S(1)} collective-permute-done((bf16[8,16,1024]{2,1,0:T(8,128)(2,1)S(1)}, bf16[8,16,1024]{2,1,0:T(8,128)(2,1)S(1)}, u32[]{:S(2)}, u32[]{:S(2)}) %collective-permute-start.15) | collective-permute-done | bytes 262176 | tf_op jit(solution)/shard_map/ppermute | solution.py:411
  58.5 3.1 %collective-permute-start.16 = (bf16[8,16,512]{2,1,0:T(8,128)(2,1)S(1)}, bf16[8,16,512]{2,1,0:T(8,128)(2,1)S(1)}, u32[]{:S(2)}, u32[]{:S(2)}) collective-permute-start(bf16[8,16,512]{2,1,0:T(8,128)(2,1)S(1)} %get-tuple-element.73), channel_id=1, source_target_pairs={{0,192},{64,128},{128,64},{192,0},{1,193},{65,129},{129,65},{193,1... | collective-permute-start | bytes 393224 | tf_op jit(solution)/shard_map/ppermute | solution.py:419
  61.6 3.2 %collective-permute-done.16.d = bf16[8,16,512]{2,1,0:T(8,128)(2,1)S(1)} collective-permute-done((bf16[8,16,512]{2,1,0:T(8,128)(2,1)S(1)}, bf16[8,16,512]{2,1,0:T(8,128)(2,1)S(1)}, u32[]{:S(2)}, u32[]{:S(2)}) %collective-permute-start.16) | collective-permute-done | bytes 131104 | tf_op jit(solution)/shard_map/ppermute | solution.py:419
  64.8 0.7 join.1
  65.6 8.4 %all-to-all-start = ((bf16[8,16,1024]{2,1,0:T(8,128)(2,1)}), bf16[8,16,1024]{2,1,0:T(8,128)(2,1)S(1)}, u32[]{:S(2)}, u32[]{:S(2)}) async-start(bf16[8,16,1024]{2,1,0:T(8,128)(2,1)} %join.1), calls=%async_computation | async-start | bytes 524288 | tf_op jit(solution)/shard_map/all_to_all | solution.py:571
  74.0 10.8 %all-to-all-done.ref = bf16[8,16,1024]{2,1,0:T(8,128)(2,1)S(1)} async-done(((bf16[8,16,1024]{2,1,0:T(8,128)(2,1)}), bf16[8,16,1024]{2,1,0:T(8,128)(2,1)S(1)}, u32[]{:S(2)}, u32[]{:S(2)}) %all-to-all-start) | async-done | bytes 262176 | tf_op jit(solution)/shard_map/all_to_all | solution.py:571
  84.8 3.0 %collective-permute-start.19 = (bf16[16,1024]{1,0:T(8,128)(2,1)S(1)}, bf16[16,1024]{1,0:T(8,128)(2,1)S(1)}, u32[]{:S(2)}, u32[]{:S(2)}) collective-permute-start(bf16[16,1024]{1,0:T(8,128)(2,1)S(1)} %depth.1.r0), channel_id=1, source_target_pairs={{0,192},{64,128},{128,64},{192,0},{1,193},{65,129},{129,65},{193,1... | collective-permute-start | bytes 98312 | tf_op jit(solution)/shard_map/ppermute | solution.py:419
  87.8 1.1 %collective-permute-start.17 = (bf16[16,1024]{1,0:T(8,128)(2,1)S(1)}, bf16[16,1024]{1,0:T(8,128)(2,1)S(1)}, u32[]{:S(2)}, u32[]{:S(2)}) collective-permute-start(bf16[16,1024]{1,0:T(8,128)(2,1)S(1)} %depth.1.r0), channel_id=1, source_target_pairs={{0,64},{64,0},{128,192},{192,128},{1,65},{65,1},{129,193},{193,129... | collective-permute-start | bytes 98312 | tf_op jit(solution)/shard_map/ppermute | solution.py:419
  89.0 2.0 %place.1 = (bf16[512,1024]{1,0:T(8,128)(2,1)}, bf16[512,1024]{1,0:T(8,128)(2,1)}) custom-call(bf16[2,448,1024]{2,1,0:T(8,128)(2,1)S(1)} %get-tuple-element.51.mid, bf16[2,64,1024]{2,1,0:T(8,128)(2,1)S(1)} %collective-permute-done.6.up, bf16[2,112,1024]{2,1,0:T(8,128)(2,1)S(1)} %collective-permute-done.7.left, ...), custom_call_target="tpu_custom_call" | custom-call | flops 268435456 | bytes 5242880 | tf_op jit(solution)/shard_map/place/pallas_call | solution.py:43
  91.0 2.3 %collective-permute-done.18.r2 = bf16[16,1024]{1,0:T(8,128)(2,1)S(1)} collective-permute-done((bf16[16,1024]{1,0:T(8,128)(2,1)S(1)}, bf16[16,1024]{1,0:T(8,128)(2,1)S(1)}, u32[]{:S(2)}, u32[]{:S(2)}) %collective-permute-start.18) | collective-permute-done | bytes 32800 | tf_op jit(solution)/shard_map/ppermute | solution.py:419
  93.3 1.2 %level.1 = (f32[16,1536]{1,0:T(8,128)}, f32[16,512]{1,0:T(8,128)}) custom-call(s32[6]{0:T(128)S(1)} %stack.27.place, bf16[16,1024]{1,0:T(8,128)(2,1)S(1)} %depth.1.r0, bf16[16,1024]{1,0:T(8,128)(2,1)S(1)} %collective-permute-done.17.r1, bf16[16,1024]{1,0:T(8,128)(2,1)S(1)} %collective-permute-done.18.r2, bf16[16,1024]{1,0:T(8,128)(2,1)S(1)} %collective-permute-done.19.r3), custom_call_target="tpu_custom_call" | custom-call | flops 131072 | bytes 524288 | tf_op jit(solution)/shard_map/level/pallas_call | solution.py:43
  (32 shorter events, 5.0 us)
Async XLA Ops:
  1.5 8.0 %collective-permute-start.2 = (s32[80,16]{1,0:T(8,128)S(1)}, s32[80,16]{1,0:T(8,128)S(1)}, u32[]{:S(2)}, u32[]{:S(2)}) collective-permute-start(s32[80,16]{1,0:T(8,128)S(1)} %copy.19.own), channel_id=1, source_target_pairs={{0,17},{1,18},{2,19},{3,20},{4,21},{5,22},{6,23},{7,24},{8,25},{9,... | collective-permute-start | bytes 15368 | tf_op jit(solution)/shard_map/ppermute | solution.py:411
  2.5 9.8 %collective-permute-start.1 = (s32[80,16]{1,0:T(8,128)S(1)}, s32[80,16]{1,0:T(8,128)S(1)}, u32[]{:S(2)}, u32[]{:S(2)}) collective-permute-start(s32[80,16]{1,0:T(8,128)S(1)} %copy.19.own), channel_id=1, source_target_pairs={{0,1},{1,2},{2,3},{3,4},{4,5},{5,6},{6,7},{7,8},{8,9},{9,10},{10,1... | collective-permute-start | bytes 15368 | tf_op jit(solution)/shard_map/ppermute | solution.py:411
  4.4 7.9 %collective-permute-start = (s32[80,16]{1,0:T(8,128)S(1)}, s32[80,16]{1,0:T(8,128)S(1)}, u32[]{:S(2)}, u32[]{:S(2)}) collective-permute-start(s32[80,16]{1,0:T(8,128)S(1)} %copy.19.own), channel_id=1, source_target_pairs={{0,16},{1,17},{2,18},{3,19},{4,20},{5,21},{6,22},{7,23},{8,24},{9,... | collective-permute-start | bytes 15368 | tf_op jit(solution)/shard_map/ppermute | solution.py:411
  7.3 10.9 %collective-permute-start.5 = (bf16[16,1024]{1,0:T(8,128)(2,1)S(1)}, bf16[16,1024]{1,0:T(8,128)(2,1)S(1)}, u32[]{:S(2)}, u32[]{:S(2)}) collective-permute-start(bf16[16,1024]{1,0:T(8,128)(2,1)S(1)} %get-tuple-element.45), channel_id=1, source_target_pairs={{0,17},{1,18},{2,19},{3,20},{4,21},{5,22},{6,23},{7,24},{8,25},{9,... | collective-permute-start | bytes 98312 | tf_op jit(solution)/shard_map/ppermute | solution.py:411
  9.4 8.9 %collective-permute-start.3 = (bf16[64,1024]{1,0:T(8,128)(2,1)S(1)}, bf16[64,1024]{1,0:T(8,128)(2,1)S(1)}, u32[]{:S(2)}, u32[]{:S(2)}) collective-permute-start(bf16[64,1024]{1,0:T(8,128)(2,1)S(1)} %get-tuple-element.43), channel_id=1, source_target_pairs={{0,16},{1,17},{2,18},{3,19},{4,20},{5,21},{6,22},{7,23},{8,24},{9,... | collective-permute-start | bytes 393224 | tf_op jit(solution)/shard_map/ppermute | solution.py:411
  9.5 8.8 %collective-permute-start.4 = (bf16[112,1024]{1,0:T(8,128)(2,1)S(1)}, bf16[112,1024]{1,0:T(8,128)(2,1)S(1)}, u32[]{:S(2)}, u32[]{:S(2)}) collective-permute-start(bf16[112,1024]{1,0:T(8,128)(2,1)S(1)} %get-tuple-element.44), channel_id=1, source_target_pairs={{0,1},{1,2},{2,3},{3,4},{4,5},{5,6},{6,7},{7,8},{8,9},{9,10},{10,1... | collective-permute-start | bytes 688136 | tf_op jit(solution)/shard_map/ppermute | solution.py:411
  12.3 0.7 copy-start.1
  23.3 5.2 %collective-permute-start.9 = (bf16[2,256,1024]{2,1,0:T(8,128)(2,1)S(1)}, bf16[2,256,1024]{2,1,0:T(8,128)(2,1)S(1)}, u32[]{:S(2)}, u32[]{:S(2)}) collective-permute-start(bf16[2,256,1024]{2,1,0:T(8,128)(2,1)S(1)} %get-tuple-element.58), channel_id=1, source_target_pairs={{0,16},{16,0},{1,17},{17,1},{2,18},{18,2},{3,19},{19,3},{4,20},{20... | collective-permute-start | bytes 3145736 | tf_op jit(solution)/shard_map/ppermute | solution.py:419
  28.4 4.4 %collective-permute-start.13 = (bf16[2,256,1024]{2,1,0:T(8,128)(2,1)S(1)}, bf16[2,256,1024]{2,1,0:T(8,128)(2,1)S(1)}, u32[]{:S(2)}, u32[]{:S(2)}) collective-permute-start(bf16[2,256,1024]{2,1,0:T(8,128)(2,1)S(1)} %get-tuple-element.67), channel_id=1, source_target_pairs={{0,16},{16,0},{1,17},{17,1},{2,18},{18,2},{3,19},{19,3},{4,20},{20... | collective-permute-start | bytes 3145736 | tf_op jit(solution)/shard_map/ppermute | solution.py:419
  29.3 15.8 %collective-permute-start.10 = (bf16[2,8,16,1024]{3,2,1,0:T(8,128)(2,1)S(1)}, bf16[2,8,16,1024]{3,2,1,0:T(8,128)(2,1)S(1)}, u32[]{:S(2)}, u32[]{:S(2)}) collective-permute-start(bf16[2,8,16,1024]{3,2,1,0:T(8,128)(2,1)S(1)} %get-tuple-element.60), channel_id=1, source_target_pairs={{0,1},{1,0},{2,3},{3,2},{4,5},{5,4},{6,7},{7,6},{8,9},{9,8},{10,11... | collective-permute-start | bytes 1572872 | tf_op jit(solution)/shard_map/ppermute | solution.py:411
  33.5 15.2 %collective-permute-start.14 = (bf16[2,8,16,1024]{3,2,1,0:T(8,128)(2,1)S(1)}, bf16[2,8,16,1024]{3,2,1,0:T(8,128)(2,1)S(1)}, u32[]{:S(2)}, u32[]{:S(2)}) collective-permute-start(bf16[2,8,16,1024]{3,2,1,0:T(8,128)(2,1)S(1)} %get-tuple-element.69), channel_id=1, source_target_pairs={{0,33},{1,32},{2,35},{3,34},{4,37},{5,36},{6,39},{7,38},{8,41},{9,... | collective-permute-start | bytes 1572872 | tf_op jit(solution)/shard_map/ppermute | solution.py:411
  41.0 0.7 copy-start
  41.7 7.0 %collective-permute-start.8 = (bf16[2,16,1024]{2,1,0:T(8,128)(2,1)S(1)}, bf16[2,16,1024]{2,1,0:T(8,128)(2,1)S(1)}, u32[]{:S(2)}, u32[]{:S(2)}) collective-permute-start(bf16[2,16,1024]{2,1,0:T(8,128)(2,1)S(1)} %get-tuple-element.54), channel_id=1, source_target_pairs={{0,63},{1,48},{2,49},{3,50},{4,51},{5,52},{6,53},{7,54},{8,55},{9,... | collective-permute-start | bytes 196616 | tf_op jit(solution)/shard_map/ppermute | solution.py:411
  45.7 9.0 %collective-permute-start.11 = (bf16[8,16,1024]{2,1,0:T(8,128)(2,1)S(1)}, bf16[8,16,1024]{2,1,0:T(8,128)(2,1)S(1)}, u32[]{:S(2)}, u32[]{:S(2)}) collective-permute-start(bf16[8,16,1024]{2,1,0:T(8,128)(2,1)S(1)} %get-tuple-element.63), channel_id=1, source_target_pairs={{0,33},{1,32},{2,35},{3,34},{4,37},{5,36},{6,39},{7,38},{8,41},{9,... | collective-permute-start | bytes 786440 | tf_op jit(solution)/shard_map/ppermute | solution.py:411
  49.4 8.6 %collective-permute-start.15 = (bf16[8,16,1024]{2,1,0:T(8,128)(2,1)S(1)}, bf16[8,16,1024]{2,1,0:T(8,128)(2,1)S(1)}, u32[]{:S(2)}, u32[]{:S(2)}) collective-permute-start(bf16[8,16,1024]{2,1,0:T(8,128)(2,1)S(1)} %get-tuple-element.71), channel_id=1, source_target_pairs={{0,1},{1,0},{2,3},{3,2},{4,5},{5,4},{6,7},{7,6},{8,9},{9,8},{10,11... | collective-permute-start | bytes 786440 | tf_op jit(solution)/shard_map/ppermute | solution.py:411
  55.3 6.3 %collective-permute-start.12 = (bf16[8,16,512]{2,1,0:T(8,128)(2,1)S(1)}, bf16[8,16,512]{2,1,0:T(8,128)(2,1)S(1)}, u32[]{:S(2)}, u32[]{:S(2)}) collective-permute-start(bf16[8,16,512]{2,1,0:T(8,128)(2,1)S(1)} %get-tuple-element.65), channel_id=1, source_target_pairs={{0,64},{64,0},{128,192},{192,128},{1,65},{65,1},{129,193},{193,129... | collective-permute-start | bytes 393224 | tf_op jit(solution)/shard_map/ppermute | solution.py:419
  58.5 6.3 %collective-permute-start.16 = (bf16[8,16,512]{2,1,0:T(8,128)(2,1)S(1)}, bf16[8,16,512]{2,1,0:T(8,128)(2,1)S(1)}, u32[]{:S(2)}, u32[]{:S(2)}) collective-permute-start(bf16[8,16,512]{2,1,0:T(8,128)(2,1)S(1)} %get-tuple-element.73), channel_id=1, source_target_pairs={{0,192},{64,128},{128,64},{192,0},{1,193},{65,129},{129,65},{193,1... | collective-permute-start | bytes 393224 | tf_op jit(solution)/shard_map/ppermute | solution.py:419
  65.6 19.2 %all-to-all-start = ((bf16[8,16,1024]{2,1,0:T(8,128)(2,1)}), bf16[8,16,1024]{2,1,0:T(8,128)(2,1)S(1)}, u32[]{:S(2)}, u32[]{:S(2)}) async-start(bf16[8,16,1024]{2,1,0:T(8,128)(2,1)} %join.1), calls=%async_computation | async-start | bytes 524288 | tf_op jit(solution)/shard_map/all_to_all | solution.py:571
  74.0 15.0 %collective-permute-start.7 = (bf16[2,112,1024]{2,1,0:T(8,128)(2,1)S(1)}, bf16[2,112,1024]{2,1,0:T(8,128)(2,1)S(1)}, u32[]{:S(2)}, u32[]{:S(2)}) collective-permute-start(bf16[2,112,1024]{2,1,0:T(8,128)(2,1)S(1)} %get-tuple-element.53), channel_id=1, source_target_pairs={{0,15},{1,0},{2,1},{3,2},{4,3},{5,4},{6,5},{7,6},{8,7},{9,8},{10,9... | collective-permute-start | bytes 1376264 | tf_op jit(solution)/shard_map/ppermute | solution.py:411
  74.0 15.0 %collective-permute-start.6 = (bf16[2,64,1024]{2,1,0:T(8,128)(2,1)}, bf16[2,64,1024]{2,1,0:T(8,128)(2,1)S(1)}, u32[]{:S(2)}, u32[]{:S(2)}) collective-permute-start(bf16[2,64,1024]{2,1,0:T(8,128)(2,1)} %copy-done), channel_id=1, source_target_pairs={{0,48},{1,49},{2,50},{3,51},{4,52},{5,53},{6,54},{7,55},{8,56},{9,... | collective-permute-start | bytes 786440 | tf_op jit(solution)/shard_map/ppermute | solution.py:411
  84.8 6.2 %collective-permute-start.19 = (bf16[16,1024]{1,0:T(8,128)(2,1)S(1)}, bf16[16,1024]{1,0:T(8,128)(2,1)S(1)}, u32[]{:S(2)}, u32[]{:S(2)}) collective-permute-start(bf16[16,1024]{1,0:T(8,128)(2,1)S(1)} %depth.1.r0), channel_id=1, source_target_pairs={{0,192},{64,128},{128,64},{192,0},{1,193},{65,129},{129,65},{193,1... | collective-permute-start | bytes 98312 | tf_op jit(solution)/shard_map/ppermute | solution.py:419
  87.8 5.4 %collective-permute-start.18 = (bf16[16,1024]{1,0:T(8,128)(2,1)S(1)}, bf16[16,1024]{1,0:T(8,128)(2,1)S(1)}, u32[]{:S(2)}, u32[]{:S(2)}) collective-permute-start(bf16[16,1024]{1,0:T(8,128)(2,1)S(1)} %depth.1.r0), channel_id=1, source_target_pairs={{0,128},{64,192},{128,0},{192,64},{1,129},{65,193},{129,1},{193,65... | collective-permute-start | bytes 98312 | tf_op jit(solution)/shard_map/ppermute | solution.py:419
  87.8 5.4 %collective-permute-start.17 = (bf16[16,1024]{1,0:T(8,128)(2,1)S(1)}, bf16[16,1024]{1,0:T(8,128)(2,1)S(1)}, u32[]{:S(2)}, u32[]{:S(2)}) collective-permute-start(bf16[16,1024]{1,0:T(8,128)(2,1)S(1)} %depth.1.r0), channel_id=1, source_target_pairs={{0,64},{64,0},{128,192},{192,128},{1,65},{65,1},{129,193},{193,129... | collective-permute-start | bytes 98312 | tf_op jit(solution)/shard_map/ppermute | solution.py:419

commit v8 on v7

--- a/solution.py
+++ b/solution.py
@@ -105,14 +105,15 @@
     diag[...] = dot(corner, held[OWN:], 1, 0).astype(BF16)
 
 
-def embed_kernel(own, up, left, diag, bt, tt, mv, wq, emb, normed, proj, tables, weight, sems):
+def embed_kernel(own, up, left, diag, bt, tt, mv, wq, emb, normed, proj, tables, masked, weight, sems):
     copies = [
         pltpu.make_async_copy(bt, tables.at[0], sems.at[0]),
         pltpu.make_async_copy(tt, tables.at[1], sems.at[1]),
-        pltpu.make_async_copy(wq, weight, sems.at[2]),
+        pltpu.make_async_copy(mv, masked, sems.at[2]),
+        pltpu.make_async_copy(wq, weight, sems.at[3]),
     ]
-    copies[0].start()
-    copies[1].start()
+    for copy in copies[:3]:
+        copy.start()
     r, j = iota((80, 16), 0), iota((80, 16), 1)
     low = jnp.where(r >= 64, r - 50, r & 31) >= 28
     late = jnp.where(r >= 64, 2 * j, j) >= LATE
@@ -140,21 +141,21 @@
 
     code_b = column(bottom, 32, source_row, lambda t: t & 15)
     code_t = column(upper, 16, lambda t: source_row(t) >> 1, lambda t: (t & 15) >> 1)
-    copies[0].wait()
-    copies[1].wait()
-    copies[2].start()
+    for copy in copies[:3]:
+        copy.wait()
+    copies[3].start()
     step = 256
     for at in range(0, TOKENS, step):
         here = slice(at, at + step)
         cb, ct = code_b[here], code_t[here]
         lane = iota((step, 512), 1)
         x = dot(hot(lane == cb), tables[0], 1, 0)
-        x = jnp.where(cb == 512, mv[...].astype(F32).reshape(1, MODEL), x)
+        x = jnp.where(cb == 512, masked[...].astype(F32).reshape(1, MODEL), x)
         x = (x + dot(hot(lane == ct), tables[1], 1, 0)).astype(BF16)
         emb[here] = x
         centred, inverse = moments(x.astype(F32))
         normed[here] = (centred * inverse).astype(BF16)
-    copies[2].wait()
+    copies[3].wait()
     proj[...] = dot(normed[...], weight[...], 1, 0).astype(BF16)
 
 
@@ -331,7 +332,8 @@
             out[u] = (a[u, :, v] + b[u, :, v].astype(F32)).astype(out.dtype)
 
 
-def parity_pair(place, a, b, tick, keep, send):
+def parity_pair(place, a, b, tick, halo, keep, send, passed):
+    passed[...] = halo[...]
     for out, u in ((keep, place[2]), (send, place[2] ^ 1)):
         out[...] = (a[u] + b[u].astype(F32)).astype(out.dtype)
 
@@ -361,7 +363,7 @@
         out[...] = (a[:, :, cut] + b[:, :, cut].astype(F32)).astype(out.dtype)
 
 
-def join_kernel(a, b, c, d, out):
+def join_kernel(a, b, c, d, arrived, out):
     out[:, :, 0 : 2 * Q] = (a[...] + b[...].astype(F32)).astype(BF16)
     out[:, :, 2 * Q :] = (c[...] + d[...].astype(F32)).astype(BF16)
 
@@ -423,10 +425,10 @@
     return permute(x, lambda la, lo: (la ^ (flip & 2), lo ^ (flip & 1)))
 
 
-def halve(name, kernel, shape, operands, specs):
+def halve(name, kernel, shape, operands, specs, more=()):
     return call(
         kernel,
-        [sds(shape, F32), sds(shape)],
+        [sds(shape, F32), sds(shape), *more],
         operands,
         specs,
         2**10,
@@ -448,11 +450,11 @@
     return halve("sum_core", kernel, (2, 8, 16, W), operands, [smem(), vmem(), vmem()])
 
 
-def sum_pair(place, keep, send, tick, c):
+def sum_pair(place, keep, send, tick, c, halo=()):
     kernel = high_pair if c % 2 else parity_pair
     recv = swap_x(send, order(c)[0])
-    specs = [smem(), vmem(), vmem(), anywhere()]
-    return halve("sum_pair", kernel, (8, 16, W), (place, keep, recv, tick), specs)
+    specs = [smem(), vmem(), vmem(), anywhere()] + [vmem()] * len(halo)
+    return halve("sum_pair", kernel, (8, 16, W), (place, keep, recv, tick, *halo), specs, [sds(h.shape) for h in halo])
 
 
 def sum_cut(place, keep, send, c):
@@ -475,7 +477,7 @@
     pin = lambda x: pltpu.with_memory_space_constraint(x, pltpu.HBM)
     grads = pin(cotangent.reshape(TOKENS, MODEL))
     bottom_table, top_table = pin(bottom_table), pin(top_table)
-    qkv_weight, out_weight = pin(qkv_weight), pin(out_weight)
+    mask_vector, qkv_weight, out_weight = pin(mask_vector), pin(qkv_weight), pin(out_weight)
     up, left, diag = call(
         slice_kernel,
         [sds((64, MODEL)), sds((MSG, MODEL)), sds((16, MODEL))],
@@ -491,11 +493,16 @@
         embed_kernel,
         [sds((TOKENS, MODEL)), sds((TOKENS, MODEL)), sds((TOKENS, 3 * HW))],
         (*near, bottom_table, top_table, mask_vector, qkv_weight),
-        [vmem()] * 4 + [hbm(), hbm(), vmem(), hbm()],
+        [vmem()] * 4 + [hbm()] * 4,
         2 * TOKENS * 1024 * 2560,
         9 * 2**20,
         name="embed",
-        scratch=[pltpu.VMEM((2, 512, MODEL), BF16), pltpu.VMEM((MODEL, 3 * HW), BF16), sems(3)],
+        scratch=[
+            pltpu.VMEM((2, 512, MODEL), BF16),
+            pltpu.VMEM((MODEL,), BF16),
+            pltpu.VMEM((MODEL, 3 * HW), BF16),
+            sems(4),
+        ],
     )
     outs = [sds((TOKENS, CW)), sds((TOKENS, 3 * CW)), sds((2, 256, W), F32), sds((2, 256, W))]
     column = pltpu.VMEM((MODEL, CW), BF16)
@@ -542,11 +549,12 @@
         ],
     )
     mid, up, left, diag = sent
-    up, left, diag = shift(up, -1, 0), shift(left, 0, -1), shift(diag, -1, -1)
-    summed = []
-    for c, (keep, send) in enumerate(cores):
-        keep, send = sum_pair(place, keep, send, diag if c else tick, c)
-        summed += sum_cut(place, keep, send, c)
+    up, diag = shift(up, -1, 0), shift(diag, -1, -1)
+    (keep0, send0), (keep1, send1) = cores
+    keep0, send0, left = sum_pair(place, keep0, send0, tick, 0, (left,))
+    keep1, send1 = sum_pair(place, keep1, send1, diag, 1)
+    left = shift(left, 0, -1)
+    summed = sum_cut(place, keep0, send0, 0) + sum_cut(place, keep1, send1, 1)
     out, gin = call(
         place_kernel,
         [sds((TOKENS, MODEL))] * 2,
@@ -561,8 +569,8 @@
     joined = call(
         join_kernel,
         sds((8, 16, 4 * Q)),
-        summed,
-        [vmem()] * 4,
+        (*summed, left),
+        [vmem()] * 4 + [anywhere()],
         2**19,
         2**21,
         limit=16,

time: 96.2 us -> 103 us (1.071)
  the two profiles are of different devices: /device:TPU:32 before, /device:TPU:2 now
where the time goes in v8:
time: 103 us; the launch traced here: 102 us
  waiting for transfers between devices  41.5 us (40%)
  starting transfers between devices  29.7 us (29%)
  Pallas kernels  29.4 us (29%)
    pallas_call x15, Pallas kernels, call(): pl.pallas_call(kernel, out_shape=outs, in_specs=specs, out_specs=jax.tree...  29.4 us
    ppermute x13, waiting for transfers between devices, permute(): return lax.ppermute(x, GRID, pairs)  23.1 us
    ppermute x13, starting transfers between devices, permute(): return lax.ppermute(x, GRID, pairs)  12.7 us
    all_to_all x1, waiting for transfers between devices, shards(): depth = lax.all_to_all(joined, 'z', 0, 0, tiled=True)  11.3 us
    ppermute x7, starting transfers between devices, swap(): lax.ppermute(x, axis, [(i, i ^ flip) for i in range(lax.axis_size(axis))])  9.8 us
    all_to_all x1, starting transfers between devices, shards(): depth = lax.all_to_all(joined, 'z', 0, 0, tiled=True)  7.24 us
    ppermute x7, waiting for transfers between devices, swap(): lax.ppermute(x, axis, [(i, i ^ flip) for i in range(lax.axis_size(axis))])  7.12 us
  transfers between devices with their start and end apart: 21, of which 9 were waited for; matrix products, arithmetic and copies ran while one was open for 0% of the time, Pallas kernels for 22%

profile of v8, /device:TPU:2, one launch (start us, length us, event | category | flops | bytes accessed | tf_op | source)
XLA Modules:
  0.0 102.4 jit_solution(13797001708241097196)
XLA Ops:
  0.6 0.8 pad_add_fusion
  1.5 1.4 %collective-permute-start.2 = (s32[80,16]{1,0:T(8,128)S(1)}, s32[80,16]{1,0:T(8,128)S(1)}, u32[]{:S(2)}, u32[]{:S(2)}) collective-permute-start(s32[80,16]{1,0:T(8,128)S(1)} %copy.19.own), channel_id=1, source_target_pairs={{0,17},{1,18},{2,19},{3,20},{4,21},{5,22},{6,23},{7,24},{8,25},{9,... | collective-permute-start | bytes 15368 | tf_op jit(solution)/shard_map/ppermute | solution.py:413
  2.9 1.5 %collective-permute-start.1 = (s32[80,16]{1,0:T(8,128)S(1)}, s32[80,16]{1,0:T(8,128)S(1)}, u32[]{:S(2)}, u32[]{:S(2)}) collective-permute-start(s32[80,16]{1,0:T(8,128)S(1)} %copy.19.own), channel_id=1, source_target_pairs={{0,1},{1,2},{2,3},{3,4},{4,5},{5,6},{6,7},{7,8},{8,9},{9,10},{10,1... | collective-permute-start | bytes 15368 | tf_op jit(solution)/shard_map/ppermute | solution.py:413
  4.4 1.7 %collective-permute-start = (s32[80,16]{1,0:T(8,128)S(1)}, s32[80,16]{1,0:T(8,128)S(1)}, u32[]{:S(2)}, u32[]{:S(2)}) collective-permute-start(s32[80,16]{1,0:T(8,128)S(1)} %copy.19.own), channel_id=1, source_target_pairs={{0,16},{1,17},{2,18},{3,19},{4,20},{5,21},{6,22},{7,23},{8,24},{9,... | collective-permute-start | bytes 15368 | tf_op jit(solution)/shard_map/ppermute | solution.py:413
  6.1 1.6 %slices.1 = (bf16[64,1024]{1,0:T(8,128)(2,1)S(1)}, bf16[112,1024]{1,0:T(8,128)(2,1)S(1)}, bf16[16,1024]{1,0:T(8,128)(2,1)S(1)}) custom-call(bf16[512,1024]{1,0:T(8,128)(2,1)} %bitcast.20), custom_call_target="tpu_custom_call" | custom-call | flops 268435456 | bytes 2097152 | tf_op jit(solution)/shard_map/slices/pallas_call | solution.py:43
  7.7 3.0 %collective-permute-start.5 = (bf16[16,1024]{1,0:T(8,128)(2,1)S(1)}, bf16[16,1024]{1,0:T(8,128)(2,1)S(1)}, u32[]{:S(2)}, u32[]{:S(2)}) collective-permute-start(bf16[16,1024]{1,0:T(8,128)(2,1)S(1)} %get-tuple-element.46), channel_id=1, source_target_pairs={{0,17},{1,18},{2,19},{3,20},{4,21},{5,22},{6,23},{7,24},{8,25},{9,... | collective-permute-start | bytes 98312 | tf_op jit(solution)/shard_map/ppermute | solution.py:413
  11.4 5.3 %embed.1 = (bf16[512,1024]{1,0:T(8,128)(2,1)S(1)}, bf16[512,1024]{1,0:T(8,128)(2,1)S(1)}, bf16[512,1536]{1,0:T(8,128)(2,1)S(1)}) custom-call(s32[80,16]{1,0:T(8,128)S(1)} %copy.19.own, s32[80,16]{1,0:T(8,128)S(1)} %collective-permute-done.up, s32[80,16]{1,0:T(8,128)S(1)} %collective-permute-done.1.left, s32[80,16]{1,0:T(8,128)S(1)} %collective-permute-done.2.diag, ...), custom_call_target="tpu_custom_call" | custom-call | flops 2684354560 | bytes 9437184 | tf_op jit(solution)/shard_map/embed/pallas_call | solution.py:43
  16.7 4.8 %collective-permute-done.3.up = bf16[64,1024]{1,0:T(8,128)(2,1)S(1)} collective-permute-done((bf16[64,1024]{1,0:T(8,128)(2,1)S(1)}, bf16[64,1024]{1,0:T(8,128)(2,1)S(1)}, u32[]{:S(2)}, u32[]{:S(2)}) %collective-permute-start.3) | collective-permute-done | bytes 131104 | tf_op jit(solution)/shard_map/ppermute | solution.py:413
  21.5 5.0 %attend.2 = (bf16[512,256]{1,0:T(8,128)(2,1)S(1)}, bf16[512,768]{1,0:T(8,128)(2,1)S(1)}, f32[2,256,1024]{2,1,0:T(8,128)S(1)}, bf16[2,256,1024]{2,1,0:T(8,128)(2,1)S(1)}, bf16[512,1024]{1,0:T(8,128)(2,1)S(1)}) custom-call(s32[6]{0:T(128)S(1)} %stack.27.place, bf16[512,1536]{1,0:T(8,128)(2,1)S(1)} %get-tuple-element.42.proj, ...), custom_call_target="tpu_custom_call" | custom-call | flops 1048576 | bytes 4096 | tf_op jit(solution)/shard_map/attend/pallas_call | solution.py:43
  26.8 4.4 %attend.3 = (bf16[512,256]{1,0:T(8,128)(2,1)S(1)}, bf16[512,768]{1,0:T(8,128)(2,1)S(1)}, f32[2,256,1024]{2,1,0:T(8,128)S(1)}, bf16[2,256,1024]{2,1,0:T(8,128)(2,1)S(1)}) custom-call(s32[6]{0:T(128)S(1)} %stack.27.place, bf16[512,1536]{1,0:T(8,128)(2,1)S(1)} %get-tuple-element.42.proj, bf16[512,1024]{1,0:T(8,128)(2,1)S(1)} %get-tuple-element.43.normed, ...), custom_call_target="tpu_custom_call" | custom-call | flops 1048576 | bytes 4096 | tf_op jit(solution)/shard_map/attend/pallas_call | solution.py:43
  31.8 0.7 sum_core.2
  32.9 1.2 %collective-permute-done.13 = bf16[2,256,1024]{2,1,0:T(8,128)(2,1)S(1)} collective-permute-done((bf16[2,256,1024]{2,1,0:T(8,128)(2,1)S(1)}, bf16[2,256,1024]{2,1,0:T(8,128)(2,1)S(1)}, u32[]{:S(2)}, u32[]{:S(2)}) %collective-permute-start.13) | collective-permute-done | bytes 1048608 | tf_op jit(solution)/shard_map/ppermute | solution.py:421
  34.1 0.7 sum_core.3
  34.9 5.2 %finish.1 = (bf16[2,448,1024]{2,1,0:T(8,128)(2,1)S(1)}, bf16[2,64,1024]{2,1,0:T(8,128)(2,1)S(1)}, bf16[2,112,1024]{2,1,0:T(8,128)(2,1)S(1)}, bf16[2,16,1024]{2,1,0:T(8,128)(2,1)S(1)}, f32[8,128]{1,0:T(8,128)S(1)}) custom-call(bf16[512,1024]{1,0:T(8,128)(2,1)S(1)} %get-tuple-element.41.emb, bf16[512,1024]{1,0:T(8,128)(2,1)S(1)} %get-tuple-element.47.cot, ...), custom_call_target="tpu_custom_call" | custom-call | flops 1048576 | bytes 4096 | tf_op jit(solution)/shard_map/finish/pallas_call | solution.py:43
  40.2 1.8 %collective-permute-start.10 = (bf16[2,16,1024]{2,1,0:T(8,128)(2,1)S(1)}, bf16[2,16,1024]{2,1,0:T(8,128)(2,1)S(1)}, u32[]{:S(2)}, u32[]{:S(2)}) collective-permute-start(bf16[2,16,1024]{2,1,0:T(8,128)(2,1)S(1)} %get-tuple-element.61), channel_id=1, source_target_pairs={{0,63},{1,48},{2,49},{3,50},{4,51},{5,52},{6,53},{7,54},{8,55},{9,... | collective-permute-start | bytes 196616 | tf_op jit(solution)/shard_map/ppermute | solution.py:413
  41.9 5.2 %collective-permute-done.8.b = bf16[2,8,16,1024]{3,2,1,0:T(8,128)(2,1)S(1)} collective-permute-done((bf16[2,8,16,1024]{3,2,1,0:T(8,128)(2,1)S(1)}, bf16[2,8,16,1024]{3,2,1,0:T(8,128)(2,1)S(1)}, u32[]{:S(2)}, u32[]{:S(2)}) %collective-permute-start.8) | collective-permute-done | bytes 524320 | tf_op jit(solution)/shard_map/ppermute | solution.py:413
  47.2 0.7 sum_pair.2
  48.9 0.9 collective-permute-done.14.b
  50.4 1.2 %collective-permute-start.15 = (bf16[8,16,1024]{2,1,0:T(8,128)(2,1)S(1)}, bf16[8,16,1024]{2,1,0:T(8,128)(2,1)S(1)}, u32[]{:S(2)}, u32[]{:S(2)}) collective-permute-start(bf16[8,16,1024]{2,1,0:T(8,128)(2,1)S(1)} %get-tuple-element.73), channel_id=1, source_target_pairs={{0,1},{1,0},{2,3},{3,2},{4,5},{5,4},{6,7},{7,6},{8,9},{9,8},{10,11... | collective-permute-start | bytes 786440 | tf_op jit(solution)/shard_map/ppermute | solution.py:413
  51.6 3.8 %collective-permute-done.11.b = bf16[8,16,1024]{2,1,0:T(8,128)(2,1)S(1)} collective-permute-done((bf16[8,16,1024]{2,1,0:T(8,128)(2,1)S(1)}, bf16[8,16,1024]{2,1,0:T(8,128)(2,1)S(1)}, u32[]{:S(2)}, u32[]{:S(2)}) %collective-permute-start.11) | collective-permute-done | bytes 262176 | tf_op jit(solution)/shard_map/ppermute | solution.py:413
  56.0 1.7 %collective-permute-start.12 = (bf16[8,16,512]{2,1,0:T(8,128)(2,1)S(1)}, bf16[8,16,512]{2,1,0:T(8,128)(2,1)S(1)}, u32[]{:S(2)}, u32[]{:S(2)}) collective-permute-start(bf16[8,16,512]{2,1,0:T(8,128)(2,1)S(1)} %get-tuple-element.67), channel_id=1, source_target_pairs={{0,64},{64,0},{128,192},{192,128},{1,65},{65,1},{129,193},{193,129... | collective-permute-start | bytes 393224 | tf_op jit(solution)/shard_map/ppermute | solution.py:421
  57.7 8.3 %collective-permute-done.15.b = bf16[8,16,1024]{2,1,0:T(8,128)(2,1)S(1)} collective-permute-done((bf16[8,16,1024]{2,1,0:T(8,128)(2,1)S(1)}, bf16[8,16,1024]{2,1,0:T(8,128)(2,1)S(1)}, u32[]{:S(2)}, u32[]{:S(2)}) %collective-permute-start.15) | collective-permute-done | bytes 262176 | tf_op jit(solution)/shard_map/ppermute | solution.py:413
  66.7 3.1 %collective-permute-start.16 = (bf16[8,16,512]{2,1,0:T(8,128)(2,1)S(1)}, bf16[8,16,512]{2,1,0:T(8,128)(2,1)S(1)}, u32[]{:S(2)}, u32[]{:S(2)}) collective-permute-start(bf16[8,16,512]{2,1,0:T(8,128)(2,1)S(1)} %get-tuple-element.75), channel_id=1, source_target_pairs={{0,192},{64,128},{128,64},{192,0},{1,193},{65,129},{129,65},{193,1... | collective-permute-start | bytes 393224 | tf_op jit(solution)/shard_map/ppermute | solution.py:421
  69.8 3.7 %collective-permute-done.16.d = bf16[8,16,512]{2,1,0:T(8,128)(2,1)S(1)} collective-permute-done((bf16[8,16,512]{2,1,0:T(8,128)(2,1)S(1)}, bf16[8,16,512]{2,1,0:T(8,128)(2,1)S(1)}, u32[]{:S(2)}, u32[]{:S(2)}) %collective-permute-start.16) | collective-permute-done | bytes 131104 | tf_op jit(solution)/shard_map/ppermute | solution.py:421
  73.4 0.7 join.1
  74.2 7.2 %all-to-all-start = ((bf16[8,16,1024]{2,1,0:T(8,128)(2,1)}), bf16[8,16,1024]{2,1,0:T(8,128)(2,1)S(1)}, u32[]{:S(2)}, u32[]{:S(2)}) async-start(bf16[8,16,1024]{2,1,0:T(8,128)(2,1)} %join.1), calls=%async_computation | async-start | bytes 524288 | tf_op jit(solution)/shard_map/all_to_all | solution.py:579
  81.4 11.3 %all-to-all-done.ref = bf16[8,16,1024]{2,1,0:T(8,128)(2,1)S(1)} async-done(((bf16[8,16,1024]{2,1,0:T(8,128)(2,1)}), bf16[8,16,1024]{2,1,0:T(8,128)(2,1)S(1)}, u32[]{:S(2)}, u32[]{:S(2)}) %all-to-all-start) | async-done | bytes 262176 | tf_op jit(solution)/shard_map/all_to_all | solution.py:579
  92.7 3.0 %collective-permute-start.19 = (bf16[16,1024]{1,0:T(8,128)(2,1)S(1)}, bf16[16,1024]{1,0:T(8,128)(2,1)S(1)}, u32[]{:S(2)}, u32[]{:S(2)}) collective-permute-start(bf16[16,1024]{1,0:T(8,128)(2,1)S(1)} %depth.1.r0), channel_id=1, source_target_pairs={{0,192},{64,128},{128,64},{192,0},{1,193},{65,129},{129,65},{193,1... | collective-permute-start | bytes 98312 | tf_op jit(solution)/shard_map/ppermute | solution.py:421
  95.7 1.2 %collective-permute-start.17 = (bf16[16,1024]{1,0:T(8,128)(2,1)S(1)}, bf16[16,1024]{1,0:T(8,128)(2,1)S(1)}, u32[]{:S(2)}, u32[]{:S(2)}) collective-permute-start(bf16[16,1024]{1,0:T(8,128)(2,1)S(1)} %depth.1.r0), channel_id=1, source_target_pairs={{0,64},{64,0},{128,192},{192,128},{1,65},{65,1},{129,193},{193,129... | collective-permute-start | bytes 98312 | tf_op jit(solution)/shard_map/ppermute | solution.py:421
  96.9 2.0 %place.1 = (bf16[512,1024]{1,0:T(8,128)(2,1)}, bf16[512,1024]{1,0:T(8,128)(2,1)}) custom-call(bf16[2,448,1024]{2,1,0:T(8,128)(2,1)S(1)} %get-tuple-element.52.mid, bf16[2,64,1024]{2,1,0:T(8,128)(2,1)S(1)} %collective-permute-done.6.up, bf16[2,112,1024]{2,1,0:T(8,128)(2,1)S(1)} %collective-permute-done.9.left.arrived, ...), custom_call_target="tpu_custom_call" | custom-call | flops 268435456 | bytes 5242880 | tf_op jit(solution)/shard_map/place/pallas_call | solution.py:43
  98.9 2.3 %collective-permute-done.18.r2 = bf16[16,1024]{1,0:T(8,128)(2,1)S(1)} collective-permute-done((bf16[16,1024]{1,0:T(8,128)(2,1)S(1)}, bf16[16,1024]{1,0:T(8,128)(2,1)S(1)}, u32[]{:S(2)}, u32[]{:S(2)}) %collective-permute-start.18) | collective-permute-done | bytes 32800 | tf_op jit(solution)/shard_map/ppermute | solution.py:421
  101.2 1.2 %level.1 = (f32[16,1536]{1,0:T(8,128)}, f32[16,512]{1,0:T(8,128)}) custom-call(s32[6]{0:T(128)S(1)} %stack.27.place, bf16[16,1024]{1,0:T(8,128)(2,1)S(1)} %depth.1.r0, bf16[16,1024]{1,0:T(8,128)(2,1)S(1)} %collective-permute-done.17.r1, bf16[16,1024]{1,0:T(8,128)(2,1)S(1)} %collective-permute-done.18.r2, bf16[16,1024]{1,0:T(8,128)(2,1)S(1)} %collective-permute-done.19.r3), custom_call_target="tpu_custom_call" | custom-call | flops 131072 | bytes 524288 | tf_op jit(solution)/shard_map/level/pallas_call | solution.py:43
  (28 shorter events, 5.1 us)
Async XLA Ops:
  1.5 9.3 %collective-permute-start.2 = (s32[80,16]{1,0:T(8,128)S(1)}, s32[80,16]{1,0:T(8,128)S(1)}, u32[]{:S(2)}, u32[]{:S(2)}) collective-permute-start(s32[80,16]{1,0:T(8,128)S(1)} %copy.19.own), channel_id=1, source_target_pairs={{0,17},{1,18},{2,19},{3,20},{4,21},{5,22},{6,23},{7,24},{8,25},{9,... | collective-permute-start | bytes 15368 | tf_op jit(solution)/shard_map/ppermute | solution.py:413
  2.9 8.5 %collective-permute-start.1 = (s32[80,16]{1,0:T(8,128)S(1)}, s32[80,16]{1,0:T(8,128)S(1)}, u32[]{:S(2)}, u32[]{:S(2)}) collective-permute-start(s32[80,16]{1,0:T(8,128)S(1)} %copy.19.own), channel_id=1, source_target_pairs={{0,1},{1,2},{2,3},{3,4},{4,5},{5,6},{6,7},{7,8},{8,9},{9,10},{10,1... | collective-permute-start | bytes 15368 | tf_op jit(solution)/shard_map/ppermute | solution.py:413
  4.4 7.0 %collective-permute-start = (s32[80,16]{1,0:T(8,128)S(1)}, s32[80,16]{1,0:T(8,128)S(1)}, u32[]{:S(2)}, u32[]{:S(2)}) collective-permute-start(s32[80,16]{1,0:T(8,128)S(1)} %copy.19.own), channel_id=1, source_target_pairs={{0,16},{1,17},{2,18},{3,19},{4,20},{5,21},{6,22},{7,23},{8,24},{9,... | collective-permute-start | bytes 15368 | tf_op jit(solution)/shard_map/ppermute | solution.py:413
  7.7 9.1 %collective-permute-start.5 = (bf16[16,1024]{1,0:T(8,128)(2,1)S(1)}, bf16[16,1024]{1,0:T(8,128)(2,1)S(1)}, u32[]{:S(2)}, u32[]{:S(2)}) collective-permute-start(bf16[16,1024]{1,0:T(8,128)(2,1)S(1)} %get-tuple-element.46), channel_id=1, source_target_pairs={{0,17},{1,18},{2,19},{3,20},{4,21},{5,22},{6,23},{7,24},{8,25},{9,... | collective-permute-start | bytes 98312 | tf_op jit(solution)/shard_map/ppermute | solution.py:413
  10.7 10.8 %collective-permute-start.3 = (bf16[64,1024]{1,0:T(8,128)(2,1)S(1)}, bf16[64,1024]{1,0:T(8,128)(2,1)S(1)}, u32[]{:S(2)}, u32[]{:S(2)}) collective-permute-start(bf16[64,1024]{1,0:T(8,128)(2,1)S(1)} %get-tuple-element.44), channel_id=1, source_target_pairs={{0,16},{1,17},{2,18},{3,19},{4,20},{5,21},{6,22},{7,23},{8,24},{9,... | collective-permute-start | bytes 393224 | tf_op jit(solution)/shard_map/ppermute | solution.py:413
  10.8 10.7 %collective-permute-start.4 = (bf16[112,1024]{1,0:T(8,128)(2,1)S(1)}, bf16[112,1024]{1,0:T(8,128)(2,1)S(1)}, u32[]{:S(2)}, u32[]{:S(2)}) collective-permute-start(bf16[112,1024]{1,0:T(8,128)(2,1)S(1)} %get-tuple-element.45), channel_id=1, source_target_pairs={{0,1},{1,2},{2,3},{3,4},{4,5},{5,6},{6,7},{7,8},{8,9},{9,10},{10,1... | collective-permute-start | bytes 688136 | tf_op jit(solution)/shard_map/ppermute | solution.py:413
  26.5 5.3 %collective-permute-start.7 = (bf16[2,256,1024]{2,1,0:T(8,128)(2,1)S(1)}, bf16[2,256,1024]{2,1,0:T(8,128)(2,1)S(1)}, u32[]{:S(2)}, u32[]{:S(2)}) collective-permute-start(bf16[2,256,1024]{2,1,0:T(8,128)(2,1)S(1)} %get-tuple-element.55), channel_id=1, source_target_pairs={{0,16},{16,0},{1,17},{17,1},{2,18},{18,2},{3,19},{19,3},{4,20},{20... | collective-permute-start | bytes 3145736 | tf_op jit(solution)/shard_map/ppermute | solution.py:421
  31.2 2.9 %collective-permute-start.13 = (bf16[2,256,1024]{2,1,0:T(8,128)(2,1)S(1)}, bf16[2,256,1024]{2,1,0:T(8,128)(2,1)S(1)}, u32[]{:S(2)}, u32[]{:S(2)}) collective-permute-start(bf16[2,256,1024]{2,1,0:T(8,128)(2,1)S(1)} %get-tuple-element.69), channel_id=1, source_target_pairs={{0,16},{16,0},{1,17},{17,1},{2,18},{18,2},{3,19},{19,3},{4,20},{20... | collective-permute-start | bytes 3145736 | tf_op jit(solution)/shard_map/ppermute | solution.py:421
  32.5 14.6 %collective-permute-start.8 = (bf16[2,8,16,1024]{3,2,1,0:T(8,128)(2,1)S(1)}, bf16[2,8,16,1024]{3,2,1,0:T(8,128)(2,1)S(1)}, u32[]{:S(2)}, u32[]{:S(2)}) collective-permute-start(bf16[2,8,16,1024]{3,2,1,0:T(8,128)(2,1)S(1)} %get-tuple-element.57), channel_id=1, source_target_pairs={{0,1},{1,0},{2,3},{3,2},{4,5},{5,4},{6,7},{7,6},{8,9},{9,8},{10,11... | collective-permute-start | bytes 1572872 | tf_op jit(solution)/shard_map/ppermute | solution.py:413
  34.8 15.0 %collective-permute-start.14 = (bf16[2,8,16,1024]{3,2,1,0:T(8,128)(2,1)S(1)}, bf16[2,8,16,1024]{3,2,1,0:T(8,128)(2,1)S(1)}, u32[]{:S(2)}, u32[]{:S(2)}) collective-permute-start(bf16[2,8,16,1024]{3,2,1,0:T(8,128)(2,1)S(1)} %get-tuple-element.71), channel_id=1, source_target_pairs={{0,33},{1,32},{2,35},{3,34},{4,37},{5,36},{6,39},{7,38},{8,41},{9,... | collective-permute-start | bytes 1572872 | tf_op jit(solution)/shard_map/ppermute | solution.py:413
  40.2 8.7 %collective-permute-start.10 = (bf16[2,16,1024]{2,1,0:T(8,128)(2,1)S(1)}, bf16[2,16,1024]{2,1,0:T(8,128)(2,1)S(1)}, u32[]{:S(2)}, u32[]{:S(2)}) collective-permute-start(bf16[2,16,1024]{2,1,0:T(8,128)(2,1)S(1)} %get-tuple-element.61), channel_id=1, source_target_pairs={{0,63},{1,48},{2,49},{3,50},{4,51},{5,52},{6,53},{7,54},{8,55},{9,... | collective-permute-start | bytes 196616 | tf_op jit(solution)/shard_map/ppermute | solution.py:413
  47.9 25.6 %collective-permute-start.9 = (bf16[2,112,1024]{2,1,0:T(8,128)(2,1)S(1)}, bf16[2,112,1024]{2,1,0:T(8,128)(2,1)S(1)}, u32[]{:S(2)}, u32[]{:S(2)}) collective-permute-start(bf16[2,112,1024]{2,1,0:T(8,128)(2,1)S(1)} %get-tuple-element.60), channel_id=1, source_target_pairs={{0,15},{1,0},{2,1},{3,2},{4,3},{5,4},{6,5},{7,6},{8,7},{9,8},{10,9... | collective-permute-start | bytes 1376264 | tf_op jit(solution)/shard_map/ppermute | solution.py:413
  48.2 7.2 %collective-permute-start.11 = (bf16[8,16,1024]{2,1,0:T(8,128)(2,1)S(1)}, bf16[8,16,1024]{2,1,0:T(8,128)(2,1)S(1)}, u32[]{:S(2)}, u32[]{:S(2)}) collective-permute-start(bf16[8,16,1024]{2,1,0:T(8,128)(2,1)S(1)} %get-tuple-element.65), channel_id=1, source_target_pairs={{0,33},{1,32},{2,35},{3,34},{4,37},{5,36},{6,39},{7,38},{8,41},{9,... | collective-permute-start | bytes 786440 | tf_op jit(solution)/shard_map/ppermute | solution.py:413
  50.4 15.6 %collective-permute-start.15 = (bf16[8,16,1024]{2,1,0:T(8,128)(2,1)S(1)}, bf16[8,16,1024]{2,1,0:T(8,128)(2,1)S(1)}, u32[]{:S(2)}, u32[]{:S(2)}) collective-permute-start(bf16[8,16,1024]{2,1,0:T(8,128)(2,1)S(1)} %get-tuple-element.73), channel_id=1, source_target_pairs={{0,1},{1,0},{2,3},{3,2},{4,5},{5,4},{6,7},{7,6},{8,9},{9,8},{10,11... | collective-permute-start | bytes 786440 | tf_op jit(solution)/shard_map/ppermute | solution.py:413
  56.0 13.7 %collective-permute-start.12 = (bf16[8,16,512]{2,1,0:T(8,128)(2,1)S(1)}, bf16[8,16,512]{2,1,0:T(8,128)(2,1)S(1)}, u32[]{:S(2)}, u32[]{:S(2)}) collective-permute-start(bf16[8,16,512]{2,1,0:T(8,128)(2,1)S(1)} %get-tuple-element.67), channel_id=1, source_target_pairs={{0,64},{64,0},{128,192},{192,128},{1,65},{65,1},{129,193},{193,129... | collective-permute-start | bytes 393224 | tf_op jit(solution)/shard_map/ppermute | solution.py:421
  66.7 6.8 %collective-permute-start.16 = (bf16[8,16,512]{2,1,0:T(8,128)(2,1)S(1)}, bf16[8,16,512]{2,1,0:T(8,128)(2,1)S(1)}, u32[]{:S(2)}, u32[]{:S(2)}) collective-permute-start(bf16[8,16,512]{2,1,0:T(8,128)(2,1)S(1)} %get-tuple-element.75), channel_id=1, source_target_pairs={{0,192},{64,128},{128,64},{192,0},{1,193},{65,129},{129,65},{193,1... | collective-permute-start | bytes 393224 | tf_op jit(solution)/shard_map/ppermute | solution.py:421
  74.2 18.5 %all-to-all-start = ((bf16[8,16,1024]{2,1,0:T(8,128)(2,1)}), bf16[8,16,1024]{2,1,0:T(8,128)(2,1)S(1)}, u32[]{:S(2)}, u32[]{:S(2)}) async-start(bf16[8,16,1024]{2,1,0:T(8,128)(2,1)} %join.1), calls=%async_computation | async-start | bytes 524288 | tf_op jit(solution)/shard_map/all_to_all | solution.py:579
  81.4 15.5 %collective-permute-start.6 = (bf16[2,64,1024]{2,1,0:T(8,128)(2,1)S(1)}, bf16[2,64,1024]{2,1,0:T(8,128)(2,1)S(1)}, u32[]{:S(2)}, u32[]{:S(2)}) collective-permute-start(bf16[2,64,1024]{2,1,0:T(8,128)(2,1)S(1)} %get-tuple-element.53), channel_id=1, source_target_pairs={{0,48},{1,49},{2,50},{3,51},{4,52},{5,53},{6,54},{7,55},{8,56},{9,... | collective-permute-start | bytes 786440 | tf_op jit(solution)/shard_map/ppermute | solution.py:413
  92.7 6.2 %collective-permute-start.19 = (bf16[16,1024]{1,0:T(8,128)(2,1)S(1)}, bf16[16,1024]{1,0:T(8,128)(2,1)S(1)}, u32[]{:S(2)}, u32[]{:S(2)}) collective-permute-start(bf16[16,1024]{1,0:T(8,128)(2,1)S(1)} %depth.1.r0), channel_id=1, source_target_pairs={{0,192},{64,128},{128,64},{192,0},{1,193},{65,129},{129,65},{193,1... | collective-permute-start | bytes 98312 | tf_op jit(solution)/shard_map/ppermute | solution.py:421
  95.7 5.4 %collective-permute-start.18 = (bf16[16,1024]{1,0:T(8,128)(2,1)S(1)}, bf16[16,1024]{1,0:T(8,128)(2,1)S(1)}, u32[]{:S(2)}, u32[]{:S(2)}) collective-permute-start(bf16[16,1024]{1,0:T(8,128)(2,1)S(1)} %depth.1.r0), channel_id=1, source_target_pairs={{0,128},{64,192},{128,0},{192,64},{1,129},{65,193},{129,1},{193,65... | collective-permute-start | bytes 98312 | tf_op jit(solution)/shard_map/ppermute | solution.py:421
  95.7 5.4 %collective-permute-start.17 = (bf16[16,1024]{1,0:T(8,128)(2,1)S(1)}, bf16[16,1024]{1,0:T(8,128)(2,1)S(1)}, u32[]{:S(2)}, u32[]{:S(2)}) collective-permute-start(bf16[16,1024]{1,0:T(8,128)(2,1)S(1)} %depth.1.r0), channel_id=1, source_target_pairs={{0,64},{64,0},{128,192},{192,128},{1,65},{65,1},{129,193},{193,129... | collective-permute-start | bytes 98312 | tf_op jit(solution)/shard_map/ppermute | solution.py:421

commit v9 on v8

--- a/solution.py
+++ b/solution.py
@@ -344,7 +344,7 @@
             out[v] = (a[u, :, v] + b[u, :, v].astype(F32)).astype(out.dtype)
 
 
-def high_pair(place, a, b, tick, keep, send):
+def high_pair(place, a, b, keep, send):
     for out, v in ((keep, place[3]), (send, place[3] ^ 1)):
         out[...] = (a[v] + b[v].astype(F32)).astype(out.dtype)
 
@@ -357,10 +357,11 @@
             out[:, :, u * Q : (u + 1) * Q] = (a[:, :, cut] + b[:, :, cut].astype(F32)).astype(out.dtype)
 
 
-def high_cut(place, a, b, keep, send):
+def high_cut(place, a, b, tick, keep, send):
     for out, u in ((keep, place[4]), (send, place[4] ^ 1)):
         cut = pl.ds(pl.multiple_of(u * 2 * Q, Q), 2 * Q)
-        out[...] = (a[:, :, cut] + b[:, :, cut].astype(F32)).astype(out.dtype)
+        for v in range(2):
+            out[v] = (a[v, :, :, cut] + b[v, :, :, cut].astype(F32)).astype(out.dtype)
 
 
 def join_kernel(a, b, c, d, arrived, out):
@@ -438,10 +439,6 @@
     )
 
 
-def order(c):
-    return (3, 1) if c % 2 else (1, 3)
-
-
 def sum_core(place, keep, send, c):
     fold = (2, 8, 2, 16, W)
     kernel = high_core if c % 2 else parity_core
@@ -450,18 +447,23 @@
     return halve("sum_core", kernel, (2, 8, 16, W), operands, [smem(), vmem(), vmem()])
 
 
-def sum_pair(place, keep, send, tick, c, halo=()):
-    kernel = high_pair if c % 2 else parity_pair
-    recv = swap_x(send, order(c)[0])
-    specs = [smem(), vmem(), vmem(), anywhere()] + [vmem()] * len(halo)
-    return halve("sum_pair", kernel, (8, 16, W), (place, keep, recv, tick, *halo), specs, [sds(h.shape) for h in halo])
-
-
-def sum_cut(place, keep, send, c):
-    recv = swap_x(send, order(c)[1])
-    kernel, flip = (high_cut, 3) if c % 2 else (parity_cut, 1)
-    keep, send = halve("sum_cut", kernel, (8, 16, 2 * Q), (place, keep, recv), [smem(), vmem(), vmem()])
-    return [keep, swap(send, "batch", flip)]
+def sum_first(place, keep, send, tick, halo):
+    adds = [smem(), vmem(), vmem()]
+    operands = (place, keep, swap_x(send, 1), tick, halo)
+    specs = adds + [anywhere(), vmem()]
+    keep, send, halo = halve("sum_pair", parity_pair, (8, 16, W), operands, specs, [sds(halo.shape)])
+    operands = (place, keep, swap_x(send, 3))
+    keep, send = halve("sum_cut", parity_cut, (8, 16, 2 * Q), operands, adds)
+    return [keep, swap(send, "batch", 1)], halo
+
+
+def sum_second(place, keep, send, tick):
+    adds = [smem(), vmem(), vmem()]
+    operands = (place, keep, swap_x(send, 3), tick)
+    keep, send = halve("sum_cut", high_cut, (2, 8, 16, 2 * Q), operands, adds + [anywhere()])
+    operands = (place, keep, swap(send, "batch", 3))
+    keep, send = halve("sum_pair", high_pair, (8, 16, 2 * Q), operands, adds)
+    return [keep, swap_x(send, 1)]
 
 
 def shards(
@@ -551,10 +553,9 @@
     mid, up, left, diag = sent
     up, diag = shift(up, -1, 0), shift(diag, -1, -1)
     (keep0, send0), (keep1, send1) = cores
-    keep0, send0, left = sum_pair(place, keep0, send0, tick, 0, (left,))
-    keep1, send1 = sum_pair(place, keep1, send1, diag, 1)
+    first, left = sum_first(place, keep0, send0, tick, left)
+    summed = first + sum_second(place, keep1, send1, diag)
     left = shift(left, 0, -1)
-    summed = sum_cut(place, keep0, send0, 0) + sum_cut(place, keep1, send1, 1)
     out, gin = call(
         place_kernel,
         [sds((TOKENS, MODEL))] * 2,

time: 103 us -> 93.9 us (0.912)
  the two profiles are of different devices: /device:TPU:2 before, /device:TPU:32 now
where the time goes in v9:
time: 93.9 us; the launch traced here: 92.7 us
  starting transfers between devices  38 us (40%)
  Pallas kernels  29.4 us (31%)
  waiting for transfers between devices  23.6 us (25%)
    pallas_call x15, Pallas kernels, call(): pl.pallas_call(kernel, out_shape=outs, in_specs=specs, out_specs=jax.tree...  29.4 us
    ppermute x13, starting transfers between devices, permute(): return lax.ppermute(x, GRID, pairs)  19.5 us
    ppermute x13, waiting for transfers between devices, permute(): return lax.ppermute(x, GRID, pairs)  10.5 us
    ppermute x7, starting transfers between devices, swap(): lax.ppermute(x, axis, [(i, i ^ flip) for i in range(lax.axis_size(axis))])  9.79 us
    all_to_all x1, waiting for transfers between devices, shards(): depth = lax.all_to_all(joined, 'z', 0, 0, tiled=True)  8.89 us
    all_to_all x1, starting transfers between devices, shards(): depth = lax.all_to_all(joined, 'z', 0, 0, tiled=True)  8.72 us
    ppermute x7, waiting for transfers between devices, swap(): lax.ppermute(x, axis, [(i, i ^ flip) for i in range(lax.axis_size(axis))])  4.16 us
  transfers between devices with their start and end apart: 21, of which 7 were waited for; matrix products, arithmetic and copies ran while one was open for 0% of the time, Pallas kernels for 24%

profile of v9, /device:TPU:32, one launch (start us, length us, event | category | flops | bytes accessed | tf_op | source)
XLA Modules:
  0.0 92.7 jit_solution(14179902559443547855)
XLA Ops:
  0.6 0.8 pad_add_fusion
  1.5 1.0 %collective-permute-start.2 = (s32[80,16]{1,0:T(8,128)S(1)}, s32[80,16]{1,0:T(8,128)S(1)}, u32[]{:S(2)}, u32[]{:S(2)}) collective-permute-start(s32[80,16]{1,0:T(8,128)S(1)} %copy.19.own), channel_id=1, source_target_pairs={{0,17},{1,18},{2,19},{3,20},{4,21},{5,22},{6,23},{7,24},{8,25},{9,... | collective-permute-start | bytes 15368 | tf_op jit(solution)/shard_map/ppermute | solution.py:414
  2.5 1.9 %collective-permute-start.1 = (s32[80,16]{1,0:T(8,128)S(1)}, s32[80,16]{1,0:T(8,128)S(1)}, u32[]{:S(2)}, u32[]{:S(2)}) collective-permute-start(s32[80,16]{1,0:T(8,128)S(1)} %copy.19.own), channel_id=1, source_target_pairs={{0,1},{1,2},{2,3},{3,4},{4,5},{5,6},{6,7},{7,8},{8,9},{9,10},{10,1... | collective-permute-start | bytes 15368 | tf_op jit(solution)/shard_map/ppermute | solution.py:414
  4.4 1.4 %collective-permute-start = (s32[80,16]{1,0:T(8,128)S(1)}, s32[80,16]{1,0:T(8,128)S(1)}, u32[]{:S(2)}, u32[]{:S(2)}) collective-permute-start(s32[80,16]{1,0:T(8,128)S(1)} %copy.19.own), channel_id=1, source_target_pairs={{0,16},{1,17},{2,18},{3,19},{4,20},{5,21},{6,22},{7,23},{8,24},{9,... | collective-permute-start | bytes 15368 | tf_op jit(solution)/shard_map/ppermute | solution.py:414
  5.8 1.6 %slices.1 = (bf16[64,1024]{1,0:T(8,128)(2,1)S(1)}, bf16[112,1024]{1,0:T(8,128)(2,1)S(1)}, bf16[16,1024]{1,0:T(8,128)(2,1)S(1)}) custom-call(bf16[512,1024]{1,0:T(8,128)(2,1)} %bitcast.20), custom_call_target="tpu_custom_call" | custom-call | flops 268435456 | bytes 2097152 | tf_op jit(solution)/shard_map/slices/pallas_call | solution.py:43
  7.3 2.1 %collective-permute-start.5 = (bf16[16,1024]{1,0:T(8,128)(2,1)S(1)}, bf16[16,1024]{1,0:T(8,128)(2,1)S(1)}, u32[]{:S(2)}, u32[]{:S(2)}) collective-permute-start(bf16[16,1024]{1,0:T(8,128)(2,1)S(1)} %get-tuple-element.46), channel_id=1, source_target_pairs={{0,17},{1,18},{2,19},{3,20},{4,21},{5,22},{6,23},{7,24},{8,25},{9,... | collective-permute-start | bytes 98312 | tf_op jit(solution)/shard_map/ppermute | solution.py:414
  9.5 2.8 %collective-permute-start.4 = (bf16[112,1024]{1,0:T(8,128)(2,1)S(1)}, bf16[112,1024]{1,0:T(8,128)(2,1)S(1)}, u32[]{:S(2)}, u32[]{:S(2)}) collective-permute-start(bf16[112,1024]{1,0:T(8,128)(2,1)S(1)} %get-tuple-element.45), channel_id=1, source_target_pairs={{0,1},{1,2},{2,3},{3,4},{4,5},{5,6},{6,7},{7,8},{8,9},{9,10},{10,1... | collective-permute-start | bytes 688136 | tf_op jit(solution)/shard_map/ppermute | solution.py:414
  12.3 5.3 %embed.1 = (bf16[512,1024]{1,0:T(8,128)(2,1)S(1)}, bf16[512,1024]{1,0:T(8,128)(2,1)S(1)}, bf16[512,1536]{1,0:T(8,128)(2,1)S(1)}) custom-call(s32[80,16]{1,0:T(8,128)S(1)} %copy.19.own, s32[80,16]{1,0:T(8,128)S(1)} %collective-permute-done.up, s32[80,16]{1,0:T(8,128)S(1)} %collective-permute-done.1.left, s32[80,16]{1,0:T(8,128)S(1)} %collective-permute-done.2.diag, ...), custom_call_target="tpu_custom_call" | custom-call | flops 2684354560 | bytes 9437184 | tf_op jit(solution)/shard_map/embed/pallas_call | solution.py:43
  18.2 5.0 %attend.2 = (bf16[512,256]{1,0:T(8,128)(2,1)S(1)}, bf16[512,768]{1,0:T(8,128)(2,1)S(1)}, f32[2,256,1024]{2,1,0:T(8,128)S(1)}, bf16[2,256,1024]{2,1,0:T(8,128)(2,1)S(1)}, bf16[512,1024]{1,0:T(8,128)(2,1)S(1)}) custom-call(s32[6]{0:T(128)S(1)} %stack.27.place, bf16[512,1536]{1,0:T(8,128)(2,1)S(1)} %get-tuple-element.42.proj, ...), custom_call_target="tpu_custom_call" | custom-call | flops 1048576 | bytes 4096 | tf_op jit(solution)/shard_map/attend/pallas_call | solution.py:43
  23.3 0.8 collective-permute-start.7
  24.0 4.4 %attend.3 = (bf16[512,256]{1,0:T(8,128)(2,1)S(1)}, bf16[512,768]{1,0:T(8,128)(2,1)S(1)}, f32[2,256,1024]{2,1,0:T(8,128)S(1)}, bf16[2,256,1024]{2,1,0:T(8,128)(2,1)S(1)}) custom-call(s32[6]{0:T(128)S(1)} %stack.27.place, bf16[512,1536]{1,0:T(8,128)(2,1)S(1)} %get-tuple-element.42.proj, bf16[512,1024]{1,0:T(8,128)(2,1)S(1)} %get-tuple-element.43.normed, ...), custom_call_target="tpu_custom_call" | custom-call | flops 1048576 | bytes 4096 | tf_op jit(solution)/shard_map/attend/pallas_call | solution.py:43
  28.5 0.7 sum_core.2
  29.3 3.6 %collective-permute-start.8 = (bf16[2,8,16,1024]{3,2,1,0:T(8,128)(2,1)S(1)}, bf16[2,8,16,1024]{3,2,1,0:T(8,128)(2,1)S(1)}, u32[]{:S(2)}, u32[]{:S(2)}) collective-permute-start(bf16[2,8,16,1024]{3,2,1,0:T(8,128)(2,1)S(1)} %get-tuple-element.57), channel_id=1, source_target_pairs={{0,1},{1,0},{2,3},{3,2},{4,5},{5,4},{6,7},{7,6},{8,9},{9,8},{10,11... | collective-permute-start | bytes 1572872 | tf_op jit(solution)/shard_map/ppermute | solution.py:414
  32.8 0.7 sum_core.3
  33.5 2.3 %collective-permute-start.14 = (bf16[2,8,16,1024]{3,2,1,0:T(8,128)(2,1)S(1)}, bf16[2,8,16,1024]{3,2,1,0:T(8,128)(2,1)S(1)}, u32[]{:S(2)}, u32[]{:S(2)}) collective-permute-start(bf16[2,8,16,1024]{3,2,1,0:T(8,128)(2,1)S(1)} %get-tuple-element.71), channel_id=1, source_target_pairs={{0,33},{1,32},{2,35},{3,34},{4,37},{5,36},{6,39},{7,38},{8,41},{9,... | collective-permute-start | bytes 1572872 | tf_op jit(solution)/shard_map/ppermute | solution.py:414
  35.8 5.2 %finish.1 = (bf16[2,448,1024]{2,1,0:T(8,128)(2,1)S(1)}, bf16[2,64,1024]{2,1,0:T(8,128)(2,1)S(1)}, bf16[2,112,1024]{2,1,0:T(8,128)(2,1)S(1)}, bf16[2,16,1024]{2,1,0:T(8,128)(2,1)S(1)}, f32[8,128]{1,0:T(8,128)S(1)}) custom-call(bf16[512,1024]{1,0:T(8,128)(2,1)S(1)} %get-tuple-element.41.emb, bf16[512,1024]{1,0:T(8,128)(2,1)S(1)} %get-tuple-element.47.cot, ...), custom_call_target="tpu_custom_call" | custom-call | flops 1048576 | bytes 4096 | tf_op jit(solution)/shard_map/finish/pallas_call | solution.py:43
  41.0 1.4 %collective-permute-start.10 = (bf16[2,16,1024]{2,1,0:T(8,128)(2,1)S(1)}, bf16[2,16,1024]{2,1,0:T(8,128)(2,1)S(1)}, u32[]{:S(2)}, u32[]{:S(2)}) collective-permute-start(bf16[2,16,1024]{2,1,0:T(8,128)(2,1)S(1)} %get-tuple-element.61), channel_id=1, source_target_pairs={{0,63},{1,48},{2,49},{3,50},{4,51},{5,52},{6,53},{7,54},{8,55},{9,... | collective-permute-start | bytes 196616 | tf_op jit(solution)/shard_map/ppermute | solution.py:414
  42.4 3.1 %collective-permute-done.8.b = bf16[2,8,16,1024]{3,2,1,0:T(8,128)(2,1)S(1)} collective-permute-done((bf16[2,8,16,1024]{3,2,1,0:T(8,128)(2,1)S(1)}, bf16[2,8,16,1024]{3,2,1,0:T(8,128)(2,1)S(1)}, u32[]{:S(2)}, u32[]{:S(2)}) %collective-permute-start.8) | collective-permute-done | bytes 524320 | tf_op jit(solution)/shard_map/ppermute | solution.py:414
  46.2 2.7 %collective-permute-start.9 = (bf16[2,112,1024]{2,1,0:T(8,128)(2,1)S(1)}, bf16[2,112,1024]{2,1,0:T(8,128)(2,1)S(1)}, u32[]{:S(2)}, u32[]{:S(2)}) collective-permute-start(bf16[2,112,1024]{2,1,0:T(8,128)(2,1)S(1)} %get-tuple-element.60), channel_id=1, source_target_pairs={{0,15},{1,0},{2,1},{3,2},{4,3},{5,4},{6,5},{7,6},{8,7},{9,8},{10,9... | collective-permute-start | bytes 1376264 | tf_op jit(solution)/shard_map/ppermute | solution.py:414
  49.7 3.1 %collective-permute-start.15 = (bf16[2,8,16,512]{3,2,1,0:T(8,128)(2,1)S(1)}, bf16[2,8,16,512]{3,2,1,0:T(8,128)(2,1)S(1)}, u32[]{:S(2)}, u32[]{:S(2)}) collective-permute-start(bf16[2,8,16,512]{3,2,1,0:T(8,128)(2,1)S(1)} %get-tuple-element.73), channel_id=1, source_target_pairs={{0,192},{64,128},{128,64},{192,0},{1,193},{65,129},{129,65},{193,1... | collective-permute-start | bytes 786440 | tf_op jit(solution)/shard_map/ppermute | solution.py:422
  52.8 4.5 %collective-permute-done.11.b = bf16[8,16,1024]{2,1,0:T(8,128)(2,1)S(1)} collective-permute-done((bf16[8,16,1024]{2,1,0:T(8,128)(2,1)S(1)}, bf16[8,16,1024]{2,1,0:T(8,128)(2,1)S(1)}, u32[]{:S(2)}, u32[]{:S(2)}) %collective-permute-start.11) | collective-permute-done | bytes 262176 | tf_op jit(solution)/shard_map/ppermute | solution.py:414
  57.9 1.7 %collective-permute-start.12 = (bf16[8,16,512]{2,1,0:T(8,128)(2,1)S(1)}, bf16[8,16,512]{2,1,0:T(8,128)(2,1)S(1)}, u32[]{:S(2)}, u32[]{:S(2)}) collective-permute-start(bf16[8,16,512]{2,1,0:T(8,128)(2,1)S(1)} %get-tuple-element.67), channel_id=1, source_target_pairs={{0,64},{64,0},{128,192},{192,128},{1,65},{65,1},{129,193},{193,129... | collective-permute-start | bytes 393224 | tf_op jit(solution)/shard_map/ppermute | solution.py:422
  60.5 2.5 %collective-permute-done.12.b = bf16[8,16,512]{2,1,0:T(8,128)(2,1)S(1)} collective-permute-done((bf16[8,16,512]{2,1,0:T(8,128)(2,1)S(1)}, bf16[8,16,512]{2,1,0:T(8,128)(2,1)S(1)}, u32[]{:S(2)}, u32[]{:S(2)}) %collective-permute-start.12) | collective-permute-done | bytes 131104 | tf_op jit(solution)/shard_map/ppermute | solution.py:422
  63.0 2.3 %collective-permute-done.16.d = bf16[8,16,512]{2,1,0:T(8,128)(2,1)S(1)} collective-permute-done((bf16[8,16,512]{2,1,0:T(8,128)(2,1)S(1)}, bf16[8,16,512]{2,1,0:T(8,128)(2,1)S(1)}, u32[]{:S(2)}, u32[]{:S(2)}) %collective-permute-start.16) | collective-permute-done | bytes 131104 | tf_op jit(solution)/shard_map/ppermute | solution.py:414
  65.2 0.7 join.1
  66.0 8.7 %all-to-all-start = ((bf16[8,16,1024]{2,1,0:T(8,128)(2,1)}), bf16[8,16,1024]{2,1,0:T(8,128)(2,1)S(1)}, u32[]{:S(2)}, u32[]{:S(2)}) async-start(bf16[8,16,1024]{2,1,0:T(8,128)(2,1)} %join.1), calls=%async_computation | async-start | bytes 524288 | tf_op jit(solution)/shard_map/all_to_all | solution.py:580
  74.7 8.9 %all-to-all-done.ref = bf16[8,16,1024]{2,1,0:T(8,128)(2,1)S(1)} async-done(((bf16[8,16,1024]{2,1,0:T(8,128)(2,1)}), bf16[8,16,1024]{2,1,0:T(8,128)(2,1)S(1)}, u32[]{:S(2)}, u32[]{:S(2)}) %all-to-all-start) | async-done | bytes 262176 | tf_op jit(solution)/shard_map/all_to_all | solution.py:580
  83.6 2.4 %collective-permute-start.19 = (bf16[16,1024]{1,0:T(8,128)(2,1)S(1)}, bf16[16,1024]{1,0:T(8,128)(2,1)S(1)}, u32[]{:S(2)}, u32[]{:S(2)}) collective-permute-start(bf16[16,1024]{1,0:T(8,128)(2,1)S(1)} %depth.1.r0), channel_id=1, source_target_pairs={{0,192},{64,128},{128,64},{192,0},{1,193},{65,129},{129,65},{193,1... | collective-permute-start | bytes 98312 | tf_op jit(solution)/shard_map/ppermute | solution.py:422
  86.5 1.3 %collective-permute-start.17 = (bf16[16,1024]{1,0:T(8,128)(2,1)S(1)}, bf16[16,1024]{1,0:T(8,128)(2,1)S(1)}, u32[]{:S(2)}, u32[]{:S(2)}) collective-permute-start(bf16[16,1024]{1,0:T(8,128)(2,1)S(1)} %depth.1.r0), channel_id=1, source_target_pairs={{0,64},{64,0},{128,192},{192,128},{1,65},{65,1},{129,193},{193,129... | collective-permute-start | bytes 98312 | tf_op jit(solution)/shard_map/ppermute | solution.py:422
  87.8 2.0 %place.1 = (bf16[512,1024]{1,0:T(8,128)(2,1)}, bf16[512,1024]{1,0:T(8,128)(2,1)}) custom-call(bf16[2,448,1024]{2,1,0:T(8,128)(2,1)S(1)} %get-tuple-element.52.mid, bf16[2,64,1024]{2,1,0:T(8,128)(2,1)S(1)} %collective-permute-done.6.up, bf16[2,112,1024]{2,1,0:T(8,128)(2,1)S(1)} %collective-permute-done.9.left.arrived, ...), custom_call_target="tpu_custom_call" | custom-call | flops 268435456 | bytes 5242880 | tf_op jit(solution)/shard_map/place/pallas_call | solution.py:43
  89.8 1.7 %collective-permute-done.18.r2 = bf16[16,1024]{1,0:T(8,128)(2,1)S(1)} collective-permute-done((bf16[16,1024]{1,0:T(8,128)(2,1)S(1)}, bf16[16,1024]{1,0:T(8,128)(2,1)S(1)}, u32[]{:S(2)}, u32[]{:S(2)}) %collective-permute-start.18) | collective-permute-done | bytes 32800 | tf_op jit(solution)/shard_map/ppermute | solution.py:422
  91.5 1.2 %level.1 = (f32[16,1536]{1,0:T(8,128)}, f32[16,512]{1,0:T(8,128)}) custom-call(s32[6]{0:T(128)S(1)} %stack.27.place, bf16[16,1024]{1,0:T(8,128)(2,1)S(1)} %depth.1.r0, bf16[16,1024]{1,0:T(8,128)(2,1)S(1)} %collective-permute-done.17.r1, bf16[16,1024]{1,0:T(8,128)(2,1)S(1)} %collective-permute-done.18.r2, bf16[16,1024]{1,0:T(8,128)(2,1)S(1)} %collective-permute-done.19.r3), custom_call_target="tpu_custom_call" | custom-call | flops 131072 | bytes 524288 | tf_op jit(solution)/shard_map/level/pallas_call | solution.py:43
  (28 shorter events, 4.3 us)
Async XLA Ops:
  1.5 8.0 %collective-permute-start.2 = (s32[80,16]{1,0:T(8,128)S(1)}, s32[80,16]{1,0:T(8,128)S(1)}, u32[]{:S(2)}, u32[]{:S(2)}) collective-permute-start(s32[80,16]{1,0:T(8,128)S(1)} %copy.19.own), channel_id=1, source_target_pairs={{0,17},{1,18},{2,19},{3,20},{4,21},{5,22},{6,23},{7,24},{8,25},{9,... | collective-permute-start | bytes 15368 | tf_op jit(solution)/shard_map/ppermute | solution.py:414
  2.5 9.8 %collective-permute-start.1 = (s32[80,16]{1,0:T(8,128)S(1)}, s32[80,16]{1,0:T(8,128)S(1)}, u32[]{:S(2)}, u32[]{:S(2)}) collective-permute-start(s32[80,16]{1,0:T(8,128)S(1)} %copy.19.own), channel_id=1, source_target_pairs={{0,1},{1,2},{2,3},{3,4},{4,5},{5,6},{6,7},{7,8},{8,9},{9,10},{10,1... | collective-permute-start | bytes 15368 | tf_op jit(solution)/shard_map/ppermute | solution.py:414
  4.4 7.9 %collective-permute-start = (s32[80,16]{1,0:T(8,128)S(1)}, s32[80,16]{1,0:T(8,128)S(1)}, u32[]{:S(2)}, u32[]{:S(2)}) collective-permute-start(s32[80,16]{1,0:T(8,128)S(1)} %copy.19.own), channel_id=1, source_target_pairs={{0,16},{1,17},{2,18},{3,19},{4,20},{5,21},{6,22},{7,23},{8,24},{9,... | collective-permute-start | bytes 15368 | tf_op jit(solution)/shard_map/ppermute | solution.py:414
  7.3 10.3 %collective-permute-start.5 = (bf16[16,1024]{1,0:T(8,128)(2,1)S(1)}, bf16[16,1024]{1,0:T(8,128)(2,1)S(1)}, u32[]{:S(2)}, u32[]{:S(2)}) collective-permute-start(bf16[16,1024]{1,0:T(8,128)(2,1)S(1)} %get-tuple-element.46), channel_id=1, source_target_pairs={{0,17},{1,18},{2,19},{3,20},{4,21},{5,22},{6,23},{7,24},{8,25},{9,... | collective-permute-start | bytes 98312 | tf_op jit(solution)/shard_map/ppermute | solution.py:414
  9.4 8.2 %collective-permute-start.3 = (bf16[64,1024]{1,0:T(8,128)(2,1)S(1)}, bf16[64,1024]{1,0:T(8,128)(2,1)S(1)}, u32[]{:S(2)}, u32[]{:S(2)}) collective-permute-start(bf16[64,1024]{1,0:T(8,128)(2,1)S(1)} %get-tuple-element.44), channel_id=1, source_target_pairs={{0,16},{1,17},{2,18},{3,19},{4,20},{5,21},{6,22},{7,23},{8,24},{9,... | collective-permute-start | bytes 393224 | tf_op jit(solution)/shard_map/ppermute | solution.py:414
  9.5 8.7 %collective-permute-start.4 = (bf16[112,1024]{1,0:T(8,128)(2,1)S(1)}, bf16[112,1024]{1,0:T(8,128)(2,1)S(1)}, u32[]{:S(2)}, u32[]{:S(2)}) collective-permute-start(bf16[112,1024]{1,0:T(8,128)(2,1)S(1)} %get-tuple-element.45), channel_id=1, source_target_pairs={{0,1},{1,2},{2,3},{3,4},{4,5},{5,6},{6,7},{7,8},{8,9},{9,10},{10,1... | collective-permute-start | bytes 688136 | tf_op jit(solution)/shard_map/ppermute | solution.py:414
  23.3 5.3 %collective-permute-start.7 = (bf16[2,256,1024]{2,1,0:T(8,128)(2,1)S(1)}, bf16[2,256,1024]{2,1,0:T(8,128)(2,1)S(1)}, u32[]{:S(2)}, u32[]{:S(2)}) collective-permute-start(bf16[2,256,1024]{2,1,0:T(8,128)(2,1)S(1)} %get-tuple-element.55), channel_id=1, source_target_pairs={{0,16},{16,0},{1,17},{17,1},{2,18},{18,2},{3,19},{19,3},{4,20},{20... | collective-permute-start | bytes 3145736 | tf_op jit(solution)/shard_map/ppermute | solution.py:422
  28.4 4.4 %collective-permute-start.13 = (bf16[2,256,1024]{2,1,0:T(8,128)(2,1)S(1)}, bf16[2,256,1024]{2,1,0:T(8,128)(2,1)S(1)}, u32[]{:S(2)}, u32[]{:S(2)}) collective-permute-start(bf16[2,256,1024]{2,1,0:T(8,128)(2,1)S(1)} %get-tuple-element.69), channel_id=1, source_target_pairs={{0,16},{16,0},{1,17},{17,1},{2,18},{18,2},{3,19},{19,3},{4,20},{20... | collective-permute-start | bytes 3145736 | tf_op jit(solution)/shard_map/ppermute | solution.py:422
  29.3 16.3 %collective-permute-start.8 = (bf16[2,8,16,1024]{3,2,1,0:T(8,128)(2,1)S(1)}, bf16[2,8,16,1024]{3,2,1,0:T(8,128)(2,1)S(1)}, u32[]{:S(2)}, u32[]{:S(2)}) collective-permute-start(bf16[2,8,16,1024]{3,2,1,0:T(8,128)(2,1)S(1)} %get-tuple-element.57), channel_id=1, source_target_pairs={{0,1},{1,0},{2,3},{3,2},{4,5},{5,4},{6,7},{7,6},{8,9},{9,8},{10,11... | collective-permute-start | bytes 1572872 | tf_op jit(solution)/shard_map/ppermute | solution.py:414
  33.5 15.5 %collective-permute-start.14 = (bf16[2,8,16,1024]{3,2,1,0:T(8,128)(2,1)S(1)}, bf16[2,8,16,1024]{3,2,1,0:T(8,128)(2,1)S(1)}, u32[]{:S(2)}, u32[]{:S(2)}) collective-permute-start(bf16[2,8,16,1024]{3,2,1,0:T(8,128)(2,1)S(1)} %get-tuple-element.71), channel_id=1, source_target_pairs={{0,33},{1,32},{2,35},{3,34},{4,37},{5,36},{6,39},{7,38},{8,41},{9,... | collective-permute-start | bytes 1572872 | tf_op jit(solution)/shard_map/ppermute | solution.py:414
  41.0 8.0 %collective-permute-start.10 = (bf16[2,16,1024]{2,1,0:T(8,128)(2,1)S(1)}, bf16[2,16,1024]{2,1,0:T(8,128)(2,1)S(1)}, u32[]{:S(2)}, u32[]{:S(2)}) collective-permute-start(bf16[2,16,1024]{2,1,0:T(8,128)(2,1)S(1)} %get-tuple-element.61), channel_id=1, source_target_pairs={{0,63},{1,48},{2,49},{3,50},{4,51},{5,52},{6,53},{7,54},{8,55},{9,... | collective-permute-start | bytes 196616 | tf_op jit(solution)/shard_map/ppermute | solution.py:414
  46.2 19.0 %collective-permute-start.9 = (bf16[2,112,1024]{2,1,0:T(8,128)(2,1)S(1)}, bf16[2,112,1024]{2,1,0:T(8,128)(2,1)S(1)}, u32[]{:S(2)}, u32[]{:S(2)}) collective-permute-start(bf16[2,112,1024]{2,1,0:T(8,128)(2,1)S(1)} %get-tuple-element.60), channel_id=1, source_target_pairs={{0,15},{1,0},{2,1},{3,2},{4,3},{5,4},{6,5},{7,6},{8,7},{9,8},{10,9... | collective-permute-start | bytes 1376264 | tf_op jit(solution)/shard_map/ppermute | solution.py:414
  49.0 8.3 %collective-permute-start.11 = (bf16[8,16,1024]{2,1,0:T(8,128)(2,1)S(1)}, bf16[8,16,1024]{2,1,0:T(8,128)(2,1)S(1)}, u32[]{:S(2)}, u32[]{:S(2)}) collective-permute-start(bf16[8,16,1024]{2,1,0:T(8,128)(2,1)S(1)} %get-tuple-element.65), channel_id=1, source_target_pairs={{0,33},{1,32},{2,35},{3,34},{4,37},{5,36},{6,39},{7,38},{8,41},{9,... | collective-permute-start | bytes 786440 | tf_op jit(solution)/shard_map/ppermute | solution.py:414
  49.7 9.9 %collective-permute-start.15 = (bf16[2,8,16,512]{3,2,1,0:T(8,128)(2,1)S(1)}, bf16[2,8,16,512]{3,2,1,0:T(8,128)(2,1)S(1)}, u32[]{:S(2)}, u32[]{:S(2)}) collective-permute-start(bf16[2,8,16,512]{3,2,1,0:T(8,128)(2,1)S(1)} %get-tuple-element.73), channel_id=1, source_target_pairs={{0,192},{64,128},{128,64},{192,0},{1,193},{65,129},{129,65},{193,1... | collective-permute-start | bytes 786440 | tf_op jit(solution)/shard_map/ppermute | solution.py:422
  57.9 5.1 %collective-permute-start.12 = (bf16[8,16,512]{2,1,0:T(8,128)(2,1)S(1)}, bf16[8,16,512]{2,1,0:T(8,128)(2,1)S(1)}, u32[]{:S(2)}, u32[]{:S(2)}) collective-permute-start(bf16[8,16,512]{2,1,0:T(8,128)(2,1)S(1)} %get-tuple-element.67), channel_id=1, source_target_pairs={{0,64},{64,0},{128,192},{192,128},{1,65},{65,1},{129,193},{193,129... | collective-permute-start | bytes 393224 | tf_op jit(solution)/shard_map/ppermute | solution.py:422
  60.2 5.1 %collective-permute-start.16 = (bf16[8,16,512]{2,1,0:T(8,128)(2,1)S(1)}, bf16[8,16,512]{2,1,0:T(8,128)(2,1)S(1)}, u32[]{:S(2)}, u32[]{:S(2)}) collective-permute-start(bf16[8,16,512]{2,1,0:T(8,128)(2,1)S(1)} %get-tuple-element.75), channel_id=1, source_target_pairs={{0,1},{1,0},{2,3},{3,2},{4,5},{5,4},{6,7},{7,6},{8,9},{9,8},{10,11... | collective-permute-start | bytes 393224 | tf_op jit(solution)/shard_map/ppermute | solution.py:414
  66.0 17.6 %all-to-all-start = ((bf16[8,16,1024]{2,1,0:T(8,128)(2,1)}), bf16[8,16,1024]{2,1,0:T(8,128)(2,1)S(1)}, u32[]{:S(2)}, u32[]{:S(2)}) async-start(bf16[8,16,1024]{2,1,0:T(8,128)(2,1)} %join.1), calls=%async_computation | async-start | bytes 524288 | tf_op jit(solution)/shard_map/all_to_all | solution.py:580
  74.7 13.1 %collective-permute-start.6 = (bf16[2,64,1024]{2,1,0:T(8,128)(2,1)S(1)}, bf16[2,64,1024]{2,1,0:T(8,128)(2,1)S(1)}, u32[]{:S(2)}, u32[]{:S(2)}) collective-permute-start(bf16[2,64,1024]{2,1,0:T(8,128)(2,1)S(1)} %get-tuple-element.53), channel_id=1, source_target_pairs={{0,48},{1,49},{2,50},{3,51},{4,52},{5,53},{6,54},{7,55},{8,56},{9,... | collective-permute-start | bytes 786440 | tf_op jit(solution)/shard_map/ppermute | solution.py:414
  83.6 6.1 %collective-permute-start.19 = (bf16[16,1024]{1,0:T(8,128)(2,1)S(1)}, bf16[16,1024]{1,0:T(8,128)(2,1)S(1)}, u32[]{:S(2)}, u32[]{:S(2)}) collective-permute-start(bf16[16,1024]{1,0:T(8,128)(2,1)S(1)} %depth.1.r0), channel_id=1, source_target_pairs={{0,192},{64,128},{128,64},{192,0},{1,193},{65,129},{129,65},{193,1... | collective-permute-start | bytes 98312 | tf_op jit(solution)/shard_map/ppermute | solution.py:422
  86.0 5.4 %collective-permute-start.18 = (bf16[16,1024]{1,0:T(8,128)(2,1)S(1)}, bf16[16,1024]{1,0:T(8,128)(2,1)S(1)}, u32[]{:S(2)}, u32[]{:S(2)}) collective-permute-start(bf16[16,1024]{1,0:T(8,128)(2,1)S(1)} %depth.1.r0), channel_id=1, source_target_pairs={{0,128},{64,192},{128,0},{192,64},{1,129},{65,193},{129,1},{193,65... | collective-permute-start | bytes 98312 | tf_op jit(solution)/shard_map/ppermute | solution.py:422
  86.5 5.0 %collective-permute-start.17 = (bf16[16,1024]{1,0:T(8,128)(2,1)S(1)}, bf16[16,1024]{1,0:T(8,128)(2,1)S(1)}, u32[]{:S(2)}, u32[]{:S(2)}) collective-permute-start(bf16[16,1024]{1,0:T(8,128)(2,1)S(1)} %depth.1.r0), channel_id=1, source_target_pairs={{0,64},{64,0},{128,192},{192,128},{1,65},{65,1},{129,193},{193,129... | collective-permute-start | bytes 98312 | tf_op jit(solution)/shard_map/ppermute | solution.py:422

commit v10 on v9

--- a/solution.py
+++ b/solution.py
@@ -105,7 +105,9 @@
     diag[...] = dot(corner, held[OWN:], 1, 0).astype(BF16)
 
 
-def embed_kernel(own, up, left, diag, bt, tt, mv, wq, emb, normed, proj, tables, masked, weight, sems):
+def embed_kernel(
+    place, own, up, left, diag, bt, tt, mv, wq, emb, normed, proj, att, share, share_bf, tables, masked, weight, sems
+):
     copies = [
         pltpu.make_async_copy(bt, tables.at[0], sems.at[0]),
         pltpu.make_async_copy(tt, tables.at[1], sems.at[1]),
@@ -157,6 +159,7 @@
         normed[here] = (centred * inverse).astype(BF16)
     copies[3].wait()
     proj[...] = dot(normed[...], weight[...], 1, 0).astype(BF16)
+    forward(0, place, proj, att, share, share_bf)
 
 
 def merge(cot, grads, up, left, diag):
@@ -171,27 +174,28 @@
         cot[64 + at : 128 + at] = values.astype(BF16)
 
 
-def attend_first(place, proj, normed, grads, up, left, diag, ow, att, gp, keep, send, cot, own, weight, sems, *held):
+def attend_first(
+    place, proj, normed, grads, up, left, diag, ow, att, share, share_bf, gp, keep, send, cot, own, weight, sems, ds
+):
     copies = [
         pltpu.make_async_copy(grads, own, sems.at[0]),
         pltpu.make_async_copy(ow.at[:, 0:CW], weight, sems.at[1]),
     ]
     for copy in copies:
         copy.start()
-    units = forward(0, place, proj, att, *held)
     copies[0].wait()
     merge(cot, own, up, left, diag)
     copies[1].wait()
-    backward(units, place, normed, cot, weight, att, gp, keep, send, *held)
+    backward(0, place, proj, normed, cot, weight, att, gp, keep, send, share, share_bf, ds)
 
 
 def attend_next(chunk, place, proj, normed, cot, ow, *refs):
     att, gp, keep, send, weight, sem, *held = refs[1:] if chunk > 1 else refs
     copy = pltpu.make_async_copy(ow.at[:, chunk * CW : (chunk + 1) * CW], weight, sem)
     copy.start()
-    units = forward(chunk, place, proj, att, *held)
+    forward(chunk, place, proj, att, *held[:2])
     copy.wait()
-    backward(units, place, normed, cot, weight, att, gp, keep, send, *held)
+    backward(chunk, place, proj, normed, cot, weight, att, gp, keep, send, *held)
 
 
 def first_lanes():
@@ -204,24 +208,29 @@
     return jnp.concatenate([jnp.where(first, x, none), jnp.where(first, none, x)], axis=0)
 
 
-def forward(chunk, place, proj, att, share, share_bf, ds):
-    tk, tq = iota((BAND, BAND), 0), iota((BAND, BAND), 1)
-
-    def side(t):
-        c = t & 15
-        return ((c >= 4) & (c < 12)).astype(jnp.int32)
-
-    same = side(tk) == side(tq)
-    whole = (tk >> 6) == (tq >> 6)
-    zero = jnp.zeros((BAND, BAND), F32)
-    plain = jnp.where(same, zero, -1e30)
-    first = jnp.where(whole | (place[0] != 0), plain, -1e30)
+def units_of(chunk, proj):
     units = []
     for p in range(CW // 128):
         for b in range(BANDS):
             here, at = slice(b * BAND, (b + 1) * BAND), chunk * CW + p * 128
             loads = [functools.partial(lambda c, h: proj[h, c : c + 128], i * HW + at, here) for i in range(3)]
             units.append((b, here, p * 128, *loads))
+    return units
+
+
+def forward(chunk, place, proj, att, share, share_bf):
+    tk, tq = iota((BAND, BAND), 0), iota((BAND, BAND), 1)
+
+    def side(t):
+        c = t & 15
+        return ((c >= 4) & (c < 12)).astype(jnp.int32)
+
+    same = side(tk) == side(tq)
+    whole = (tk >> 6) == (tq >> 6)
+    zero = jnp.zeros((BAND, BAND), F32)
+    plain = jnp.where(same, zero, -1e30)
+    first = jnp.where(whole | (place[0] != 0), plain, -1e30)
+    units = units_of(chunk, proj)
     for u, (b, here, at, q, k, v) in enumerate(units):
         share[u] = dot(split(k()), q(), 1, 1).reshape(2, BAND, BAND) * 0.125 + (first if b == 0 else plain)
     for u in range(len(units)):
@@ -232,10 +241,10 @@
         share_bf[u] = e.astype(BF16).reshape(2 * BAND, BAND)
     for u, (b, here, at, q, k, v) in enumerate(units):
         att[here, at : at + 128] = dot(share_bf[u], split(v()), 0, 0).astype(BF16)
-    return units
-
-
-def backward(units, place, normed, cot, ow, att, gp, keep, send, share, share_bf, ds):
+
+
+def backward(chunk, place, proj, normed, cot, ow, att, gp, keep, send, share, share_bf, ds):
+    units = units_of(chunk, proj)
     grad = dot(cot[...], ow[...], 1, 0).astype(BF16)
     lane = first_lanes()
 
@@ -491,11 +500,13 @@
         scratch=[pltpu.VMEM((TOKENS, MODEL), BF16), pltpu.SemaphoreType.DMA],
     )
     up, left, diag = shift(up, 1, 0), shift(left, 0, 1), shift(diag, 1, 1)
-    emb, normed, proj = call(
+    units = BANDS * CW // 128
+    score, pairs = (units, 2, BAND, BAND), (units, 2 * BAND, BAND)
+    emb, normed, proj, att, share, share_bf = call(
         embed_kernel,
-        [sds((TOKENS, MODEL)), sds((TOKENS, MODEL)), sds((TOKENS, 3 * HW))],
-        (*near, bottom_table, top_table, mask_vector, qkv_weight),
-        [vmem()] * 4 + [hbm()] * 4,
+        [sds((TOKENS, MODEL)), sds((TOKENS, MODEL)), sds((TOKENS, 3 * HW)), sds((TOKENS, CW)), sds(score, F32), sds(pairs)],
+        (place, *near, bottom_table, top_table, mask_vector, qkv_weight),
+        [smem()] + [vmem()] * 4 + [hbm()] * 4,
         2 * TOKENS * 1024 * 2560,
         9 * 2**20,
         name="embed",
@@ -506,26 +517,25 @@
             sems(4),
         ],
     )
-    outs = [sds((TOKENS, CW)), sds((TOKENS, 3 * CW)), sds((2, 256, W), F32), sds((2, 256, W))]
-    column = pltpu.VMEM((MODEL, CW), BF16)
-    units = BANDS * CW // 128
-    held = [pltpu.VMEM((units, 2, BAND, BAND), F32)] + [pltpu.VMEM((units, 2 * BAND, BAND), BF16)] * 2
-    att, gp, keep, send, cot = call(
+    outs = [sds((TOKENS, 3 * CW)), sds((2, 256, W), F32), sds((2, 256, W))]
+    column, ds = pltpu.VMEM((MODEL, CW), BF16), pltpu.VMEM(pairs, BF16)
+    held = [pltpu.VMEM(score, F32), pltpu.VMEM(pairs, BF16), ds]
+    gp, keep, send, cot = call(
         attend_first,
         outs + [sds((TOKENS, MODEL))],
-        (place, proj, normed, grads, up, left, diag, out_weight),
-        [smem(), vmem(), vmem(), hbm(), vmem(), vmem(), vmem(), hbm()],
+        (place, proj, normed, grads, up, left, diag, out_weight, att, share, share_bf),
+        [smem(), vmem(), vmem(), hbm(), vmem(), vmem(), vmem(), hbm(), vmem(), vmem(), vmem()],
         2**20,
         2**12,
         name="attend",
-        scratch=[pltpu.VMEM((TOKENS, MODEL), BF16), column, sems(2), *held],
+        scratch=[pltpu.VMEM((TOKENS, MODEL), BF16), column, sems(2), ds],
     )
     parts, cores = [(att, gp)], [sum_core(place, keep, send, 0)]
     for c in range(1, CHUNKS):
         after = [cores[c - 2][0]] if c > 1 else []
         att, gp, keep, send = call(
             functools.partial(attend_next, c),
-            outs,
+            [sds((TOKENS, CW))] + outs,
             (place, proj, normed, cot, out_weight, *after),
             [smem(), vmem(), vmem(), vmem(), hbm()] + [anywhere()] * len(after),
             2**20,

time: 93.9 us -> 94 us (level)
  Pallas kernels: 29.4 us -> 30.7 us
  waiting for transfers between devices: 23.6 us -> 22.5 us
    pallas_call x15, Pallas kernels: 29.4 us -> 30.7 us  [call(): pl.pallas_call(kernel, out_shape=outs, in_specs=specs, out_specs=jax.tree...]
    ppermute x13, waiting for transfers between devices: 10.5 us -> 9.44 us  [permute(): return lax.ppermute(x, GRID, pairs)]
  transfers between devices with their start and end apart: 21 -> 21, of which waited for: 7 -> 6; matrix products, arithmetic and copies ran while one was open for 0% -> 0% of each run, Pallas kernels for 24% -> 26%
where the time goes in v10:
time: 94 us; the launch traced here: 92.7 us
  starting transfers between devices  37.8 us (40%)
  Pallas kernels  30.7 us (33%)
  waiting for transfers between devices  22.5 us (24%)
    pallas_call x15, Pallas kernels, call(): pl.pallas_call(kernel, out_shape=outs, in_specs=specs, out_specs=jax.tree...  30.7 us
    ppermute x13, starting transfers between devices, permute(): return lax.ppermute(x, GRID, pairs)  19.3 us
    ppermute x7, starting transfers between devices, swap(): lax.ppermute(x, axis, [(i, i ^ flip) for i in range(lax.axis_size(axis))])  9.8 us
    ppermute x13, waiting for transfers between devices, permute(): return lax.ppermute(x, GRID, pairs)  9.44 us
    all_to_all x1, starting transfers between devices, shards(): depth = lax.all_to_all(joined, 'z', 0, 0, tiled=True)  8.7 us
    all_to_all x1, waiting for transfers between devices, shards(): depth = lax.all_to_all(joined, 'z', 0, 0, tiled=True)  8.67 us
    ppermute x7, waiting for transfers between devices, swap(): lax.ppermute(x, axis, [(i, i ^ flip) for i in range(lax.axis_size(axis))])  4.42 us
  transfers between devices with their start and end apart: 21, of which 6 were waited for; matrix products, arithmetic and copies ran while one was open for 0% of the time, Pallas kernels for 26%

profile of v10, /device:TPU:32, one launch (start us, length us, event | category | flops | bytes accessed | tf_op | source)
XLA Modules:
  0.0 92.7 jit_solution(1833723150910168624)
XLA Ops:
  0.6 0.8 pad_add_fusion
  1.5 1.0 %collective-permute-start.2 = (s32[80,16]{1,0:T(8,128)S(1)}, s32[80,16]{1,0:T(8,128)S(1)}, u32[]{:S(2)}, u32[]{:S(2)}) collective-permute-start(s32[80,16]{1,0:T(8,128)S(1)} %copy.19.own), channel_id=1, source_target_pairs={{0,17},{1,18},{2,19},{3,20},{4,21},{5,22},{6,23},{7,24},{8,25},{9,... | collective-permute-start | bytes 15368 | tf_op jit(solution)/shard_map/ppermute | solution.py:423
  2.5 1.9 %collective-permute-start.1 = (s32[80,16]{1,0:T(8,128)S(1)}, s32[80,16]{1,0:T(8,128)S(1)}, u32[]{:S(2)}, u32[]{:S(2)}) collective-permute-start(s32[80,16]{1,0:T(8,128)S(1)} %copy.19.own), channel_id=1, source_target_pairs={{0,1},{1,2},{2,3},{3,4},{4,5},{5,6},{6,7},{7,8},{8,9},{9,10},{10,1... | collective-permute-start | bytes 15368 | tf_op jit(solution)/shard_map/ppermute | solution.py:423
  4.4 1.4 %collective-permute-start = (s32[80,16]{1,0:T(8,128)S(1)}, s32[80,16]{1,0:T(8,128)S(1)}, u32[]{:S(2)}, u32[]{:S(2)}) collective-permute-start(s32[80,16]{1,0:T(8,128)S(1)} %copy.19.own), channel_id=1, source_target_pairs={{0,16},{1,17},{2,18},{3,19},{4,20},{5,21},{6,22},{7,23},{8,24},{9,... | collective-permute-start | bytes 15368 | tf_op jit(solution)/shard_map/ppermute | solution.py:423
  5.8 1.6 %slices.1 = (bf16[64,1024]{1,0:T(8,128)(2,1)S(1)}, bf16[112,1024]{1,0:T(8,128)(2,1)S(1)}, bf16[16,1024]{1,0:T(8,128)(2,1)S(1)}) custom-call(bf16[512,1024]{1,0:T(8,128)(2,1)} %bitcast.20), custom_call_target="tpu_custom_call" | custom-call | flops 268435456 | bytes 2097152 | tf_op jit(solution)/shard_map/slices/pallas_call | solution.py:43
  7.3 2.1 %collective-permute-start.5 = (bf16[16,1024]{1,0:T(8,128)(2,1)S(1)}, bf16[16,1024]{1,0:T(8,128)(2,1)S(1)}, u32[]{:S(2)}, u32[]{:S(2)}) collective-permute-start(bf16[16,1024]{1,0:T(8,128)(2,1)S(1)} %get-tuple-element.48), channel_id=1, source_target_pairs={{0,17},{1,18},{2,19},{3,20},{4,21},{5,22},{6,23},{7,24},{8,25},{9,... | collective-permute-start | bytes 98312 | tf_op jit(solution)/shard_map/ppermute | solution.py:423
  9.5 2.8 %collective-permute-start.4 = (bf16[112,1024]{1,0:T(8,128)(2,1)S(1)}, bf16[112,1024]{1,0:T(8,128)(2,1)S(1)}, u32[]{:S(2)}, u32[]{:S(2)}) collective-permute-start(bf16[112,1024]{1,0:T(8,128)(2,1)S(1)} %get-tuple-element.47), channel_id=1, source_target_pairs={{0,1},{1,2},{2,3},{3,4},{4,5},{5,6},{6,7},{7,8},{8,9},{9,10},{10,1... | collective-permute-start | bytes 688136 | tf_op jit(solution)/shard_map/ppermute | solution.py:423
  12.3 6.5 %embed.1 = (bf16[512,1024]{1,0:T(8,128)(2,1)S(1)}, bf16[512,1024]{1,0:T(8,128)(2,1)S(1)}, bf16[512,1536]{1,0:T(8,128)(2,1)S(1)}, bf16[512,256]{1,0:T(8,128)(2,1)...) custom-call(s32[6]{0:T(128)S(1)} %stack.27.place, s32[80,16]{1,0:T(8,128)S(1)} %copy.19.own, ...), custom_call_target="tpu_custom_call" | custom-call | flops 2684354560 | bytes 9437184 | tf_op jit(solution)/shard_map/embed/pallas_call | solution.py:43
  18.9 5.0 %attend.2 = (bf16[512,768]{1,0:T(8,128)(2,1)S(1)}, f32[2,256,1024]{2,1,0:T(8,128)S(1)}, bf16[2,256,1024]{2,1,0:T(8,128)(2,1)S(1)}, bf16[512,1024]{1,0:T(8,128)(2,1)S(1)}) custom-call(s32[6]{0:T(128)S(1)} %stack.27.place, bf16[512,1536]{1,0:T(8,128)(2,1)S(1)} %get-tuple-element.44.proj, bf16[512,1024]{1,0:T(8,128)(2,1)S(1)} %get-tuple-element.45.normed, ...), custom_call_target="tpu_custom_call" | custom-call | flops 1048576 | bytes 4096 | tf_op jit(solution)/shard_map/attend/pallas_call | solution.py:43
  24.2 4.4 %attend.3 = (bf16[512,256]{1,0:T(8,128)(2,1)S(1)}, bf16[512,768]{1,0:T(8,128)(2,1)S(1)}, f32[2,256,1024]{2,1,0:T(8,128)S(1)}, bf16[2,256,1024]{2,1,0:T(8,128)(2,1)S(1)}) custom-call(s32[6]{0:T(128)S(1)} %stack.27.place, bf16[512,1536]{1,0:T(8,128)(2,1)S(1)} %get-tuple-element.44.proj, bf16[512,1024]{1,0:T(8,128)(2,1)S(1)} %get-tuple-element.45.normed, ...), custom_call_target="tpu_custom_call" | custom-call | flops 1048576 | bytes 4096 | tf_op jit(solution)/shard_map/attend/pallas_call | solution.py:43
  29.2 0.7 sum_core.2
  29.9 3.0 %collective-permute-start.8 = (bf16[2,8,16,1024]{3,2,1,0:T(8,128)(2,1)S(1)}, bf16[2,8,16,1024]{3,2,1,0:T(8,128)(2,1)S(1)}, u32[]{:S(2)}, u32[]{:S(2)}) collective-permute-start(bf16[2,8,16,1024]{3,2,1,0:T(8,128)(2,1)S(1)} %get-tuple-element.61), channel_id=1, source_target_pairs={{0,1},{1,0},{2,3},{3,2},{4,5},{5,4},{6,7},{7,6},{8,9},{9,8},{10,11... | collective-permute-start | bytes 1572872 | tf_op jit(solution)/shard_map/ppermute | solution.py:423
  32.9 0.7 sum_core.3
  33.6 2.2 %collective-permute-start.14 = (bf16[2,8,16,1024]{3,2,1,0:T(8,128)(2,1)S(1)}, bf16[2,8,16,1024]{3,2,1,0:T(8,128)(2,1)S(1)}, u32[]{:S(2)}, u32[]{:S(2)}) collective-permute-start(bf16[2,8,16,1024]{3,2,1,0:T(8,128)(2,1)S(1)} %get-tuple-element.75), channel_id=1, source_target_pairs={{0,33},{1,32},{2,35},{3,34},{4,37},{5,36},{6,39},{7,38},{8,41},{9,... | collective-permute-start | bytes 1572872 | tf_op jit(solution)/shard_map/ppermute | solution.py:423
  35.8 5.2 %finish.1 = (bf16[2,448,1024]{2,1,0:T(8,128)(2,1)S(1)}, bf16[2,64,1024]{2,1,0:T(8,128)(2,1)S(1)}, bf16[2,112,1024]{2,1,0:T(8,128)(2,1)S(1)}, bf16[2,16,1024]{2,1,0:T(8,128)(2,1)S(1)}, f32[8,128]{1,0:T(8,128)S(1)}) custom-call(bf16[512,1024]{1,0:T(8,128)(2,1)S(1)} %get-tuple-element.43.emb, bf16[512,1024]{1,0:T(8,128)(2,1)S(1)} %get-tuple-element.52.cot, ...), custom_call_target="tpu_custom_call" | custom-call | flops 1048576 | bytes 4096 | tf_op jit(solution)/shard_map/finish/pallas_call | solution.py:43
  41.1 1.4 %collective-permute-start.10 = (bf16[2,16,1024]{2,1,0:T(8,128)(2,1)S(1)}, bf16[2,16,1024]{2,1,0:T(8,128)(2,1)S(1)}, u32[]{:S(2)}, u32[]{:S(2)}) collective-permute-start(bf16[2,16,1024]{2,1,0:T(8,128)(2,1)S(1)} %get-tuple-element.65), channel_id=1, source_target_pairs={{0,63},{1,48},{2,49},{3,50},{4,51},{5,52},{6,53},{7,54},{8,55},{9,... | collective-permute-start | bytes 196616 | tf_op jit(solution)/shard_map/ppermute | solution.py:423
  42.5 3.1 %collective-permute-done.8.b = bf16[2,8,16,1024]{3,2,1,0:T(8,128)(2,1)S(1)} collective-permute-done((bf16[2,8,16,1024]{3,2,1,0:T(8,128)(2,1)S(1)}, bf16[2,8,16,1024]{3,2,1,0:T(8,128)(2,1)S(1)}, u32[]{:S(2)}, u32[]{:S(2)}) %collective-permute-start.8) | collective-permute-done | bytes 524320 | tf_op jit(solution)/shard_map/ppermute | solution.py:423
  45.6 0.7 sum_pair.2
  46.3 2.7 %collective-permute-start.9 = (bf16[2,112,1024]{2,1,0:T(8,128)(2,1)S(1)}, bf16[2,112,1024]{2,1,0:T(8,128)(2,1)S(1)}, u32[]{:S(2)}, u32[]{:S(2)}) collective-permute-start(bf16[2,112,1024]{2,1,0:T(8,128)(2,1)S(1)} %get-tuple-element.64), channel_id=1, source_target_pairs={{0,15},{1,0},{2,1},{3,2},{4,3},{5,4},{6,5},{7,6},{8,7},{9,8},{10,9... | collective-permute-start | bytes 1376264 | tf_op jit(solution)/shard_map/ppermute | solution.py:423
  50.2 3.1 %collective-permute-start.15 = (bf16[2,8,16,512]{3,2,1,0:T(8,128)(2,1)S(1)}, bf16[2,8,16,512]{3,2,1,0:T(8,128)(2,1)S(1)}, u32[]{:S(2)}, u32[]{:S(2)}) collective-permute-start(bf16[2,8,16,512]{3,2,1,0:T(8,128)(2,1)S(1)} %get-tuple-element.77), channel_id=1, source_target_pairs={{0,192},{64,128},{128,64},{192,0},{1,193},{65,129},{129,65},{193,1... | collective-permute-start | bytes 786440 | tf_op jit(solution)/shard_map/ppermute | solution.py:431
  53.3 4.0 %collective-permute-done.11.b = bf16[8,16,1024]{2,1,0:T(8,128)(2,1)S(1)} collective-permute-done((bf16[8,16,1024]{2,1,0:T(8,128)(2,1)S(1)}, bf16[8,16,1024]{2,1,0:T(8,128)(2,1)S(1)}, u32[]{:S(2)}, u32[]{:S(2)}) %collective-permute-start.11) | collective-permute-done | bytes 262176 | tf_op jit(solution)/shard_map/ppermute | solution.py:423
  57.9 1.7 %collective-permute-start.12 = (bf16[8,16,512]{2,1,0:T(8,128)(2,1)S(1)}, bf16[8,16,512]{2,1,0:T(8,128)(2,1)S(1)}, u32[]{:S(2)}, u32[]{:S(2)}) collective-permute-start(bf16[8,16,512]{2,1,0:T(8,128)(2,1)S(1)} %get-tuple-element.71), channel_id=1, source_target_pairs={{0,64},{64,0},{128,192},{192,128},{1,65},{65,1},{129,193},{193,129... | collective-permute-start | bytes 393224 | tf_op jit(solution)/shard_map/ppermute | solution.py:431
  60.5 2.5 %collective-permute-done.12.b = bf16[8,16,512]{2,1,0:T(8,128)(2,1)S(1)} collective-permute-done((bf16[8,16,512]{2,1,0:T(8,128)(2,1)S(1)}, bf16[8,16,512]{2,1,0:T(8,128)(2,1)S(1)}, u32[]{:S(2)}, u32[]{:S(2)}) %collective-permute-start.12) | collective-permute-done | bytes 131104 | tf_op jit(solution)/shard_map/ppermute | solution.py:431
  63.0 2.3 %collective-permute-done.16.d = bf16[8,16,512]{2,1,0:T(8,128)(2,1)S(1)} collective-permute-done((bf16[8,16,512]{2,1,0:T(8,128)(2,1)S(1)}, bf16[8,16,512]{2,1,0:T(8,128)(2,1)S(1)}, u32[]{:S(2)}, u32[]{:S(2)}) %collective-permute-start.16) | collective-permute-done | bytes 131104 | tf_op jit(solution)/shard_map/ppermute | solution.py:423
  65.3 0.7 join.1
  66.0 8.7 %all-to-all-start = ((bf16[8,16,1024]{2,1,0:T(8,128)(2,1)}), bf16[8,16,1024]{2,1,0:T(8,128)(2,1)S(1)}, u32[]{:S(2)}, u32[]{:S(2)}) async-start(bf16[8,16,1024]{2,1,0:T(8,128)(2,1)} %join.1), calls=%async_computation | async-start | bytes 524288 | tf_op jit(solution)/shard_map/all_to_all | solution.py:590
  74.7 8.7 %all-to-all-done.ref = bf16[8,16,1024]{2,1,0:T(8,128)(2,1)S(1)} async-done(((bf16[8,16,1024]{2,1,0:T(8,128)(2,1)}), bf16[8,16,1024]{2,1,0:T(8,128)(2,1)S(1)}, u32[]{:S(2)}, u32[]{:S(2)}) %all-to-all-start) | async-done | bytes 262176 | tf_op jit(solution)/shard_map/all_to_all | solution.py:590
  83.4 2.6 %collective-permute-start.19 = (bf16[16,1024]{1,0:T(8,128)(2,1)S(1)}, bf16[16,1024]{1,0:T(8,128)(2,1)S(1)}, u32[]{:S(2)}, u32[]{:S(2)}) collective-permute-start(bf16[16,1024]{1,0:T(8,128)(2,1)S(1)} %depth.1.r0), channel_id=1, source_target_pairs={{0,192},{64,128},{128,64},{192,0},{1,193},{65,129},{129,65},{193,1... | collective-permute-start | bytes 98312 | tf_op jit(solution)/shard_map/ppermute | solution.py:431
  86.6 1.1 %collective-permute-start.17 = (bf16[16,1024]{1,0:T(8,128)(2,1)S(1)}, bf16[16,1024]{1,0:T(8,128)(2,1)S(1)}, u32[]{:S(2)}, u32[]{:S(2)}) collective-permute-start(bf16[16,1024]{1,0:T(8,128)(2,1)S(1)} %depth.1.r0), channel_id=1, source_target_pairs={{0,64},{64,0},{128,192},{192,128},{1,65},{65,1},{129,193},{193,129... | collective-permute-start | bytes 98312 | tf_op jit(solution)/shard_map/ppermute | solution.py:431
  87.6 2.0 %place.1 = (bf16[512,1024]{1,0:T(8,128)(2,1)}, bf16[512,1024]{1,0:T(8,128)(2,1)}) custom-call(bf16[2,448,1024]{2,1,0:T(8,128)(2,1)S(1)} %get-tuple-element.56.mid, bf16[2,64,1024]{2,1,0:T(8,128)(2,1)S(1)} %collective-permute-done.6.up, bf16[2,112,1024]{2,1,0:T(8,128)(2,1)S(1)} %collective-permute-done.9.left.arrived, ...), custom_call_target="tpu_custom_call" | custom-call | flops 268435456 | bytes 5242880 | tf_op jit(solution)/shard_map/place/pallas_call | solution.py:43
  89.6 1.9 %collective-permute-done.18.r2 = bf16[16,1024]{1,0:T(8,128)(2,1)S(1)} collective-permute-done((bf16[16,1024]{1,0:T(8,128)(2,1)S(1)}, bf16[16,1024]{1,0:T(8,128)(2,1)S(1)}, u32[]{:S(2)}, u32[]{:S(2)}) %collective-permute-start.18) | collective-permute-done | bytes 32800 | tf_op jit(solution)/shard_map/ppermute | solution.py:431
  91.5 1.2 %level.1 = (f32[16,1536]{1,0:T(8,128)}, f32[16,512]{1,0:T(8,128)}) custom-call(s32[6]{0:T(128)S(1)} %stack.27.place, bf16[16,1024]{1,0:T(8,128)(2,1)S(1)} %depth.1.r0, bf16[16,1024]{1,0:T(8,128)(2,1)S(1)} %collective-permute-done.17.r1, bf16[16,1024]{1,0:T(8,128)(2,1)S(1)} %collective-permute-done.18.r2, bf16[16,1024]{1,0:T(8,128)(2,1)S(1)} %collective-permute-done.19.r3), custom_call_target="tpu_custom_call" | custom-call | flops 131072 | bytes 524288 | tf_op jit(solution)/shard_map/level/pallas_call | solution.py:43
  (28 shorter events, 4.3 us)
Async XLA Ops:
  1.5 8.0 %collective-permute-start.2 = (s32[80,16]{1,0:T(8,128)S(1)}, s32[80,16]{1,0:T(8,128)S(1)}, u32[]{:S(2)}, u32[]{:S(2)}) collective-permute-start(s32[80,16]{1,0:T(8,128)S(1)} %copy.19.own), channel_id=1, source_target_pairs={{0,17},{1,18},{2,19},{3,20},{4,21},{5,22},{6,23},{7,24},{8,25},{9,... | collective-permute-start | bytes 15368 | tf_op jit(solution)/shard_map/ppermute | solution.py:423
  2.5 9.8 %collective-permute-start.1 = (s32[80,16]{1,0:T(8,128)S(1)}, s32[80,16]{1,0:T(8,128)S(1)}, u32[]{:S(2)}, u32[]{:S(2)}) collective-permute-start(s32[80,16]{1,0:T(8,128)S(1)} %copy.19.own), channel_id=1, source_target_pairs={{0,1},{1,2},{2,3},{3,4},{4,5},{5,6},{6,7},{7,8},{8,9},{9,10},{10,1... | collective-permute-start | bytes 15368 | tf_op jit(solution)/shard_map/ppermute | solution.py:423
  4.4 7.9 %collective-permute-start = (s32[80,16]{1,0:T(8,128)S(1)}, s32[80,16]{1,0:T(8,128)S(1)}, u32[]{:S(2)}, u32[]{:S(2)}) collective-permute-start(s32[80,16]{1,0:T(8,128)S(1)} %copy.19.own), channel_id=1, source_target_pairs={{0,16},{1,17},{2,18},{3,19},{4,20},{5,21},{6,22},{7,23},{8,24},{9,... | collective-permute-start | bytes 15368 | tf_op jit(solution)/shard_map/ppermute | solution.py:423
  7.3 11.5 %collective-permute-start.5 = (bf16[16,1024]{1,0:T(8,128)(2,1)S(1)}, bf16[16,1024]{1,0:T(8,128)(2,1)S(1)}, u32[]{:S(2)}, u32[]{:S(2)}) collective-permute-start(bf16[16,1024]{1,0:T(8,128)(2,1)S(1)} %get-tuple-element.48), channel_id=1, source_target_pairs={{0,17},{1,18},{2,19},{3,20},{4,21},{5,22},{6,23},{7,24},{8,25},{9,... | collective-permute-start | bytes 98312 | tf_op jit(solution)/shard_map/ppermute | solution.py:423
  9.4 9.4 %collective-permute-start.3 = (bf16[64,1024]{1,0:T(8,128)(2,1)S(1)}, bf16[64,1024]{1,0:T(8,128)(2,1)S(1)}, u32[]{:S(2)}, u32[]{:S(2)}) collective-permute-start(bf16[64,1024]{1,0:T(8,128)(2,1)S(1)} %get-tuple-element.46), channel_id=1, source_target_pairs={{0,16},{1,17},{2,18},{3,19},{4,20},{5,21},{6,22},{7,23},{8,24},{9,... | collective-permute-start | bytes 393224 | tf_op jit(solution)/shard_map/ppermute | solution.py:423
  9.5 9.4 %collective-permute-start.4 = (bf16[112,1024]{1,0:T(8,128)(2,1)S(1)}, bf16[112,1024]{1,0:T(8,128)(2,1)S(1)}, u32[]{:S(2)}, u32[]{:S(2)}) collective-permute-start(bf16[112,1024]{1,0:T(8,128)(2,1)S(1)} %get-tuple-element.47), channel_id=1, source_target_pairs={{0,1},{1,2},{2,3},{3,4},{4,5},{5,6},{6,7},{7,8},{8,9},{9,10},{10,1... | collective-permute-start | bytes 688136 | tf_op jit(solution)/shard_map/ppermute | solution.py:423
  23.9 5.3 %collective-permute-start.7 = (bf16[2,256,1024]{2,1,0:T(8,128)(2,1)S(1)}, bf16[2,256,1024]{2,1,0:T(8,128)(2,1)S(1)}, u32[]{:S(2)}, u32[]{:S(2)}) collective-permute-start(bf16[2,256,1024]{2,1,0:T(8,128)(2,1)S(1)} %get-tuple-element.59), channel_id=1, source_target_pairs={{0,16},{16,0},{1,17},{17,1},{2,18},{18,2},{3,19},{19,3},{4,20},{20... | collective-permute-start | bytes 3145736 | tf_op jit(solution)/shard_map/ppermute | solution.py:431
  28.6 4.3 %collective-permute-start.13 = (bf16[2,256,1024]{2,1,0:T(8,128)(2,1)S(1)}, bf16[2,256,1024]{2,1,0:T(8,128)(2,1)S(1)}, u32[]{:S(2)}, u32[]{:S(2)}) collective-permute-start(bf16[2,256,1024]{2,1,0:T(8,128)(2,1)S(1)} %get-tuple-element.73), channel_id=1, source_target_pairs={{0,16},{16,0},{1,17},{17,1},{2,18},{18,2},{3,19},{19,3},{4,20},{20... | collective-permute-start | bytes 3145736 | tf_op jit(solution)/shard_map/ppermute | solution.py:431
  29.9 15.7 %collective-permute-start.8 = (bf16[2,8,16,1024]{3,2,1,0:T(8,128)(2,1)S(1)}, bf16[2,8,16,1024]{3,2,1,0:T(8,128)(2,1)S(1)}, u32[]{:S(2)}, u32[]{:S(2)}) collective-permute-start(bf16[2,8,16,1024]{3,2,1,0:T(8,128)(2,1)S(1)} %get-tuple-element.61), channel_id=1, source_target_pairs={{0,1},{1,0},{2,3},{3,2},{4,5},{5,4},{6,7},{7,6},{8,9},{9,8},{10,11... | collective-permute-start | bytes 1572872 | tf_op jit(solution)/shard_map/ppermute | solution.py:423
  33.6 15.9 %collective-permute-start.14 = (bf16[2,8,16,1024]{3,2,1,0:T(8,128)(2,1)S(1)}, bf16[2,8,16,1024]{3,2,1,0:T(8,128)(2,1)S(1)}, u32[]{:S(2)}, u32[]{:S(2)}) collective-permute-start(bf16[2,8,16,1024]{3,2,1,0:T(8,128)(2,1)S(1)} %get-tuple-element.75), channel_id=1, source_target_pairs={{0,33},{1,32},{2,35},{3,34},{4,37},{5,36},{6,39},{7,38},{8,41},{9,... | collective-permute-start | bytes 1572872 | tf_op jit(solution)/shard_map/ppermute | solution.py:423
  41.1 8.5 %collective-permute-start.10 = (bf16[2,16,1024]{2,1,0:T(8,128)(2,1)S(1)}, bf16[2,16,1024]{2,1,0:T(8,128)(2,1)S(1)}, u32[]{:S(2)}, u32[]{:S(2)}) collective-permute-start(bf16[2,16,1024]{2,1,0:T(8,128)(2,1)S(1)} %get-tuple-element.65), channel_id=1, source_target_pairs={{0,63},{1,48},{2,49},{3,50},{4,51},{5,52},{6,53},{7,54},{8,55},{9,... | collective-permute-start | bytes 196616 | tf_op jit(solution)/shard_map/ppermute | solution.py:423
  46.3 19.0 %collective-permute-start.9 = (bf16[2,112,1024]{2,1,0:T(8,128)(2,1)S(1)}, bf16[2,112,1024]{2,1,0:T(8,128)(2,1)S(1)}, u32[]{:S(2)}, u32[]{:S(2)}) collective-permute-start(bf16[2,112,1024]{2,1,0:T(8,128)(2,1)S(1)} %get-tuple-element.64), channel_id=1, source_target_pairs={{0,15},{1,0},{2,1},{3,2},{4,3},{5,4},{6,5},{7,6},{8,7},{9,8},{10,9... | collective-permute-start | bytes 1376264 | tf_op jit(solution)/shard_map/ppermute | solution.py:423
  49.0 8.3 %collective-permute-start.11 = (bf16[8,16,1024]{2,1,0:T(8,128)(2,1)S(1)}, bf16[8,16,1024]{2,1,0:T(8,128)(2,1)S(1)}, u32[]{:S(2)}, u32[]{:S(2)}) collective-permute-start(bf16[8,16,1024]{2,1,0:T(8,128)(2,1)S(1)} %get-tuple-element.69), channel_id=1, source_target_pairs={{0,33},{1,32},{2,35},{3,34},{4,37},{5,36},{6,39},{7,38},{8,41},{9,... | collective-permute-start | bytes 786440 | tf_op jit(solution)/shard_map/ppermute | solution.py:423
  50.2 9.4 %collective-permute-start.15 = (bf16[2,8,16,512]{3,2,1,0:T(8,128)(2,1)S(1)}, bf16[2,8,16,512]{3,2,1,0:T(8,128)(2,1)S(1)}, u32[]{:S(2)}, u32[]{:S(2)}) collective-permute-start(bf16[2,8,16,512]{3,2,1,0:T(8,128)(2,1)S(1)} %get-tuple-element.77), channel_id=1, source_target_pairs={{0,192},{64,128},{128,64},{192,0},{1,193},{65,129},{129,65},{193,1... | collective-permute-start | bytes 786440 | tf_op jit(solution)/shard_map/ppermute | solution.py:431
  57.9 5.1 %collective-permute-start.12 = (bf16[8,16,512]{2,1,0:T(8,128)(2,1)S(1)}, bf16[8,16,512]{2,1,0:T(8,128)(2,1)S(1)}, u32[]{:S(2)}, u32[]{:S(2)}) collective-permute-start(bf16[8,16,512]{2,1,0:T(8,128)(2,1)S(1)} %get-tuple-element.71), channel_id=1, source_target_pairs={{0,64},{64,0},{128,192},{192,128},{1,65},{65,1},{129,193},{193,129... | collective-permute-start | bytes 393224 | tf_op jit(solution)/shard_map/ppermute | solution.py:431
  60.2 5.1 %collective-permute-start.16 = (bf16[8,16,512]{2,1,0:T(8,128)(2,1)S(1)}, bf16[8,16,512]{2,1,0:T(8,128)(2,1)S(1)}, u32[]{:S(2)}, u32[]{:S(2)}) collective-permute-start(bf16[8,16,512]{2,1,0:T(8,128)(2,1)S(1)} %get-tuple-element.79), channel_id=1, source_target_pairs={{0,1},{1,0},{2,3},{3,2},{4,5},{5,4},{6,7},{7,6},{8,9},{9,8},{10,11... | collective-permute-start | bytes 393224 | tf_op jit(solution)/shard_map/ppermute | solution.py:423
  66.0 17.4 %all-to-all-start = ((bf16[8,16,1024]{2,1,0:T(8,128)(2,1)}), bf16[8,16,1024]{2,1,0:T(8,128)(2,1)S(1)}, u32[]{:S(2)}, u32[]{:S(2)}) async-start(bf16[8,16,1024]{2,1,0:T(8,128)(2,1)} %join.1), calls=%async_computation | async-start | bytes 524288 | tf_op jit(solution)/shard_map/all_to_all | solution.py:590
  74.7 12.9 %collective-permute-start.6 = (bf16[2,64,1024]{2,1,0:T(8,128)(2,1)S(1)}, bf16[2,64,1024]{2,1,0:T(8,128)(2,1)S(1)}, u32[]{:S(2)}, u32[]{:S(2)}) collective-permute-start(bf16[2,64,1024]{2,1,0:T(8,128)(2,1)S(1)} %get-tuple-element.57), channel_id=1, source_target_pairs={{0,48},{1,49},{2,50},{3,51},{4,52},{5,53},{6,54},{7,55},{8,56},{9,... | collective-permute-start | bytes 786440 | tf_op jit(solution)/shard_map/ppermute | solution.py:423
  83.4 6.1 %collective-permute-start.19 = (bf16[16,1024]{1,0:T(8,128)(2,1)S(1)}, bf16[16,1024]{1,0:T(8,128)(2,1)S(1)}, u32[]{:S(2)}, u32[]{:S(2)}) collective-permute-start(bf16[16,1024]{1,0:T(8,128)(2,1)S(1)} %depth.1.r0), channel_id=1, source_target_pairs={{0,192},{64,128},{128,64},{192,0},{1,193},{65,129},{129,65},{193,1... | collective-permute-start | bytes 98312 | tf_op jit(solution)/shard_map/ppermute | solution.py:431
  86.1 5.4 %collective-permute-start.18 = (bf16[16,1024]{1,0:T(8,128)(2,1)S(1)}, bf16[16,1024]{1,0:T(8,128)(2,1)S(1)}, u32[]{:S(2)}, u32[]{:S(2)}) collective-permute-start(bf16[16,1024]{1,0:T(8,128)(2,1)S(1)} %depth.1.r0), channel_id=1, source_target_pairs={{0,128},{64,192},{128,0},{192,64},{1,129},{65,193},{129,1},{193,65... | collective-permute-start | bytes 98312 | tf_op jit(solution)/shard_map/ppermute | solution.py:431
  86.6 5.0 %collective-permute-start.17 = (bf16[16,1024]{1,0:T(8,128)(2,1)S(1)}, bf16[16,1024]{1,0:T(8,128)(2,1)S(1)}, u32[]{:S(2)}, u32[]{:S(2)}) collective-permute-start(bf16[16,1024]{1,0:T(8,128)(2,1)S(1)} %depth.1.r0), channel_id=1, source_target_pairs={{0,64},{64,0},{128,192},{192,128},{1,65},{65,1},{129,193},{193,129... | collective-permute-start | bytes 98312 | tf_op jit(solution)/shard_map/ppermute | solution.py:431

commit v11 on v10

--- a/solution.py
+++ b/solution.py
@@ -105,14 +105,14 @@
     diag[...] = dot(corner, held[OWN:], 1, 0).astype(BF16)
 
 
-def embed_kernel(
-    place, own, up, left, diag, bt, tt, mv, wq, emb, normed, proj, att, share, share_bf, tables, masked, weight, sems
-):
+def embed_kernel(place, own, up, left, diag, bt, tt, mv, wq, ow, *refs):
+    emb, normed, proj, att, share, share_bf, last, tables, masked, weight, sems = refs
     copies = [
         pltpu.make_async_copy(bt, tables.at[0], sems.at[0]),
         pltpu.make_async_copy(tt, tables.at[1], sems.at[1]),
         pltpu.make_async_copy(mv, masked, sems.at[2]),
         pltpu.make_async_copy(wq, weight, sems.at[3]),
+        pltpu.make_async_copy(ow, last, sems.at[4]),
     ]
     for copy in copies[:3]:
         copy.start()
@@ -146,6 +146,7 @@
     for copy in copies[:3]:
         copy.wait()
     copies[3].start()
+    copies[4].start()
     step = 256
     for at in range(0, TOKENS, step):
         here = slice(at, at + step)
@@ -160,6 +161,7 @@
     copies[3].wait()
     proj[...] = dot(normed[...], weight[...], 1, 0).astype(BF16)
     forward(0, place, proj, att, share, share_bf)
+    copies[4].wait()
 
 
 def merge(cot, grads, up, left, diag):
@@ -174,28 +176,14 @@
         cot[64 + at : 128 + at] = values.astype(BF16)
 
 
-def attend_first(
-    place, proj, normed, grads, up, left, diag, ow, att, share, share_bf, gp, keep, send, cot, own, weight, sems, ds
-):
-    copies = [
-        pltpu.make_async_copy(grads, own, sems.at[0]),
-        pltpu.make_async_copy(ow.at[:, 0:CW], weight, sems.at[1]),
-    ]
-    for copy in copies:
-        copy.start()
-    copies[0].wait()
-    merge(cot, own, up, left, diag)
-    copies[1].wait()
-    backward(0, place, proj, normed, cot, weight, att, gp, keep, send, share, share_bf, ds)
-
-
-def attend_next(chunk, place, proj, normed, cot, ow, *refs):
-    att, gp, keep, send, weight, sem, *held = refs[1:] if chunk > 1 else refs
-    copy = pltpu.make_async_copy(ow.at[:, chunk * CW : (chunk + 1) * CW], weight, sem)
-    copy.start()
+def attend_first(place, proj, normed, grads, up, left, diag, ow, att, share, share_bf, gp, keep, send, cot, ds):
+    merge(cot, grads, up, left, diag)
+    backward(0, place, proj, normed, cot, ow, att, gp, keep, send, share, share_bf, ds)
+
+
+def attend_next(chunk, place, proj, normed, cot, ow, att, gp, keep, send, *held):
     forward(chunk, place, proj, att, *held[:2])
-    copy.wait()
-    backward(chunk, place, proj, normed, cot, weight, att, gp, keep, send, *held)
+    backward(chunk, place, proj, normed, cot, ow, att, gp, keep, send, *held)
 
 
 def first_lanes():
@@ -245,7 +233,7 @@
 
 def backward(chunk, place, proj, normed, cot, ow, att, gp, keep, send, share, share_bf, ds):
     units = units_of(chunk, proj)
-    grad = dot(cot[...], ow[...], 1, 0).astype(BF16)
+    grad = dot(cot[...], ow[:, chunk * CW : (chunk + 1) * CW], 1, 0).astype(BF16)
     lane = first_lanes()
 
     def pick(x):
@@ -271,16 +259,11 @@
             out[half, :, 3 * CW :] = dot(cot[:, cut], att[...], 0, 0).astype(out.dtype)
 
 
-def finish_kernel(emb, cot, wq, ow, *refs):
+def finish_kernel(emb, cot, wq, last, *refs):
     atts, gps = refs[:CHUNKS], refs[CHUNKS : 2 * CHUNKS]
-    mid, up, left, diag, tick, weight, last, big, sems = refs[2 * CHUNKS :]
-    copies = [
-        pltpu.make_async_copy(ow, last, sems.at[0]),
-        pltpu.make_async_copy(wq, weight, sems.at[1]),
-    ]
-    for copy in copies:
-        copy.start()
-    copies[0].wait()
+    mid, up, left, diag, tick, weight, big, sem = refs[2 * CHUNKS :]
+    copy = pltpu.make_async_copy(wq, weight, sem)
+    copy.start()
 
     def put(i, block, values):
         if block == 0:
@@ -305,7 +288,7 @@
     att = jnp.concatenate([a[...] for a in atts], axis=1)
     big[...] = dot(att, last[...], 1, 1)
     each(0, lambda here, x, branch: x + branch)
-    copies[1].wait()
+    copy.wait()
     parts = []
     for i in range(3):
         parts += [g[:, i * CW : (i + 1) * CW] for g in gps]
@@ -489,24 +472,32 @@
     grads = pin(cotangent.reshape(TOKENS, MODEL))
     bottom_table, top_table = pin(bottom_table), pin(top_table)
     mask_vector, qkv_weight, out_weight = pin(mask_vector), pin(qkv_weight), pin(out_weight)
-    up, left, diag = call(
+    up, left, diag, grads = call(
         slice_kernel,
-        [sds((64, MODEL)), sds((MSG, MODEL)), sds((16, MODEL))],
+        [sds((64, MODEL)), sds((MSG, MODEL)), sds((16, MODEL)), sds((TOKENS, MODEL))],
         (grads,),
         [hbm()],
         2**28,
         2**21,
         name="slices",
-        scratch=[pltpu.VMEM((TOKENS, MODEL), BF16), pltpu.SemaphoreType.DMA],
+        scratch=[pltpu.SemaphoreType.DMA],
     )
     up, left, diag = shift(up, 1, 0), shift(left, 0, 1), shift(diag, 1, 1)
     units = BANDS * CW // 128
     score, pairs = (units, 2, BAND, BAND), (units, 2 * BAND, BAND)
-    emb, normed, proj, att, share, share_bf = call(
+    emb, normed, proj, att, share, share_bf, last = call(
         embed_kernel,
-        [sds((TOKENS, MODEL)), sds((TOKENS, MODEL)), sds((TOKENS, 3 * HW)), sds((TOKENS, CW)), sds(score, F32), sds(pairs)],
-        (place, *near, bottom_table, top_table, mask_vector, qkv_weight),
-        [smem()] + [vmem()] * 4 + [hbm()] * 4,
+        [
+            sds((TOKENS, MODEL)),
+            sds((TOKENS, MODEL)),
+            sds((TOKENS, 3 * HW)),
+            sds((TOKENS, CW)),
+            sds(score, F32),
+            sds(pairs),
+            sds((MODEL, HW)),
+        ],
+        (place, *near, bottom_table, top_table, mask_vector, qkv_weight, out_weight),
+        [smem()] + [vmem()] * 4 + [hbm()] * 5,
         2 * TOKENS * 1024 * 2560,
         9 * 2**20,
         name="embed",
@@ -514,50 +505,48 @@
             pltpu.VMEM((2, 512, MODEL), BF16),
             pltpu.VMEM((MODEL,), BF16),
             pltpu.VMEM((MODEL, 3 * HW), BF16),
-            sems(4),
+            sems(5),
         ],
     )
     outs = [sds((TOKENS, 3 * CW)), sds((2, 256, W), F32), sds((2, 256, W))]
-    column, ds = pltpu.VMEM((MODEL, CW), BF16), pltpu.VMEM(pairs, BF16)
+    ds = pltpu.VMEM(pairs, BF16)
     held = [pltpu.VMEM(score, F32), pltpu.VMEM(pairs, BF16), ds]
     gp, keep, send, cot = call(
         attend_first,
         outs + [sds((TOKENS, MODEL))],
-        (place, proj, normed, grads, up, left, diag, out_weight, att, share, share_bf),
-        [smem(), vmem(), vmem(), hbm(), vmem(), vmem(), vmem(), hbm(), vmem(), vmem(), vmem()],
+        (place, proj, normed, grads, up, left, diag, last, att, share, share_bf),
+        [smem()] + [vmem()] * 10,
         2**20,
         2**12,
         name="attend",
-        scratch=[pltpu.VMEM((TOKENS, MODEL), BF16), column, sems(2), ds],
+        scratch=[ds],
     )
     parts, cores = [(att, gp)], [sum_core(place, keep, send, 0)]
     for c in range(1, CHUNKS):
-        after = [cores[c - 2][0]] if c > 1 else []
         att, gp, keep, send = call(
             functools.partial(attend_next, c),
             [sds((TOKENS, CW))] + outs,
-            (place, proj, normed, cot, out_weight, *after),
-            [smem(), vmem(), vmem(), vmem(), hbm()] + [anywhere()] * len(after),
+            (place, proj, normed, cot, last),
+            [smem()] + [vmem()] * 4,
             2**20,
             2**12,
             name="attend",
-            scratch=[column, pltpu.SemaphoreType.DMA, *held],
+            scratch=held,
         )
         parts.append((att, gp))
         cores.append(sum_core(place, keep, send, c))
     *sent, tick = call(
         finish_kernel,
         [sds((2, OWN, MODEL)), sds((2, 64, MODEL)), sds((2, MSG, MODEL)), sds((2, 16, MODEL)), sds((8, 128), F32)],
-        (emb, cot, qkv_weight, out_weight, *[p[0] for p in parts], *[p[1] for p in parts]),
-        [vmem(), vmem(), hbm(), hbm()] + [vmem()] * 2 * CHUNKS,
+        (emb, cot, qkv_weight, last, *[p[0] for p in parts], *[p[1] for p in parts]),
+        [vmem(), vmem(), hbm(), vmem()] + [vmem()] * 2 * CHUNKS,
         2**20,
         2**12,
         name="finish",
         scratch=[
             pltpu.VMEM((MODEL, 3 * HW), BF16),
-            pltpu.VMEM((MODEL, HW), BF16),
             pltpu.VMEM((TOKENS, MODEL), F32),
-            sems(2),
+            pltpu.SemaphoreType.DMA,
         ],
     )
     mid, up, left, diag = sent

time: 94 us -> 91.7 us (0.976)
  Pallas kernels: 30.7 us -> 28.4 us
    pallas_call x15, Pallas kernels: 30.7 us -> 28.4 us  [call(): pl.pallas_call(kernel, out_shape=outs, in_specs=specs, out_specs=jax.tree...]
  transfers between devices with their start and end apart: 21 -> 21, of which waited for: 6 -> 6; matrix products, arithmetic and copies ran while one was open for 0% -> 0% of each run, Pallas kernels for 26% -> 25%
where the time goes in v11:
time: 91.7 us; the launch traced here: 90.5 us
  starting transfers between devices  37.6 us (41%)
  Pallas kernels  28.4 us (31%)
  waiting for transfers between devices  22.8 us (25%)
    pallas_call x15, Pallas kernels, call(): pl.pallas_call(kernel, out_shape=outs, in_specs=specs, out_specs=jax.tree...  28.4 us
    ppermute x13, starting transfers between devices, permute(): return lax.ppermute(x, GRID, pairs)  19.3 us
    ppermute x7, starting transfers between devices, swap(): lax.ppermute(x, axis, [(i, i ^ flip) for i in range(lax.axis_size(axis))])  9.78 us
    ppermute x13, waiting for transfers between devices, permute(): return lax.ppermute(x, GRID, pairs)  9.74 us
    all_to_all x1, waiting for transfers between devices, shards(): depth = lax.all_to_all(joined, 'z', 0, 0, tiled=True)  8.67 us
    all_to_all x1, starting transfers between devices, shards(): depth = lax.all_to_all(joined, 'z', 0, 0, tiled=True)  8.51 us
    ppermute x7, waiting for transfers between devices, swap(): lax.ppermute(x, axis, [(i, i ^ flip) for i in range(lax.axis_size(axis))])  4.36 us
  transfers between devices with their start and end apart: 21, of which 6 were waited for; matrix products, arithmetic and copies ran while one was open for 0% of the time, Pallas kernels for 25%

profile of v11, /device:TPU:32, one launch (start us, length us, event | category | flops | bytes accessed | tf_op | source)
XLA Modules:
  0.0 90.5 jit_solution(10690827098705997939)
XLA Ops:
  0.6 0.8 pad_add_fusion
  1.5 1.0 %collective-permute-start.2 = (s32[80,16]{1,0:T(8,128)S(1)}, s32[80,16]{1,0:T(8,128)S(1)}, u32[]{:S(2)}, u32[]{:S(2)}) collective-permute-start(s32[80,16]{1,0:T(8,128)S(1)} %copy.19.own), channel_id=1, source_target_pairs={{0,17},{1,18},{2,19},{3,20},{4,21},{5,22},{6,23},{7,24},{8,25},{9,... | collective-permute-start | bytes 15368 | tf_op jit(solution)/shard_map/ppermute | solution.py:406
  2.5 1.9 %collective-permute-start.1 = (s32[80,16]{1,0:T(8,128)S(1)}, s32[80,16]{1,0:T(8,128)S(1)}, u32[]{:S(2)}, u32[]{:S(2)}) collective-permute-start(s32[80,16]{1,0:T(8,128)S(1)} %copy.19.own), channel_id=1, source_target_pairs={{0,1},{1,2},{2,3},{3,4},{4,5},{5,6},{6,7},{7,8},{8,9},{9,10},{10,1... | collective-permute-start | bytes 15368 | tf_op jit(solution)/shard_map/ppermute | solution.py:406
  4.4 1.4 %collective-permute-start = (s32[80,16]{1,0:T(8,128)S(1)}, s32[80,16]{1,0:T(8,128)S(1)}, u32[]{:S(2)}, u32[]{:S(2)}) collective-permute-start(s32[80,16]{1,0:T(8,128)S(1)} %copy.19.own), channel_id=1, source_target_pairs={{0,16},{1,17},{2,18},{3,19},{4,20},{5,21},{6,22},{7,23},{8,24},{9,... | collective-permute-start | bytes 15368 | tf_op jit(solution)/shard_map/ppermute | solution.py:406
  5.8 1.6 %slices.1 = (bf16[64,1024]{1,0:T(8,128)(2,1)S(1)}, bf16[112,1024]{1,0:T(8,128)(2,1)S(1)}, bf16[16,1024]{1,0:T(8,128)(2,1)S(1)}, bf16[512,1024]{1,0:T(8,128)(2,1)S(1)}) custom-call(bf16[512,1024]{1,0:T(8,128)(2,1)} %bitcast.20), custom_call_target="tpu_custom_call" | custom-call | flops 268435456 | bytes 2097152 | tf_op jit(solution)/shard_map/slices/pallas_call | solution.py:43
  7.3 2.1 %collective-permute-start.5 = (bf16[16,1024]{1,0:T(8,128)(2,1)S(1)}, bf16[16,1024]{1,0:T(8,128)(2,1)S(1)}, u32[]{:S(2)}, u32[]{:S(2)}) collective-permute-start(bf16[16,1024]{1,0:T(8,128)(2,1)S(1)} %get-tuple-element.51), channel_id=1, source_target_pairs={{0,17},{1,18},{2,19},{3,20},{4,21},{5,22},{6,23},{7,24},{8,25},{9,... | collective-permute-start | bytes 98312 | tf_op jit(solution)/shard_map/ppermute | solution.py:406
  9.5 2.8 %collective-permute-start.4 = (bf16[112,1024]{1,0:T(8,128)(2,1)S(1)}, bf16[112,1024]{1,0:T(8,128)(2,1)S(1)}, u32[]{:S(2)}, u32[]{:S(2)}) collective-permute-start(bf16[112,1024]{1,0:T(8,128)(2,1)S(1)} %get-tuple-element.50), channel_id=1, source_target_pairs={{0,1},{1,2},{2,3},{3,4},{4,5},{5,6},{6,7},{7,8},{8,9},{9,10},{10,1... | collective-permute-start | bytes 688136 | tf_op jit(solution)/shard_map/ppermute | solution.py:406
  12.3 6.5 %embed.1 = (bf16[512,1024]{1,0:T(8,128)(2,1)S(1)}, bf16[512,1024]{1,0:T(8,128)(2,1)S(1)}, bf16[512,1536]{1,0:T(8,128)(2,1)S(1)}, bf16[512,256]{1,0:T(8,128)(2,1)...) custom-call(s32[6]{0:T(128)S(1)} %stack.27.place, ...), custom_call_target="tpu_custom_call" | custom-call | flops 2684354560 | bytes 9437184 | tf_op jit(solution)/shard_map/embed/pallas_call | solution.py:43
  18.9 3.6 %attend.2 = (bf16[512,768]{1,0:T(8,128)(2,1)S(1)}, f32[2,256,1024]{2,1,0:T(8,128)S(1)}, bf16[2,256,1024]{2,1,0:T(8,128)(2,1)S(1)}, bf16[512,1024]{1,0:T(8,128)(2,1)S(1)}) custom-call(s32[6]{0:T(128)S(1)} %stack.27.place, bf16[512,1536]{1,0:T(8,128)(2,1)S(1)} %get-tuple-element.46.proj, bf16[512,1024]{1,0:T(8,128)(2,1)S(1)} %get-tuple-element.47.normed, ...), custom_call_target="tpu_custom_call" | custom-call | flops 1048576 | bytes 4096 | tf_op jit(solution)/shard_map/attend/pallas_call | solution.py:43
  22.8 3.8 %attend.3 = (bf16[512,256]{1,0:T(8,128)(2,1)S(1)}, bf16[512,768]{1,0:T(8,128)(2,1)S(1)}, f32[2,256,1024]{2,1,0:T(8,128)S(1)}, bf16[2,256,1024]{2,1,0:T(8,128)(2,1)S(1)}) custom-call(s32[6]{0:T(128)S(1)} %stack.27.place, bf16[512,1536]{1,0:T(8,128)(2,1)S(1)} %get-tuple-element.46.proj, bf16[512,1024]{1,0:T(8,128)(2,1)S(1)} %get-tuple-element.47.normed, ...), custom_call_target="tpu_custom_call" | custom-call | flops 1048576 | bytes 4096 | tf_op jit(solution)/shard_map/attend/pallas_call | solution.py:43
  27.2 0.7 sum_core.2
  28.0 2.9 %collective-permute-start.8 = (bf16[2,8,16,1024]{3,2,1,0:T(8,128)(2,1)S(1)}, bf16[2,8,16,1024]{3,2,1,0:T(8,128)(2,1)S(1)}, u32[]{:S(2)}, u32[]{:S(2)}) collective-permute-start(bf16[2,8,16,1024]{3,2,1,0:T(8,128)(2,1)S(1)} %get-tuple-element.65), channel_id=1, source_target_pairs={{0,1},{1,0},{2,3},{3,2},{4,5},{5,4},{6,7},{7,6},{8,9},{9,8},{10,11... | collective-permute-start | bytes 1572872 | tf_op jit(solution)/shard_map/ppermute | solution.py:406
  30.9 0.7 sum_core.3
  31.6 2.3 %collective-permute-start.14 = (bf16[2,8,16,1024]{3,2,1,0:T(8,128)(2,1)S(1)}, bf16[2,8,16,1024]{3,2,1,0:T(8,128)(2,1)S(1)}, u32[]{:S(2)}, u32[]{:S(2)}) collective-permute-start(bf16[2,8,16,1024]{3,2,1,0:T(8,128)(2,1)S(1)} %get-tuple-element.79), channel_id=1, source_target_pairs={{0,33},{1,32},{2,35},{3,34},{4,37},{5,36},{6,39},{7,38},{8,41},{9,... | collective-permute-start | bytes 1572872 | tf_op jit(solution)/shard_map/ppermute | solution.py:406
  33.9 4.9 %finish.1 = (bf16[2,448,1024]{2,1,0:T(8,128)(2,1)S(1)}, bf16[2,64,1024]{2,1,0:T(8,128)(2,1)S(1)}, bf16[2,112,1024]{2,1,0:T(8,128)(2,1)S(1)}, bf16[2,16,1024]{2,1,0:T(8,128)(2,1)S(1)}, f32[8,128]{1,0:T(8,128)S(1)}) custom-call(bf16[512,1024]{1,0:T(8,128)(2,1)S(1)} %get-tuple-element.45.emb, bf16[512,1024]{1,0:T(8,128)(2,1)S(1)} %get-tuple-element.56.cot, ...), custom_call_target="tpu_custom_call" | custom-call | flops 1048576 | bytes 4096 | tf_op jit(solution)/shard_map/finish/pallas_call | solution.py:43
  38.8 1.4 %collective-permute-start.10 = (bf16[2,16,1024]{2,1,0:T(8,128)(2,1)S(1)}, bf16[2,16,1024]{2,1,0:T(8,128)(2,1)S(1)}, u32[]{:S(2)}, u32[]{:S(2)}) collective-permute-start(bf16[2,16,1024]{2,1,0:T(8,128)(2,1)S(1)} %get-tuple-element.69), channel_id=1, source_target_pairs={{0,63},{1,48},{2,49},{3,50},{4,51},{5,52},{6,53},{7,54},{8,55},{9,... | collective-permute-start | bytes 196616 | tf_op jit(solution)/shard_map/ppermute | solution.py:406
  40.2 3.4 %collective-permute-done.8.b = bf16[2,8,16,1024]{3,2,1,0:T(8,128)(2,1)S(1)} collective-permute-done((bf16[2,8,16,1024]{3,2,1,0:T(8,128)(2,1)S(1)}, bf16[2,8,16,1024]{3,2,1,0:T(8,128)(2,1)S(1)}, u32[]{:S(2)}, u32[]{:S(2)}) %collective-permute-start.8) | collective-permute-done | bytes 524320 | tf_op jit(solution)/shard_map/ppermute | solution.py:406
  43.6 0.7 sum_pair.2
  44.3 2.7 %collective-permute-start.9 = (bf16[2,112,1024]{2,1,0:T(8,128)(2,1)S(1)}, bf16[2,112,1024]{2,1,0:T(8,128)(2,1)S(1)}, u32[]{:S(2)}, u32[]{:S(2)}) collective-permute-start(bf16[2,112,1024]{2,1,0:T(8,128)(2,1)S(1)} %get-tuple-element.68), channel_id=1, source_target_pairs={{0,15},{1,0},{2,1},{3,2},{4,3},{5,4},{6,5},{7,6},{8,7},{9,8},{10,9... | collective-permute-start | bytes 1376264 | tf_op jit(solution)/shard_map/ppermute | solution.py:406
  48.3 3.1 %collective-permute-start.15 = (bf16[2,8,16,512]{3,2,1,0:T(8,128)(2,1)S(1)}, bf16[2,8,16,512]{3,2,1,0:T(8,128)(2,1)S(1)}, u32[]{:S(2)}, u32[]{:S(2)}) collective-permute-start(bf16[2,8,16,512]{3,2,1,0:T(8,128)(2,1)S(1)} %get-tuple-element.81), channel_id=1, source_target_pairs={{0,192},{64,128},{128,64},{192,0},{1,193},{65,129},{129,65},{193,1... | collective-permute-start | bytes 786440 | tf_op jit(solution)/shard_map/ppermute | solution.py:414
  51.3 4.0 %collective-permute-done.11.b = bf16[8,16,1024]{2,1,0:T(8,128)(2,1)S(1)} collective-permute-done((bf16[8,16,1024]{2,1,0:T(8,128)(2,1)S(1)}, bf16[8,16,1024]{2,1,0:T(8,128)(2,1)S(1)}, u32[]{:S(2)}, u32[]{:S(2)}) %collective-permute-start.11) | collective-permute-done | bytes 262176 | tf_op jit(solution)/shard_map/ppermute | solution.py:406
  56.0 1.7 %collective-permute-start.12 = (bf16[8,16,512]{2,1,0:T(8,128)(2,1)S(1)}, bf16[8,16,512]{2,1,0:T(8,128)(2,1)S(1)}, u32[]{:S(2)}, u32[]{:S(2)}) collective-permute-start(bf16[8,16,512]{2,1,0:T(8,128)(2,1)S(1)} %get-tuple-element.75), channel_id=1, source_target_pairs={{0,64},{64,0},{128,192},{192,128},{1,65},{65,1},{129,193},{193,129... | collective-permute-start | bytes 393224 | tf_op jit(solution)/shard_map/ppermute | solution.py:414
  58.6 2.5 %collective-permute-done.12.b = bf16[8,16,512]{2,1,0:T(8,128)(2,1)S(1)} collective-permute-done((bf16[8,16,512]{2,1,0:T(8,128)(2,1)S(1)}, bf16[8,16,512]{2,1,0:T(8,128)(2,1)S(1)}, u32[]{:S(2)}, u32[]{:S(2)}) %collective-permute-start.12) | collective-permute-done | bytes 131104 | tf_op jit(solution)/shard_map/ppermute | solution.py:414
  61.0 2.3 %collective-permute-done.16.d = bf16[8,16,512]{2,1,0:T(8,128)(2,1)S(1)} collective-permute-done((bf16[8,16,512]{2,1,0:T(8,128)(2,1)S(1)}, bf16[8,16,512]{2,1,0:T(8,128)(2,1)S(1)}, u32[]{:S(2)}, u32[]{:S(2)}) %collective-permute-start.16) | collective-permute-done | bytes 131104 | tf_op jit(solution)/shard_map/ppermute | solution.py:406
  63.3 0.7 join.1
  64.1 8.5 %all-to-all-start = ((bf16[8,16,1024]{2,1,0:T(8,128)(2,1)}), bf16[8,16,1024]{2,1,0:T(8,128)(2,1)S(1)}, u32[]{:S(2)}, u32[]{:S(2)}) async-start(bf16[8,16,1024]{2,1,0:T(8,128)(2,1)} %join.1), calls=%async_computation | async-start | bytes 524288 | tf_op jit(solution)/shard_map/all_to_all | solution.py:579
  72.6 8.7 %all-to-all-done.ref = bf16[8,16,1024]{2,1,0:T(8,128)(2,1)S(1)} async-done(((bf16[8,16,1024]{2,1,0:T(8,128)(2,1)}), bf16[8,16,1024]{2,1,0:T(8,128)(2,1)S(1)}, u32[]{:S(2)}, u32[]{:S(2)}) %all-to-all-start) | async-done | bytes 262176 | tf_op jit(solution)/shard_map/all_to_all | solution.py:579
  81.3 2.6 %collective-permute-start.19 = (bf16[16,1024]{1,0:T(8,128)(2,1)S(1)}, bf16[16,1024]{1,0:T(8,128)(2,1)S(1)}, u32[]{:S(2)}, u32[]{:S(2)}) collective-permute-start(bf16[16,1024]{1,0:T(8,128)(2,1)S(1)} %depth.1.r0), channel_id=1, source_target_pairs={{0,192},{64,128},{128,64},{192,0},{1,193},{65,129},{129,65},{193,1... | collective-permute-start | bytes 98312 | tf_op jit(solution)/shard_map/ppermute | solution.py:414
  84.3 1.1 %collective-permute-start.17 = (bf16[16,1024]{1,0:T(8,128)(2,1)S(1)}, bf16[16,1024]{1,0:T(8,128)(2,1)S(1)}, u32[]{:S(2)}, u32[]{:S(2)}) collective-permute-start(bf16[16,1024]{1,0:T(8,128)(2,1)S(1)} %depth.1.r0), channel_id=1, source_target_pairs={{0,64},{64,0},{128,192},{192,128},{1,65},{65,1},{129,193},{193,129... | collective-permute-start | bytes 98312 | tf_op jit(solution)/shard_map/ppermute | solution.py:414
  85.5 2.0 %place.1 = (bf16[512,1024]{1,0:T(8,128)(2,1)}, bf16[512,1024]{1,0:T(8,128)(2,1)}) custom-call(bf16[2,448,1024]{2,1,0:T(8,128)(2,1)S(1)} %get-tuple-element.60.mid, bf16[2,64,1024]{2,1,0:T(8,128)(2,1)S(1)} %collective-permute-done.6.up, bf16[2,112,1024]{2,1,0:T(8,128)(2,1)S(1)} %collective-permute-done.9.left.arrived, ...), custom_call_target="tpu_custom_call" | custom-call | flops 268435456 | bytes 5242880 | tf_op jit(solution)/shard_map/place/pallas_call | solution.py:43
  87.4 1.9 %collective-permute-done.18.r2 = bf16[16,1024]{1,0:T(8,128)(2,1)S(1)} collective-permute-done((bf16[16,1024]{1,0:T(8,128)(2,1)S(1)}, bf16[16,1024]{1,0:T(8,128)(2,1)S(1)}, u32[]{:S(2)}, u32[]{:S(2)}) %collective-permute-start.18) | collective-permute-done | bytes 32800 | tf_op jit(solution)/shard_map/ppermute | solution.py:414
  89.3 1.2 %level.1 = (f32[16,1536]{1,0:T(8,128)}, f32[16,512]{1,0:T(8,128)}) custom-call(s32[6]{0:T(128)S(1)} %stack.27.place, bf16[16,1024]{1,0:T(8,128)(2,1)S(1)} %depth.1.r0, bf16[16,1024]{1,0:T(8,128)(2,1)S(1)} %collective-permute-done.17.r1, bf16[16,1024]{1,0:T(8,128)(2,1)S(1)} %collective-permute-done.18.r2, bf16[16,1024]{1,0:T(8,128)(2,1)S(1)} %collective-permute-done.19.r3), custom_call_target="tpu_custom_call" | custom-call | flops 131072 | bytes 524288 | tf_op jit(solution)/shard_map/level/pallas_call | solution.py:43
  (28 shorter events, 4.3 us)
Async XLA Ops:
  1.5 8.0 %collective-permute-start.2 = (s32[80,16]{1,0:T(8,128)S(1)}, s32[80,16]{1,0:T(8,128)S(1)}, u32[]{:S(2)}, u32[]{:S(2)}) collective-permute-start(s32[80,16]{1,0:T(8,128)S(1)} %copy.19.own), channel_id=1, source_target_pairs={{0,17},{1,18},{2,19},{3,20},{4,21},{5,22},{6,23},{7,24},{8,25},{9,... | collective-permute-start | bytes 15368 | tf_op jit(solution)/shard_map/ppermute | solution.py:406
  2.5 9.8 %collective-permute-start.1 = (s32[80,16]{1,0:T(8,128)S(1)}, s32[80,16]{1,0:T(8,128)S(1)}, u32[]{:S(2)}, u32[]{:S(2)}) collective-permute-start(s32[80,16]{1,0:T(8,128)S(1)} %copy.19.own), channel_id=1, source_target_pairs={{0,1},{1,2},{2,3},{3,4},{4,5},{5,6},{6,7},{7,8},{8,9},{9,10},{10,1... | collective-permute-start | bytes 15368 | tf_op jit(solution)/shard_map/ppermute | solution.py:406
  4.4 7.9 %collective-permute-start = (s32[80,16]{1,0:T(8,128)S(1)}, s32[80,16]{1,0:T(8,128)S(1)}, u32[]{:S(2)}, u32[]{:S(2)}) collective-permute-start(s32[80,16]{1,0:T(8,128)S(1)} %copy.19.own), channel_id=1, source_target_pairs={{0,16},{1,17},{2,18},{3,19},{4,20},{5,21},{6,22},{7,23},{8,24},{9,... | collective-permute-start | bytes 15368 | tf_op jit(solution)/shard_map/ppermute | solution.py:406
  7.3 11.5 %collective-permute-start.5 = (bf16[16,1024]{1,0:T(8,128)(2,1)S(1)}, bf16[16,1024]{1,0:T(8,128)(2,1)S(1)}, u32[]{:S(2)}, u32[]{:S(2)}) collective-permute-start(bf16[16,1024]{1,0:T(8,128)(2,1)S(1)} %get-tuple-element.51), channel_id=1, source_target_pairs={{0,17},{1,18},{2,19},{3,20},{4,21},{5,22},{6,23},{7,24},{8,25},{9,... | collective-permute-start | bytes 98312 | tf_op jit(solution)/shard_map/ppermute | solution.py:406
  9.4 9.5 %collective-permute-start.3 = (bf16[64,1024]{1,0:T(8,128)(2,1)S(1)}, bf16[64,1024]{1,0:T(8,128)(2,1)S(1)}, u32[]{:S(2)}, u32[]{:S(2)}) collective-permute-start(bf16[64,1024]{1,0:T(8,128)(2,1)S(1)} %get-tuple-element.49), channel_id=1, source_target_pairs={{0,16},{1,17},{2,18},{3,19},{4,20},{5,21},{6,22},{7,23},{8,24},{9,... | collective-permute-start | bytes 393224 | tf_op jit(solution)/shard_map/ppermute | solution.py:406
  9.5 9.4 %collective-permute-start.4 = (bf16[112,1024]{1,0:T(8,128)(2,1)S(1)}, bf16[112,1024]{1,0:T(8,128)(2,1)S(1)}, u32[]{:S(2)}, u32[]{:S(2)}) collective-permute-start(bf16[112,1024]{1,0:T(8,128)(2,1)S(1)} %get-tuple-element.50), channel_id=1, source_target_pairs={{0,1},{1,2},{2,3},{3,4},{4,5},{5,6},{6,7},{7,8},{8,9},{9,10},{10,1... | collective-permute-start | bytes 688136 | tf_op jit(solution)/shard_map/ppermute | solution.py:406
  22.5 4.7 %collective-permute-start.7 = (bf16[2,256,1024]{2,1,0:T(8,128)(2,1)S(1)}, bf16[2,256,1024]{2,1,0:T(8,128)(2,1)S(1)}, u32[]{:S(2)}, u32[]{:S(2)}) collective-permute-start(bf16[2,256,1024]{2,1,0:T(8,128)(2,1)S(1)} %get-tuple-element.63), channel_id=1, source_target_pairs={{0,16},{16,0},{1,17},{17,1},{2,18},{18,2},{3,19},{19,3},{4,20},{20... | collective-permute-start | bytes 3145736 | tf_op jit(solution)/shard_map/ppermute | solution.py:414
  26.6 4.2 %collective-permute-start.13 = (bf16[2,256,1024]{2,1,0:T(8,128)(2,1)S(1)}, bf16[2,256,1024]{2,1,0:T(8,128)(2,1)S(1)}, u32[]{:S(2)}, u32[]{:S(2)}) collective-permute-start(bf16[2,256,1024]{2,1,0:T(8,128)(2,1)S(1)} %get-tuple-element.77), channel_id=1, source_target_pairs={{0,16},{16,0},{1,17},{17,1},{2,18},{18,2},{3,19},{19,3},{4,20},{20... | collective-permute-start | bytes 3145736 | tf_op jit(solution)/shard_map/ppermute | solution.py:414
  28.0 15.7 %collective-permute-start.8 = (bf16[2,8,16,1024]{3,2,1,0:T(8,128)(2,1)S(1)}, bf16[2,8,16,1024]{3,2,1,0:T(8,128)(2,1)S(1)}, u32[]{:S(2)}, u32[]{:S(2)}) collective-permute-start(bf16[2,8,16,1024]{3,2,1,0:T(8,128)(2,1)S(1)} %get-tuple-element.65), channel_id=1, source_target_pairs={{0,1},{1,0},{2,3},{3,2},{4,5},{5,4},{6,7},{7,6},{8,9},{9,8},{10,11... | collective-permute-start | bytes 1572872 | tf_op jit(solution)/shard_map/ppermute | solution.py:406
  31.6 16.0 %collective-permute-start.14 = (bf16[2,8,16,1024]{3,2,1,0:T(8,128)(2,1)S(1)}, bf16[2,8,16,1024]{3,2,1,0:T(8,128)(2,1)S(1)}, u32[]{:S(2)}, u32[]{:S(2)}) collective-permute-start(bf16[2,8,16,1024]{3,2,1,0:T(8,128)(2,1)S(1)} %get-tuple-element.79), channel_id=1, source_target_pairs={{0,33},{1,32},{2,35},{3,34},{4,37},{5,36},{6,39},{7,38},{8,41},{9,... | collective-permute-start | bytes 1572872 | tf_op jit(solution)/shard_map/ppermute | solution.py:406
  38.8 8.8 %collective-permute-start.10 = (bf16[2,16,1024]{2,1,0:T(8,128)(2,1)S(1)}, bf16[2,16,1024]{2,1,0:T(8,128)(2,1)S(1)}, u32[]{:S(2)}, u32[]{:S(2)}) collective-permute-start(bf16[2,16,1024]{2,1,0:T(8,128)(2,1)S(1)} %get-tuple-element.69), channel_id=1, source_target_pairs={{0,63},{1,48},{2,49},{3,50},{4,51},{5,52},{6,53},{7,54},{8,55},{9,... | collective-permute-start | bytes 196616 | tf_op jit(solution)/shard_map/ppermute | solution.py:406
  44.3 19.0 %collective-permute-start.9 = (bf16[2,112,1024]{2,1,0:T(8,128)(2,1)S(1)}, bf16[2,112,1024]{2,1,0:T(8,128)(2,1)S(1)}, u32[]{:S(2)}, u32[]{:S(2)}) collective-permute-start(bf16[2,112,1024]{2,1,0:T(8,128)(2,1)S(1)} %get-tuple-element.68), channel_id=1, source_target_pairs={{0,15},{1,0},{2,1},{3,2},{4,3},{5,4},{6,5},{7,6},{8,7},{9,8},{10,9... | collective-permute-start | bytes 1376264 | tf_op jit(solution)/shard_map/ppermute | solution.py:406
  47.0 8.3 %collective-permute-start.11 = (bf16[8,16,1024]{2,1,0:T(8,128)(2,1)S(1)}, bf16[8,16,1024]{2,1,0:T(8,128)(2,1)S(1)}, u32[]{:S(2)}, u32[]{:S(2)}) collective-permute-start(bf16[8,16,1024]{2,1,0:T(8,128)(2,1)S(1)} %get-tuple-element.73), channel_id=1, source_target_pairs={{0,33},{1,32},{2,35},{3,34},{4,37},{5,36},{6,39},{7,38},{8,41},{9,... | collective-permute-start | bytes 786440 | tf_op jit(solution)/shard_map/ppermute | solution.py:406
  48.3 9.4 %collective-permute-start.15 = (bf16[2,8,16,512]{3,2,1,0:T(8,128)(2,1)S(1)}, bf16[2,8,16,512]{3,2,1,0:T(8,128)(2,1)S(1)}, u32[]{:S(2)}, u32[]{:S(2)}) collective-permute-start(bf16[2,8,16,512]{3,2,1,0:T(8,128)(2,1)S(1)} %get-tuple-element.81), channel_id=1, source_target_pairs={{0,192},{64,128},{128,64},{192,0},{1,193},{65,129},{129,65},{193,1... | collective-permute-start | bytes 786440 | tf_op jit(solution)/shard_map/ppermute | solution.py:414
  56.0 5.1 %collective-permute-start.12 = (bf16[8,16,512]{2,1,0:T(8,128)(2,1)S(1)}, bf16[8,16,512]{2,1,0:T(8,128)(2,1)S(1)}, u32[]{:S(2)}, u32[]{:S(2)}) collective-permute-start(bf16[8,16,512]{2,1,0:T(8,128)(2,1)S(1)} %get-tuple-element.75), channel_id=1, source_target_pairs={{0,64},{64,0},{128,192},{192,128},{1,65},{65,1},{129,193},{193,129... | collective-permute-start | bytes 393224 | tf_op jit(solution)/shard_map/ppermute | solution.py:414
  58.2 5.1 %collective-permute-start.16 = (bf16[8,16,512]{2,1,0:T(8,128)(2,1)S(1)}, bf16[8,16,512]{2,1,0:T(8,128)(2,1)S(1)}, u32[]{:S(2)}, u32[]{:S(2)}) collective-permute-start(bf16[8,16,512]{2,1,0:T(8,128)(2,1)S(1)} %get-tuple-element.83), channel_id=1, source_target_pairs={{0,1},{1,0},{2,3},{3,2},{4,5},{5,4},{6,7},{7,6},{8,9},{9,8},{10,11... | collective-permute-start | bytes 393224 | tf_op jit(solution)/shard_map/ppermute | solution.py:406
  64.1 17.2 %all-to-all-start = ((bf16[8,16,1024]{2,1,0:T(8,128)(2,1)}), bf16[8,16,1024]{2,1,0:T(8,128)(2,1)S(1)}, u32[]{:S(2)}, u32[]{:S(2)}) async-start(bf16[8,16,1024]{2,1,0:T(8,128)(2,1)} %join.1), calls=%async_computation | async-start | bytes 524288 | tf_op jit(solution)/shard_map/all_to_all | solution.py:579
  72.6 12.9 %collective-permute-start.6 = (bf16[2,64,1024]{2,1,0:T(8,128)(2,1)S(1)}, bf16[2,64,1024]{2,1,0:T(8,128)(2,1)S(1)}, u32[]{:S(2)}, u32[]{:S(2)}) collective-permute-start(bf16[2,64,1024]{2,1,0:T(8,128)(2,1)S(1)} %get-tuple-element.61), channel_id=1, source_target_pairs={{0,48},{1,49},{2,50},{3,51},{4,52},{5,53},{6,54},{7,55},{8,56},{9,... | collective-permute-start | bytes 786440 | tf_op jit(solution)/shard_map/ppermute | solution.py:406
  81.3 6.1 %collective-permute-start.19 = (bf16[16,1024]{1,0:T(8,128)(2,1)S(1)}, bf16[16,1024]{1,0:T(8,128)(2,1)S(1)}, u32[]{:S(2)}, u32[]{:S(2)}) collective-permute-start(bf16[16,1024]{1,0:T(8,128)(2,1)S(1)} %depth.1.r0), channel_id=1, source_target_pairs={{0,192},{64,128},{128,64},{192,0},{1,193},{65,129},{129,65},{193,1... | collective-permute-start | bytes 98312 | tf_op jit(solution)/shard_map/ppermute | solution.py:414
  83.9 5.4 %collective-permute-start.18 = (bf16[16,1024]{1,0:T(8,128)(2,1)S(1)}, bf16[16,1024]{1,0:T(8,128)(2,1)S(1)}, u32[]{:S(2)}, u32[]{:S(2)}) collective-permute-start(bf16[16,1024]{1,0:T(8,128)(2,1)S(1)} %depth.1.r0), channel_id=1, source_target_pairs={{0,128},{64,192},{128,0},{192,64},{1,129},{65,193},{129,1},{193,65... | collective-permute-start | bytes 98312 | tf_op jit(solution)/shard_map/ppermute | solution.py:414
  84.3 5.0 %collective-permute-start.17 = (bf16[16,1024]{1,0:T(8,128)(2,1)S(1)}, bf16[16,1024]{1,0:T(8,128)(2,1)S(1)}, u32[]{:S(2)}, u32[]{:S(2)}) collective-permute-start(bf16[16,1024]{1,0:T(8,128)(2,1)S(1)} %depth.1.r0), channel_id=1, source_target_pairs={{0,64},{64,0},{128,192},{192,128},{1,65},{65,1},{129,193},{193,129... | collective-permute-start | bytes 98312 | tf_op jit(solution)/shard_map/ppermute | solution.py:414
